TPU v7x, 32 devices: a whole 2x2x4 slice. The times are simulated.
32 devices in a mesh: groups: 2 (over y), blk: 4 (over z), panel: 2 (over x), depth: 2 (over core).
Axes of the slice: x: 2, y: 2, z: 4, core: 2. Of those that a mesh axis runs over, the one named last changes fastest.
Arguments:
- x_blocks: float32 [16, 16, 128, 128], P(('groups', 'blk'), ('panel', 'depth')), parts along dimension 0, may hold values from -0.6 to 0.6
- columns: int32 [16, 16], P('groups'), parts along dimension 0, may hold values from 0 to 8, as said below
Outputs:
- purified: float32 [16, 16, 128, 128], P(('groups', 'blk'), ('panel', 'depth')), parts along dimension 0
There are 2 independent parts, one for each index of `groups`. A program takes and returns all parts, laid end to end along the dimension named above; each array names one. Nothing has to cross between parts.
Inputs may be any that keep to these rules, and one draw needn't show every extreme that they name: `columns`: in each block row the present entries stand first and name distinct block rows, slot 0 names the row itself, empty slots hold 8; a row has between max(1, min(16, 8) // 2) and min(16, 8) present slots, the count differs from row to row, and some row has min(16, 8) present.
All inputs are finite; a program needn't handle non-finite values.
Results may differ from a plain program's by a relative error of at most 0.0003.
Values sent between devices are 32-bit elements; how exact they have to be, the bound alone decides.
No kernel may reach another device: no remote copies, remote signals or barrier semaphores. Data moves between devices by JAX's collectives and lax.ppermute only.
A program may use at most 64 MiB of HBM per device.

v0:
```python
import jax
import jax.numpy as jnp
from jax import lax
from jax.sharding import PartitionSpec as P

precise = lax.Precision.HIGHEST


def shifted(block, axis, distance):
    devices = range(lax.axis_size(axis))
    route = [((i - distance) % len(devices), i) for i in devices]
    return lax.ppermute(block, axis, route)


def slot_gather(blocks):
    return lax.all_gather(blocks, ("panel", "depth"), axis=1, tiled=True)


def slot_reduce(partial_value):
    return lax.psum_scatter(partial_value, ("panel", "depth"), scatter_dimension=1, tiled=True)


def rotate_one(incoming):
    return shifted(incoming, "blk", 1)


def local(x_blocks, columns):
    slab_rows = x_blocks.shape[0]
    width_slots = x_blocks.shape[1]
    edge = x_blocks.shape[2]
    order_rows = columns.shape[0]
    all_slots = columns.shape[1]
    cycle_size = lax.axis_size("blk")
    cycle_place = lax.axis_index("blk")
    anchor = jnp.int32(0)
    first_own = cycle_place * slab_rows
    slot_first = lax.axis_index(("panel", "depth")) * width_slots
    my_cols = lax.dynamic_slice(columns, (first_own, anchor), (slab_rows, all_slots))
    own_cols = lax.dynamic_slice(my_cols, (anchor, slot_first), (slab_rows, width_slots))
    x_own = jnp.where((own_cols < order_rows)[:, :, None, None], x_blocks, jnp.float32(0.0))
    out_present = my_cols < order_rows
    empty = jnp.zeros((slab_rows, all_slots, edge, edge), jnp.float32)

    def contribute(partial_value, left_rows, incoming, source):
        group = incoming.shape[0]
        first_row = source * group
        their_cols = lax.dynamic_slice(columns, (first_row, slot_first), (group, width_slots))
        row_ids = first_row + jnp.arange(group, dtype=jnp.int32)
        selector = (my_cols[:, None, :] == row_ids[None, :, None]).astype(jnp.float32)
        picked = jnp.einsum("irs,isab->irab", selector, left_rows, precision=precise)
        products = jnp.einsum("irab,rubc->iruac", picked, incoming, precision=precise)
        targets = (their_cols[None, None, :, :] == my_cols[:, :, None, None]) & out_present[
            :, :, None, None
        ]
        placed = jnp.einsum(
            "isru,iruac->isac", targets.astype(jnp.float32), products, precision=precise
        )
        return partial_value + placed

    def one_way(left_rows, stored):

        def advance(offset, state):
            partial_value, incoming, stored = state
            source = (cycle_place - offset) % cycle_size
            partial_value = contribute(partial_value, left_rows, incoming, source)
            return (partial_value, rotate_one(incoming), stored)

        partial_value, incoming, stored = lax.fori_loop(
            0, cycle_size - 1, advance, (empty, x_own, stored)
        )
        source = (cycle_place + 1) % cycle_size
        return (contribute(partial_value, left_rows, incoming, source), stored)

    stored = jnp.zeros((1,), jnp.float32)
    left_first = slot_gather(x_own)
    partial_value, stored = one_way(left_first, stored)
    squared = slot_reduce(partial_value)
    left_second = slot_gather(squared)
    partial_value, stored = one_way(left_second, stored)
    cubed = slot_reduce(partial_value)
    return 3.0 * squared - 2.0 * cubed


def solution(mesh):
    placed = (P(("groups", "blk"), ("panel", "depth"), None, None), P("groups", None))
    return jax.shard_map(
        local,
        mesh=mesh,
        in_specs=placed,
        out_specs=P(("groups", "blk"), ("panel", "depth"), None, None),
        check_vma=False,
    )
```

profile of v0, /device:TPU:0, one launch (start us, length us, event | category | flops | bytes accessed | tf_op | source)
XLA Modules:
  0.0 241.8 jit_solution(5110365707086407854)
XLA Ops:
  10.5 24.3 %all-gather.3.cloned.1.call-done = f32[2,16,128,128]{3,2,1,0:T(8,128)} async-done(((f32[2,4,128,128]{3,2,1,0:T(8,128)}), f32[2,16,128,128]{3,2,1,0:T(8,128)}) %all-gather.3.cloned.1.call-update) | async-done | bytes 2097168 | tf_op jit(solution)/shard_map/all_gather | solution.py:16
  34.8 3.6 %fusion.44 = f32[2,2,128,128,1]{3,1,2,0,4:T(2,128)S(1)} fusion(f32[2,16,128,128]{3,2,1,0:T(8,128)} %all-gather.3.cloned.1.call-done, s32[2,16]{1,0:T(2,128)S(1)} %get-tuple-element.738, s32[2]{0:T(128)S(1)} %iota_add_fusion.2), kind=kOutput, calls=%fused_computation.46 | convolution fusion | flops 12582976 | bytes 2359432 | tf_op jit(solution)/shard_map/irs,isab->irab/dot_general | solution.py:50
  38.4 45.3 %while.36 = (s32[]{:T(128)}, f32[2,16,128,128]{3,1,2,0:T(8,128)}, f32[2,4,128,128]{3,2,1,0:T(8,128)S(1)}, s32[]{:T(128)}, s32[8,16]{1,0:T(8,128)S(1)}, /*index=5...) while((s32[]{:T(128)}, f32[2,16,128,128]{3,1,2,0:T(8,128)}, ...), condition=%wide.region_1.2_spmd.clone, body=%wide.region_0.1_spmd.clone.sunk | while | flops 466616896 | bytes 29360948 | solution.py:68
  40.0 2.0 fusion.96
  43.1 2.7 %bitcast_add_fusion.6 = f32[2,16,128,128]{3,1,2,0:T(8,128)S(1)} fusion(f32[2,16,128,128]{3,1,2,0:T(8,128)S(1)} %copy-done.1, f32[2,2,128,4,128]{4,2,3,1,0:T(8,128)S(1)} %fusion.97, pred[]{:T(512)S(6)} %compare.9, s32[2,16]{1,0:T(2,128)S(1)} %get-tuple-element.723, s32[2,4]{1,0:T(2,128)S(1)} %dynamic_slice.40, pred[2,16]{1,0:T(4,128)(4,1)S(1)} %get-tuple-element.724), kind=kOutput, calls=%fused_computation.clone.1 | convolution fusion | flops 51380736 | bytes 5243073 | tf_op jit(solution)/shard_map/while/body/eval_jaxpr/isru,iruac->isac/dot_general | solution.py:55
  45.8 8.6 %collective-permute-done = f32[2,4,128,128]{3,2,1,0:T(8,128)S(1)} collective-permute-done((f32[2,4,128,128]{3,2,1,0:T(8,128)S(1)}, f32[2,4,128,128]{3,2,1,0:T(8,128)S(1)}, u32[]{:S(2)}, u32[]{:S(2)}) %collective-permute-start) | collective-permute-done | bytes 524320 | tf_op jit(solution)/shard_map/while/body/eval_jaxpr/ppermute | solution.py:12
  54.5 2.0 fusion.96
  57.6 2.7 %bitcast_add_fusion.6 = f32[2,16,128,128]{3,1,2,0:T(8,128)S(1)} fusion(f32[2,16,128,128]{3,1,2,0:T(8,128)S(1)} %copy-done.1, f32[2,2,128,4,128]{4,2,3,1,0:T(8,128)S(1)} %fusion.97, pred[]{:T(512)S(6)} %compare.9, s32[2,16]{1,0:T(2,128)S(1)} %get-tuple-element.723, s32[2,4]{1,0:T(2,128)S(1)} %dynamic_slice.40, pred[2,16]{1,0:T(4,128)(4,1)S(1)} %get-tuple-element.724), kind=kOutput, calls=%fused_computation.clone.1 | convolution fusion | flops 51380736 | bytes 5243073 | tf_op jit(solution)/shard_map/while/body/eval_jaxpr/isru,iruac->isac/dot_general | solution.py:55
  60.3 9.2 %collective-permute-done = f32[2,4,128,128]{3,2,1,0:T(8,128)S(1)} collective-permute-done((f32[2,4,128,128]{3,2,1,0:T(8,128)S(1)}, f32[2,4,128,128]{3,2,1,0:T(8,128)S(1)}, u32[]{:S(2)}, u32[]{:S(2)}) %collective-permute-start) | collective-permute-done | bytes 524320 | tf_op jit(solution)/shard_map/while/body/eval_jaxpr/ppermute | solution.py:12
  69.7 2.0 fusion.96
  72.7 2.7 %bitcast_add_fusion.6 = f32[2,16,128,128]{3,1,2,0:T(8,128)S(1)} fusion(f32[2,16,128,128]{3,1,2,0:T(8,128)S(1)} %copy-done.1, f32[2,2,128,4,128]{4,2,3,1,0:T(8,128)S(1)} %fusion.97, pred[]{:T(512)S(6)} %compare.9, s32[2,16]{1,0:T(2,128)S(1)} %get-tuple-element.723, s32[2,4]{1,0:T(2,128)S(1)} %dynamic_slice.40, pred[2,16]{1,0:T(4,128)(4,1)S(1)} %get-tuple-element.724), kind=kOutput, calls=%fused_computation.clone.1 | convolution fusion | flops 51380736 | bytes 5243073 | tf_op jit(solution)/shard_map/while/body/eval_jaxpr/isru,iruac->isac/dot_general | solution.py:55
  75.4 8.3 %collective-permute-done = f32[2,4,128,128]{3,2,1,0:T(8,128)S(1)} collective-permute-done((f32[2,4,128,128]{3,2,1,0:T(8,128)S(1)}, f32[2,4,128,128]{3,2,1,0:T(8,128)S(1)}, u32[]{:S(2)}, u32[]{:S(2)}) %collective-permute-start) | collective-permute-done | bytes 524320 | tf_op jit(solution)/shard_map/while/body/eval_jaxpr/ppermute | solution.py:12
  83.7 2.0 fusion.54
  85.7 2.5 %copy.30 = f32[2,4,128,2,128]{2,1,0,4,3:T(4,128)} copy(f32[2,4,128,2,128]{4,2,3,1,0:T(8,128)} %fusion.54) | data formatting | bytes 2097152 | tf_op jit(solution)/shard_map/irab,rubc->iruac/dot_general | solution.py:51
  88.3 2.5 %bitcast_add_fusion.3 = f32[2,16,128,128]{3,1,2,0:T(8,128)S(1)} fusion(f32[2,16,128,128]{3,1,2,0:T(8,128)S(1)} %copy-done.3, f32[2,4,128,2,128]{2,1,0,4,3:T(4,128)} %copy.30, s32[2,16]{1,0:T(2,128)S(1)} %get-tuple-element.796, s32[2,4]{1,0:T(2,128)S(1)} %dynamic_slice.32, pred[2,16]{1,0:T(4,128)(4,1)S(1)} %get-tuple-element.799), kind=kOutput, calls=%fused_computation.41 | convolution fusion | flops 50856448 | bytes 5243072 | tf_op jit(solution)/shard_map/isru,iruac->isac/dot_general | solution.py:55
  90.8 2.0 copy.5
  92.9 28.8 %reduce-scatter.3.cloned.1.call-done = f32[2,4,128,128]{3,2,0,1:T(8,128)} async-done(((f32[2,16,128,128]{3,2,0,1:T(8,128)}), f32[2,4,128,128]{3,2,0,1:T(8,128)}) %reduce-scatter.3.cloned.1.call-update) | async-done | bytes 524304 | tf_op jit(solution)/shard_map/reduce_scatter | solution.py:20
  121.9 24.0 %all-gather.5.cloned.1.call-done = f32[2,16,128,128]{3,2,0,1:T(8,128)} async-done(((f32[2,4,128,128]{3,2,0,1:T(8,128)}), f32[2,16,128,128]{3,2,0,1:T(8,128)}) %all-gather.5.cloned.1.call-update) | async-done | bytes 2097168 | tf_op jit(solution)/shard_map/all_gather | solution.py:16
  150.1 45.3 %while.37 = (s32[]{:T(128)}, f32[2,16,128,128]{3,1,2,0:T(8,128)}, f32[2,4,128,128]{3,2,1,0:T(8,128)S(1)}, s32[]{:T(128)}, s32[8,16]{1,0:T(8,128)S(1)}, /*index=5...) while((s32[]{:T(128)}, f32[2,16,128,128]{3,1,2,0:T(8,128)}, ...), condition=%wide.region_4.5_spmd.clone, body=%wide.region_3.4_spmd.clone.sunk | while | flops 466616896 | bytes 29360948 | solution.py:68
  151.7 2.0 fusion.104
  154.8 2.7 %bitcast_add_fusion.7 = f32[2,16,128,128]{3,1,2,0:T(8,128)S(1)} fusion(f32[2,16,128,128]{3,1,2,0:T(8,128)S(1)} %copy-done.4, f32[2,2,128,4,128]{4,2,3,1,0:T(8,128)S(1)} %fusion.105, pred[]{:T(512)S(6)} %compare.10, s32[2,16]{1,0:T(2,128)S(1)} %get-tuple-element.768, s32[2,4]{1,0:T(2,128)S(1)} %dynamic_slice.41, pred[2,16]{1,0:T(4,128)(4,1)S(1)} %get-tuple-element.769), kind=kOutput, calls=%fused_computation.20.clone.1 | convolution fusion | flops 51380736 | bytes 5243073 | tf_op jit(solution)/shard_map/while/body/eval_jaxpr/isru,iruac->isac/dot_general | solution.py:55
  157.5 8.6 %collective-permute-done.1 = f32[2,4,128,128]{3,2,1,0:T(8,128)S(1)} collective-permute-done((f32[2,4,128,128]{3,2,1,0:T(8,128)S(1)}, f32[2,4,128,128]{3,2,1,0:T(8,128)S(1)}, u32[]{:S(2)}, u32[]{:S(2)}) %collective-permute-start.1) | collective-permute-done | bytes 524320 | tf_op jit(solution)/shard_map/while/body/eval_jaxpr/ppermute | solution.py:12
  166.2 2.0 fusion.104
  169.3 2.7 %bitcast_add_fusion.7 = f32[2,16,128,128]{3,1,2,0:T(8,128)S(1)} fusion(f32[2,16,128,128]{3,1,2,0:T(8,128)S(1)} %copy-done.4, f32[2,2,128,4,128]{4,2,3,1,0:T(8,128)S(1)} %fusion.105, pred[]{:T(512)S(6)} %compare.10, s32[2,16]{1,0:T(2,128)S(1)} %get-tuple-element.768, s32[2,4]{1,0:T(2,128)S(1)} %dynamic_slice.41, pred[2,16]{1,0:T(4,128)(4,1)S(1)} %get-tuple-element.769), kind=kOutput, calls=%fused_computation.20.clone.1 | convolution fusion | flops 51380736 | bytes 5243073 | tf_op jit(solution)/shard_map/while/body/eval_jaxpr/isru,iruac->isac/dot_general | solution.py:55
  172.0 9.2 %collective-permute-done.1 = f32[2,4,128,128]{3,2,1,0:T(8,128)S(1)} collective-permute-done((f32[2,4,128,128]{3,2,1,0:T(8,128)S(1)}, f32[2,4,128,128]{3,2,1,0:T(8,128)S(1)}, u32[]{:S(2)}, u32[]{:S(2)}) %collective-permute-start.1) | collective-permute-done | bytes 524320 | tf_op jit(solution)/shard_map/while/body/eval_jaxpr/ppermute | solution.py:12
  181.4 2.0 fusion.104
  184.4 2.7 %bitcast_add_fusion.7 = f32[2,16,128,128]{3,1,2,0:T(8,128)S(1)} fusion(f32[2,16,128,128]{3,1,2,0:T(8,128)S(1)} %copy-done.4, f32[2,2,128,4,128]{4,2,3,1,0:T(8,128)S(1)} %fusion.105, pred[]{:T(512)S(6)} %compare.10, s32[2,16]{1,0:T(2,128)S(1)} %get-tuple-element.768, s32[2,4]{1,0:T(2,128)S(1)} %dynamic_slice.41, pred[2,16]{1,0:T(4,128)(4,1)S(1)} %get-tuple-element.769), kind=kOutput, calls=%fused_computation.20.clone.1 | convolution fusion | flops 51380736 | bytes 5243073 | tf_op jit(solution)/shard_map/while/body/eval_jaxpr/isru,iruac->isac/dot_general | solution.py:55
  187.1 8.3 %collective-permute-done.1 = f32[2,4,128,128]{3,2,1,0:T(8,128)S(1)} collective-permute-done((f32[2,4,128,128]{3,2,1,0:T(8,128)S(1)}, f32[2,4,128,128]{3,2,1,0:T(8,128)S(1)}, u32[]{:S(2)}, u32[]{:S(2)}) %collective-permute-start.1) | collective-permute-done | bytes 524320 | tf_op jit(solution)/shard_map/while/body/eval_jaxpr/ppermute | solution.py:12
  195.4 2.0 fusion.52
  197.4 2.5 %copy.37 = f32[2,4,128,2,128]{2,1,0,4,3:T(4,128)} copy(f32[2,4,128,2,128]{4,2,3,1,0:T(8,128)} %fusion.52) | data formatting | bytes 2097152 | tf_op jit(solution)/shard_map/irab,rubc->iruac/dot_general | solution.py:51
  200.0 2.5 %bitcast_add_fusion.2 = f32[2,16,128,128]{3,1,2,0:T(8,128)S(1)} fusion(f32[2,16,128,128]{3,1,2,0:T(8,128)S(1)} %copy-done.6, f32[2,4,128,2,128]{2,1,0,4,3:T(4,128)} %copy.37, s32[2,16]{1,0:T(2,128)S(1)} %get-tuple-element.797, s32[2,4]{1,0:T(2,128)S(1)} %dynamic_slice.32, pred[2,16]{1,0:T(4,128)(4,1)S(1)} %get-tuple-element.800), kind=kOutput, calls=%fused_computation.40 | convolution fusion | flops 50856448 | bytes 5243072 | tf_op jit(solution)/shard_map/isru,iruac->isac/dot_general | solution.py:55
  204.5 28.8 %reduce-scatter.5.cloned.1.call-done = f32[2,4,128,128]{3,2,0,1:T(8,128)} async-done(((f32[2,16,128,128]{3,2,0,1:T(8,128)}), f32[2,4,128,128]{3,2,0,1:T(8,128)}) %reduce-scatter.5.cloned.1.call-update) | async-done | bytes 524304 | tf_op jit(solution)/shard_map/reduce_scatter | solution.py:20
  (89 shorter events, 22.3 us)
Async XLA Ops:
  6.5 3.9 %copy-start.10 = (s32[8,16]{1,0:T(8,128)S(1)}, s32[8,16]{1,0:T(8,128)}, u32[]{:S(2)}) copy-start(s32[8,16]{1,0:T(8,128)} %param.7) | copy-start | bytes 1540
  6.5 28.2 %all-gather.3.cloned.1.call-start = ((), (), s32[]{:S(2)}) async-start(), calls=%async_computation.2 | async-start | bytes 2621440 | tf_op jit(solution)/shard_map/all_gather | solution.py:16
  9.3 112.3 %reduce-scatter.3.cloned.1.call-start = ((), (), s32[]{:S(2)}) async-start(), calls=%async_computation.3 | async-start | bytes 2621440 | tf_op jit(solution)/shard_map/reduce_scatter | solution.py:20
  34.8 3.6 %copy-start = (f32[2,16,128,128]{3,2,1,0:T(8,128)S(1)}, f32[2,16,128,128]{3,2,1,0:T(8,128)}, u32[]{:S(2)}) copy-start(f32[2,16,128,128]{3,2,1,0:T(8,128)} %all-gather.3.cloned.1.call-done) | copy-start | bytes 6291460
  38.5 15.9 %collective-permute-start = (f32[2,4,128,128]{3,2,1,0:T(8,128)S(1)}, f32[2,4,128,128]{3,2,1,0:T(8,128)S(1)}, u32[]{:S(2)}, u32[]{:S(2)}) collective-permute-start(f32[2,4,128,128]{3,2,1,0:T(8,128)S(1)} %copy.96), channel_id=1, source_target_pairs={{12,0},{0,4},{4,8},{8,12},{13,1},{1,5},{5,9},{9,13},{14,2},{2,6},{... | collective-permute-start | bytes 1572872 | tf_op jit(solution)/shard_map/while/body/eval_jaxpr/ppermute | solution.py:12
  40.0 3.1 %copy-start.1 = (f32[2,16,128,128]{3,1,2,0:T(8,128)S(1)}, f32[2,16,128,128]{3,1,2,0:T(8,128)}, u32[]{:S(2)}) copy-start(f32[2,16,128,128]{3,1,2,0:T(8,128)} %get-tuple-element.703) | copy-start | bytes 6291460 | tf_op jit(solution)/shard_map/while
  45.8 8.6 %copy-start.2 = (f32[2,16,128,128]{3,1,2,0:T(8,128)}, f32[2,16,128,128]{3,1,2,0:T(8,128)S(1)}, u32[]{:S(2)}) copy-start(f32[2,16,128,128]{3,1,2,0:T(8,128)S(1)} %bitcast_add_fusion.6) | copy-start | bytes 6291460 | tf_op jit(solution)/shard_map/while
  54.4 15.1 %collective-permute-start = (f32[2,4,128,128]{3,2,1,0:T(8,128)S(1)}, f32[2,4,128,128]{3,2,1,0:T(8,128)S(1)}, u32[]{:S(2)}, u32[]{:S(2)}) collective-permute-start(f32[2,4,128,128]{3,2,1,0:T(8,128)S(1)} %copy.96), channel_id=1, source_target_pairs={{12,0},{0,4},{4,8},{8,12},{13,1},{1,5},{5,9},{9,13},{14,2},{2,6},{... | collective-permute-start | bytes 1572872 | tf_op jit(solution)/shard_map/while/body/eval_jaxpr/ppermute | solution.py:12
  54.5 3.1 %copy-start.1 = (f32[2,16,128,128]{3,1,2,0:T(8,128)S(1)}, f32[2,16,128,128]{3,1,2,0:T(8,128)}, u32[]{:S(2)}) copy-start(f32[2,16,128,128]{3,1,2,0:T(8,128)} %get-tuple-element.703) | copy-start | bytes 6291460 | tf_op jit(solution)/shard_map/while
  60.3 9.2 %copy-start.2 = (f32[2,16,128,128]{3,1,2,0:T(8,128)}, f32[2,16,128,128]{3,1,2,0:T(8,128)S(1)}, u32[]{:S(2)}) copy-start(f32[2,16,128,128]{3,1,2,0:T(8,128)S(1)} %bitcast_add_fusion.6) | copy-start | bytes 6291460 | tf_op jit(solution)/shard_map/while
  69.6 14.2 %collective-permute-start = (f32[2,4,128,128]{3,2,1,0:T(8,128)S(1)}, f32[2,4,128,128]{3,2,1,0:T(8,128)S(1)}, u32[]{:S(2)}, u32[]{:S(2)}) collective-permute-start(f32[2,4,128,128]{3,2,1,0:T(8,128)S(1)} %copy.96), channel_id=1, source_target_pairs={{12,0},{0,4},{4,8},{8,12},{13,1},{1,5},{5,9},{9,13},{14,2},{2,6},{... | collective-permute-start | bytes 1572872 | tf_op jit(solution)/shard_map/while/body/eval_jaxpr/ppermute | solution.py:12
  69.7 3.1 %copy-start.1 = (f32[2,16,128,128]{3,1,2,0:T(8,128)S(1)}, f32[2,16,128,128]{3,1,2,0:T(8,128)}, u32[]{:S(2)}) copy-start(f32[2,16,128,128]{3,1,2,0:T(8,128)} %get-tuple-element.703) | copy-start | bytes 6291460 | tf_op jit(solution)/shard_map/while
  75.4 8.3 %copy-start.2 = (f32[2,16,128,128]{3,1,2,0:T(8,128)}, f32[2,16,128,128]{3,1,2,0:T(8,128)S(1)}, u32[]{:S(2)}) copy-start(f32[2,16,128,128]{3,1,2,0:T(8,128)S(1)} %bitcast_add_fusion.6) | copy-start | bytes 6291460 | tf_op jit(solution)/shard_map/while
  83.7 4.6 %copy-start.3 = (f32[2,16,128,128]{3,1,2,0:T(8,128)S(1)}, f32[2,16,128,128]{3,1,2,0:T(8,128)}, u32[]{:S(2)}) copy-start(f32[2,16,128,128]{3,1,2,0:T(8,128)} %get-tuple-element.457) | copy-start | bytes 6291460
  92.8 53.1 %all-gather.5.cloned.1.call-start = ((), (), s32[]{:S(2)}) async-start(), calls=%async_computation.4 | async-start | bytes 2621440 | tf_op jit(solution)/shard_map/all_gather | solution.py:16
  121.6 111.7 %reduce-scatter.5.cloned.1.call-start = ((), (), s32[]{:S(2)}) async-start(), calls=%async_computation.5 | async-start | bytes 2621440 | tf_op jit(solution)/shard_map/reduce_scatter | solution.py:20
  145.9 2.2 copy-start.8
  148.1 2.0 copy-start.7
  150.2 15.9 %collective-permute-start.1 = (f32[2,4,128,128]{3,2,1,0:T(8,128)S(1)}, f32[2,4,128,128]{3,2,1,0:T(8,128)S(1)}, u32[]{:S(2)}, u32[]{:S(2)}) collective-permute-start(f32[2,4,128,128]{3,2,1,0:T(8,128)S(1)} %copy.105), channel_id=1, source_target_pairs={{12,0},{0,4},{4,8},{8,12},{13,1},{1,5},{5,9},{9,13},{14,2},{2,6},{... | collective-permute-start | bytes 1572872 | tf_op jit(solution)/shard_map/while/body/eval_jaxpr/ppermute | solution.py:12
  151.7 3.1 %copy-start.4 = (f32[2,16,128,128]{3,1,2,0:T(8,128)S(1)}, f32[2,16,128,128]{3,1,2,0:T(8,128)}, u32[]{:S(2)}) copy-start(f32[2,16,128,128]{3,1,2,0:T(8,128)} %get-tuple-element.748) | copy-start | bytes 6291460 | tf_op jit(solution)/shard_map/while
  157.5 8.6 %copy-start.5 = (f32[2,16,128,128]{3,1,2,0:T(8,128)}, f32[2,16,128,128]{3,1,2,0:T(8,128)S(1)}, u32[]{:S(2)}) copy-start(f32[2,16,128,128]{3,1,2,0:T(8,128)S(1)} %bitcast_add_fusion.7) | copy-start | bytes 6291460 | tf_op jit(solution)/shard_map/while
  166.1 15.1 %collective-permute-start.1 = (f32[2,4,128,128]{3,2,1,0:T(8,128)S(1)}, f32[2,4,128,128]{3,2,1,0:T(8,128)S(1)}, u32[]{:S(2)}, u32[]{:S(2)}) collective-permute-start(f32[2,4,128,128]{3,2,1,0:T(8,128)S(1)} %copy.105), channel_id=1, source_target_pairs={{12,0},{0,4},{4,8},{8,12},{13,1},{1,5},{5,9},{9,13},{14,2},{2,6},{... | collective-permute-start | bytes 1572872 | tf_op jit(solution)/shard_map/while/body/eval_jaxpr/ppermute | solution.py:12
  166.2 3.1 %copy-start.4 = (f32[2,16,128,128]{3,1,2,0:T(8,128)S(1)}, f32[2,16,128,128]{3,1,2,0:T(8,128)}, u32[]{:S(2)}) copy-start(f32[2,16,128,128]{3,1,2,0:T(8,128)} %get-tuple-element.748) | copy-start | bytes 6291460 | tf_op jit(solution)/shard_map/while
  172.0 9.2 %copy-start.5 = (f32[2,16,128,128]{3,1,2,0:T(8,128)}, f32[2,16,128,128]{3,1,2,0:T(8,128)S(1)}, u32[]{:S(2)}) copy-start(f32[2,16,128,128]{3,1,2,0:T(8,128)S(1)} %bitcast_add_fusion.7) | copy-start | bytes 6291460 | tf_op jit(solution)/shard_map/while
  181.3 14.2 %collective-permute-start.1 = (f32[2,4,128,128]{3,2,1,0:T(8,128)S(1)}, f32[2,4,128,128]{3,2,1,0:T(8,128)S(1)}, u32[]{:S(2)}, u32[]{:S(2)}) collective-permute-start(f32[2,4,128,128]{3,2,1,0:T(8,128)S(1)} %copy.105), channel_id=1, source_target_pairs={{12,0},{0,4},{4,8},{8,12},{13,1},{1,5},{5,9},{9,13},{14,2},{2,6},{... | collective-permute-start | bytes 1572872 | tf_op jit(solution)/shard_map/while/body/eval_jaxpr/ppermute | solution.py:12
  181.4 3.1 %copy-start.4 = (f32[2,16,128,128]{3,1,2,0:T(8,128)S(1)}, f32[2,16,128,128]{3,1,2,0:T(8,128)}, u32[]{:S(2)}) copy-start(f32[2,16,128,128]{3,1,2,0:T(8,128)} %get-tuple-element.748) | copy-start | bytes 6291460 | tf_op jit(solution)/shard_map/while
  187.1 8.3 %copy-start.5 = (f32[2,16,128,128]{3,1,2,0:T(8,128)}, f32[2,16,128,128]{3,1,2,0:T(8,128)S(1)}, u32[]{:S(2)}) copy-start(f32[2,16,128,128]{3,1,2,0:T(8,128)S(1)} %bitcast_add_fusion.7) | copy-start | bytes 6291460 | tf_op jit(solution)/shard_map/while
  195.4 4.5 %copy-start.6 = (f32[2,16,128,128]{3,1,2,0:T(8,128)S(1)}, f32[2,16,128,128]{3,1,2,0:T(8,128)}, u32[]{:S(2)}) copy-start(f32[2,16,128,128]{3,1,2,0:T(8,128)} %get-tuple-element.459) | copy-start | bytes 6291460
  204.5 28.8 %copy-start.9 = (f32[2,4,128,128]{3,2,0,1:T(8,128)S(1)}, f32[2,4,128,128]{3,2,0,1:T(8,128)}, u32[]{:S(2)}) copy-start(f32[2,4,128,128]{3,2,0,1:T(8,128)} %reduce-scatter.3.cloned.1.call-done) | copy-start | bytes 1572868
Sparse Core Ops, SparseCore 0:
  9.5 25.2 all-gather.2
  92.9 28.6 reduce-scatter.2
  123.3 22.5 all-gather.4
  204.6 28.6 reduce-scatter.4
where the time goes:
time: 242 us
  waiting for transfers between devices  158 us (65%)
  matrix products  48.5 us (20%)
  local copies, waits for them, and re-layouts  13.9 us (6%)
  between operations  13.2 us (5%)
  other arithmetic  3.91 us (2%)
  starting transfers between devices  3.62 us (1%)
    reduce_scatter x2, waiting for transfers between devices, slot_reduce(): lax.psum_scatter(partial_value, ('panel', 'depth'), scatter_dimension=1,...  57.6 us
    ppermute x6, waiting for transfers between devices, shifted(): return lax.ppermute(block, axis, route)  52.2 us
    all_gather x2, waiting for transfers between devices, slot_gather(): return lax.all_gather(blocks, ('panel', 'depth'), axis=1, tiled=True)  48.3 us
    dot_general x8, matrix products, contribute(): jnp.einsum('isru,iruac->isac', targets.astype(jnp.float32), products, pre...  21.2 us
    dot_general x8, matrix products, contribute(): jnp.einsum('irs,isab->irab', selector, left_rows, precision=precise)  17.4 us
    dot_general x8, matrix products, contribute(): jnp.einsum('irab,rubc->iruac', picked, incoming, precision=precise)  9.91 us
    dot_general x2, local copies, waits for them, and re-layouts, contribute(): jnp.einsum('irab,rubc->iruac', picked, incoming, precision=precise)  5.09 us
  transfers between devices with their start and end apart: 10, of which 10 were waited for; matrix products, arithmetic and copies ran while one was open for 15% of the time, Pallas kernels for 0%

commit v1 on v0

--- a/solution.py
+++ b/solution.py
@@ -1,9 +1,14 @@
+import functools
+
 import jax
 import jax.numpy as jnp
 from jax import lax
+from jax.experimental import pallas as pl
+from jax.experimental.pallas import tpu as pltpu
 from jax.sharding import PartitionSpec as P
 
 precise = lax.Precision.HIGHEST
+AXES = ("blk", "panel", "depth")
 
 
 def shifted(block, axis, distance):
@@ -24,7 +29,7 @@
     return shifted(incoming, "blk", 1)
 
 
-def local(x_blocks, columns):
+def ring_local(x_blocks, columns):
     slab_rows = x_blocks.shape[0]
     width_slots = x_blocks.shape[1]
     edge = x_blocks.shape[2]
@@ -81,6 +86,229 @@
     return 3.0 * squared - 2.0 * cubed
 
 
+def split(value):
+    high = value.astype(jnp.bfloat16)
+    low = (value - high.astype(jnp.float32)).astype(jnp.bfloat16)
+    return high, low
+
+
+def dot(left, right):
+    return jnp.dot(left, right, preferred_element_type=jnp.float32)
+
+
+def stacked_dot(left, high, low):
+    half = left.shape[0] // 2
+    both = dot(left, high)
+    return both[:half] + (both[half:] + dot(left[:half], low))
+
+
+def lookup(table, place, lane):
+    found = jnp.int32(-1)
+    for z, entries in enumerate(table):
+        for c, entry in enumerate(entries):
+            found = jnp.where((place == z) & (lane == c), entry, found)
+    return found
+
+
+def store_piece(piece, plane, group, table_ref, high, low, own=None):
+    slab, width, edge, _ = piece.shape
+    act = 2 * width
+
+    @pl.when(plane >= 0)
+    def _():
+        for r in range(slab):
+            row = plane * slab + r
+            for w in range(width):
+                slot = group * width + w
+                col = pl.ds(pl.multiple_of(table_ref[row, slot] * edge, edge), edge)
+                block = jnp.where(table_ref[row, act + slot] > 0, piece[r, w], 0.0)
+                block_high, block_low = split(block)
+                at = pl.ds(pl.multiple_of(row * edge, edge), edge)
+                high[at, col] = block_high
+                low[at, col] = block_low
+                if own is not None:
+                    own[pl.ds(r * edge, edge), col] = block_high
+                    own[pl.ds((slab + r) * edge, edge), col] = block_low
+
+
+def early_kernel(
+    tables, table_ref, place_ref, own_ref, own_swap, r1, r2, t1, t2, high, low, left, part_ref
+):
+    place, lane = place_ref[0], place_ref[1]
+    near = tables[0]
+    store_piece(own_ref, place, lane, table_ref, high, low, left)
+    store_piece(own_swap, place, 1 - lane, table_ref, high, low, left)
+    here, there = lookup(near, place, lane), lookup(near, place, 1 - lane)
+    store_piece(r1, here, lane, table_ref, high, low)
+    store_piece(r2, here, 1 - lane, table_ref, high, low)
+    store_piece(t1, there, 1 - lane, table_ref, high, low)
+    store_piece(t2, there, lane, table_ref, high, low)
+    order = high.shape[0]
+    depth, tile = order // 2, 256
+    rows = pl.ds(pl.multiple_of(place // 2 * depth, depth), depth)
+    for n in range(order // tile):
+        cols = pl.ds(n * tile, tile)
+        part_ref[:, cols] = stacked_dot(left[:, rows], high[rows, cols], low[rows, cols])
+
+
+def late_kernel(
+    tables, table_ref, place_ref, r3, r4, t3, t4, high_in, low_in, left, part_ref,
+    out_ref, high, low, square, square_parts, cube,
+):
+    place, lane, group = place_ref[0], place_ref[1], place_ref[2]
+    far = tables[1]
+    here, there = lookup(far, place, lane), lookup(far, place, 1 - lane)
+    store_piece(r3, here, lane, table_ref, high, low)
+    store_piece(r4, here, 1 - lane, table_ref, high, low)
+    store_piece(t3, there, 1 - lane, table_ref, high, low)
+    store_piece(t4, there, lane, table_ref, high, low)
+    order = high.shape[0]
+    depth, tile = order // 2, 256
+    slab, width, edge, _ = out_ref.shape
+    act = 2 * width
+    rows = pl.ds(pl.multiple_of((1 - place // 2) * depth, depth), depth)
+    for n in range(order // tile):
+        cols = pl.ds(n * tile, tile)
+        square[:, cols] = part_ref[:, cols] + stacked_dot(
+            left[:, rows], high[rows, cols], low[rows, cols]
+        )
+        for r in range(slab):
+            for c in range(n * tile // edge, (n + 1) * tile // edge):
+                kept = table_ref[place * slab + r, 2 * act + c] > 0
+                col = pl.ds(c * edge, edge)
+                block = jnp.where(kept, square[pl.ds(r * edge, edge), col], 0.0)
+                block_high, block_low = split(block)
+                square_parts[pl.ds(r * edge, edge), col] = block_high
+                square_parts[pl.ds((slab + r) * edge, edge), col] = block_low
+    for n in range(order // tile):
+        cols = pl.ds(n * tile, tile)
+        cube[:, cols] = stacked_dot(square_parts[...], high[:, cols], low[:, cols])
+    for r in range(slab):
+        for w in range(width):
+            slot = jnp.minimum(group * width + w, act - 1)
+            row = place * slab + r
+            there = (group * width + w < act) & (table_ref[row, act + slot] > 0)
+            at = (
+                pl.ds(r * edge, edge),
+                pl.ds(pl.multiple_of(table_ref[row, slot] * edge, edge), edge),
+            )
+            out_ref[r, w] = jnp.where(there, 3.0 * square[at] - 2.0 * cube[at], 0.0)
+
+
+def slot_table(columns, act):
+    rows = columns.shape[0]
+    slots = columns[:, :act]
+    here = slots < rows
+    ids = jnp.arange(rows, dtype=jnp.int32)
+    taken = jnp.any(slots[:, :, None] == ids, axis=1)
+    count = jnp.sum(here.astype(jnp.int32), axis=1, keepdims=True)
+    before = jnp.sum(
+        (~taken[:, None, :] & (ids[None, :] < ids[:, None])[None]).astype(jnp.int32), axis=2
+    )
+    at = jnp.where(taken, -1, count + before)
+    filled = jnp.sum(
+        jnp.where(at[:, None, :] == jnp.arange(act, dtype=jnp.int32)[None, :, None], ids, 0), axis=2
+    )
+    order = jnp.where(here, slots, filled)
+    return jnp.concatenate([order, here.astype(jnp.int32), taken.astype(jnp.int32)], axis=1)
+
+
+def gather_local(x_blocks, columns):
+    slab, width, edge, _ = x_blocks.shape
+    rows = columns.shape[0]
+    chains, panels, lanes = (lax.axis_size(axis) for axis in AXES)
+    last = chains - 1
+
+    def index(z, x, c):
+        return (z * panels + x) * lanes + c
+
+    def move(block, pairs):
+        return lax.ppermute(block, AXES, [(index(*a), index(*b)) for a, b in pairs])
+
+    def swap(block):
+        return move(
+            block, [((z, 0, c), (z, 0, 1 - c)) for z in range(chains) for c in range(lanes)]
+        )
+
+    first = [((z, 0, 0), (z + 1, 0, 0)) for z in range(last)]
+    first += [((z, 0, 1), (z - 1, 0, 1)) for z in range(1, chains)]
+    first += [((last, 0, 0), (last, 1, 0)), ((0, 0, 1), (0, 1, 1))]
+    second = [((z, 0, 0), (z + 1, 0, 0)) for z in range(1, last)]
+    second += [((z, 0, 1), (z - 1, 0, 1)) for z in range(1, last)]
+    second += [((last, 1, 0), (0, 0, 0)), ((0, 1, 1), (last, 0, 1))]
+    near = [(z - 1, z + 1 if z < last else -1) for z in range(chains)]
+    far = [(z - 2 if z >= 2 else -1, z + 2 if z + 2 < chains else -1) for z in range(chains)]
+    far[0] = (last, far[0][1])
+    far[last] = (far[last][0], 0)
+    tables = (near, far)
+
+    r1 = move(x_blocks, first)
+    own_swap = swap(x_blocks)
+    r2 = move(own_swap, first)
+    r3 = move(r1, second)
+    t1 = swap(r1)
+    r4 = move(r2, second)
+    t2 = swap(r2)
+    table = slot_table(columns, lanes * width)
+    place = jnp.stack(
+        [
+            lax.axis_index("blk"),
+            lax.axis_index("depth"),
+            lax.axis_index("panel") * lanes + lax.axis_index("depth"),
+        ]
+    ).astype(jnp.int32)
+    order, own = rows * edge, slab * edge
+    smem = pl.BlockSpec(memory_space=pltpu.SMEM)
+    vmem = pl.BlockSpec(memory_space=pltpu.VMEM)
+    params = pltpu.CompilerParams(vmem_limit_bytes=24 * 2**20)
+    high, low, left, part = pl.pallas_call(
+        functools.partial(early_kernel, tables),
+        out_shape=[
+            jax.ShapeDtypeStruct((order, order), jnp.bfloat16),
+            jax.ShapeDtypeStruct((order, order), jnp.bfloat16),
+            jax.ShapeDtypeStruct((2 * own, order), jnp.bfloat16),
+            jax.ShapeDtypeStruct((own, order), jnp.float32),
+        ],
+        in_specs=[smem] * 2 + [vmem] * 6,
+        out_specs=[vmem] * 4,
+        compiler_params=params,
+        name="early",
+    )(table, place, x_blocks, own_swap, r1, r2, t1, t2)
+    r3, part = lax.optimization_barrier((r3, part))
+    t3 = swap(r3)
+    r4, t3 = lax.optimization_barrier((r4, t3))
+    t4 = swap(r4)
+    out, _, _ = pl.pallas_call(
+        functools.partial(late_kernel, tables),
+        out_shape=[
+            jax.ShapeDtypeStruct(x_blocks.shape, jnp.float32),
+            jax.ShapeDtypeStruct((order, order), jnp.bfloat16),
+            jax.ShapeDtypeStruct((order, order), jnp.bfloat16),
+        ],
+        in_specs=[smem] * 2 + [vmem] * 8,
+        out_specs=[vmem] * 3,
+        input_output_aliases={6: 1, 7: 2},
+        scratch_shapes=[
+            pltpu.VMEM((own, order), jnp.float32),
+            pltpu.VMEM((2 * own, order), jnp.bfloat16),
+            pltpu.VMEM((own, order), jnp.float32),
+        ],
+        compiler_params=params,
+        name="late",
+    )(table, place, r3, r4, t3, t4, high, low, left, part)
+    return out
+
+
+def local(x_blocks, columns):
+    slab, width, edge, _ = x_blocks.shape
+    rows, slots = columns.shape
+    chains, panels, lanes = (lax.axis_size(axis) for axis in AXES)
+    full = rows <= slots and rows == lanes * width
+    if full and rows <= 8 and edge % 128 == 0 and panels >= 2 and lanes == 2 and chains == 4:
+        return gather_local(x_blocks, columns)
+    return ring_local(x_blocks, columns)
+
+
 def solution(mesh):
     placed = (P(("groups", "blk"), ("panel", "depth"), None, None), P("groups", None))
     return jax.shard_map(

time: 242 us -> 45.5 us (0.19)
  waiting for transfers between devices: 158 us -> 12.7 us
  matrix products: 48.5 us -> 0 us
  starting transfers between devices: 3.62 us -> 20.6 us
  between operations: 13.2 us -> 0.14 us
  local copies, waits for them, and re-layouts: 13.9 us -> 1.04 us
  Pallas kernels: 0 us -> 7.6 us
    reduce_scatter x2 -> x0, waiting for transfers between devices: 57.6 us -> none  [slot_reduce(): lax.psum_scatter(partial_value, ('panel', 'depth'), scatter_dimension=1,...]
    dot_general x24 -> x0, matrix products: 48.5 us -> none  [the longest x8 21.2 us: contribute(): jnp.einsum('isru,iruac->isac', targets.astype(jnp.float32), products, pre...]
    all_gather x2 -> x0, waiting for transfers between devices: 48.3 us -> none  [slot_gather(): return lax.all_gather(blocks, ('panel', 'depth'), axis=1, tiled=True)]
    ppermute x6 -> x9, waiting for transfers between devices: 52.2 us -> 12.7 us  [move(): return lax.ppermute(block, AXES, [(index(*a), index(*b)) for a, b in pairs])]
    ppermute x6 -> x9, starting transfers between devices: 3.31 us -> 20.6 us  [move(): return lax.ppermute(block, AXES, [(index(*a), index(*b)) for a, b in pairs])]
    pallas_call x0 -> x2, Pallas kernels: none -> 7.6 us  [the longest x1 4.99 us: gather_local(): pl.pallas_call(functools.partial(late_kernel, tables), out_shape=[jax.Sha...]
    dot_general x2 -> x0, local copies, waits for them, and re-layouts: 5.09 us -> none  [contribute(): jnp.einsum('irab,rubc->iruac', picked, incoming, precision=precise)]
    add x2 -> x0, local copies, waits for them, and re-layouts: 3.94 us -> none  [contribute(): return partial_value + placed]
  transfers between devices with their start and end apart: 10 -> 9, of which waited for: 10 -> 5; matrix products, arithmetic and copies ran while one was open for 15% -> 7% of each run, Pallas kernels for 0% -> 6%
where the time goes in v1:
time: 45.5 us; the launch traced here: 45 us
  starting transfers between devices  20.6 us (45%)
  waiting for transfers between devices  12.7 us (28%)
  Pallas kernels  7.6 us (17%)
  other arithmetic  2.94 us (6%)
  local copies, waits for them, and re-layouts  1.04 us (2%)
    ppermute x9, starting transfers between devices, move(): return lax.ppermute(block, AXES, [(index(*a), index(*b)) for a, b in pairs])  20.6 us
    ppermute x9, waiting for transfers between devices, move(): return lax.ppermute(block, AXES, [(index(*a), index(*b)) for a, b in pairs])  12.7 us
    pallas_call x1, Pallas kernels, gather_local(): pl.pallas_call(functools.partial(late_kernel, tables), out_shape=[jax.Sha...  4.99 us
    pallas_call x1, Pallas kernels, gather_local(): pl.pallas_call(functools.partial(early_kernel, tables), out_shape=[jax.Sh...  2.61 us
    unnamed x2, local copies, waits for them, and re-layouts  1.04 us
  transfers between devices with their start and end apart: 9, of which 5 were waited for; matrix products, arithmetic and copies ran while one was open for 7% of the time, Pallas kernels for 6%

profile of v1, /device:TPU:0, one launch (start us, length us, event | category | flops | bytes accessed | tf_op | source)
XLA Modules:
  0.0 45.0 jit_solution(14695368243493330760)
XLA Ops:
  0.0 5.0 %collective-permute-start = (f32[2,4,128,128]{3,2,1,0:T(8,128)}, f32[2,4,128,128]{3,2,1,0:T(8,128)S(1)}, u32[]{:S(2)}, u32[]{:S(2)}) collective-permute-start(f32[2,4,128,128]{3,2,1,0:T(8,128)} %own_ref.1), channel_id=1, source_target_pairs={{0,4},{4,8},{8,12},{5,1},{9,5},{13,9},{12,14},{1,3},{16,20},{20,24... | collective-permute-start | bytes 1572872 | tf_op jit(solution)/shard_map/ppermute | solution.py:226
  5.0 1.9 %collective-permute-start.2 = (f32[2,4,128,128]{3,2,1,0:T(8,128)}, f32[2,4,128,128]{3,2,1,0:T(8,128)S(1)}, u32[]{:S(2)}, u32[]{:S(2)}) collective-permute-start(f32[2,4,128,128]{3,2,1,0:T(8,128)} %own_ref.1), channel_id=1, source_target_pairs={{0,1},{1,0},{4,5},{5,4},{8,9},{9,8},{12,13},{13,12},{16,17},{17,16... | collective-permute-start | bytes 1572872 | tf_op jit(solution)/shard_map/ppermute | solution.py:226
  6.9 0.8 %fusion.1 = (s32[8]{0:T(128)S(1)}, s32[8,8]{1,0:T(8,128)S(1)}) fusion(s32[8,16]{1,0:T(8,128)} %param.3), kind=kLoop, calls=%fused_computation.11 | loop fusion | flops 184 | bytes 544 | tf_op jit(solution)/shard_map/reduce_sum | solution.py:204
  7.7 0.1 fusion
  7.8 1.2 %collective-permute-done.2.own_swap = f32[2,4,128,128]{3,2,1,0:T(8,128)S(1)} collective-permute-done((f32[2,4,128,128]{3,2,1,0:T(8,128)}, f32[2,4,128,128]{3,2,1,0:T(8,128)S(1)}, u32[]{:S(2)}, u32[]{:S(2)}) %collective-permute-start.2) | collective-permute-done | bytes 524320 | tf_op jit(solution)/shard_map/ppermute | solution.py:226
  9.0 3.5 %collective-permute-start.3 = (f32[2,4,128,128]{3,2,1,0:T(8,128)S(1)}, f32[2,4,128,128]{3,2,1,0:T(8,128)S(1)}, u32[]{:S(2)}, u32[]{:S(2)}) collective-permute-start(f32[2,4,128,128]{3,2,1,0:T(8,128)S(1)} %collective-permute-done.2.own_swap), channel_id=1, source_target_pairs={{0,4},{4,8},{8,12},{5,1},{9,5},{13,9},{12,14},{1,3},{16,20},{20,24... | collective-permute-start | bytes 1572872 | tf_op jit(solution)/shard_map/ppermute | solution.py:226
  12.5 0.1 pad_add_fusion.1.place_ref
  12.5 0.2 convert_reduce_fusion
  12.8 0.1 add_select_fusion
  12.8 0.2 select_reduce_fusion
  13.0 0.0 collective-permute-done.r1
  13.1 1.9 %collective-permute-start.4 = (f32[2,4,128,128]{3,2,1,0:T(8,128)S(1)}, f32[2,4,128,128]{3,2,1,0:T(8,128)S(1)}, u32[]{:S(2)}, u32[]{:S(2)}) collective-permute-start(f32[2,4,128,128]{3,2,1,0:T(8,128)S(1)} %collective-permute-done.r1), channel_id=1, source_target_pairs={{0,1},{1,0},{4,5},{5,4},{8,9},{9,8},{12,13},{13,12},{16,17},{17,16... | collective-permute-start | bytes 1572872 | tf_op jit(solution)/shard_map/ppermute | solution.py:226
  15.0 1.3 %collective-permute-start.1 = (f32[2,4,128,128]{3,2,1,0:T(8,128)S(1)}, f32[2,4,128,128]{3,2,1,0:T(8,128)S(1)}, u32[]{:S(2)}, u32[]{:S(2)}) collective-permute-start(f32[2,4,128,128]{3,2,1,0:T(8,128)S(1)} %collective-permute-done.r1), channel_id=1, source_target_pairs={{4,8},{8,12},{5,1},{9,5},{14,0},{3,13},{20,24},{24,28},{21,17},{25... | collective-permute-start | bytes 1572872 | tf_op jit(solution)/shard_map/ppermute | solution.py:226
  16.3 2.8 %collective-permute-done.3.r2 = f32[2,4,128,128]{3,2,1,0:T(8,128)S(1)} collective-permute-done((f32[2,4,128,128]{3,2,1,0:T(8,128)S(1)}, f32[2,4,128,128]{3,2,1,0:T(8,128)S(1)}, u32[]{:S(2)}, u32[]{:S(2)}) %collective-permute-start.3) | collective-permute-done | bytes 524320 | tf_op jit(solution)/shard_map/ppermute | solution.py:226
  19.1 1.9 %collective-permute-start.5 = (f32[2,4,128,128]{3,2,1,0:T(8,128)S(1)}, f32[2,4,128,128]{3,2,1,0:T(8,128)S(1)}, u32[]{:S(2)}, u32[]{:S(2)}) collective-permute-start(f32[2,4,128,128]{3,2,1,0:T(8,128)S(1)} %collective-permute-done.3.r2), channel_id=1, source_target_pairs={{0,1},{1,0},{4,5},{5,4},{8,9},{9,8},{12,13},{13,12},{16,17},{17,16... | collective-permute-start | bytes 1572872 | tf_op jit(solution)/shard_map/ppermute | solution.py:226
  21.0 0.7 %compare_convert_fusion = s32[8,8]{1,0:T(8,128)S(1)} fusion(s32[8,16]{1,0:T(8,128)} %param.3), kind=kLoop, calls=%fused_computation.6 | loop fusion | flops 128 | bytes 512 | tf_op jit(solution)/shard_map/convert_element_type | solution.py:204
  21.7 0.7 %compare_select_fusion = s32[8,8]{1,0:T(8,128)S(1)} fusion(s32[8,8]{1,0:T(8,128)S(1)} %select_reduce_fusion, s32[8,16]{1,0:T(8,128)} %param.3), kind=kLoop, calls=%fused_computation.5 | loop fusion | flops 128 | bytes 768 | tf_op jit(solution)/shard_map/jit(_where)/select_n | solution.py:212
  22.4 0.1 pad_add_fusion.table_ref
  22.5 1.3 %collective-permute-start.6 = (f32[2,4,128,128]{3,2,1,0:T(8,128)S(1)}, f32[2,4,128,128]{3,2,1,0:T(8,128)S(1)}, u32[]{:S(2)}, u32[]{:S(2)}) collective-permute-start(f32[2,4,128,128]{3,2,1,0:T(8,128)S(1)} %collective-permute-done.3.r2), channel_id=1, source_target_pairs={{4,8},{8,12},{5,1},{9,5},{14,0},{3,13},{20,24},{24,28},{21,17},{25... | collective-permute-start | bytes 1572872 | tf_op jit(solution)/shard_map/ppermute | solution.py:226
  23.8 0.0 collective-permute-done.4.t1
  23.8 0.0 collective-permute-done.5.t2
  23.8 0.0 copy-start
  23.8 1.0 %copy-done = f32[2,4,128,128]{3,2,1,0:T(8,128)S(1)} copy-done((f32[2,4,128,128]{3,2,1,0:T(8,128)S(1)}, f32[2,4,128,128]{3,2,1,0:T(8,128)}, u32[]{:S(2)}) %copy-start) | copy-done | bytes 524312
  24.8 2.6 %early.1 = (bf16[1024,1024]{1,0:T(8,128)(2,1)S(1)}, bf16[1024,1024]{1,0:T(8,128)(2,1)S(1)}, bf16[512,1024]{1,0:T(8,128)(2,1)S(1)}, f32[256,1024]{1,0:T(8,128)S(1)}) custom-call(s32[8,24]{1,0:T(8,128)S(1)} %pad_add_fusion.table_ref, s32[3]{0:T(128)S(1)} %pad_add_fusion.1.place_ref, f32[2,4,128,128]{3,2,1,0:T(8,128)S(1)} %copy-done, ...), custom_call_target="tpu_custom_call" | custom-call | tf_op jit(solution)/shard_map/early/pallas_call | solution.py:264
  27.5 1.3 %collective-permute-done.1.r3 = f32[2,4,128,128]{3,2,1,0:T(8,128)S(1)} collective-permute-done((f32[2,4,128,128]{3,2,1,0:T(8,128)S(1)}, f32[2,4,128,128]{3,2,1,0:T(8,128)S(1)}, u32[]{:S(2)}, u32[]{:S(2)}) %collective-permute-start.1) | collective-permute-done | bytes 524320 | tf_op jit(solution)/shard_map/ppermute | solution.py:226
  28.8 1.9 %collective-permute-start.7 = (f32[2,4,128,128]{3,2,1,0:T(8,128)S(1)}, f32[2,4,128,128]{3,2,1,0:T(8,128)S(1)}, u32[]{:S(2)}, u32[]{:S(2)}) collective-permute-start(f32[2,4,128,128]{3,2,1,0:T(8,128)S(1)} %collective-permute-done.1.r3), channel_id=1, source_target_pairs={{0,1},{1,0},{4,5},{5,4},{8,9},{9,8},{12,13},{13,12},{16,17},{17,16... | collective-permute-start | bytes 1572872 | tf_op jit(solution)/shard_map/ppermute | solution.py:226
  30.7 5.6 %collective-permute-done.6.r4 = f32[2,4,128,128]{3,2,1,0:T(8,128)S(1)} collective-permute-done((f32[2,4,128,128]{3,2,1,0:T(8,128)S(1)}, f32[2,4,128,128]{3,2,1,0:T(8,128)S(1)}, u32[]{:S(2)}, u32[]{:S(2)}) %collective-permute-start.6) | collective-permute-done | bytes 524320 | tf_op jit(solution)/shard_map/ppermute | solution.py:226
  36.2 0.0 collective-permute-done.7.t3
  36.2 1.9 %collective-permute-start.8 = (f32[2,4,128,128]{3,2,1,0:T(8,128)S(1)}, f32[2,4,128,128]{3,2,1,0:T(8,128)S(1)}, u32[]{:S(2)}, u32[]{:S(2)}) collective-permute-start(f32[2,4,128,128]{3,2,1,0:T(8,128)S(1)} %collective-permute-done.6.r4), channel_id=1, source_target_pairs={{0,1},{1,0},{4,5},{5,4},{8,9},{9,8},{12,13},{13,12},{16,17},{17,16... | collective-permute-start | bytes 1572872 | tf_op jit(solution)/shard_map/ppermute | solution.py:226
  38.2 1.9 %collective-permute-done.8.t4 = f32[2,4,128,128]{3,2,1,0:T(8,128)S(1)} collective-permute-done((f32[2,4,128,128]{3,2,1,0:T(8,128)S(1)}, f32[2,4,128,128]{3,2,1,0:T(8,128)S(1)}, u32[]{:S(2)}, u32[]{:S(2)}) %collective-permute-start.8) | collective-permute-done | bytes 524320 | tf_op jit(solution)/shard_map/ppermute | solution.py:226
  40.0 5.0 %late.1 = (f32[2,4,128,128]{3,2,1,0:T(8,128)}, bf16[1024,1024]{1,0:T(8,128)(2,1)S(1)}, bf16[1024,1024]{1,0:T(8,128)(2,1)S(1)}) custom-call(s32[8,24]{1,0:T(8,128)S(1)} %pad_add_fusion.table_ref, s32[3]{0:T(128)S(1)} %pad_add_fusion.1.place_ref, f32[2,4,128,128]{3,2,1,0:T(8,128)S(1)} %collective-permute-done.1.r3, ...), custom_call_target="tpu_custom_call", output_to_operand_aliasing={{1}: (6, {}), {2}: (7, {})} | custom-call | tf_op jit(solution)/shard_map/late/pallas_call | solution.py:281
  (1 shorter events, 0.0 us)
Async XLA Ops:
  0.0 13.0 %collective-permute-start = (f32[2,4,128,128]{3,2,1,0:T(8,128)}, f32[2,4,128,128]{3,2,1,0:T(8,128)S(1)}, u32[]{:S(2)}, u32[]{:S(2)}) collective-permute-start(f32[2,4,128,128]{3,2,1,0:T(8,128)} %own_ref.1), channel_id=1, source_target_pairs={{0,4},{4,8},{8,12},{5,1},{9,5},{13,9},{12,14},{1,3},{16,20},{20,24... | collective-permute-start | bytes 1572872 | tf_op jit(solution)/shard_map/ppermute | solution.py:226
  5.0 4.0 %collective-permute-start.2 = (f32[2,4,128,128]{3,2,1,0:T(8,128)}, f32[2,4,128,128]{3,2,1,0:T(8,128)S(1)}, u32[]{:S(2)}, u32[]{:S(2)}) collective-permute-start(f32[2,4,128,128]{3,2,1,0:T(8,128)} %own_ref.1), channel_id=1, source_target_pairs={{0,1},{1,0},{4,5},{5,4},{8,9},{9,8},{12,13},{13,12},{16,17},{17,16... | collective-permute-start | bytes 1572872 | tf_op jit(solution)/shard_map/ppermute | solution.py:226
  9.0 10.1 %collective-permute-start.3 = (f32[2,4,128,128]{3,2,1,0:T(8,128)S(1)}, f32[2,4,128,128]{3,2,1,0:T(8,128)S(1)}, u32[]{:S(2)}, u32[]{:S(2)}) collective-permute-start(f32[2,4,128,128]{3,2,1,0:T(8,128)S(1)} %collective-permute-done.2.own_swap), channel_id=1, source_target_pairs={{0,4},{4,8},{8,12},{5,1},{9,5},{13,9},{12,14},{1,3},{16,20},{20,24... | collective-permute-start | bytes 1572872 | tf_op jit(solution)/shard_map/ppermute | solution.py:226
  13.1 10.7 %collective-permute-start.4 = (f32[2,4,128,128]{3,2,1,0:T(8,128)S(1)}, f32[2,4,128,128]{3,2,1,0:T(8,128)S(1)}, u32[]{:S(2)}, u32[]{:S(2)}) collective-permute-start(f32[2,4,128,128]{3,2,1,0:T(8,128)S(1)} %collective-permute-done.r1), channel_id=1, source_target_pairs={{0,1},{1,0},{4,5},{5,4},{8,9},{9,8},{12,13},{13,12},{16,17},{17,16... | collective-permute-start | bytes 1572872 | tf_op jit(solution)/shard_map/ppermute | solution.py:226
  15.0 13.8 %collective-permute-start.1 = (f32[2,4,128,128]{3,2,1,0:T(8,128)S(1)}, f32[2,4,128,128]{3,2,1,0:T(8,128)S(1)}, u32[]{:S(2)}, u32[]{:S(2)}) collective-permute-start(f32[2,4,128,128]{3,2,1,0:T(8,128)S(1)} %collective-permute-done.r1), channel_id=1, source_target_pairs={{4,8},{8,12},{5,1},{9,5},{14,0},{3,13},{20,24},{24,28},{21,17},{25... | collective-permute-start | bytes 1572872 | tf_op jit(solution)/shard_map/ppermute | solution.py:226
  19.1 4.7 %collective-permute-start.5 = (f32[2,4,128,128]{3,2,1,0:T(8,128)S(1)}, f32[2,4,128,128]{3,2,1,0:T(8,128)S(1)}, u32[]{:S(2)}, u32[]{:S(2)}) collective-permute-start(f32[2,4,128,128]{3,2,1,0:T(8,128)S(1)} %collective-permute-done.3.r2), channel_id=1, source_target_pairs={{0,1},{1,0},{4,5},{5,4},{8,9},{9,8},{12,13},{13,12},{16,17},{17,16... | collective-permute-start | bytes 1572872 | tf_op jit(solution)/shard_map/ppermute | solution.py:226
  22.5 13.8 %collective-permute-start.6 = (f32[2,4,128,128]{3,2,1,0:T(8,128)S(1)}, f32[2,4,128,128]{3,2,1,0:T(8,128)S(1)}, u32[]{:S(2)}, u32[]{:S(2)}) collective-permute-start(f32[2,4,128,128]{3,2,1,0:T(8,128)S(1)} %collective-permute-done.3.r2), channel_id=1, source_target_pairs={{4,8},{8,12},{5,1},{9,5},{14,0},{3,13},{20,24},{24,28},{21,17},{25... | collective-permute-start | bytes 1572872 | tf_op jit(solution)/shard_map/ppermute | solution.py:226
  23.8 1.0 %copy-start = (f32[2,4,128,128]{3,2,1,0:T(8,128)S(1)}, f32[2,4,128,128]{3,2,1,0:T(8,128)}, u32[]{:S(2)}) copy-start(f32[2,4,128,128]{3,2,1,0:T(8,128)} %own_ref.1) | copy-start | bytes 1572868
  28.8 7.5 %collective-permute-start.7 = (f32[2,4,128,128]{3,2,1,0:T(8,128)S(1)}, f32[2,4,128,128]{3,2,1,0:T(8,128)S(1)}, u32[]{:S(2)}, u32[]{:S(2)}) collective-permute-start(f32[2,4,128,128]{3,2,1,0:T(8,128)S(1)} %collective-permute-done.1.r3), channel_id=1, source_target_pairs={{0,1},{1,0},{4,5},{5,4},{8,9},{9,8},{12,13},{13,12},{16,17},{17,16... | collective-permute-start | bytes 1572872 | tf_op jit(solution)/shard_map/ppermute | solution.py:226
  36.2 3.8 %collective-permute-start.8 = (f32[2,4,128,128]{3,2,1,0:T(8,128)S(1)}, f32[2,4,128,128]{3,2,1,0:T(8,128)S(1)}, u32[]{:S(2)}, u32[]{:S(2)}) collective-permute-start(f32[2,4,128,128]{3,2,1,0:T(8,128)S(1)} %collective-permute-done.6.r4), channel_id=1, source_target_pairs={{0,1},{1,0},{4,5},{5,4},{8,9},{9,8},{12,13},{13,12},{16,17},{17,16... | collective-permute-start | bytes 1572872 | tf_op jit(solution)/shard_map/ppermute | solution.py:226

commit v2 on v1

--- a/solution.py
+++ b/solution.py
@@ -8,7 +8,7 @@
 from jax.sharding import PartitionSpec as P
 
 precise = lax.Precision.HIGHEST
-AXES = ("blk", "panel", "depth")
+AXES = ("groups", "blk", "panel", "depth")
 
 
 def shifted(block, axis, distance):
@@ -216,40 +216,50 @@
 def gather_local(x_blocks, columns):
     slab, width, edge, _ = x_blocks.shape
     rows = columns.shape[0]
-    chains, panels, lanes = (lax.axis_size(axis) for axis in AXES)
+    groups, chains, panels, lanes = (lax.axis_size(axis) for axis in AXES)
     last = chains - 1
 
-    def index(z, x, c):
-        return (z * panels + x) * lanes + c
-
-    def move(block, pairs):
-        return lax.ppermute(block, AXES, [(index(*a), index(*b)) for a, b in pairs])
+    def index(g, place):
+        z, x, c = place
+        return (((g % groups) * chains + z) * panels + x) * lanes + c
+
+    def move(block, cycles):
+        pairs = [(cycle[i - 1], cycle[i]) for cycle in cycles for i in range(len(cycle))]
+        busy = {a for a, _ in pairs}
+        route = [(index(g, a), index(g, b)) for g in range(groups) for a, b in pairs]
+        for z in range(chains):
+            for x in range(panels):
+                idle = [(z, x, c) for c in range(lanes) if (z, x, c) not in busy]
+                for g in range(groups):
+                    if len(idle) == lanes:
+                        route += [(index(g, idle[c - 1]), index(g, idle[c])) for c in range(lanes)]
+                    else:
+                        route += [(index(g, a), index(g + 1, a)) for a in idle]
+        return lax.ppermute(block, AXES, route)
 
     def swap(block):
-        return move(
-            block, [((z, 0, c), (z, 0, 1 - c)) for z in range(chains) for c in range(lanes)]
-        )
-
-    first = [((z, 0, 0), (z + 1, 0, 0)) for z in range(last)]
-    first += [((z, 0, 1), (z - 1, 0, 1)) for z in range(1, chains)]
-    first += [((last, 0, 0), (last, 1, 0)), ((0, 0, 1), (0, 1, 1))]
-    second = [((z, 0, 0), (z + 1, 0, 0)) for z in range(1, last)]
-    second += [((z, 0, 1), (z - 1, 0, 1)) for z in range(1, last)]
-    second += [((last, 1, 0), (0, 0, 0)), ((0, 1, 1), (last, 0, 1))]
+        return move(block, [])
+
+    up = [(z, 0, 0) for z in range(chains)] + [(last, 1, 0)]
+    down = [(z, 0, 1) for z in reversed(range(chains))] + [(0, 1, 1)]
+    first = [up + [(last, 1, 1)] + down + [(0, 1, 0)]]
+    second = [up, down]
     near = [(z - 1, z + 1 if z < last else -1) for z in range(chains)]
     far = [(z - 2 if z >= 2 else -1, z + 2 if z + 2 < chains else -1) for z in range(chains)]
     far[0] = (last, far[0][1])
     far[last] = (far[last][0], 0)
     tables = (near, far)
 
+    table = slot_table(columns, lanes * width)
     r1 = move(x_blocks, first)
     own_swap = swap(x_blocks)
     r2 = move(own_swap, first)
+    r1, table = lax.optimization_barrier((r1, table))
     r3 = move(r1, second)
     t1 = swap(r1)
     r4 = move(r2, second)
     t2 = swap(r2)
-    table = slot_table(columns, lanes * width)
+
     place = jnp.stack(
         [
             lax.axis_index("blk"),
@@ -302,7 +312,7 @@
 def local(x_blocks, columns):
     slab, width, edge, _ = x_blocks.shape
     rows, slots = columns.shape
-    chains, panels, lanes = (lax.axis_size(axis) for axis in AXES)
+    _, chains, panels, lanes = (lax.axis_size(axis) for axis in AXES)
     full = rows <= slots and rows == lanes * width
     if full and rows <= 8 and edge % 128 == 0 and panels >= 2 and lanes == 2 and chains == 4:
         return gather_local(x_blocks, columns)

time: 45.5 us -> 41 us (0.901)
  starting transfers between devices: 20.6 us -> 8.3 us
  waiting for transfers between devices: 12.7 us -> 20.8 us
    ppermute x9, starting transfers between devices: 20.6 us -> 8.3 us  [move(): return lax.ppermute(block, AXES, route)]
    ppermute x9, waiting for transfers between devices: 12.7 us -> 20.8 us  [move(): return lax.ppermute(block, AXES, route)]
  transfers between devices with their start and end apart: 9 -> 9, of which waited for: 5 -> 6; matrix products, arithmetic and copies ran while one was open for 7% -> 7% of each run, Pallas kernels for 6% -> 6%
where the time goes in v2:
time: 41 us; the launch traced here: 40.7 us
  waiting for transfers between devices  20.8 us (51%)
  starting transfers between devices  8.3 us (20%)
  Pallas kernels  7.61 us (19%)
  other arithmetic  2.93 us (7%)
  local copies, waits for them, and re-layouts  1.04 us (3%)
    ppermute x9, waiting for transfers between devices, move(): return lax.ppermute(block, AXES, route)  20.8 us
    ppermute x9, starting transfers between devices, move(): return lax.ppermute(block, AXES, route)  8.3 us
    pallas_call x1, Pallas kernels, gather_local(): pl.pallas_call(functools.partial(late_kernel, tables), out_shape=[jax.Sha...  5 us
    pallas_call x1, Pallas kernels, gather_local(): pl.pallas_call(functools.partial(early_kernel, tables), out_shape=[jax.Sh...  2.61 us
    unnamed x2, local copies, waits for them, and re-layouts  1.04 us
  transfers between devices with their start and end apart: 9, of which 6 were waited for; matrix products, arithmetic and copies ran while one was open for 7% of the time, Pallas kernels for 6%

profile of v2, /device:TPU:0, one launch (start us, length us, event | category | flops | bytes accessed | tf_op | source)
XLA Modules:
  0.0 40.7 jit_solution(1193737221638556282)
XLA Ops:
  0.0 3.0 %collective-permute-start = (f32[2,4,128,128]{3,2,1,0:T(8,128)}, f32[2,4,128,128]{3,2,1,0:T(8,128)S(1)}, u32[]{:S(2)}, u32[]{:S(2)}) collective-permute-start(f32[2,4,128,128]{3,2,1,0:T(8,128)} %own_ref.1), channel_id=1, source_target_pairs={{2,0},{0,4},{4,8},{8,12},{12,14},{14,15},{15,13},{13,9},{9,5},{5,1... | collective-permute-start | bytes 1572872 | tf_op jit(solution)/shard_map/ppermute | solution.py:238
  3.0 0.0 collective-permute-start.2
  3.0 0.8 %fusion.1 = (s32[8]{0:T(128)S(1)}, s32[8,8]{1,0:T(8,128)S(1)}) fusion(s32[8,16]{1,0:T(8,128)} %param.3), kind=kLoop, calls=%fused_computation.11 | loop fusion | flops 184 | bytes 544 | tf_op jit(solution)/shard_map/reduce_sum | solution.py:204
  3.8 0.1 fusion
  3.9 0.2 convert_reduce_fusion
  4.2 0.1 add_select_fusion
  4.2 0.2 select_reduce_fusion
  4.4 0.7 %collective-permute-done.2.own_swap = f32[2,4,128,128]{3,2,1,0:T(8,128)S(1)} collective-permute-done((f32[2,4,128,128]{3,2,1,0:T(8,128)}, f32[2,4,128,128]{3,2,1,0:T(8,128)S(1)}, u32[]{:S(2)}, u32[]{:S(2)}) %collective-permute-start.2) | collective-permute-done | bytes 524320 | tf_op jit(solution)/shard_map/ppermute | solution.py:238
  5.1 1.6 %collective-permute-start.3 = (f32[2,4,128,128]{3,2,1,0:T(8,128)S(1)}, f32[2,4,128,128]{3,2,1,0:T(8,128)S(1)}, u32[]{:S(2)}, u32[]{:S(2)}) collective-permute-start(f32[2,4,128,128]{3,2,1,0:T(8,128)S(1)} %collective-permute-done.2.own_swap), channel_id=1, source_target_pairs={{2,0},{0,4},{4,8},{8,12},{12,14},{14,15},{15,13},{13,9},{9,5},{5,1... | collective-permute-start | bytes 1572872 | tf_op jit(solution)/shard_map/ppermute | solution.py:238
  6.7 0.7 %compare_convert_fusion = s32[8,8]{1,0:T(8,128)S(1)} fusion(s32[8,16]{1,0:T(8,128)} %param.3), kind=kLoop, calls=%fused_computation.6 | loop fusion | flops 128 | bytes 512 | tf_op jit(solution)/shard_map/convert_element_type | solution.py:204
  7.4 0.7 %compare_select_fusion = s32[8,8]{1,0:T(8,128)S(1)} fusion(s32[8,8]{1,0:T(8,128)S(1)} %select_reduce_fusion, s32[8,16]{1,0:T(8,128)} %param.3), kind=kLoop, calls=%fused_computation.5 | loop fusion | flops 128 | bytes 768 | tf_op jit(solution)/shard_map/jit(_where)/select_n | solution.py:212
  8.1 0.1 pad_add_fusion.table_ref
  8.2 2.1 %collective-permute-done.r1 = f32[2,4,128,128]{3,2,1,0:T(8,128)S(1)} collective-permute-done((f32[2,4,128,128]{3,2,1,0:T(8,128)}, f32[2,4,128,128]{3,2,1,0:T(8,128)S(1)}, u32[]{:S(2)}, u32[]{:S(2)}) %collective-permute-start) | collective-permute-done | bytes 524320 | tf_op jit(solution)/shard_map/ppermute | solution.py:238
  10.3 0.0 collective-permute-start.4
  10.3 5.6 %collective-permute-done.3.r2 = f32[2,4,128,128]{3,2,1,0:T(8,128)S(1)} collective-permute-done((f32[2,4,128,128]{3,2,1,0:T(8,128)S(1)}, f32[2,4,128,128]{3,2,1,0:T(8,128)S(1)}, u32[]{:S(2)}, u32[]{:S(2)}) %collective-permute-start.3) | collective-permute-done | bytes 524320 | tf_op jit(solution)/shard_map/ppermute | solution.py:238
  15.9 0.0 collective-permute-start.5
  15.9 2.1 %collective-permute-start.1 = (f32[2,4,128,128]{3,2,1,0:T(8,128)S(1)}, f32[2,4,128,128]{3,2,1,0:T(8,128)S(1)}, u32[]{:S(2)}, u32[]{:S(2)}) collective-permute-start(f32[2,4,128,128]{3,2,1,0:T(8,128)S(1)} %collective-permute-done.r1), channel_id=1, source_target_pairs={{14,0},{0,4},{4,8},{8,12},{12,14},{3,13},{13,9},{9,5},{5,1},{1,3},... | collective-permute-start | bytes 1572872 | tf_op jit(solution)/shard_map/ppermute | solution.py:238
  18.0 0.1 pad_add_fusion.1.place_ref
  18.1 1.6 %collective-permute-start.6 = (f32[2,4,128,128]{3,2,1,0:T(8,128)S(1)}, f32[2,4,128,128]{3,2,1,0:T(8,128)S(1)}, u32[]{:S(2)}, u32[]{:S(2)}) collective-permute-start(f32[2,4,128,128]{3,2,1,0:T(8,128)S(1)} %collective-permute-done.3.r2), channel_id=1, source_target_pairs={{14,0},{0,4},{4,8},{8,12},{12,14},{3,13},{13,9},{9,5},{5,1},{1,3},... | collective-permute-start | bytes 1572872 | tf_op jit(solution)/shard_map/ppermute | solution.py:238
  19.7 0.0 collective-permute-done.4.t1
  19.7 0.0 collective-permute-done.5.t2
  19.7 0.0 copy-start
  19.7 1.0 %copy-done = f32[2,4,128,128]{3,2,1,0:T(8,128)S(1)} copy-done((f32[2,4,128,128]{3,2,1,0:T(8,128)S(1)}, f32[2,4,128,128]{3,2,1,0:T(8,128)}, u32[]{:S(2)}) %copy-start) | copy-done | bytes 524312
  20.7 2.6 %early.1 = (bf16[1024,1024]{1,0:T(8,128)(2,1)S(1)}, bf16[1024,1024]{1,0:T(8,128)(2,1)S(1)}, bf16[512,1024]{1,0:T(8,128)(2,1)S(1)}, f32[256,1024]{1,0:T(8,128)S(1)}) custom-call(s32[8,24]{1,0:T(8,128)S(1)} %pad_add_fusion.table_ref, s32[3]{0:T(128)S(1)} %pad_add_fusion.1.place_ref, f32[2,4,128,128]{3,2,1,0:T(8,128)S(1)} %copy-done, ...), custom_call_target="tpu_custom_call" | custom-call | tf_op jit(solution)/shard_map/early/pallas_call | solution.py:274
  23.4 4.8 %collective-permute-done.1.r3 = f32[2,4,128,128]{3,2,1,0:T(8,128)S(1)} collective-permute-done((f32[2,4,128,128]{3,2,1,0:T(8,128)S(1)}, f32[2,4,128,128]{3,2,1,0:T(8,128)S(1)}, u32[]{:S(2)}, u32[]{:S(2)}) %collective-permute-start.1) | collective-permute-done | bytes 524320 | tf_op jit(solution)/shard_map/ppermute | solution.py:238
  28.1 0.0 collective-permute-start.7
  28.2 5.6 %collective-permute-done.6.r4 = f32[2,4,128,128]{3,2,1,0:T(8,128)S(1)} collective-permute-done((f32[2,4,128,128]{3,2,1,0:T(8,128)S(1)}, f32[2,4,128,128]{3,2,1,0:T(8,128)S(1)}, u32[]{:S(2)}, u32[]{:S(2)}) %collective-permute-start.6) | collective-permute-done | bytes 524320 | tf_op jit(solution)/shard_map/ppermute | solution.py:238
  33.8 0.0 collective-permute-done.7.t3
  33.8 0.0 collective-permute-start.8
  33.8 1.9 %collective-permute-done.8.t4 = f32[2,4,128,128]{3,2,1,0:T(8,128)S(1)} collective-permute-done((f32[2,4,128,128]{3,2,1,0:T(8,128)S(1)}, f32[2,4,128,128]{3,2,1,0:T(8,128)S(1)}, u32[]{:S(2)}, u32[]{:S(2)}) %collective-permute-start.8) | collective-permute-done | bytes 524320 | tf_op jit(solution)/shard_map/ppermute | solution.py:238
  35.7 5.0 %late.1 = (f32[2,4,128,128]{3,2,1,0:T(8,128)}, bf16[1024,1024]{1,0:T(8,128)(2,1)S(1)}, bf16[1024,1024]{1,0:T(8,128)(2,1)S(1)}) custom-call(s32[8,24]{1,0:T(8,128)S(1)} %pad_add_fusion.table_ref, s32[3]{0:T(128)S(1)} %pad_add_fusion.1.place_ref, f32[2,4,128,128]{3,2,1,0:T(8,128)S(1)} %collective-permute-done.1.r3, ...), custom_call_target="tpu_custom_call", output_to_operand_aliasing={{1}: (6, {}), {2}: (7, {})} | custom-call | tf_op jit(solution)/shard_map/late/pallas_call | solution.py:291
  (1 shorter events, 0.0 us)
Async XLA Ops:
  0.0 10.3 %collective-permute-start = (f32[2,4,128,128]{3,2,1,0:T(8,128)}, f32[2,4,128,128]{3,2,1,0:T(8,128)S(1)}, u32[]{:S(2)}, u32[]{:S(2)}) collective-permute-start(f32[2,4,128,128]{3,2,1,0:T(8,128)} %own_ref.1), channel_id=1, source_target_pairs={{2,0},{0,4},{4,8},{8,12},{12,14},{14,15},{15,13},{13,9},{9,5},{5,1... | collective-permute-start | bytes 1572872 | tf_op jit(solution)/shard_map/ppermute | solution.py:238
  3.0 2.1 %collective-permute-start.2 = (f32[2,4,128,128]{3,2,1,0:T(8,128)}, f32[2,4,128,128]{3,2,1,0:T(8,128)S(1)}, u32[]{:S(2)}, u32[]{:S(2)}) collective-permute-start(f32[2,4,128,128]{3,2,1,0:T(8,128)} %own_ref.1), channel_id=1, source_target_pairs={{1,0},{0,1},{17,16},{16,17},{3,2},{2,3},{19,18},{18,19},{5,4},{4,5... | collective-permute-start | bytes 1572872 | tf_op jit(solution)/shard_map/ppermute | solution.py:238
  5.1 10.8 %collective-permute-start.3 = (f32[2,4,128,128]{3,2,1,0:T(8,128)S(1)}, f32[2,4,128,128]{3,2,1,0:T(8,128)S(1)}, u32[]{:S(2)}, u32[]{:S(2)}) collective-permute-start(f32[2,4,128,128]{3,2,1,0:T(8,128)S(1)} %collective-permute-done.2.own_swap), channel_id=1, source_target_pairs={{2,0},{0,4},{4,8},{8,12},{12,14},{14,15},{15,13},{13,9},{9,5},{5,1... | collective-permute-start | bytes 1572872 | tf_op jit(solution)/shard_map/ppermute | solution.py:238
  10.3 9.4 %collective-permute-start.4 = (f32[2,4,128,128]{3,2,1,0:T(8,128)S(1)}, f32[2,4,128,128]{3,2,1,0:T(8,128)S(1)}, u32[]{:S(2)}, u32[]{:S(2)}) collective-permute-start(f32[2,4,128,128]{3,2,1,0:T(8,128)S(1)} %collective-permute-done.r1), channel_id=1, source_target_pairs={{1,0},{0,1},{17,16},{16,17},{3,2},{2,3},{19,18},{18,19},{5,4},{4,5... | collective-permute-start | bytes 1572872 | tf_op jit(solution)/shard_map/ppermute | solution.py:238
  15.9 3.8 %collective-permute-start.5 = (f32[2,4,128,128]{3,2,1,0:T(8,128)S(1)}, f32[2,4,128,128]{3,2,1,0:T(8,128)S(1)}, u32[]{:S(2)}, u32[]{:S(2)}) collective-permute-start(f32[2,4,128,128]{3,2,1,0:T(8,128)S(1)} %collective-permute-done.3.r2), channel_id=1, source_target_pairs={{1,0},{0,1},{17,16},{16,17},{3,2},{2,3},{19,18},{18,19},{5,4},{4,5... | collective-permute-start | bytes 1572872 | tf_op jit(solution)/shard_map/ppermute | solution.py:238
  15.9 12.2 %collective-permute-start.1 = (f32[2,4,128,128]{3,2,1,0:T(8,128)S(1)}, f32[2,4,128,128]{3,2,1,0:T(8,128)S(1)}, u32[]{:S(2)}, u32[]{:S(2)}) collective-permute-start(f32[2,4,128,128]{3,2,1,0:T(8,128)S(1)} %collective-permute-done.r1), channel_id=1, source_target_pairs={{14,0},{0,4},{4,8},{8,12},{12,14},{3,13},{13,9},{9,5},{5,1},{1,3},... | collective-permute-start | bytes 1572872 | tf_op jit(solution)/shard_map/ppermute | solution.py:238
  18.1 15.7 %collective-permute-start.6 = (f32[2,4,128,128]{3,2,1,0:T(8,128)S(1)}, f32[2,4,128,128]{3,2,1,0:T(8,128)S(1)}, u32[]{:S(2)}, u32[]{:S(2)}) collective-permute-start(f32[2,4,128,128]{3,2,1,0:T(8,128)S(1)} %collective-permute-done.3.r2), channel_id=1, source_target_pairs={{14,0},{0,4},{4,8},{8,12},{12,14},{3,13},{13,9},{9,5},{5,1},{1,3},... | collective-permute-start | bytes 1572872 | tf_op jit(solution)/shard_map/ppermute | solution.py:238
  19.7 1.0 %copy-start = (f32[2,4,128,128]{3,2,1,0:T(8,128)S(1)}, f32[2,4,128,128]{3,2,1,0:T(8,128)}, u32[]{:S(2)}) copy-start(f32[2,4,128,128]{3,2,1,0:T(8,128)} %own_ref.1) | copy-start | bytes 1572868
  28.1 5.6 %collective-permute-start.7 = (f32[2,4,128,128]{3,2,1,0:T(8,128)S(1)}, f32[2,4,128,128]{3,2,1,0:T(8,128)S(1)}, u32[]{:S(2)}, u32[]{:S(2)}) collective-permute-start(f32[2,4,128,128]{3,2,1,0:T(8,128)S(1)} %collective-permute-done.1.r3), channel_id=1, source_target_pairs={{1,0},{0,1},{17,16},{16,17},{3,2},{2,3},{19,18},{18,19},{5,4},{4,5... | collective-permute-start | bytes 1572872 | tf_op jit(solution)/shard_map/ppermute | solution.py:238
  33.8 1.9 %collective-permute-start.8 = (f32[2,4,128,128]{3,2,1,0:T(8,128)S(1)}, f32[2,4,128,128]{3,2,1,0:T(8,128)S(1)}, u32[]{:S(2)}, u32[]{:S(2)}) collective-permute-start(f32[2,4,128,128]{3,2,1,0:T(8,128)S(1)} %collective-permute-done.6.r4), channel_id=1, source_target_pairs={{1,0},{0,1},{17,16},{16,17},{3,2},{2,3},{19,18},{18,19},{5,4},{4,5... | collective-permute-start | bytes 1572872 | tf_op jit(solution)/shard_map/ppermute | solution.py:238

commit v3 on v2

--- a/solution.py
+++ b/solution.py
@@ -132,17 +132,22 @@
 
 
 def early_kernel(
-    tables, table_ref, place_ref, own_ref, own_swap, r1, r2, t1, t2, high, low, left, part_ref
+    tables, table_ref, place_ref, own_hbm, own_swap, r1, r2, t1, t2, r3,
+    high, low, left, part_ref, own_ref, own_sem,
 ):
     place, lane = place_ref[0], place_ref[1]
-    near = tables[0]
-    store_piece(own_ref, place, lane, table_ref, high, low, left)
+    near, far = tables
+    own_copy = pltpu.make_async_copy(own_hbm, own_ref, own_sem)
+    own_copy.start()
+    here, there = lookup(near, place, lane), lookup(near, place, 1 - lane)
     store_piece(own_swap, place, 1 - lane, table_ref, high, low, left)
-    here, there = lookup(near, place, lane), lookup(near, place, 1 - lane)
     store_piece(r1, here, lane, table_ref, high, low)
     store_piece(r2, here, 1 - lane, table_ref, high, low)
     store_piece(t1, there, 1 - lane, table_ref, high, low)
     store_piece(t2, there, lane, table_ref, high, low)
+    store_piece(r3, lookup(far, place, lane), lane, table_ref, high, low)
+    own_copy.wait()
+    store_piece(own_ref, place, lane, table_ref, high, low, left)
     order = high.shape[0]
     depth, tile = order // 2, 256
     rows = pl.ds(pl.multiple_of(place // 2 * depth, depth), depth)
@@ -152,15 +157,14 @@
 
 
 def late_kernel(
-    tables, table_ref, place_ref, r3, r4, t3, t4, high_in, low_in, left, part_ref,
-    out_ref, high, low, square, square_parts, cube,
+    tables, table_ref, place_ref, r4, t3, t4, high_in, low_in, left, part_ref,
+    out_ref, high, low, square, square_parts,
 ):
     place, lane, group = place_ref[0], place_ref[1], place_ref[2]
     far = tables[1]
     here, there = lookup(far, place, lane), lookup(far, place, 1 - lane)
-    store_piece(r3, here, lane, table_ref, high, low)
+    store_piece(t3, there, 1 - lane, table_ref, high, low)
     store_piece(r4, here, 1 - lane, table_ref, high, low)
-    store_piece(t3, there, 1 - lane, table_ref, high, low)
     store_piece(t4, there, lane, table_ref, high, low)
     order = high.shape[0]
     depth, tile = order // 2, 256
@@ -178,21 +182,26 @@
                 col = pl.ds(c * edge, edge)
                 block = jnp.where(kept, square[pl.ds(r * edge, edge), col], 0.0)
                 block_high, block_low = split(block)
-                square_parts[pl.ds(r * edge, edge), col] = block_high
-                square_parts[pl.ds((slab + r) * edge, edge), col] = block_low
-    for n in range(order // tile):
-        cols = pl.ds(n * tile, tile)
-        cube[:, cols] = stacked_dot(square_parts[...], high[:, cols], low[:, cols])
+                square_parts[pl.ds(2 * r * edge, edge), col] = block_high
+                square_parts[pl.ds((2 * r + 1) * edge, edge), col] = block_low
     for r in range(slab):
-        for w in range(width):
-            slot = jnp.minimum(group * width + w, act - 1)
-            row = place * slab + r
-            there = (group * width + w < act) & (table_ref[row, act + slot] > 0)
-            at = (
-                pl.ds(r * edge, edge),
-                pl.ds(pl.multiple_of(table_ref[row, slot] * edge, edge), edge),
+        row = place * slab + r
+        left_parts = square_parts[pl.ds(2 * r * edge, 2 * edge), :]
+        for w in range(0, width, 2):
+            slots = [jnp.minimum(group * width + w + k, act - 1) for k in range(2)]
+            cols = [
+                pl.ds(pl.multiple_of(table_ref[row, slot] * edge, edge), edge) for slot in slots
+            ]
+            cube = stacked_dot(
+                left_parts,
+                jnp.concatenate([high[:, col] for col in cols], axis=1),
+                jnp.concatenate([low[:, col] for col in cols], axis=1),
             )
-            out_ref[r, w] = jnp.where(there, 3.0 * square[at] - 2.0 * cube[at], 0.0)
+            for k in range(2):
+                there = (group * width + w + k < act) & (table_ref[row, act + slots[k]] > 0)
+                value = 3.0 * square[pl.ds(r * edge, edge), cols[k]]
+                value = value - 2.0 * cube[:, k * edge : (k + 1) * edge]
+                out_ref[r, w + k] = jnp.where(there, value, 0.0)
 
 
 def slot_table(columns, act):
@@ -279,14 +288,14 @@
             jax.ShapeDtypeStruct((2 * own, order), jnp.bfloat16),
             jax.ShapeDtypeStruct((own, order), jnp.float32),
         ],
-        in_specs=[smem] * 2 + [vmem] * 6,
+        in_specs=[smem] * 2 + [pl.BlockSpec(memory_space=pltpu.HBM)] + [vmem] * 6,
         out_specs=[vmem] * 4,
+        scratch_shapes=[pltpu.VMEM(x_blocks.shape, jnp.float32), pltpu.SemaphoreType.DMA],
         compiler_params=params,
         name="early",
-    )(table, place, x_blocks, own_swap, r1, r2, t1, t2)
-    r3, part = lax.optimization_barrier((r3, part))
+    )(table, place, x_blocks, own_swap, r1, r2, t1, t2, r3)
     t3 = swap(r3)
-    r4, t3 = lax.optimization_barrier((r4, t3))
+    r4, part = lax.optimization_barrier((r4, part))
     t4 = swap(r4)
     out, _, _ = pl.pallas_call(
         functools.partial(late_kernel, tables),
@@ -295,17 +304,16 @@
             jax.ShapeDtypeStruct((order, order), jnp.bfloat16),
             jax.ShapeDtypeStruct((order, order), jnp.bfloat16),
         ],
-        in_specs=[smem] * 2 + [vmem] * 8,
+        in_specs=[smem] * 2 + [vmem] * 7,
         out_specs=[vmem] * 3,
-        input_output_aliases={6: 1, 7: 2},
+        input_output_aliases={5: 1, 6: 2},
         scratch_shapes=[
             pltpu.VMEM((own, order), jnp.float32),
             pltpu.VMEM((2 * own, order), jnp.bfloat16),
-            pltpu.VMEM((own, order), jnp.float32),
         ],
         compiler_params=params,
         name="late",
-    )(table, place, r3, r4, t3, t4, high, low, left, part)
+    )(table, place, r4, t3, t4, high, low, left, part)
     return out
 
 
@@ -313,7 +321,7 @@
     slab, width, edge, _ = x_blocks.shape
     rows, slots = columns.shape
     _, chains, panels, lanes = (lax.axis_size(axis) for axis in AXES)
-    full = rows <= slots and rows == lanes * width
+    full = rows <= slots and rows == lanes * width and width % 2 == 0
     if full and rows <= 8 and edge % 128 == 0 and panels >= 2 and lanes == 2 and chains == 4:
         return gather_local(x_blocks, columns)
     return ring_local(x_blocks, columns)

time: 41 us -> 37.1 us (0.905)
  the two profiles are of different devices: /device:TPU:0 before, /device:TPU:25 now
where the time goes in v3:
time: 37.1 us; the launch traced here: 36.8 us
  waiting for transfers between devices  18.2 us (49%)
  Pallas kernels  7.71 us (21%)
  starting transfers between devices  6.89 us (19%)
  other arithmetic  2.93 us (8%)
  local copies, waits for them, and re-layouts  1.04 us (3%)
    ppermute x9, waiting for transfers between devices, move(): return lax.ppermute(block, AXES, route)  18.2 us
    ppermute x9, starting transfers between devices, move(): return lax.ppermute(block, AXES, route)  6.89 us
    pallas_call x1, Pallas kernels, gather_local(): pl.pallas_call(functools.partial(late_kernel, tables), out_shape=[jax.Sha...  4.39 us
    pallas_call x1, Pallas kernels, gather_local(): pl.pallas_call(functools.partial(early_kernel, tables), out_shape=[jax.Sh...  3.32 us
    unnamed x2, local copies, waits for them, and re-layouts  1.04 us
    reduce_sum x1, other arithmetic, slot_table(): count = jnp.sum(here.astype(jnp.int32), axis=1, keepdims=True)  0.8 us
  transfers between devices with their start and end apart: 9, of which 6 were waited for; matrix products, arithmetic and copies ran while one was open for 8% of the time, Pallas kernels for 9%

profile of v3, /device:TPU:25, one launch (start us, length us, event | category | flops | bytes accessed | tf_op | source)
XLA Modules:
  0.0 36.8 jit_solution(3181063469156513503)
XLA Ops:
  0.0 0.2 collective-permute-start
  0.2 2.0 %collective-permute-start.1 = (f32[2,4,128,128]{3,2,1,0:T(8,128)}, f32[2,4,128,128]{3,2,1,0:T(8,128)S(1)}, u32[]{:S(2)}, u32[]{:S(2)}) collective-permute-start(f32[2,4,128,128]{3,2,1,0:T(8,128)} %own_hbm.1), channel_id=1, source_target_pairs={{1,0},{0,1},{17,16},{16,17},{3,2},{2,3},{19,18},{18,19},{5,4},{4,5... | collective-permute-start | bytes 1572872 | tf_op jit(solution)/shard_map/ppermute | solution.py:247
  2.2 0.8 %fusion.1 = (s32[8]{0:T(128)S(1)}, s32[8,8]{1,0:T(8,128)S(1)}) fusion(s32[8,16]{1,0:T(8,128)} %param.3), kind=kLoop, calls=%fused_computation.11 | loop fusion | flops 184 | bytes 544 | tf_op jit(solution)/shard_map/reduce_sum | solution.py:213
  3.0 0.1 fusion
  3.1 0.2 convert_reduce_fusion
  3.3 0.1 add_select_fusion
  3.4 0.2 select_reduce_fusion
  3.6 0.3 collective-permute-done.1.own_swap
  3.9 0.3 collective-permute-start.2
  4.2 0.7 %compare_convert_fusion = s32[8,8]{1,0:T(8,128)S(1)} fusion(s32[8,16]{1,0:T(8,128)} %param.3), kind=kLoop, calls=%fused_computation.6 | loop fusion | flops 128 | bytes 512 | tf_op jit(solution)/shard_map/convert_element_type | solution.py:213
  4.9 0.7 %compare_select_fusion = s32[8,8]{1,0:T(8,128)S(1)} fusion(s32[8,8]{1,0:T(8,128)S(1)} %select_reduce_fusion, s32[8,16]{1,0:T(8,128)} %param.3), kind=kLoop, calls=%fused_computation.5 | loop fusion | flops 128 | bytes 768 | tf_op jit(solution)/shard_map/jit(_where)/select_n | solution.py:221
  5.5 0.1 pad_add_fusion.table_ref
  5.6 2.9 %collective-permute-done.r1 = f32[2,4,128,128]{3,2,1,0:T(8,128)S(1)} collective-permute-done((f32[2,4,128,128]{3,2,1,0:T(8,128)}, f32[2,4,128,128]{3,2,1,0:T(8,128)S(1)}, u32[]{:S(2)}, u32[]{:S(2)}) %collective-permute-start) | collective-permute-done | bytes 524320 | tf_op jit(solution)/shard_map/ppermute | solution.py:247
  8.5 0.2 collective-permute-start.6
  8.7 2.9 %collective-permute-start.4 = (f32[2,4,128,128]{3,2,1,0:T(8,128)S(1)}, f32[2,4,128,128]{3,2,1,0:T(8,128)S(1)}, u32[]{:S(2)}, u32[]{:S(2)}) collective-permute-start(f32[2,4,128,128]{3,2,1,0:T(8,128)S(1)} %collective-permute-done.r1), channel_id=1, source_target_pairs={{1,0},{0,1},{17,16},{16,17},{3,2},{2,3},{19,18},{18,19},{5,4},{4,5... | collective-permute-start | bytes 1572872 | tf_op jit(solution)/shard_map/ppermute | solution.py:247
  11.6 8.2 %collective-permute-done.2.r2 = f32[2,4,128,128]{3,2,1,0:T(8,128)S(1)} collective-permute-done((f32[2,4,128,128]{3,2,1,0:T(8,128)S(1)}, f32[2,4,128,128]{3,2,1,0:T(8,128)S(1)}, u32[]{:S(2)}, u32[]{:S(2)}) %collective-permute-start.2) | collective-permute-done | bytes 524320 | tf_op jit(solution)/shard_map/ppermute | solution.py:247
  19.8 0.0 collective-permute-start.5
  19.8 0.0 collective-permute-start.3
  19.8 0.1 pad_add_fusion.1.place_ref
  19.9 0.0 collective-permute-done.6.r3
  19.9 1.4 %collective-permute-start.7 = (f32[2,4,128,128]{3,2,1,0:T(8,128)S(1)}, f32[2,4,128,128]{3,2,1,0:T(8,128)S(1)}, u32[]{:S(2)}, u32[]{:S(2)}) collective-permute-start(f32[2,4,128,128]{3,2,1,0:T(8,128)S(1)} %collective-permute-done.6.r3), channel_id=1, source_target_pairs={{1,0},{0,1},{17,16},{16,17},{3,2},{2,3},{19,18},{18,19},{5,4},{4,5... | collective-permute-start | bytes 1572872 | tf_op jit(solution)/shard_map/ppermute | solution.py:247
  21.3 0.0 collective-permute-done.4.t1
  21.3 0.5 %collective-permute-done.5.t2 = f32[2,4,128,128]{3,2,1,0:T(8,128)} collective-permute-done((f32[2,4,128,128]{3,2,1,0:T(8,128)S(1)}, f32[2,4,128,128]{3,2,1,0:T(8,128)}, u32[]{:S(2)}, u32[]{:S(2)}) %collective-permute-start.5) | collective-permute-done | bytes 524320 | tf_op jit(solution)/shard_map/ppermute | solution.py:247
  21.8 0.0 copy-start
  21.8 1.0 %copy-done = f32[2,4,128,128]{3,2,1,0:T(8,128)S(1)} copy-done((f32[2,4,128,128]{3,2,1,0:T(8,128)S(1)}, f32[2,4,128,128]{3,2,1,0:T(8,128)}, u32[]{:S(2)}) %copy-start) | copy-done | bytes 524312
  22.9 3.3 %early.1 = (bf16[1024,1024]{1,0:T(8,128)(2,1)S(1)}, bf16[1024,1024]{1,0:T(8,128)(2,1)S(1)}, bf16[512,1024]{1,0:T(8,128)(2,1)S(1)}, f32[256,1024]{1,0:T(8,128)S(1)}) custom-call(s32[8,24]{1,0:T(8,128)S(1)} %pad_add_fusion.table_ref, s32[3]{0:T(128)S(1)} %pad_add_fusion.1.place_ref, f32[2,4,128,128]{3,2,1,0:T(8,128)S(1)} %copy-done, ...), custom_call_target="tpu_custom_call" | custom-call | tf_op jit(solution)/shard_map/early/pallas_call | solution.py:283
  26.2 4.3 %collective-permute-done.3.r4 = f32[2,4,128,128]{3,2,1,0:T(8,128)S(1)} collective-permute-done((f32[2,4,128,128]{3,2,1,0:T(8,128)S(1)}, f32[2,4,128,128]{3,2,1,0:T(8,128)S(1)}, u32[]{:S(2)}, u32[]{:S(2)}) %collective-permute-start.3) | collective-permute-done | bytes 524320 | tf_op jit(solution)/shard_map/ppermute | solution.py:247
  30.5 0.0 collective-permute-start.8
  30.5 0.0 collective-permute-done.7.t3
  30.5 1.9 %collective-permute-done.8.t4 = f32[2,4,128,128]{3,2,1,0:T(8,128)S(1)} collective-permute-done((f32[2,4,128,128]{3,2,1,0:T(8,128)S(1)}, f32[2,4,128,128]{3,2,1,0:T(8,128)S(1)}, u32[]{:S(2)}, u32[]{:S(2)}) %collective-permute-start.8) | collective-permute-done | bytes 524320 | tf_op jit(solution)/shard_map/ppermute | solution.py:247
  32.4 4.4 %late.1 = (f32[2,4,128,128]{3,2,1,0:T(8,128)}, bf16[1024,1024]{1,0:T(8,128)(2,1)S(1)}, bf16[1024,1024]{1,0:T(8,128)(2,1)S(1)}) custom-call(s32[8,24]{1,0:T(8,128)S(1)} %pad_add_fusion.table_ref, s32[3]{0:T(128)S(1)} %pad_add_fusion.1.place_ref, f32[2,4,128,128]{3,2,1,0:T(8,128)S(1)} %collective-permute-done.3.r4, ...), custom_call_target="tpu_custom_call", output_to_operand_aliasing={{1}: (5, {}), {2}: (6, {})} | custom-call | tf_op jit(solution)/shard_map/late/pallas_call | solution.py:300
  (1 shorter events, 0.0 us)
Async XLA Ops:
  0.0 8.5 %collective-permute-start = (f32[2,4,128,128]{3,2,1,0:T(8,128)}, f32[2,4,128,128]{3,2,1,0:T(8,128)S(1)}, u32[]{:S(2)}, u32[]{:S(2)}) collective-permute-start(f32[2,4,128,128]{3,2,1,0:T(8,128)} %own_hbm.1), channel_id=1, source_target_pairs={{2,0},{0,4},{4,8},{8,12},{12,14},{14,15},{15,13},{13,9},{9,5},{5,1... | collective-permute-start | bytes 1572872 | tf_op jit(solution)/shard_map/ppermute | solution.py:247
  0.2 3.7 %collective-permute-start.1 = (f32[2,4,128,128]{3,2,1,0:T(8,128)}, f32[2,4,128,128]{3,2,1,0:T(8,128)S(1)}, u32[]{:S(2)}, u32[]{:S(2)}) collective-permute-start(f32[2,4,128,128]{3,2,1,0:T(8,128)} %own_hbm.1), channel_id=1, source_target_pairs={{1,0},{0,1},{17,16},{16,17},{3,2},{2,3},{19,18},{18,19},{5,4},{4,5... | collective-permute-start | bytes 1572872 | tf_op jit(solution)/shard_map/ppermute | solution.py:247
  3.9 15.9 %collective-permute-start.2 = (f32[2,4,128,128]{3,2,1,0:T(8,128)S(1)}, f32[2,4,128,128]{3,2,1,0:T(8,128)S(1)}, u32[]{:S(2)}, u32[]{:S(2)}) collective-permute-start(f32[2,4,128,128]{3,2,1,0:T(8,128)S(1)} %collective-permute-done.1.own_swap), channel_id=1, source_target_pairs={{2,0},{0,4},{4,8},{8,12},{12,14},{14,15},{15,13},{13,9},{9,5},{5,1... | collective-permute-start | bytes 1572872 | tf_op jit(solution)/shard_map/ppermute | solution.py:247
  8.5 11.3 %collective-permute-start.6 = (f32[2,4,128,128]{3,2,1,0:T(8,128)S(1)}, f32[2,4,128,128]{3,2,1,0:T(8,128)S(1)}, u32[]{:S(2)}, u32[]{:S(2)}) collective-permute-start(f32[2,4,128,128]{3,2,1,0:T(8,128)S(1)} %collective-permute-done.r1), channel_id=1, source_target_pairs={{14,0},{0,4},{4,8},{8,12},{12,14},{3,13},{13,9},{9,5},{5,1},{1,3},... | collective-permute-start | bytes 1572872 | tf_op jit(solution)/shard_map/ppermute | solution.py:247
  8.7 12.6 %collective-permute-start.4 = (f32[2,4,128,128]{3,2,1,0:T(8,128)S(1)}, f32[2,4,128,128]{3,2,1,0:T(8,128)S(1)}, u32[]{:S(2)}, u32[]{:S(2)}) collective-permute-start(f32[2,4,128,128]{3,2,1,0:T(8,128)S(1)} %collective-permute-done.r1), channel_id=1, source_target_pairs={{1,0},{0,1},{17,16},{16,17},{3,2},{2,3},{19,18},{18,19},{5,4},{4,5... | collective-permute-start | bytes 1572872 | tf_op jit(solution)/shard_map/ppermute | solution.py:247
  19.8 2.0 %collective-permute-start.5 = (f32[2,4,128,128]{3,2,1,0:T(8,128)S(1)}, f32[2,4,128,128]{3,2,1,0:T(8,128)}, u32[]{:S(2)}, u32[]{:S(2)}) collective-permute-start(f32[2,4,128,128]{3,2,1,0:T(8,128)S(1)} %collective-permute-done.2.r2), channel_id=1, source_target_pairs={{1,0},{0,1},{17,16},{16,17},{3,2},{2,3},{19,18},{18,19},{5,4},{4,5... | collective-permute-start | bytes 1572872 | tf_op jit(solution)/shard_map/ppermute | solution.py:247
  19.8 10.7 %collective-permute-start.3 = (f32[2,4,128,128]{3,2,1,0:T(8,128)S(1)}, f32[2,4,128,128]{3,2,1,0:T(8,128)S(1)}, u32[]{:S(2)}, u32[]{:S(2)}) collective-permute-start(f32[2,4,128,128]{3,2,1,0:T(8,128)S(1)} %collective-permute-done.2.r2), channel_id=1, source_target_pairs={{14,0},{0,4},{4,8},{8,12},{12,14},{3,13},{13,9},{9,5},{5,1},{1,3},... | collective-permute-start | bytes 1572872 | tf_op jit(solution)/shard_map/ppermute | solution.py:247
  19.9 10.7 %collective-permute-start.7 = (f32[2,4,128,128]{3,2,1,0:T(8,128)S(1)}, f32[2,4,128,128]{3,2,1,0:T(8,128)S(1)}, u32[]{:S(2)}, u32[]{:S(2)}) collective-permute-start(f32[2,4,128,128]{3,2,1,0:T(8,128)S(1)} %collective-permute-done.6.r3), channel_id=1, source_target_pairs={{1,0},{0,1},{17,16},{16,17},{3,2},{2,3},{19,18},{18,19},{5,4},{4,5... | collective-permute-start | bytes 1572872 | tf_op jit(solution)/shard_map/ppermute | solution.py:247
  21.8 1.0 %copy-start = (f32[2,4,128,128]{3,2,1,0:T(8,128)S(1)}, f32[2,4,128,128]{3,2,1,0:T(8,128)}, u32[]{:S(2)}) copy-start(f32[2,4,128,128]{3,2,1,0:T(8,128)} %own_hbm.1) | copy-start | bytes 1572868
  30.5 1.9 %collective-permute-start.8 = (f32[2,4,128,128]{3,2,1,0:T(8,128)S(1)}, f32[2,4,128,128]{3,2,1,0:T(8,128)S(1)}, u32[]{:S(2)}, u32[]{:S(2)}) collective-permute-start(f32[2,4,128,128]{3,2,1,0:T(8,128)S(1)} %collective-permute-done.3.r4), channel_id=1, source_target_pairs={{1,0},{0,1},{17,16},{16,17},{3,2},{2,3},{19,18},{18,19},{5,4},{4,5... | collective-permute-start | bytes 1572872 | tf_op jit(solution)/shard_map/ppermute | solution.py:247

commit v4 on v3

--- a/solution.py
+++ b/solution.py
@@ -249,6 +249,11 @@
     def swap(block):
         return move(block, [])
 
+    def move_only(block, chains_of):
+        pairs = [(chain[i], chain[i + 1]) for chain in chains_of for i in range(len(chain) - 1)]
+        route = [(index(g, a), index(g, b)) for g in range(groups) for a, b in pairs]
+        return lax.ppermute(block, AXES, route)
+
     up = [(z, 0, 0) for z in range(chains)] + [(last, 1, 0)]
     down = [(z, 0, 1) for z in reversed(range(chains))] + [(0, 1, 1)]
     first = [up + [(last, 1, 1)] + down + [(0, 1, 0)]]
@@ -262,7 +267,7 @@
     table = slot_table(columns, lanes * width)
     r1 = move(x_blocks, first)
     own_swap = swap(x_blocks)
-    r2 = move(own_swap, first)
+    r2 = move_only(own_swap, [up, down])
     r1, table = lax.optimization_barrier((r1, table))
     r3 = move(r1, second)
     t1 = swap(r1)

time: 37.1 us -> 34.8 us (0.938)
  the two profiles are of different devices: /device:TPU:25 before, /device:TPU:0 now
where the time goes in v4:
time: 34.8 us; the launch traced here: 34.5 us
  waiting for transfers between devices  11.6 us (33%)
  starting transfers between devices  11.1 us (32%)
  Pallas kernels  7.75 us (22%)
  other arithmetic  2.94 us (8%)
  local copies, waits for them, and re-layouts  1.04 us (3%)
    ppermute x8, waiting for transfers between devices, move(): return lax.ppermute(block, AXES, route)  8.46 us
    ppermute x8, starting transfers between devices, move(): return lax.ppermute(block, AXES, route)  7.63 us
    pallas_call x1, Pallas kernels, gather_local(): pl.pallas_call(functools.partial(late_kernel, tables), out_shape=[jax.Sha...  4.43 us
    ppermute x1, starting transfers between devices, move_only(): return lax.ppermute(block, AXES, route)  3.5 us
    pallas_call x1, Pallas kernels, gather_local(): pl.pallas_call(functools.partial(early_kernel, tables), out_shape=[jax.Sh...  3.31 us
    ppermute x1, waiting for transfers between devices, move_only(): return lax.ppermute(block, AXES, route)  3.13 us
    unnamed x2, local copies, waits for them, and re-layouts  1.04 us
    reduce_sum x1, other arithmetic, slot_table(): count = jnp.sum(here.astype(jnp.int32), axis=1, keepdims=True)  0.8 us
  transfers between devices with their start and end apart: 9, of which 6 were waited for; matrix products, arithmetic and copies ran while one was open for 9% of the time, Pallas kernels for 10%

profile of v4, /device:TPU:0, one launch (start us, length us, event | category | flops | bytes accessed | tf_op | source)
XLA Modules:
  0.0 34.5 jit_solution(8111417424062634170)
XLA Ops:
  0.0 3.0 %collective-permute-start = (f32[2,4,128,128]{3,2,1,0:T(8,128)}, f32[2,4,128,128]{3,2,1,0:T(8,128)S(1)}, u32[]{:S(2)}, u32[]{:S(2)}) collective-permute-start(f32[2,4,128,128]{3,2,1,0:T(8,128)} %own_hbm.1), channel_id=1, source_target_pairs={{2,0},{0,4},{4,8},{8,12},{12,14},{14,15},{15,13},{13,9},{9,5},{5,1... | collective-permute-start | bytes 1572872 | tf_op jit(solution)/shard_map/ppermute | solution.py:247
  3.0 0.0 collective-permute-start.1
  3.0 0.8 %fusion.1 = (s32[8]{0:T(128)S(1)}, s32[8,8]{1,0:T(8,128)S(1)}) fusion(s32[8,16]{1,0:T(8,128)} %param.3), kind=kLoop, calls=%fused_computation.11 | loop fusion | flops 184 | bytes 544 | tf_op jit(solution)/shard_map/reduce_sum | solution.py:213
  3.8 0.1 fusion
  3.9 0.2 convert_reduce_fusion
  4.2 0.1 add_select_fusion
  4.2 0.2 select_reduce_fusion
  4.4 0.7 %collective-permute-done.1.own_swap = f32[2,4,128,128]{3,2,1,0:T(8,128)S(1)} collective-permute-done((f32[2,4,128,128]{3,2,1,0:T(8,128)}, f32[2,4,128,128]{3,2,1,0:T(8,128)S(1)}, u32[]{:S(2)}, u32[]{:S(2)}) %collective-permute-start.1) | collective-permute-done | bytes 524320 | tf_op jit(solution)/shard_map/ppermute | solution.py:247
  5.1 3.5 %collective-permute-start.2 = (f32[2,4,128,128]{3,2,1,0:T(8,128)S(1)}, f32[2,4,128,128]{3,2,1,0:T(8,128)S(1)}, u32[]{:S(2)}, u32[]{:S(2)}) collective-permute-start(f32[2,4,128,128]{3,2,1,0:T(8,128)S(1)} %collective-permute-done.1.own_swap), channel_id=1, source_target_pairs={{0,4},{4,8},{8,12},{12,14},{13,9},{9,5},{5,1},{1,3},{16,20},{20,24... | collective-permute-start | bytes 1572872 | tf_op jit(solution)/shard_map/ppermute | solution.py:255
  8.7 0.7 %compare_convert_fusion = s32[8,8]{1,0:T(8,128)S(1)} fusion(s32[8,16]{1,0:T(8,128)} %param.3), kind=kLoop, calls=%fused_computation.6 | loop fusion | flops 128 | bytes 512 | tf_op jit(solution)/shard_map/convert_element_type | solution.py:213
  9.3 0.7 %compare_select_fusion = s32[8,8]{1,0:T(8,128)S(1)} fusion(s32[8,8]{1,0:T(8,128)S(1)} %select_reduce_fusion, s32[8,16]{1,0:T(8,128)} %param.3), kind=kLoop, calls=%fused_computation.5 | loop fusion | flops 128 | bytes 768 | tf_op jit(solution)/shard_map/jit(_where)/select_n | solution.py:221
  10.0 0.1 pad_add_fusion.table_ref
  10.1 0.2 collective-permute-done.r1
  10.3 2.1 %collective-permute-start.6 = (f32[2,4,128,128]{3,2,1,0:T(8,128)S(1)}, f32[2,4,128,128]{3,2,1,0:T(8,128)S(1)}, u32[]{:S(2)}, u32[]{:S(2)}) collective-permute-start(f32[2,4,128,128]{3,2,1,0:T(8,128)S(1)} %collective-permute-done.r1), channel_id=1, source_target_pairs={{14,0},{0,4},{4,8},{8,12},{12,14},{3,13},{13,9},{9,5},{5,1},{1,3},... | collective-permute-start | bytes 1572872 | tf_op jit(solution)/shard_map/ppermute | solution.py:247
  12.4 0.0 collective-permute-start.4
  12.4 3.1 %collective-permute-done.2.r2 = f32[2,4,128,128]{3,2,1,0:T(8,128)S(1)} collective-permute-done((f32[2,4,128,128]{3,2,1,0:T(8,128)S(1)}, f32[2,4,128,128]{3,2,1,0:T(8,128)S(1)}, u32[]{:S(2)}, u32[]{:S(2)}) %collective-permute-start.2) | collective-permute-done | bytes 524320 | tf_op jit(solution)/shard_map/ppermute | solution.py:255
  15.6 0.0 collective-permute-start.5
  15.6 2.5 %collective-permute-start.3 = (f32[2,4,128,128]{3,2,1,0:T(8,128)S(1)}, f32[2,4,128,128]{3,2,1,0:T(8,128)S(1)}, u32[]{:S(2)}, u32[]{:S(2)}) collective-permute-start(f32[2,4,128,128]{3,2,1,0:T(8,128)S(1)} %collective-permute-done.2.r2), channel_id=1, source_target_pairs={{14,0},{0,4},{4,8},{8,12},{12,14},{3,13},{13,9},{9,5},{5,1},{1,3},... | collective-permute-start | bytes 1572872 | tf_op jit(solution)/shard_map/ppermute | solution.py:247
  18.0 0.1 pad_add_fusion.1.place_ref
  18.1 4.4 %collective-permute-done.6.r3 = f32[2,4,128,128]{3,2,1,0:T(8,128)S(1)} collective-permute-done((f32[2,4,128,128]{3,2,1,0:T(8,128)S(1)}, f32[2,4,128,128]{3,2,1,0:T(8,128)S(1)}, u32[]{:S(2)}, u32[]{:S(2)}) %collective-permute-start.6) | collective-permute-done | bytes 524320 | tf_op jit(solution)/shard_map/ppermute | solution.py:247
  22.5 0.0 collective-permute-start.7
  22.5 0.0 collective-permute-done.4.t1
  22.5 0.0 collective-permute-done.5.t2
  22.5 0.0 copy-start
  22.6 1.0 %copy-done = f32[2,4,128,128]{3,2,1,0:T(8,128)S(1)} copy-done((f32[2,4,128,128]{3,2,1,0:T(8,128)S(1)}, f32[2,4,128,128]{3,2,1,0:T(8,128)}, u32[]{:S(2)}) %copy-start) | copy-done | bytes 524312
  23.6 3.3 %early.1 = (bf16[1024,1024]{1,0:T(8,128)(2,1)S(1)}, bf16[1024,1024]{1,0:T(8,128)(2,1)S(1)}, bf16[512,1024]{1,0:T(8,128)(2,1)S(1)}, f32[256,1024]{1,0:T(8,128)S(1)}) custom-call(s32[8,24]{1,0:T(8,128)S(1)} %pad_add_fusion.table_ref, s32[3]{0:T(128)S(1)} %pad_add_fusion.1.place_ref, f32[2,4,128,128]{3,2,1,0:T(8,128)S(1)} %copy-done, ...), custom_call_target="tpu_custom_call" | custom-call | tf_op jit(solution)/shard_map/early/pallas_call | solution.py:288
  26.9 1.2 %collective-permute-done.3.r4 = f32[2,4,128,128]{3,2,1,0:T(8,128)S(1)} collective-permute-done((f32[2,4,128,128]{3,2,1,0:T(8,128)S(1)}, f32[2,4,128,128]{3,2,1,0:T(8,128)S(1)}, u32[]{:S(2)}, u32[]{:S(2)}) %collective-permute-start.3) | collective-permute-done | bytes 524320 | tf_op jit(solution)/shard_map/ppermute | solution.py:247
  28.1 0.0 collective-permute-start.8
  28.2 0.0 collective-permute-done.7.t3
  28.2 1.9 %collective-permute-done.8.t4 = f32[2,4,128,128]{3,2,1,0:T(8,128)S(1)} collective-permute-done((f32[2,4,128,128]{3,2,1,0:T(8,128)S(1)}, f32[2,4,128,128]{3,2,1,0:T(8,128)S(1)}, u32[]{:S(2)}, u32[]{:S(2)}) %collective-permute-start.8) | collective-permute-done | bytes 524320 | tf_op jit(solution)/shard_map/ppermute | solution.py:247
  30.1 4.4 %late.1 = (f32[2,4,128,128]{3,2,1,0:T(8,128)}, bf16[1024,1024]{1,0:T(8,128)(2,1)S(1)}, bf16[1024,1024]{1,0:T(8,128)(2,1)S(1)}) custom-call(s32[8,24]{1,0:T(8,128)S(1)} %pad_add_fusion.table_ref, s32[3]{0:T(128)S(1)} %pad_add_fusion.1.place_ref, f32[2,4,128,128]{3,2,1,0:T(8,128)S(1)} %collective-permute-done.3.r4, ...), custom_call_target="tpu_custom_call", output_to_operand_aliasing={{1}: (5, {}), {2}: (6, {})} | custom-call | tf_op jit(solution)/shard_map/late/pallas_call | solution.py:305
  (1 shorter events, 0.0 us)
Async XLA Ops:
  0.0 10.3 %collective-permute-start = (f32[2,4,128,128]{3,2,1,0:T(8,128)}, f32[2,4,128,128]{3,2,1,0:T(8,128)S(1)}, u32[]{:S(2)}, u32[]{:S(2)}) collective-permute-start(f32[2,4,128,128]{3,2,1,0:T(8,128)} %own_hbm.1), channel_id=1, source_target_pairs={{2,0},{0,4},{4,8},{8,12},{12,14},{14,15},{15,13},{13,9},{9,5},{5,1... | collective-permute-start | bytes 1572872 | tf_op jit(solution)/shard_map/ppermute | solution.py:247
  3.0 2.1 %collective-permute-start.1 = (f32[2,4,128,128]{3,2,1,0:T(8,128)}, f32[2,4,128,128]{3,2,1,0:T(8,128)S(1)}, u32[]{:S(2)}, u32[]{:S(2)}) collective-permute-start(f32[2,4,128,128]{3,2,1,0:T(8,128)} %own_hbm.1), channel_id=1, source_target_pairs={{1,0},{0,1},{17,16},{16,17},{3,2},{2,3},{19,18},{18,19},{5,4},{4,5... | collective-permute-start | bytes 1572872 | tf_op jit(solution)/shard_map/ppermute | solution.py:247
  5.1 10.4 %collective-permute-start.2 = (f32[2,4,128,128]{3,2,1,0:T(8,128)S(1)}, f32[2,4,128,128]{3,2,1,0:T(8,128)S(1)}, u32[]{:S(2)}, u32[]{:S(2)}) collective-permute-start(f32[2,4,128,128]{3,2,1,0:T(8,128)S(1)} %collective-permute-done.1.own_swap), channel_id=1, source_target_pairs={{0,4},{4,8},{8,12},{12,14},{13,9},{9,5},{5,1},{1,3},{16,20},{20,24... | collective-permute-start | bytes 1572872 | tf_op jit(solution)/shard_map/ppermute | solution.py:255
  10.3 12.2 %collective-permute-start.6 = (f32[2,4,128,128]{3,2,1,0:T(8,128)S(1)}, f32[2,4,128,128]{3,2,1,0:T(8,128)S(1)}, u32[]{:S(2)}, u32[]{:S(2)}) collective-permute-start(f32[2,4,128,128]{3,2,1,0:T(8,128)S(1)} %collective-permute-done.r1), channel_id=1, source_target_pairs={{14,0},{0,4},{4,8},{8,12},{12,14},{3,13},{13,9},{9,5},{5,1},{1,3},... | collective-permute-start | bytes 1572872 | tf_op jit(solution)/shard_map/ppermute | solution.py:247
  12.4 10.1 %collective-permute-start.4 = (f32[2,4,128,128]{3,2,1,0:T(8,128)S(1)}, f32[2,4,128,128]{3,2,1,0:T(8,128)S(1)}, u32[]{:S(2)}, u32[]{:S(2)}) collective-permute-start(f32[2,4,128,128]{3,2,1,0:T(8,128)S(1)} %collective-permute-done.r1), channel_id=1, source_target_pairs={{1,0},{0,1},{17,16},{16,17},{3,2},{2,3},{19,18},{18,19},{5,4},{4,5... | collective-permute-start | bytes 1572872 | tf_op jit(solution)/shard_map/ppermute | solution.py:247
  15.6 7.0 %collective-permute-start.5 = (f32[2,4,128,128]{3,2,1,0:T(8,128)S(1)}, f32[2,4,128,128]{3,2,1,0:T(8,128)}, u32[]{:S(2)}, u32[]{:S(2)}) collective-permute-start(f32[2,4,128,128]{3,2,1,0:T(8,128)S(1)} %collective-permute-done.2.r2), channel_id=1, source_target_pairs={{1,0},{0,1},{17,16},{16,17},{3,2},{2,3},{19,18},{18,19},{5,4},{4,5... | collective-permute-start | bytes 1572872 | tf_op jit(solution)/shard_map/ppermute | solution.py:247
  15.6 12.6 %collective-permute-start.3 = (f32[2,4,128,128]{3,2,1,0:T(8,128)S(1)}, f32[2,4,128,128]{3,2,1,0:T(8,128)S(1)}, u32[]{:S(2)}, u32[]{:S(2)}) collective-permute-start(f32[2,4,128,128]{3,2,1,0:T(8,128)S(1)} %collective-permute-done.2.r2), channel_id=1, source_target_pairs={{14,0},{0,4},{4,8},{8,12},{12,14},{3,13},{13,9},{9,5},{5,1},{1,3},... | collective-permute-start | bytes 1572872 | tf_op jit(solution)/shard_map/ppermute | solution.py:247
  22.5 5.6 %collective-permute-start.7 = (f32[2,4,128,128]{3,2,1,0:T(8,128)S(1)}, f32[2,4,128,128]{3,2,1,0:T(8,128)S(1)}, u32[]{:S(2)}, u32[]{:S(2)}) collective-permute-start(f32[2,4,128,128]{3,2,1,0:T(8,128)S(1)} %collective-permute-done.6.r3), channel_id=1, source_target_pairs={{1,0},{0,1},{17,16},{16,17},{3,2},{2,3},{19,18},{18,19},{5,4},{4,5... | collective-permute-start | bytes 1572872 | tf_op jit(solution)/shard_map/ppermute | solution.py:247
  22.5 1.0 %copy-start = (f32[2,4,128,128]{3,2,1,0:T(8,128)S(1)}, f32[2,4,128,128]{3,2,1,0:T(8,128)}, u32[]{:S(2)}) copy-start(f32[2,4,128,128]{3,2,1,0:T(8,128)} %own_hbm.1) | copy-start | bytes 1572868
  28.1 1.9 %collective-permute-start.8 = (f32[2,4,128,128]{3,2,1,0:T(8,128)S(1)}, f32[2,4,128,128]{3,2,1,0:T(8,128)S(1)}, u32[]{:S(2)}, u32[]{:S(2)}) collective-permute-start(f32[2,4,128,128]{3,2,1,0:T(8,128)S(1)} %collective-permute-done.3.r4), channel_id=1, source_target_pairs={{1,0},{0,1},{17,16},{16,17},{3,2},{2,3},{19,18},{18,19},{5,4},{4,5... | collective-permute-start | bytes 1572872 | tf_op jit(solution)/shard_map/ppermute | solution.py:247

commit v5 on v4

--- a/solution.py
+++ b/solution.py
@@ -131,6 +131,17 @@
                     own[pl.ds((slab + r) * edge, edge), col] = block_low
 
 
+def add_plane(plane, left, high, low, part_ref):
+    depth, tile = part_ref.shape[0], 256
+
+    @pl.when(plane >= 0)
+    def _():
+        rows = pl.ds(pl.multiple_of(plane * depth, depth), depth)
+        for n in range(part_ref.shape[1] // tile):
+            cols = pl.ds(n * tile, tile)
+            part_ref[:, cols] += stacked_dot(left[:, rows], high[rows, cols], low[rows, cols])
+
+
 def early_kernel(
     tables, table_ref, place_ref, own_hbm, own_swap, r1, r2, t1, t2, r3,
     high, low, left, part_ref, own_ref, own_sem,
@@ -140,6 +151,7 @@
     own_copy = pltpu.make_async_copy(own_hbm, own_ref, own_sem)
     own_copy.start()
     here, there = lookup(near, place, lane), lookup(near, place, 1 - lane)
+    part_ref[...] = jnp.zeros_like(part_ref)
     store_piece(own_swap, place, 1 - lane, table_ref, high, low, left)
     store_piece(r1, here, lane, table_ref, high, low)
     store_piece(r2, here, 1 - lane, table_ref, high, low)
@@ -148,42 +160,40 @@
     store_piece(r3, lookup(far, place, lane), lane, table_ref, high, low)
     own_copy.wait()
     store_piece(own_ref, place, lane, table_ref, high, low, left)
-    order = high.shape[0]
-    depth, tile = order // 2, 256
-    rows = pl.ds(pl.multiple_of(place // 2 * depth, depth), depth)
-    for n in range(order // tile):
-        cols = pl.ds(n * tile, tile)
-        part_ref[:, cols] = stacked_dot(left[:, rows], high[rows, cols], low[rows, cols])
-
-
-def late_kernel(
-    tables, table_ref, place_ref, r4, t3, t4, high_in, low_in, left, part_ref,
-    out_ref, high, low, square, square_parts,
+    for plane in (place, here, there):
+        add_plane(plane, left, high, low, part_ref)
+
+
+def middle_kernel(
+    tables, table_ref, place_ref, r4, t3, high_in, low_in, left, part_in, high, low, part_ref
 ):
-    place, lane, group = place_ref[0], place_ref[1], place_ref[2]
+    place, lane = place_ref[0], place_ref[1]
     far = tables[1]
     here, there = lookup(far, place, lane), lookup(far, place, 1 - lane)
     store_piece(t3, there, 1 - lane, table_ref, high, low)
     store_piece(r4, here, 1 - lane, table_ref, high, low)
+    add_plane(here, left, high, low, part_ref)
+
+
+def late_kernel(
+    tables, table_ref, place_ref, t4, high_in, low_in, left, part_in,
+    out_hbm, high, low, square, square_parts, out_ref, out_sem,
+):
+    place, lane, group = place_ref[0], place_ref[1], place_ref[2]
+    there = lookup(tables[1], place, 1 - lane)
     store_piece(t4, there, lane, table_ref, high, low)
-    order = high.shape[0]
-    depth, tile = order // 2, 256
+    add_plane(there, left, high, low, square)
     slab, width, edge, _ = out_ref.shape
     act = 2 * width
-    rows = pl.ds(pl.multiple_of((1 - place // 2) * depth, depth), depth)
-    for n in range(order // tile):
-        cols = pl.ds(n * tile, tile)
-        square[:, cols] = part_ref[:, cols] + stacked_dot(
-            left[:, rows], high[rows, cols], low[rows, cols]
-        )
-        for r in range(slab):
-            for c in range(n * tile // edge, (n + 1) * tile // edge):
-                kept = table_ref[place * slab + r, 2 * act + c] > 0
-                col = pl.ds(c * edge, edge)
-                block = jnp.where(kept, square[pl.ds(r * edge, edge), col], 0.0)
-                block_high, block_low = split(block)
-                square_parts[pl.ds(2 * r * edge, edge), col] = block_high
-                square_parts[pl.ds((2 * r + 1) * edge, edge), col] = block_low
+    for r in range(slab):
+        for c in range(square.shape[1] // edge):
+            kept = table_ref[place * slab + r, 2 * act + c] > 0
+            col = pl.ds(c * edge, edge)
+            block = jnp.where(kept, square[pl.ds(r * edge, edge), col], 0.0)
+            block_high, block_low = split(block)
+            square_parts[pl.ds(2 * r * edge, edge), col] = block_high
+            square_parts[pl.ds((2 * r + 1) * edge, edge), col] = block_low
+    copies = []
     for r in range(slab):
         row = place * slab + r
         left_parts = square_parts[pl.ds(2 * r * edge, 2 * edge), :]
@@ -202,6 +212,13 @@
                 value = 3.0 * square[pl.ds(r * edge, edge), cols[k]]
                 value = value - 2.0 * cube[:, k * edge : (k + 1) * edge]
                 out_ref[r, w + k] = jnp.where(there, value, 0.0)
+            ready = (r, pl.ds(w, 2))
+            copies.append(
+                pltpu.make_async_copy(out_ref.at[ready], out_hbm.at[ready], out_sem.at[len(copies)])
+            )
+            copies[-1].start()
+    for copy in copies:
+        copy.wait()
 
 
 def slot_table(columns, act):
@@ -302,23 +319,30 @@
     t3 = swap(r3)
     r4, part = lax.optimization_barrier((r4, part))
     t4 = swap(r4)
-    out, _, _ = pl.pallas_call(
+    dense = [jax.ShapeDtypeStruct(a.shape, a.dtype) for a in (high, low, part)]
+    high, low, part = pl.pallas_call(
+        functools.partial(middle_kernel, tables),
+        out_shape=dense,
+        in_specs=[smem] * 2 + [vmem] * 6,
+        out_specs=[vmem] * 3,
+        input_output_aliases={4: 0, 5: 1, 7: 2},
+        compiler_params=params,
+        name="middle",
+    )(table, place, r4, t3, high, low, left, part)
+    out, _, _, _ = pl.pallas_call(
         functools.partial(late_kernel, tables),
-        out_shape=[
-            jax.ShapeDtypeStruct(x_blocks.shape, jnp.float32),
-            jax.ShapeDtypeStruct((order, order), jnp.bfloat16),
-            jax.ShapeDtypeStruct((order, order), jnp.bfloat16),
-        ],
-        in_specs=[smem] * 2 + [vmem] * 7,
-        out_specs=[vmem] * 3,
-        input_output_aliases={5: 1, 6: 2},
+        out_shape=[jax.ShapeDtypeStruct(x_blocks.shape, jnp.float32)] + dense,
+        in_specs=[smem] * 2 + [vmem] * 5,
+        out_specs=[pl.BlockSpec(memory_space=pltpu.HBM)] + [vmem] * 3,
+        input_output_aliases={3: 1, 4: 2, 6: 3},
         scratch_shapes=[
-            pltpu.VMEM((own, order), jnp.float32),
             pltpu.VMEM((2 * own, order), jnp.bfloat16),
+            pltpu.VMEM(x_blocks.shape, jnp.float32),
+            pltpu.SemaphoreType.DMA((slab * width // 2,)),
         ],
         compiler_params=params,
         name="late",
-    )(table, place, r4, t3, t4, high, low, left, part)
+    )(table, place, t4, high, low, left, part)
     return out
 
 

time: 34.8 us -> 34 us (0.977)
  waiting for transfers between devices: 11.6 us -> 9.82 us
  Pallas kernels: 7.75 us -> 8.73 us
    ppermute x8, waiting for transfers between devices: 8.46 us -> 6.69 us  [move(): return lax.ppermute(block, AXES, route)]
    pallas_call x0 -> x1, Pallas kernels: none -> 1.53 us  [gather_local(): pl.pallas_call(functools.partial(middle_kernel, tables), out_shape=dense,...]
    pallas_call x1, Pallas kernels: 4.43 us -> 3.66 us  [gather_local(): pl.pallas_call(functools.partial(late_kernel, tables), out_shape=[jax.Sha...]
  transfers between devices with their start and end apart: 9 -> 9, of which waited for: 6 -> 6; matrix products, arithmetic and copies ran while one was open for 9% -> 9% of each run, Pallas kernels for 10% -> 15%
where the time goes in v5:
time: 34 us; the launch traced here: 33.7 us
  starting transfers between devices  11.1 us (33%)
  waiting for transfers between devices  9.82 us (29%)
  Pallas kernels  8.73 us (26%)
  other arithmetic  2.94 us (9%)
  local copies, waits for them, and re-layouts  1.04 us (3%)
    ppermute x8, starting transfers between devices, move(): return lax.ppermute(block, AXES, route)  7.63 us
    ppermute x8, waiting for transfers between devices, move(): return lax.ppermute(block, AXES, route)  6.69 us
    pallas_call x1, Pallas kernels, gather_local(): pl.pallas_call(functools.partial(late_kernel, tables), out_shape=[jax.Sha...  3.66 us
    pallas_call x1, Pallas kernels, gather_local(): pl.pallas_call(functools.partial(early_kernel, tables), out_shape=[jax.Sh...  3.54 us
    ppermute x1, starting transfers between devices, move_only(): return lax.ppermute(block, AXES, route)  3.5 us
    ppermute x1, waiting for transfers between devices, move_only(): return lax.ppermute(block, AXES, route)  3.13 us
    pallas_call x1, Pallas kernels, gather_local(): pl.pallas_call(functools.partial(middle_kernel, tables), out_shape=dense,...  1.53 us
    unnamed x2, local copies, waits for them, and re-layouts  1.04 us
  transfers between devices with their start and end apart: 9, of which 6 were waited for; matrix products, arithmetic and copies ran while one was open for 9% of the time, Pallas kernels for 15%

profile of v5, /device:TPU:0, one launch (start us, length us, event | category | flops | bytes accessed | tf_op | source)
XLA Modules:
  0.0 33.7 jit_solution(12508789099549039865)
XLA Ops:
  0.0 3.0 %collective-permute-start = (f32[2,4,128,128]{3,2,1,0:T(8,128)}, f32[2,4,128,128]{3,2,1,0:T(8,128)S(1)}, u32[]{:S(2)}, u32[]{:S(2)}) collective-permute-start(f32[2,4,128,128]{3,2,1,0:T(8,128)} %own_hbm.1), channel_id=1, source_target_pairs={{2,0},{0,4},{4,8},{8,12},{12,14},{14,15},{15,13},{13,9},{9,5},{5,1... | collective-permute-start | bytes 1572872 | tf_op jit(solution)/shard_map/ppermute | solution.py:264
  3.0 0.0 collective-permute-start.1
  3.0 0.8 %fusion.1 = (s32[8]{0:T(128)S(1)}, s32[8,8]{1,0:T(8,128)S(1)}) fusion(s32[8,16]{1,0:T(8,128)} %param.3), kind=kLoop, calls=%fused_computation.11 | loop fusion | flops 184 | bytes 544 | tf_op jit(solution)/shard_map/reduce_sum | solution.py:230
  3.8 0.1 fusion
  3.9 0.2 convert_reduce_fusion
  4.2 0.1 add_select_fusion
  4.2 0.2 select_reduce_fusion
  4.4 0.7 %collective-permute-done.1.own_swap = f32[2,4,128,128]{3,2,1,0:T(8,128)S(1)} collective-permute-done((f32[2,4,128,128]{3,2,1,0:T(8,128)}, f32[2,4,128,128]{3,2,1,0:T(8,128)S(1)}, u32[]{:S(2)}, u32[]{:S(2)}) %collective-permute-start.1) | collective-permute-done | bytes 524320 | tf_op jit(solution)/shard_map/ppermute | solution.py:264
  5.1 3.5 %collective-permute-start.2 = (f32[2,4,128,128]{3,2,1,0:T(8,128)S(1)}, f32[2,4,128,128]{3,2,1,0:T(8,128)S(1)}, u32[]{:S(2)}, u32[]{:S(2)}) collective-permute-start(f32[2,4,128,128]{3,2,1,0:T(8,128)S(1)} %collective-permute-done.1.own_swap), channel_id=1, source_target_pairs={{0,4},{4,8},{8,12},{12,14},{13,9},{9,5},{5,1},{1,3},{16,20},{20,24... | collective-permute-start | bytes 1572872 | tf_op jit(solution)/shard_map/ppermute | solution.py:272
  8.7 0.7 %compare_convert_fusion = s32[8,8]{1,0:T(8,128)S(1)} fusion(s32[8,16]{1,0:T(8,128)} %param.3), kind=kLoop, calls=%fused_computation.6 | loop fusion | flops 128 | bytes 512 | tf_op jit(solution)/shard_map/convert_element_type | solution.py:230
  9.3 0.7 %compare_select_fusion = s32[8,8]{1,0:T(8,128)S(1)} fusion(s32[8,8]{1,0:T(8,128)S(1)} %select_reduce_fusion, s32[8,16]{1,0:T(8,128)} %param.3), kind=kLoop, calls=%fused_computation.5 | loop fusion | flops 128 | bytes 768 | tf_op jit(solution)/shard_map/jit(_where)/select_n | solution.py:238
  10.0 0.1 pad_add_fusion.table_ref
  10.1 0.2 collective-permute-done.r1
  10.3 2.1 %collective-permute-start.6 = (f32[2,4,128,128]{3,2,1,0:T(8,128)S(1)}, f32[2,4,128,128]{3,2,1,0:T(8,128)S(1)}, u32[]{:S(2)}, u32[]{:S(2)}) collective-permute-start(f32[2,4,128,128]{3,2,1,0:T(8,128)S(1)} %collective-permute-done.r1), channel_id=1, source_target_pairs={{14,0},{0,4},{4,8},{8,12},{12,14},{3,13},{13,9},{9,5},{5,1},{1,3},... | collective-permute-start | bytes 1572872 | tf_op jit(solution)/shard_map/ppermute | solution.py:264
  12.4 0.0 collective-permute-start.4
  12.4 3.1 %collective-permute-done.2.r2 = f32[2,4,128,128]{3,2,1,0:T(8,128)S(1)} collective-permute-done((f32[2,4,128,128]{3,2,1,0:T(8,128)S(1)}, f32[2,4,128,128]{3,2,1,0:T(8,128)S(1)}, u32[]{:S(2)}, u32[]{:S(2)}) %collective-permute-start.2) | collective-permute-done | bytes 524320 | tf_op jit(solution)/shard_map/ppermute | solution.py:272
  15.6 0.0 collective-permute-start.5
  15.6 2.5 %collective-permute-start.3 = (f32[2,4,128,128]{3,2,1,0:T(8,128)S(1)}, f32[2,4,128,128]{3,2,1,0:T(8,128)S(1)}, u32[]{:S(2)}, u32[]{:S(2)}) collective-permute-start(f32[2,4,128,128]{3,2,1,0:T(8,128)S(1)} %collective-permute-done.2.r2), channel_id=1, source_target_pairs={{14,0},{0,4},{4,8},{8,12},{12,14},{3,13},{13,9},{9,5},{5,1},{1,3},... | collective-permute-start | bytes 1572872 | tf_op jit(solution)/shard_map/ppermute | solution.py:264
  18.0 0.1 pad_add_fusion.1.place_ref
  18.1 4.4 %collective-permute-done.6.r3 = f32[2,4,128,128]{3,2,1,0:T(8,128)S(1)} collective-permute-done((f32[2,4,128,128]{3,2,1,0:T(8,128)S(1)}, f32[2,4,128,128]{3,2,1,0:T(8,128)S(1)}, u32[]{:S(2)}, u32[]{:S(2)}) %collective-permute-start.6) | collective-permute-done | bytes 524320 | tf_op jit(solution)/shard_map/ppermute | solution.py:264
  22.5 0.0 collective-permute-start.8
  22.5 0.0 collective-permute-done.4.t1
  22.5 0.0 collective-permute-done.5.t2
  22.5 0.0 copy-start
  22.6 1.0 %copy-done = f32[2,4,128,128]{3,2,1,0:T(8,128)S(1)} copy-done((f32[2,4,128,128]{3,2,1,0:T(8,128)S(1)}, f32[2,4,128,128]{3,2,1,0:T(8,128)}, u32[]{:S(2)}) %copy-start) | copy-done | bytes 524312
  23.6 3.5 %early.1 = (bf16[1024,1024]{1,0:T(8,128)(2,1)S(1)}, bf16[1024,1024]{1,0:T(8,128)(2,1)S(1)}, bf16[512,1024]{1,0:T(8,128)(2,1)S(1)}, f32[256,1024]{1,0:T(8,128)S(1)}) custom-call(s32[8,24]{1,0:T(8,128)S(1)} %pad_add_fusion.table_ref, s32[3]{0:T(128)S(1)} %pad_add_fusion.1.place_ref, f32[2,4,128,128]{3,2,1,0:T(8,128)S(1)} %copy-done, ...), custom_call_target="tpu_custom_call" | custom-call | tf_op jit(solution)/shard_map/early/pallas_call | solution.py:305
  27.1 1.0 %collective-permute-done.3.r4 = f32[2,4,128,128]{3,2,1,0:T(8,128)S(1)} collective-permute-done((f32[2,4,128,128]{3,2,1,0:T(8,128)S(1)}, f32[2,4,128,128]{3,2,1,0:T(8,128)S(1)}, u32[]{:S(2)}, u32[]{:S(2)}) %collective-permute-start.3) | collective-permute-done | bytes 524320 | tf_op jit(solution)/shard_map/ppermute | solution.py:264
  28.1 0.0 collective-permute-start.7
  28.2 0.0 collective-permute-done.8.t3
  28.2 1.5 %middle.1 = (bf16[1024,1024]{1,0:T(8,128)(2,1)S(1)}, bf16[1024,1024]{1,0:T(8,128)(2,1)S(1)}, f32[256,1024]{1,0:T(8,128)S(1)}) custom-call(s32[8,24]{1,0:T(8,128)S(1)} %pad_add_fusion.table_ref, s32[3]{0:T(128)S(1)} %pad_add_fusion.1.place_ref, ...), custom_call_target="tpu_custom_call", output_to_operand_aliasing={{0}: (4, {}), {1}: (5, {}), {2}: (7, {})} | custom-call | tf_op jit(solution)/shard_map/middle/pallas_call | solution.py:323
  29.7 0.4 %collective-permute-done.7.t4 = f32[2,4,128,128]{3,2,1,0:T(8,128)S(1)} collective-permute-done((f32[2,4,128,128]{3,2,1,0:T(8,128)S(1)}, f32[2,4,128,128]{3,2,1,0:T(8,128)S(1)}, u32[]{:S(2)}, u32[]{:S(2)}) %collective-permute-start.7) | collective-permute-done | bytes 524320 | tf_op jit(solution)/shard_map/ppermute | solution.py:264
  30.1 3.7 %late.1 = (f32[2,4,128,128]{3,2,1,0:T(8,128)}, bf16[1024,1024]{1,0:T(8,128)(2,1)S(1)}, bf16[1024,1024]{1,0:T(8,128)(2,1)S(1)}, f32[256,1024]{1,0:T(8,128)S(1)}) custom-call(s32[8,24]{1,0:T(8,128)S(1)} %pad_add_fusion.table_ref, s32[3]{0:T(128)S(1)} %pad_add_fusion.1.place_ref, ...), custom_call_target="tpu_custom_call", output_to_operand_aliasing={{1}: (3, {}), {2}: (4, {}), {3}: (6, {})} | custom-call | tf_op jit(solution)/shard_map/late/pallas_call | solution.py:332
  (1 shorter events, 0.0 us)
Async XLA Ops:
  0.0 10.3 %collective-permute-start = (f32[2,4,128,128]{3,2,1,0:T(8,128)}, f32[2,4,128,128]{3,2,1,0:T(8,128)S(1)}, u32[]{:S(2)}, u32[]{:S(2)}) collective-permute-start(f32[2,4,128,128]{3,2,1,0:T(8,128)} %own_hbm.1), channel_id=1, source_target_pairs={{2,0},{0,4},{4,8},{8,12},{12,14},{14,15},{15,13},{13,9},{9,5},{5,1... | collective-permute-start | bytes 1572872 | tf_op jit(solution)/shard_map/ppermute | solution.py:264
  3.0 2.1 %collective-permute-start.1 = (f32[2,4,128,128]{3,2,1,0:T(8,128)}, f32[2,4,128,128]{3,2,1,0:T(8,128)S(1)}, u32[]{:S(2)}, u32[]{:S(2)}) collective-permute-start(f32[2,4,128,128]{3,2,1,0:T(8,128)} %own_hbm.1), channel_id=1, source_target_pairs={{1,0},{0,1},{17,16},{16,17},{3,2},{2,3},{19,18},{18,19},{5,4},{4,5... | collective-permute-start | bytes 1572872 | tf_op jit(solution)/shard_map/ppermute | solution.py:264
  5.1 10.4 %collective-permute-start.2 = (f32[2,4,128,128]{3,2,1,0:T(8,128)S(1)}, f32[2,4,128,128]{3,2,1,0:T(8,128)S(1)}, u32[]{:S(2)}, u32[]{:S(2)}) collective-permute-start(f32[2,4,128,128]{3,2,1,0:T(8,128)S(1)} %collective-permute-done.1.own_swap), channel_id=1, source_target_pairs={{0,4},{4,8},{8,12},{12,14},{13,9},{9,5},{5,1},{1,3},{16,20},{20,24... | collective-permute-start | bytes 1572872 | tf_op jit(solution)/shard_map/ppermute | solution.py:272
  10.3 12.2 %collective-permute-start.6 = (f32[2,4,128,128]{3,2,1,0:T(8,128)S(1)}, f32[2,4,128,128]{3,2,1,0:T(8,128)S(1)}, u32[]{:S(2)}, u32[]{:S(2)}) collective-permute-start(f32[2,4,128,128]{3,2,1,0:T(8,128)S(1)} %collective-permute-done.r1), channel_id=1, source_target_pairs={{14,0},{0,4},{4,8},{8,12},{12,14},{3,13},{13,9},{9,5},{5,1},{1,3},... | collective-permute-start | bytes 1572872 | tf_op jit(solution)/shard_map/ppermute | solution.py:264
  12.4 10.1 %collective-permute-start.4 = (f32[2,4,128,128]{3,2,1,0:T(8,128)S(1)}, f32[2,4,128,128]{3,2,1,0:T(8,128)S(1)}, u32[]{:S(2)}, u32[]{:S(2)}) collective-permute-start(f32[2,4,128,128]{3,2,1,0:T(8,128)S(1)} %collective-permute-done.r1), channel_id=1, source_target_pairs={{1,0},{0,1},{17,16},{16,17},{3,2},{2,3},{19,18},{18,19},{5,4},{4,5... | collective-permute-start | bytes 1572872 | tf_op jit(solution)/shard_map/ppermute | solution.py:264
  15.6 7.0 %collective-permute-start.5 = (f32[2,4,128,128]{3,2,1,0:T(8,128)S(1)}, f32[2,4,128,128]{3,2,1,0:T(8,128)}, u32[]{:S(2)}, u32[]{:S(2)}) collective-permute-start(f32[2,4,128,128]{3,2,1,0:T(8,128)S(1)} %collective-permute-done.2.r2), channel_id=1, source_target_pairs={{1,0},{0,1},{17,16},{16,17},{3,2},{2,3},{19,18},{18,19},{5,4},{4,5... | collective-permute-start | bytes 1572872 | tf_op jit(solution)/shard_map/ppermute | solution.py:264
  15.6 12.6 %collective-permute-start.3 = (f32[2,4,128,128]{3,2,1,0:T(8,128)S(1)}, f32[2,4,128,128]{3,2,1,0:T(8,128)S(1)}, u32[]{:S(2)}, u32[]{:S(2)}) collective-permute-start(f32[2,4,128,128]{3,2,1,0:T(8,128)S(1)} %collective-permute-done.2.r2), channel_id=1, source_target_pairs={{14,0},{0,4},{4,8},{8,12},{12,14},{3,13},{13,9},{9,5},{5,1},{1,3},... | collective-permute-start | bytes 1572872 | tf_op jit(solution)/shard_map/ppermute | solution.py:264
  22.5 5.6 %collective-permute-start.8 = (f32[2,4,128,128]{3,2,1,0:T(8,128)S(1)}, f32[2,4,128,128]{3,2,1,0:T(8,128)S(1)}, u32[]{:S(2)}, u32[]{:S(2)}) collective-permute-start(f32[2,4,128,128]{3,2,1,0:T(8,128)S(1)} %collective-permute-done.6.r3), channel_id=1, source_target_pairs={{1,0},{0,1},{17,16},{16,17},{3,2},{2,3},{19,18},{18,19},{5,4},{4,5... | collective-permute-start | bytes 1572872 | tf_op jit(solution)/shard_map/ppermute | solution.py:264
  22.5 1.0 %copy-start = (f32[2,4,128,128]{3,2,1,0:T(8,128)S(1)}, f32[2,4,128,128]{3,2,1,0:T(8,128)}, u32[]{:S(2)}) copy-start(f32[2,4,128,128]{3,2,1,0:T(8,128)} %own_hbm.1) | copy-start | bytes 1572868
  28.1 1.9 %collective-permute-start.7 = (f32[2,4,128,128]{3,2,1,0:T(8,128)S(1)}, f32[2,4,128,128]{3,2,1,0:T(8,128)S(1)}, u32[]{:S(2)}, u32[]{:S(2)}) collective-permute-start(f32[2,4,128,128]{3,2,1,0:T(8,128)S(1)} %collective-permute-done.3.r4), channel_id=1, source_target_pairs={{1,0},{0,1},{17,16},{16,17},{3,2},{2,3},{19,18},{18,19},{5,4},{4,5... | collective-permute-start | bytes 1572872 | tf_op jit(solution)/shard_map/ppermute | solution.py:264

commit v6 on v5

--- a/solution.py
+++ b/solution.py
@@ -143,10 +143,10 @@
 
 
 def early_kernel(
-    tables, table_ref, place_ref, own_hbm, own_swap, r1, r2, t1, t2, r3,
+    tables, table_ref, own_hbm, own_swap, r1, r2, t1, t2, r3,
     high, low, left, part_ref, own_ref, own_sem,
 ):
-    place, lane = place_ref[0], place_ref[1]
+    place, lane = lax.axis_index("blk"), lax.axis_index("depth")
     near, far = tables
     own_copy = pltpu.make_async_copy(own_hbm, own_ref, own_sem)
     own_copy.start()
@@ -165,9 +165,9 @@
 
 
 def middle_kernel(
-    tables, table_ref, place_ref, r4, t3, high_in, low_in, left, part_in, high, low, part_ref
+    tables, table_ref, r4, t3, high_in, low_in, left, part_in, high, low, part_ref
 ):
-    place, lane = place_ref[0], place_ref[1]
+    place, lane = lax.axis_index("blk"), lax.axis_index("depth")
     far = tables[1]
     here, there = lookup(far, place, lane), lookup(far, place, 1 - lane)
     store_piece(t3, there, 1 - lane, table_ref, high, low)
@@ -176,10 +176,11 @@
 
 
 def late_kernel(
-    tables, table_ref, place_ref, t4, high_in, low_in, left, part_in,
+    tables, table_ref, t4, high_in, low_in, left, part_in,
     out_hbm, high, low, square, square_parts, out_ref, out_sem,
 ):
-    place, lane, group = place_ref[0], place_ref[1], place_ref[2]
+    place, lane = lax.axis_index("blk"), lax.axis_index("depth")
+    group = lax.axis_index("panel") * 2 + lane
     there = lookup(tables[1], place, 1 - lane)
     store_piece(t4, there, lane, table_ref, high, low)
     add_plane(there, left, high, low, square)
@@ -291,17 +292,14 @@
     r4 = move(r2, second)
     t2 = swap(r2)
 
-    place = jnp.stack(
-        [
-            lax.axis_index("blk"),
-            lax.axis_index("depth"),
-            lax.axis_index("panel") * lanes + lax.axis_index("depth"),
-        ]
-    ).astype(jnp.int32)
     order, own = rows * edge, slab * edge
+    table = pltpu.with_memory_space_constraint(table, pltpu.SMEM)
     smem = pl.BlockSpec(memory_space=pltpu.SMEM)
     vmem = pl.BlockSpec(memory_space=pltpu.VMEM)
     params = pltpu.CompilerParams(vmem_limit_bytes=24 * 2**20)
+    def held(*arrays):
+        return [pltpu.with_memory_space_constraint(a, pltpu.VMEM) for a in arrays]
+
     high, low, left, part = pl.pallas_call(
         functools.partial(early_kernel, tables),
         out_shape=[
@@ -310,12 +308,12 @@
             jax.ShapeDtypeStruct((2 * own, order), jnp.bfloat16),
             jax.ShapeDtypeStruct((own, order), jnp.float32),
         ],
-        in_specs=[smem] * 2 + [pl.BlockSpec(memory_space=pltpu.HBM)] + [vmem] * 6,
+        in_specs=[smem] + [pl.BlockSpec(memory_space=pltpu.HBM)] + [vmem] * 6,
         out_specs=[vmem] * 4,
         scratch_shapes=[pltpu.VMEM(x_blocks.shape, jnp.float32), pltpu.SemaphoreType.DMA],
         compiler_params=params,
         name="early",
-    )(table, place, x_blocks, own_swap, r1, r2, t1, t2, r3)
+    )(table, pltpu.with_memory_space_constraint(x_blocks, pltpu.HBM), own_swap, r1, r2, t1, t2, r3)
     t3 = swap(r3)
     r4, part = lax.optimization_barrier((r4, part))
     t4 = swap(r4)
@@ -323,18 +321,18 @@
     high, low, part = pl.pallas_call(
         functools.partial(middle_kernel, tables),
         out_shape=dense,
-        in_specs=[smem] * 2 + [vmem] * 6,
+        in_specs=[smem] + [vmem] * 6,
         out_specs=[vmem] * 3,
-        input_output_aliases={4: 0, 5: 1, 7: 2},
+        input_output_aliases={3: 0, 4: 1, 6: 2},
         compiler_params=params,
         name="middle",
-    )(table, place, r4, t3, high, low, left, part)
+    )(table, r4, t3, *held(high, low, left, part))
     out, _, _, _ = pl.pallas_call(
         functools.partial(late_kernel, tables),
         out_shape=[jax.ShapeDtypeStruct(x_blocks.shape, jnp.float32)] + dense,
-        in_specs=[smem] * 2 + [vmem] * 5,
+        in_specs=[smem] + [vmem] * 5,
         out_specs=[pl.BlockSpec(memory_space=pltpu.HBM)] + [vmem] * 3,
-        input_output_aliases={3: 1, 4: 2, 6: 3},
+        input_output_aliases={2: 1, 3: 2, 5: 3},
         scratch_shapes=[
             pltpu.VMEM((2 * own, order), jnp.bfloat16),
             pltpu.VMEM(x_blocks.shape, jnp.float32),
@@ -342,7 +340,7 @@
         ],
         compiler_params=params,
         name="late",
-    )(table, place, t4, high, low, left, part)
+    )(table, t4, *held(high, low, left, part))
     return out
 
 

time: 34 us -> 34 us (level)
  waiting for transfers between devices: 9.82 us -> 11.4 us
  local copies, waits for them, and re-layouts: 1.04 us -> 0 us
  Pallas kernels: 8.73 us -> 8.34 us
    ppermute x8, waiting for transfers between devices: 6.69 us -> 8.22 us  [move(): return lax.ppermute(block, AXES, route)]
    unnamed x2 -> x0, local copies, waits for them, and re-layouts: 1.04 us -> none
    pallas_call x1, Pallas kernels: 3.54 us -> 3.12 us  [gather_local(): pl.pallas_call(functools.partial(early_kernel, tables), out_shape=[jax.Sh...]
  transfers between devices with their start and end apart: 9 -> 9, of which waited for: 6 -> 6; matrix products, arithmetic and copies ran while one was open for 9% -> 8% of each run, Pallas kernels for 15% -> 14%
where the time goes in v6:
time: 34 us; the launch traced here: 33.7 us
  waiting for transfers between devices  11.4 us (34%)
  starting transfers between devices  11.1 us (33%)
  Pallas kernels  8.34 us (25%)
  other arithmetic  2.86 us (8%)
    ppermute x8, waiting for transfers between devices, move(): return lax.ppermute(block, AXES, route)  8.22 us
    ppermute x8, starting transfers between devices, move(): return lax.ppermute(block, AXES, route)  7.63 us
    pallas_call x1, Pallas kernels, gather_local(): pl.pallas_call(functools.partial(late_kernel, tables), out_shape=[jax.Sha...  3.68 us
    ppermute x1, starting transfers between devices, move_only(): return lax.ppermute(block, AXES, route)  3.5 us
    ppermute x1, waiting for transfers between devices, move_only(): return lax.ppermute(block, AXES, route)  3.13 us
    pallas_call x1, Pallas kernels, gather_local(): pl.pallas_call(functools.partial(early_kernel, tables), out_shape=[jax.Sh...  3.12 us
    pallas_call x1, Pallas kernels, gather_local(): pl.pallas_call(functools.partial(middle_kernel, tables), out_shape=dense,...  1.54 us
    reduce_sum x1, other arithmetic, slot_table(): count = jnp.sum(here.astype(jnp.int32), axis=1, keepdims=True)  0.8 us
  transfers between devices with their start and end apart: 9, of which 6 were waited for; matrix products, arithmetic and copies ran while one was open for 8% of the time, Pallas kernels for 14%

profile of v6, /device:TPU:0, one launch (start us, length us, event | category | flops | bytes accessed | tf_op | source)
XLA Modules:
  0.0 33.7 jit_solution(6784266680456367218)
XLA Ops:
  0.0 3.0 %collective-permute-start = (f32[2,4,128,128]{3,2,1,0:T(8,128)}, f32[2,4,128,128]{3,2,1,0:T(8,128)S(1)}, u32[]{:S(2)}, u32[]{:S(2)}) collective-permute-start(f32[2,4,128,128]{3,2,1,0:T(8,128)} %own_hbm.1), channel_id=1, source_target_pairs={{2,0},{0,4},{4,8},{8,12},{12,14},{14,15},{15,13},{13,9},{9,5},{5,1... | collective-permute-start | bytes 1572872 | tf_op jit(solution)/shard_map/ppermute | solution.py:265
  3.0 0.0 collective-permute-start.1
  3.0 0.8 %fusion.1 = (s32[8]{0:T(128)S(1)}, s32[8,8]{1,0:T(8,128)S(1)}) fusion(s32[8,16]{1,0:T(8,128)} %param.3), kind=kLoop, calls=%fused_computation.10 | loop fusion | flops 184 | bytes 544 | tf_op jit(solution)/shard_map/reduce_sum | solution.py:231
  3.8 0.1 fusion
  3.9 0.2 convert_reduce_fusion
  4.2 0.1 add_select_fusion
  4.2 0.2 select_reduce_fusion
  4.4 0.7 %collective-permute-done.1.own_swap = f32[2,4,128,128]{3,2,1,0:T(8,128)S(1)} collective-permute-done((f32[2,4,128,128]{3,2,1,0:T(8,128)}, f32[2,4,128,128]{3,2,1,0:T(8,128)S(1)}, u32[]{:S(2)}, u32[]{:S(2)}) %collective-permute-start.1) | collective-permute-done | bytes 524320 | tf_op jit(solution)/shard_map/ppermute | solution.py:265
  5.1 3.5 %collective-permute-start.2 = (f32[2,4,128,128]{3,2,1,0:T(8,128)S(1)}, f32[2,4,128,128]{3,2,1,0:T(8,128)S(1)}, u32[]{:S(2)}, u32[]{:S(2)}) collective-permute-start(f32[2,4,128,128]{3,2,1,0:T(8,128)S(1)} %collective-permute-done.1.own_swap), channel_id=1, source_target_pairs={{0,4},{4,8},{8,12},{12,14},{13,9},{9,5},{5,1},{1,3},{16,20},{20,24... | collective-permute-start | bytes 1572872 | tf_op jit(solution)/shard_map/ppermute | solution.py:273
  8.7 0.7 %compare_convert_fusion = s32[8,8]{1,0:T(8,128)S(1)} fusion(s32[8,16]{1,0:T(8,128)} %param.3), kind=kLoop, calls=%fused_computation.6 | loop fusion | flops 128 | bytes 512 | tf_op jit(solution)/shard_map/convert_element_type | solution.py:231
  9.3 0.7 %compare_select_fusion = s32[8,8]{1,0:T(8,128)S(1)} fusion(s32[8,8]{1,0:T(8,128)S(1)} %select_reduce_fusion, s32[8,16]{1,0:T(8,128)} %param.3), kind=kLoop, calls=%fused_computation.5 | loop fusion | flops 128 | bytes 768 | tf_op jit(solution)/shard_map/jit(_where)/select_n | solution.py:239
  10.0 0.1 pad_add_fusion.table_ref
  10.1 0.2 collective-permute-done.r1
  10.3 2.1 %collective-permute-start.6 = (f32[2,4,128,128]{3,2,1,0:T(8,128)S(1)}, f32[2,4,128,128]{3,2,1,0:T(8,128)S(1)}, u32[]{:S(2)}, u32[]{:S(2)}) collective-permute-start(f32[2,4,128,128]{3,2,1,0:T(8,128)S(1)} %collective-permute-done.r1), channel_id=1, source_target_pairs={{14,0},{0,4},{4,8},{8,12},{12,14},{3,13},{13,9},{9,5},{5,1},{1,3},... | collective-permute-start | bytes 1572872 | tf_op jit(solution)/shard_map/ppermute | solution.py:265
  12.4 0.0 collective-permute-start.4
  12.4 3.1 %collective-permute-done.2.r2 = f32[2,4,128,128]{3,2,1,0:T(8,128)S(1)} collective-permute-done((f32[2,4,128,128]{3,2,1,0:T(8,128)S(1)}, f32[2,4,128,128]{3,2,1,0:T(8,128)S(1)}, u32[]{:S(2)}, u32[]{:S(2)}) %collective-permute-start.2) | collective-permute-done | bytes 524320 | tf_op jit(solution)/shard_map/ppermute | solution.py:273
  15.6 0.0 collective-permute-start.5
  15.6 2.5 %collective-permute-start.3 = (f32[2,4,128,128]{3,2,1,0:T(8,128)S(1)}, f32[2,4,128,128]{3,2,1,0:T(8,128)S(1)}, u32[]{:S(2)}, u32[]{:S(2)}) collective-permute-start(f32[2,4,128,128]{3,2,1,0:T(8,128)S(1)} %collective-permute-done.2.r2), channel_id=1, source_target_pairs={{14,0},{0,4},{4,8},{8,12},{12,14},{3,13},{13,9},{9,5},{5,1},{1,3},... | collective-permute-start | bytes 1572872 | tf_op jit(solution)/shard_map/ppermute | solution.py:265
  18.0 4.5 %collective-permute-done.6.r3 = f32[2,4,128,128]{3,2,1,0:T(8,128)S(1)} collective-permute-done((f32[2,4,128,128]{3,2,1,0:T(8,128)S(1)}, f32[2,4,128,128]{3,2,1,0:T(8,128)S(1)}, u32[]{:S(2)}, u32[]{:S(2)}) %collective-permute-start.6) | collective-permute-done | bytes 524320 | tf_op jit(solution)/shard_map/ppermute | solution.py:265
  22.5 0.0 collective-permute-start.8
  22.5 0.0 collective-permute-done.4.t1
  22.5 0.0 collective-permute-done.5.t2
  22.5 3.1 %early.1 = (bf16[1024,1024]{1,0:T(8,128)(2,1)S(1)}, bf16[1024,1024]{1,0:T(8,128)(2,1)S(1)}, bf16[512,1024]{1,0:T(8,128)(2,1)S(1)}, f32[256,1024]{1,0:T(8,128)S(1)}) custom-call(s32[8,24]{1,0:T(8,128)S(1)} %pad_add_fusion.table_ref, f32[2,4,128,128]{3,2,1,0:T(8,128)} %own_hbm.1, f32[2,4,128,128]{3,2,1,0:T(8,128)S(1)} %collective-permute-done.1.own_swap, ...), custom_call_target="tpu_custom_call" | custom-call | tf_op jit(solution)/shard_map/early/pallas_call | solution.py:303
  25.7 2.5 %collective-permute-done.3.r4 = f32[2,4,128,128]{3,2,1,0:T(8,128)S(1)} collective-permute-done((f32[2,4,128,128]{3,2,1,0:T(8,128)S(1)}, f32[2,4,128,128]{3,2,1,0:T(8,128)S(1)}, u32[]{:S(2)}, u32[]{:S(2)}) %collective-permute-start.3) | collective-permute-done | bytes 524320 | tf_op jit(solution)/shard_map/ppermute | solution.py:265
  28.1 0.0 collective-permute-start.7
  28.2 0.0 collective-permute-done.8.t3
  28.2 1.5 %middle.1 = (bf16[1024,1024]{1,0:T(8,128)(2,1)S(1)}, bf16[1024,1024]{1,0:T(8,128)(2,1)S(1)}, f32[256,1024]{1,0:T(8,128)S(1)}) custom-call(s32[8,24]{1,0:T(8,128)S(1)} %pad_add_fusion.table_ref, f32[2,4,128,128]{3,2,1,0:T(8,128)S(1)} %collective-permute-done.3.r4, ...), custom_call_target="tpu_custom_call", output_to_operand_aliasing={{0}: (3, {}), {1}: (4, {}), {2}: (6, {})} | custom-call | tf_op jit(solution)/shard_map/middle/pallas_call | solution.py:321
  29.7 0.4 %collective-permute-done.7.t4 = f32[2,4,128,128]{3,2,1,0:T(8,128)S(1)} collective-permute-done((f32[2,4,128,128]{3,2,1,0:T(8,128)S(1)}, f32[2,4,128,128]{3,2,1,0:T(8,128)S(1)}, u32[]{:S(2)}, u32[]{:S(2)}) %collective-permute-start.7) | collective-permute-done | bytes 524320 | tf_op jit(solution)/shard_map/ppermute | solution.py:265
  30.1 3.7 %late.1 = (f32[2,4,128,128]{3,2,1,0:T(8,128)}, bf16[1024,1024]{1,0:T(8,128)(2,1)S(1)}, bf16[1024,1024]{1,0:T(8,128)(2,1)S(1)}, f32[256,1024]{1,0:T(8,128)S(1)}) custom-call(s32[8,24]{1,0:T(8,128)S(1)} %pad_add_fusion.table_ref, f32[2,4,128,128]{3,2,1,0:T(8,128)S(1)} %collective-permute-done.7.t4, ...), custom_call_target="tpu_custom_call", output_to_operand_aliasing={{1}: (2, {}), {2}: (3, {}), {3}: (5, {})} | custom-call | tf_op jit(solution)/shard_map/late/pallas_call | solution.py:330
  (1 shorter events, 0.0 us)
Async XLA Ops:
  0.0 10.3 %collective-permute-start = (f32[2,4,128,128]{3,2,1,0:T(8,128)}, f32[2,4,128,128]{3,2,1,0:T(8,128)S(1)}, u32[]{:S(2)}, u32[]{:S(2)}) collective-permute-start(f32[2,4,128,128]{3,2,1,0:T(8,128)} %own_hbm.1), channel_id=1, source_target_pairs={{2,0},{0,4},{4,8},{8,12},{12,14},{14,15},{15,13},{13,9},{9,5},{5,1... | collective-permute-start | bytes 1572872 | tf_op jit(solution)/shard_map/ppermute | solution.py:265
  3.0 2.1 %collective-permute-start.1 = (f32[2,4,128,128]{3,2,1,0:T(8,128)}, f32[2,4,128,128]{3,2,1,0:T(8,128)S(1)}, u32[]{:S(2)}, u32[]{:S(2)}) collective-permute-start(f32[2,4,128,128]{3,2,1,0:T(8,128)} %own_hbm.1), channel_id=1, source_target_pairs={{1,0},{0,1},{17,16},{16,17},{3,2},{2,3},{19,18},{18,19},{5,4},{4,5... | collective-permute-start | bytes 1572872 | tf_op jit(solution)/shard_map/ppermute | solution.py:265
  5.1 10.4 %collective-permute-start.2 = (f32[2,4,128,128]{3,2,1,0:T(8,128)S(1)}, f32[2,4,128,128]{3,2,1,0:T(8,128)S(1)}, u32[]{:S(2)}, u32[]{:S(2)}) collective-permute-start(f32[2,4,128,128]{3,2,1,0:T(8,128)S(1)} %collective-permute-done.1.own_swap), channel_id=1, source_target_pairs={{0,4},{4,8},{8,12},{12,14},{13,9},{9,5},{5,1},{1,3},{16,20},{20,24... | collective-permute-start | bytes 1572872 | tf_op jit(solution)/shard_map/ppermute | solution.py:273
  10.3 12.2 %collective-permute-start.6 = (f32[2,4,128,128]{3,2,1,0:T(8,128)S(1)}, f32[2,4,128,128]{3,2,1,0:T(8,128)S(1)}, u32[]{:S(2)}, u32[]{:S(2)}) collective-permute-start(f32[2,4,128,128]{3,2,1,0:T(8,128)S(1)} %collective-permute-done.r1), channel_id=1, source_target_pairs={{14,0},{0,4},{4,8},{8,12},{12,14},{3,13},{13,9},{9,5},{5,1},{1,3},... | collective-permute-start | bytes 1572872 | tf_op jit(solution)/shard_map/ppermute | solution.py:265
  12.4 10.1 %collective-permute-start.4 = (f32[2,4,128,128]{3,2,1,0:T(8,128)S(1)}, f32[2,4,128,128]{3,2,1,0:T(8,128)S(1)}, u32[]{:S(2)}, u32[]{:S(2)}) collective-permute-start(f32[2,4,128,128]{3,2,1,0:T(8,128)S(1)} %collective-permute-done.r1), channel_id=1, source_target_pairs={{1,0},{0,1},{17,16},{16,17},{3,2},{2,3},{19,18},{18,19},{5,4},{4,5... | collective-permute-start | bytes 1572872 | tf_op jit(solution)/shard_map/ppermute | solution.py:265
  15.6 7.0 %collective-permute-start.5 = (f32[2,4,128,128]{3,2,1,0:T(8,128)S(1)}, f32[2,4,128,128]{3,2,1,0:T(8,128)S(1)}, u32[]{:S(2)}, u32[]{:S(2)}) collective-permute-start(f32[2,4,128,128]{3,2,1,0:T(8,128)S(1)} %collective-permute-done.2.r2), channel_id=1, source_target_pairs={{1,0},{0,1},{17,16},{16,17},{3,2},{2,3},{19,18},{18,19},{5,4},{4,5... | collective-permute-start | bytes 1572872 | tf_op jit(solution)/shard_map/ppermute | solution.py:265
  15.6 12.6 %collective-permute-start.3 = (f32[2,4,128,128]{3,2,1,0:T(8,128)S(1)}, f32[2,4,128,128]{3,2,1,0:T(8,128)S(1)}, u32[]{:S(2)}, u32[]{:S(2)}) collective-permute-start(f32[2,4,128,128]{3,2,1,0:T(8,128)S(1)} %collective-permute-done.2.r2), channel_id=1, source_target_pairs={{14,0},{0,4},{4,8},{8,12},{12,14},{3,13},{13,9},{9,5},{5,1},{1,3},... | collective-permute-start | bytes 1572872 | tf_op jit(solution)/shard_map/ppermute | solution.py:265
  22.5 5.6 %collective-permute-start.8 = (f32[2,4,128,128]{3,2,1,0:T(8,128)S(1)}, f32[2,4,128,128]{3,2,1,0:T(8,128)S(1)}, u32[]{:S(2)}, u32[]{:S(2)}) collective-permute-start(f32[2,4,128,128]{3,2,1,0:T(8,128)S(1)} %collective-permute-done.6.r3), channel_id=1, source_target_pairs={{1,0},{0,1},{17,16},{16,17},{3,2},{2,3},{19,18},{18,19},{5,4},{4,5... | collective-permute-start | bytes 1572872 | tf_op jit(solution)/shard_map/ppermute | solution.py:265
  28.1 1.9 %collective-permute-start.7 = (f32[2,4,128,128]{3,2,1,0:T(8,128)S(1)}, f32[2,4,128,128]{3,2,1,0:T(8,128)S(1)}, u32[]{:S(2)}, u32[]{:S(2)}) collective-permute-start(f32[2,4,128,128]{3,2,1,0:T(8,128)S(1)} %collective-permute-done.3.r4), channel_id=1, source_target_pairs={{1,0},{0,1},{17,16},{16,17},{3,2},{2,3},{19,18},{18,19},{5,4},{4,5... | collective-permute-start | bytes 1572872 | tf_op jit(solution)/shard_map/ppermute | solution.py:265

commit v7 on v6

--- a/solution.py
+++ b/solution.py
@@ -137,8 +137,10 @@
     @pl.when(plane >= 0)
     def _():
         rows = pl.ds(pl.multiple_of(plane * depth, depth), depth)
-        for n in range(part_ref.shape[1] // tile):
-            cols = pl.ds(n * tile, tile)
+
+        @pl.loop(0, part_ref.shape[1] // tile)
+        def _(n):
+            cols = pl.ds(pl.multiple_of(n * tile, tile), tile)
             part_ref[:, cols] += stacked_dot(left[:, rows], high[rows, cols], low[rows, cols])
 
 
@@ -186,40 +188,40 @@
     add_plane(there, left, high, low, square)
     slab, width, edge, _ = out_ref.shape
     act = 2 * width
-    for r in range(slab):
-        for c in range(square.shape[1] // edge):
+    @pl.loop(0, square.shape[1] // edge)
+    def _(c):
+        col = pl.ds(pl.multiple_of(c * edge, edge), edge)
+        for r in range(slab):
             kept = table_ref[place * slab + r, 2 * act + c] > 0
-            col = pl.ds(c * edge, edge)
             block = jnp.where(kept, square[pl.ds(r * edge, edge), col], 0.0)
             block_high, block_low = split(block)
             square_parts[pl.ds(2 * r * edge, edge), col] = block_high
             square_parts[pl.ds((2 * r + 1) * edge, edge), col] = block_low
-    copies = []
-    for r in range(slab):
+
+    def leave(r, w, number):
+        ready = (r, pl.ds(w, 2))
+        return pltpu.make_async_copy(out_ref.at[ready], out_hbm.at[ready], out_sem.at[number])
+
+    @pl.loop(0, slab * width // 2)
+    def _(number):
+        r, w = number // (width // 2), number % (width // 2) * 2
         row = place * slab + r
-        left_parts = square_parts[pl.ds(2 * r * edge, 2 * edge), :]
-        for w in range(0, width, 2):
-            slots = [jnp.minimum(group * width + w + k, act - 1) for k in range(2)]
-            cols = [
-                pl.ds(pl.multiple_of(table_ref[row, slot] * edge, edge), edge) for slot in slots
-            ]
-            cube = stacked_dot(
-                left_parts,
-                jnp.concatenate([high[:, col] for col in cols], axis=1),
-                jnp.concatenate([low[:, col] for col in cols], axis=1),
-            )
-            for k in range(2):
-                there = (group * width + w + k < act) & (table_ref[row, act + slots[k]] > 0)
-                value = 3.0 * square[pl.ds(r * edge, edge), cols[k]]
-                value = value - 2.0 * cube[:, k * edge : (k + 1) * edge]
-                out_ref[r, w + k] = jnp.where(there, value, 0.0)
-            ready = (r, pl.ds(w, 2))
-            copies.append(
-                pltpu.make_async_copy(out_ref.at[ready], out_hbm.at[ready], out_sem.at[len(copies)])
-            )
-            copies[-1].start()
-    for copy in copies:
-        copy.wait()
+        slots = [jnp.minimum(group * width + w + k, act - 1) for k in range(2)]
+        cols = [pl.ds(pl.multiple_of(table_ref[row, slot] * edge, edge), edge) for slot in slots]
+        cube = stacked_dot(
+            square_parts[pl.ds(pl.multiple_of(2 * r * edge, edge), 2 * edge), :],
+            jnp.concatenate([high[:, col] for col in cols], axis=1),
+            jnp.concatenate([low[:, col] for col in cols], axis=1),
+        )
+        for k in range(2):
+            there = (group * width + w + k < act) & (table_ref[row, act + slots[k]] > 0)
+            value = 3.0 * square[pl.ds(pl.multiple_of(r * edge, edge), edge), cols[k]]
+            value = value - 2.0 * cube[:, k * edge : (k + 1) * edge]
+            out_ref[r, w + k] = jnp.where(there, value, 0.0)
+        leave(r, w, number).start()
+
+    for number in range(slab * width // 2):
+        leave(number // (width // 2), number % (width // 2) * 2, number).wait()
 
 
 def slot_table(columns, act):

time: 34 us -> 35.4 us (1.041)
  Pallas kernels: 8.34 us -> 11.1 us
  waiting for transfers between devices: 11.4 us -> 9.96 us
    ppermute x8, waiting for transfers between devices: 8.22 us -> 6.82 us  [move(): return lax.ppermute(block, AXES, route)]
    pallas_call x1, Pallas kernels: 3.68 us -> 4.84 us  [gather_local(): pl.pallas_call(functools.partial(late_kernel, tables), out_shape=[jax.Sha...]
    pallas_call x1, Pallas kernels: 3.12 us -> 4.17 us  [gather_local(): pl.pallas_call(functools.partial(early_kernel, tables), out_shape=[jax.Sh...]
    pallas_call x1, Pallas kernels: 1.54 us -> 2.07 us  [gather_local(): pl.pallas_call(functools.partial(middle_kernel, tables), out_shape=dense,...]
  transfers between devices with their start and end apart: 9 -> 9, of which waited for: 6 -> 5; matrix products, arithmetic and copies ran while one was open for 8% -> 8% of each run, Pallas kernels for 14% -> 18%
where the time goes in v7:
time: 35.4 us; the launch traced here: 35.1 us
  starting transfers between devices  11.1 us (31%)
  Pallas kernels  11.1 us (31%)
  waiting for transfers between devices  9.96 us (28%)
  other arithmetic  2.86 us (8%)
    ppermute x8, starting transfers between devices, move(): return lax.ppermute(block, AXES, route)  7.63 us
    ppermute x8, waiting for transfers between devices, move(): return lax.ppermute(block, AXES, route)  6.82 us
    pallas_call x1, Pallas kernels, gather_local(): pl.pallas_call(functools.partial(late_kernel, tables), out_shape=[jax.Sha...  4.84 us
    pallas_call x1, Pallas kernels, gather_local(): pl.pallas_call(functools.partial(early_kernel, tables), out_shape=[jax.Sh...  4.17 us
    ppermute x1, starting transfers between devices, move_only(): return lax.ppermute(block, AXES, route)  3.5 us
    ppermute x1, waiting for transfers between devices, move_only(): return lax.ppermute(block, AXES, route)  3.13 us
    pallas_call x1, Pallas kernels, gather_local(): pl.pallas_call(functools.partial(middle_kernel, tables), out_shape=dense,...  2.07 us
    reduce_sum x1, other arithmetic, slot_table(): count = jnp.sum(here.astype(jnp.int32), axis=1, keepdims=True)  0.8 us
  transfers between devices with their start and end apart: 9, of which 5 were waited for; matrix products, arithmetic and copies ran while one was open for 8% of the time, Pallas kernels for 18%

profile of v7, /device:TPU:0, one launch (start us, length us, event | category | flops | bytes accessed | tf_op | source)
XLA Modules:
  0.0 35.1 jit_solution(2579228232574957101)
XLA Ops:
  0.0 3.0 %collective-permute-start = (f32[2,4,128,128]{3,2,1,0:T(8,128)}, f32[2,4,128,128]{3,2,1,0:T(8,128)S(1)}, u32[]{:S(2)}, u32[]{:S(2)}) collective-permute-start(f32[2,4,128,128]{3,2,1,0:T(8,128)} %own_hbm.1), channel_id=1, source_target_pairs={{2,0},{0,4},{4,8},{8,12},{12,14},{14,15},{15,13},{13,9},{9,5},{5,1... | collective-permute-start | bytes 1572872 | tf_op jit(solution)/shard_map/ppermute | solution.py:267
  3.0 0.0 collective-permute-start.1
  3.0 0.8 %fusion.1 = (s32[8]{0:T(128)S(1)}, s32[8,8]{1,0:T(8,128)S(1)}) fusion(s32[8,16]{1,0:T(8,128)} %param.3), kind=kLoop, calls=%fused_computation.10 | loop fusion | flops 184 | bytes 544 | tf_op jit(solution)/shard_map/reduce_sum | solution.py:233
  3.8 0.1 fusion
  3.9 0.2 convert_reduce_fusion
  4.2 0.1 add_select_fusion
  4.2 0.2 select_reduce_fusion
  4.4 0.7 %collective-permute-done.1.own_swap = f32[2,4,128,128]{3,2,1,0:T(8,128)S(1)} collective-permute-done((f32[2,4,128,128]{3,2,1,0:T(8,128)}, f32[2,4,128,128]{3,2,1,0:T(8,128)S(1)}, u32[]{:S(2)}, u32[]{:S(2)}) %collective-permute-start.1) | collective-permute-done | bytes 524320 | tf_op jit(solution)/shard_map/ppermute | solution.py:267
  5.1 3.5 %collective-permute-start.2 = (f32[2,4,128,128]{3,2,1,0:T(8,128)S(1)}, f32[2,4,128,128]{3,2,1,0:T(8,128)S(1)}, u32[]{:S(2)}, u32[]{:S(2)}) collective-permute-start(f32[2,4,128,128]{3,2,1,0:T(8,128)S(1)} %collective-permute-done.1.own_swap), channel_id=1, source_target_pairs={{0,4},{4,8},{8,12},{12,14},{13,9},{9,5},{5,1},{1,3},{16,20},{20,24... | collective-permute-start | bytes 1572872 | tf_op jit(solution)/shard_map/ppermute | solution.py:275
  8.7 0.7 %compare_convert_fusion = s32[8,8]{1,0:T(8,128)S(1)} fusion(s32[8,16]{1,0:T(8,128)} %param.3), kind=kLoop, calls=%fused_computation.6 | loop fusion | flops 128 | bytes 512 | tf_op jit(solution)/shard_map/convert_element_type | solution.py:233
  9.3 0.7 %compare_select_fusion = s32[8,8]{1,0:T(8,128)S(1)} fusion(s32[8,8]{1,0:T(8,128)S(1)} %select_reduce_fusion, s32[8,16]{1,0:T(8,128)} %param.3), kind=kLoop, calls=%fused_computation.5 | loop fusion | flops 128 | bytes 768 | tf_op jit(solution)/shard_map/jit(_where)/select_n | solution.py:241
  10.0 0.1 pad_add_fusion.table_ref
  10.1 0.2 collective-permute-done.r1
  10.3 2.1 %collective-permute-start.6 = (f32[2,4,128,128]{3,2,1,0:T(8,128)S(1)}, f32[2,4,128,128]{3,2,1,0:T(8,128)S(1)}, u32[]{:S(2)}, u32[]{:S(2)}) collective-permute-start(f32[2,4,128,128]{3,2,1,0:T(8,128)S(1)} %collective-permute-done.r1), channel_id=1, source_target_pairs={{14,0},{0,4},{4,8},{8,12},{12,14},{3,13},{13,9},{9,5},{5,1},{1,3},... | collective-permute-start | bytes 1572872 | tf_op jit(solution)/shard_map/ppermute | solution.py:267
  12.4 0.0 collective-permute-start.4
  12.4 3.1 %collective-permute-done.2.r2 = f32[2,4,128,128]{3,2,1,0:T(8,128)S(1)} collective-permute-done((f32[2,4,128,128]{3,2,1,0:T(8,128)S(1)}, f32[2,4,128,128]{3,2,1,0:T(8,128)S(1)}, u32[]{:S(2)}, u32[]{:S(2)}) %collective-permute-start.2) | collective-permute-done | bytes 524320 | tf_op jit(solution)/shard_map/ppermute | solution.py:275
  15.6 0.0 collective-permute-start.5
  15.6 2.5 %collective-permute-start.3 = (f32[2,4,128,128]{3,2,1,0:T(8,128)S(1)}, f32[2,4,128,128]{3,2,1,0:T(8,128)S(1)}, u32[]{:S(2)}, u32[]{:S(2)}) collective-permute-start(f32[2,4,128,128]{3,2,1,0:T(8,128)S(1)} %collective-permute-done.2.r2), channel_id=1, source_target_pairs={{14,0},{0,4},{4,8},{8,12},{12,14},{3,13},{13,9},{9,5},{5,1},{1,3},... | collective-permute-start | bytes 1572872 | tf_op jit(solution)/shard_map/ppermute | solution.py:267
  18.0 4.5 %collective-permute-done.6.r3 = f32[2,4,128,128]{3,2,1,0:T(8,128)S(1)} collective-permute-done((f32[2,4,128,128]{3,2,1,0:T(8,128)S(1)}, f32[2,4,128,128]{3,2,1,0:T(8,128)S(1)}, u32[]{:S(2)}, u32[]{:S(2)}) %collective-permute-start.6) | collective-permute-done | bytes 524320 | tf_op jit(solution)/shard_map/ppermute | solution.py:267
  22.5 0.0 collective-permute-start.8
  22.5 0.0 collective-permute-done.4.t1
  22.5 0.0 collective-permute-done.5.t2
  22.5 4.2 %early.1 = (bf16[1024,1024]{1,0:T(8,128)(2,1)S(1)}, bf16[1024,1024]{1,0:T(8,128)(2,1)S(1)}, bf16[512,1024]{1,0:T(8,128)(2,1)S(1)}, f32[256,1024]{1,0:T(8,128)S(1)}) custom-call(s32[8,24]{1,0:T(8,128)S(1)} %pad_add_fusion.table_ref, f32[2,4,128,128]{3,2,1,0:T(8,128)} %own_hbm.1, f32[2,4,128,128]{3,2,1,0:T(8,128)S(1)} %collective-permute-done.1.own_swap, ...), custom_call_target="tpu_custom_call" | custom-call | tf_op jit(solution)/shard_map/early/pallas_call | solution.py:305
  26.7 1.4 %collective-permute-done.3.r4 = f32[2,4,128,128]{3,2,1,0:T(8,128)S(1)} collective-permute-done((f32[2,4,128,128]{3,2,1,0:T(8,128)S(1)}, f32[2,4,128,128]{3,2,1,0:T(8,128)S(1)}, u32[]{:S(2)}, u32[]{:S(2)}) %collective-permute-start.3) | collective-permute-done | bytes 524320 | tf_op jit(solution)/shard_map/ppermute | solution.py:267
  28.1 0.0 collective-permute-start.7
  28.2 0.0 collective-permute-done.8.t3
  28.2 2.1 %middle.1 = (bf16[1024,1024]{1,0:T(8,128)(2,1)S(1)}, bf16[1024,1024]{1,0:T(8,128)(2,1)S(1)}, f32[256,1024]{1,0:T(8,128)S(1)}) custom-call(s32[8,24]{1,0:T(8,128)S(1)} %pad_add_fusion.table_ref, f32[2,4,128,128]{3,2,1,0:T(8,128)S(1)} %collective-permute-done.3.r4, ...), custom_call_target="tpu_custom_call", output_to_operand_aliasing={{0}: (3, {}), {1}: (4, {}), {2}: (6, {})} | custom-call | tf_op jit(solution)/shard_map/middle/pallas_call | solution.py:323
  30.2 0.0 collective-permute-done.7.t4
  30.2 4.8 %late.1 = (f32[2,4,128,128]{3,2,1,0:T(8,128)}, bf16[1024,1024]{1,0:T(8,128)(2,1)S(1)}, bf16[1024,1024]{1,0:T(8,128)(2,1)S(1)}, f32[256,1024]{1,0:T(8,128)S(1)}) custom-call(s32[8,24]{1,0:T(8,128)S(1)} %pad_add_fusion.table_ref, f32[2,4,128,128]{3,2,1,0:T(8,128)S(1)} %collective-permute-done.7.t4, ...), custom_call_target="tpu_custom_call", output_to_operand_aliasing={{1}: (2, {}), {2}: (3, {}), {3}: (5, {})} | custom-call | tf_op jit(solution)/shard_map/late/pallas_call | solution.py:332
  (1 shorter events, 0.0 us)
Async XLA Ops:
  0.0 10.3 %collective-permute-start = (f32[2,4,128,128]{3,2,1,0:T(8,128)}, f32[2,4,128,128]{3,2,1,0:T(8,128)S(1)}, u32[]{:S(2)}, u32[]{:S(2)}) collective-permute-start(f32[2,4,128,128]{3,2,1,0:T(8,128)} %own_hbm.1), channel_id=1, source_target_pairs={{2,0},{0,4},{4,8},{8,12},{12,14},{14,15},{15,13},{13,9},{9,5},{5,1... | collective-permute-start | bytes 1572872 | tf_op jit(solution)/shard_map/ppermute | solution.py:267
  3.0 2.1 %collective-permute-start.1 = (f32[2,4,128,128]{3,2,1,0:T(8,128)}, f32[2,4,128,128]{3,2,1,0:T(8,128)S(1)}, u32[]{:S(2)}, u32[]{:S(2)}) collective-permute-start(f32[2,4,128,128]{3,2,1,0:T(8,128)} %own_hbm.1), channel_id=1, source_target_pairs={{1,0},{0,1},{17,16},{16,17},{3,2},{2,3},{19,18},{18,19},{5,4},{4,5... | collective-permute-start | bytes 1572872 | tf_op jit(solution)/shard_map/ppermute | solution.py:267
  5.1 10.4 %collective-permute-start.2 = (f32[2,4,128,128]{3,2,1,0:T(8,128)S(1)}, f32[2,4,128,128]{3,2,1,0:T(8,128)S(1)}, u32[]{:S(2)}, u32[]{:S(2)}) collective-permute-start(f32[2,4,128,128]{3,2,1,0:T(8,128)S(1)} %collective-permute-done.1.own_swap), channel_id=1, source_target_pairs={{0,4},{4,8},{8,12},{12,14},{13,9},{9,5},{5,1},{1,3},{16,20},{20,24... | collective-permute-start | bytes 1572872 | tf_op jit(solution)/shard_map/ppermute | solution.py:275
  10.3 12.2 %collective-permute-start.6 = (f32[2,4,128,128]{3,2,1,0:T(8,128)S(1)}, f32[2,4,128,128]{3,2,1,0:T(8,128)S(1)}, u32[]{:S(2)}, u32[]{:S(2)}) collective-permute-start(f32[2,4,128,128]{3,2,1,0:T(8,128)S(1)} %collective-permute-done.r1), channel_id=1, source_target_pairs={{14,0},{0,4},{4,8},{8,12},{12,14},{3,13},{13,9},{9,5},{5,1},{1,3},... | collective-permute-start | bytes 1572872 | tf_op jit(solution)/shard_map/ppermute | solution.py:267
  12.4 10.1 %collective-permute-start.4 = (f32[2,4,128,128]{3,2,1,0:T(8,128)S(1)}, f32[2,4,128,128]{3,2,1,0:T(8,128)S(1)}, u32[]{:S(2)}, u32[]{:S(2)}) collective-permute-start(f32[2,4,128,128]{3,2,1,0:T(8,128)S(1)} %collective-permute-done.r1), channel_id=1, source_target_pairs={{1,0},{0,1},{17,16},{16,17},{3,2},{2,3},{19,18},{18,19},{5,4},{4,5... | collective-permute-start | bytes 1572872 | tf_op jit(solution)/shard_map/ppermute | solution.py:267
  15.6 7.0 %collective-permute-start.5 = (f32[2,4,128,128]{3,2,1,0:T(8,128)S(1)}, f32[2,4,128,128]{3,2,1,0:T(8,128)S(1)}, u32[]{:S(2)}, u32[]{:S(2)}) collective-permute-start(f32[2,4,128,128]{3,2,1,0:T(8,128)S(1)} %collective-permute-done.2.r2), channel_id=1, source_target_pairs={{1,0},{0,1},{17,16},{16,17},{3,2},{2,3},{19,18},{18,19},{5,4},{4,5... | collective-permute-start | bytes 1572872 | tf_op jit(solution)/shard_map/ppermute | solution.py:267
  15.6 12.6 %collective-permute-start.3 = (f32[2,4,128,128]{3,2,1,0:T(8,128)S(1)}, f32[2,4,128,128]{3,2,1,0:T(8,128)S(1)}, u32[]{:S(2)}, u32[]{:S(2)}) collective-permute-start(f32[2,4,128,128]{3,2,1,0:T(8,128)S(1)} %collective-permute-done.2.r2), channel_id=1, source_target_pairs={{14,0},{0,4},{4,8},{8,12},{12,14},{3,13},{13,9},{9,5},{5,1},{1,3},... | collective-permute-start | bytes 1572872 | tf_op jit(solution)/shard_map/ppermute | solution.py:267
  22.5 5.6 %collective-permute-start.8 = (f32[2,4,128,128]{3,2,1,0:T(8,128)S(1)}, f32[2,4,128,128]{3,2,1,0:T(8,128)S(1)}, u32[]{:S(2)}, u32[]{:S(2)}) collective-permute-start(f32[2,4,128,128]{3,2,1,0:T(8,128)S(1)} %collective-permute-done.6.r3), channel_id=1, source_target_pairs={{1,0},{0,1},{17,16},{16,17},{3,2},{2,3},{19,18},{18,19},{5,4},{4,5... | collective-permute-start | bytes 1572872 | tf_op jit(solution)/shard_map/ppermute | solution.py:267
  28.1 2.1 %collective-permute-start.7 = (f32[2,4,128,128]{3,2,1,0:T(8,128)S(1)}, f32[2,4,128,128]{3,2,1,0:T(8,128)S(1)}, u32[]{:S(2)}, u32[]{:S(2)}) collective-permute-start(f32[2,4,128,128]{3,2,1,0:T(8,128)S(1)} %collective-permute-done.3.r4), channel_id=1, source_target_pairs={{1,0},{0,1},{17,16},{16,17},{3,2},{2,3},{19,18},{18,19},{5,4},{4,5... | collective-permute-start | bytes 1572872 | tf_op jit(solution)/shard_map/ppermute | solution.py:267

commit v8 on v6

--- a/solution.py
+++ b/solution.py
@@ -110,82 +110,102 @@
     return found
 
 
-def store_piece(piece, plane, group, table_ref, high, low, own=None):
-    slab, width, edge, _ = piece.shape
+def store_row(blocks, row, group, table_ref, high, low, own=None, own_row=0):
+    width, edge, _ = blocks.shape
     act = 2 * width
+    at = pl.ds(pl.multiple_of(row * edge, edge), edge)
+    for w in range(width):
+        slot = group * width + w
+        col = pl.ds(pl.multiple_of(table_ref[row, slot] * edge, edge), edge)
+        block = jnp.where(table_ref[row, act + slot] > 0, blocks[w], 0.0)
+        block_high, block_low = split(block)
+        high[at, col] = block_high
+        low[at, col] = block_low
+        if own is not None:
+            own[pl.ds(own_row * edge, edge), col] = block_high
+            own[pl.ds((own_row + 2) * edge, edge), col] = block_low
+
+
+def store_piece(piece, code, sender, table_ref, high, low):
+    @pl.when(code >= 0)
+    def _():
+        part = code % 4
+        row = code // 4 * 2 + part % 2
+        group = jnp.where(part < 2, sender, 1 - sender)
+        store_row(piece.at[0], row, group, table_ref, high, low)
+
+
+def add_rows(first, depth, left, high, low, part_ref):
+    rows = pl.ds(pl.multiple_of(first, depth), depth)
+    tile = 256
+    for n in range(part_ref.shape[1] // tile):
+        cols = pl.ds(n * tile, tile)
+        part_ref[:, cols] += stacked_dot(left[:, rows], high[rows, cols], low[rows, cols])
+
+
+def add_plane(plane, left, high, low, part_ref):
+    depth = part_ref.shape[0]
 
     @pl.when(plane >= 0)
     def _():
-        for r in range(slab):
-            row = plane * slab + r
-            for w in range(width):
-                slot = group * width + w
-                col = pl.ds(pl.multiple_of(table_ref[row, slot] * edge, edge), edge)
-                block = jnp.where(table_ref[row, act + slot] > 0, piece[r, w], 0.0)
-                block_high, block_low = split(block)
-                at = pl.ds(pl.multiple_of(row * edge, edge), edge)
-                high[at, col] = block_high
-                low[at, col] = block_low
-                if own is not None:
-                    own[pl.ds(r * edge, edge), col] = block_high
-                    own[pl.ds((slab + r) * edge, edge), col] = block_low
-
-
-def add_plane(plane, left, high, low, part_ref):
-    depth, tile = part_ref.shape[0], 256
-
-    @pl.when(plane >= 0)
-    def _():
-        rows = pl.ds(pl.multiple_of(plane * depth, depth), depth)
-        for n in range(part_ref.shape[1] // tile):
-            cols = pl.ds(n * tile, tile)
-            part_ref[:, cols] += stacked_dot(left[:, rows], high[rows, cols], low[rows, cols])
-
-
-def early_kernel(
-    tables, table_ref, own_hbm, own_swap, r1, r2, t1, t2, r3,
-    high, low, left, part_ref, own_ref, own_sem,
-):
+        add_rows(plane * depth, depth, left, high, low, part_ref)
+
+
+def store_pieces(pieces, codes, place, lane, table_ref, high, low):
+    for (received, swapped), table in zip(pieces, codes):
+        store_piece(received, lookup(table, place, lane), lane, table_ref, high, low)
+        store_piece(swapped, lookup(table, place, 1 - lane), 1 - lane, table_ref, high, low)
+
+
+def early_kernel(tables, table_ref, own_hbm, s0, s1, *refs):
+    near, _, _, codes = tables
+    pieces, (high, low, left, part_ref, own_ref, own_sem) = refs[:-6], refs[-6:]
     place, lane = lax.axis_index("blk"), lax.axis_index("depth")
-    near, far = tables
     own_copy = pltpu.make_async_copy(own_hbm, own_ref, own_sem)
     own_copy.start()
-    here, there = lookup(near, place, lane), lookup(near, place, 1 - lane)
     part_ref[...] = jnp.zeros_like(part_ref)
-    store_piece(own_swap, place, 1 - lane, table_ref, high, low, left)
-    store_piece(r1, here, lane, table_ref, high, low)
-    store_piece(r2, here, 1 - lane, table_ref, high, low)
-    store_piece(t1, there, 1 - lane, table_ref, high, low)
-    store_piece(t2, there, lane, table_ref, high, low)
-    store_piece(r3, lookup(far, place, lane), lane, table_ref, high, low)
+    for r, swapped in enumerate((s0, s1)):
+        store_row(swapped.at[0], place * 2 + r, 1 - lane, table_ref, high, low, left, r)
+    pairs = list(zip(pieces[::2], pieces[1::2]))
+    store_pieces(pairs, codes[: len(pairs)], place, lane, table_ref, high, low)
     own_copy.wait()
-    store_piece(own_ref, place, lane, table_ref, high, low, left)
-    for plane in (place, here, there):
+    for r in range(2):
+        store_row(own_ref.at[r], place * 2 + r, lane, table_ref, high, low, left, r)
+    for plane in (place, lookup(near, place, lane), lookup(near, place, 1 - lane)):
         add_plane(plane, left, high, low, part_ref)
 
 
-def middle_kernel(
-    tables, table_ref, r4, t3, high_in, low_in, left, part_in, high, low, part_ref
-):
+def middle_kernel(tables, table_ref, *refs):
+    _, far, helped, codes = tables
+    pieces, (_, _, left, _, high, low, part_ref) = refs[:-7], refs[-7:]
     place, lane = lax.axis_index("blk"), lax.axis_index("depth")
-    far = tables[1]
-    here, there = lookup(far, place, lane), lookup(far, place, 1 - lane)
-    store_piece(t3, there, 1 - lane, table_ref, high, low)
-    store_piece(r4, here, 1 - lane, table_ref, high, low)
-    add_plane(here, left, high, low, part_ref)
+    pairs = list(zip(pieces[::2], pieces[1::2]))
+    store_pieces(pairs, codes[-1 - len(pairs) : -1], place, lane, table_ref, high, low)
+    edge = part_ref.shape[0] // 2
+    add_plane(lookup(helped, place, lane), left, high, low, part_ref)
+    add_rows(lookup(far, place, lane) * 2 * edge, edge, left, high, low, part_ref)
 
 
 def late_kernel(
-    tables, table_ref, t4, high_in, low_in, left, part_in,
+    tables, table_ref, r8, t8, high_in, low_in, left, part_in,
     out_hbm, high, low, square, square_parts, out_ref, out_sem,
 ):
+    _, far, _, codes = tables
     place, lane = lax.axis_index("blk"), lax.axis_index("depth")
     group = lax.axis_index("panel") * 2 + lane
-    there = lookup(tables[1], place, 1 - lane)
-    store_piece(t4, there, lane, table_ref, high, low)
-    add_plane(there, left, high, low, square)
     slab, width, edge, _ = out_ref.shape
     act = 2 * width
+    received = lookup(codes[-1], place, lane) >= 0
+    last_row = lookup(far, place, lane) * 2 + 1
+    store_row(
+        jnp.where(received, r8[0], t8[0]),
+        last_row,
+        jnp.where(received, 1 - lane, lane),
+        table_ref,
+        high,
+        low,
+    )
+    add_rows(last_row * edge, edge, left, high, low, square)
     for r in range(slab):
         for c in range(square.shape[1] // edge):
             kept = table_ref[place * slab + r, 2 * act + c] > 0
@@ -267,30 +287,54 @@
     def swap(block):
         return move(block, [])
 
-    def move_only(block, chains_of):
-        pairs = [(chain[i], chain[i + 1]) for chain in chains_of for i in range(len(chain) - 1)]
-        route = [(index(g, a), index(g, b)) for g in range(groups) for a, b in pairs]
-        return lax.ppermute(block, AXES, route)
-
-    up = [(z, 0, 0) for z in range(chains)] + [(last, 1, 0)]
-    down = [(z, 0, 1) for z in reversed(range(chains))] + [(0, 1, 1)]
-    first = [up + [(last, 1, 1)] + down + [(0, 1, 0)]]
-    second = [up, down]
+    up = [(z, 0, 0) for z in range(chains)]
+    down = [(z, 0, 1) for z in reversed(range(chains))]
+    up_helper, down_helper = (last, 1, 0), (0, 1, 1)
+    crossing = [up + [up_helper, (last, 1, 1)] + down + [down_helper, (0, 1, 0)]]
+    helping = [up + [up_helper], down + [down_helper]]
+    inside = [up + down]
+    here = tuple(lax.axis_index(axis) for axis in AXES[1:])
+    helper = functools.reduce(
+        jnp.logical_or,
+        [
+            functools.reduce(jnp.logical_and, [i == j for i, j in zip(here, place)])
+            for place in (up_helper, down_helper)
+        ],
+    )
+
+    def help_with(received, block):
+        return jnp.where(helper, received, block)
+
+    codes = []
+    for hop in range(8):
+        table = []
+        for z in range(chains):
+            below, above = z - 1 - hop // 4, z + 1 + hop // 4
+            table.append(
+                [
+                    below * 4 + hop % 4 if below >= 0 else -1,
+                    above * 4 + hop % 4 if above < chains else -1,
+                ]
+            )
+        if 2 <= hop < 6:
+            table[0][0] = last * 4 + hop - 2
+            table[last][1] = hop - 2
+        codes.append(table)
     near = [(z - 1, z + 1 if z < last else -1) for z in range(chains)]
-    far = [(z - 2 if z >= 2 else -1, z + 2 if z + 2 < chains else -1) for z in range(chains)]
-    far[0] = (last, far[0][1])
-    far[last] = (far[last][0], 0)
-    tables = (near, far)
+    far = [((z + 2) % chains,) * 2 for z in range(chains)]
+    helped = [(last if z == 0 else 0 if z == last else -1,) * 2 for z in range(chains)]
+    tables = (near, far, helped, codes)
 
     table = slot_table(columns, lanes * width)
-    r1 = move(x_blocks, first)
-    own_swap = swap(x_blocks)
-    r2 = move_only(own_swap, [up, down])
-    r1, table = lax.optimization_barrier((r1, table))
-    r3 = move(r1, second)
-    t1 = swap(r1)
-    r4 = move(r2, second)
-    t2 = swap(r2)
+    x0, x1 = x_blocks[:1], x_blocks[1:]
+    r1, r2 = move(x0, crossing), move(x1, crossing)
+    s0, s1 = swap(x0), swap(x1)
+    r3 = move(help_with(r1, s0), helping)
+    r4 = move(help_with(r2, s1), helping)
+    r5 = move(help_with(r3, r1), helping)
+    r6 = move(help_with(r4, r2), helping)
+    r7, r8 = move(r3, inside), move(r4, inside)
+    t1, t2, t3, t4, t5, t6, t7 = [swap(r) for r in (r1, r2, r3, r4, r5, r6, r7)]
 
     order, own = rows * edge, slab * edge
     table = pltpu.with_memory_space_constraint(table, pltpu.SMEM)
@@ -300,6 +344,7 @@
     def held(*arrays):
         return [pltpu.with_memory_space_constraint(a, pltpu.VMEM) for a in arrays]
 
+    near_pieces = (r1, t1, r2, t2, r3, t3, r4, t4)
     high, low, left, part = pl.pallas_call(
         functools.partial(early_kernel, tables),
         out_shape=[
@@ -308,31 +353,32 @@
             jax.ShapeDtypeStruct((2 * own, order), jnp.bfloat16),
             jax.ShapeDtypeStruct((own, order), jnp.float32),
         ],
-        in_specs=[smem] + [pl.BlockSpec(memory_space=pltpu.HBM)] + [vmem] * 6,
+        in_specs=[smem, pl.BlockSpec(memory_space=pltpu.HBM)] + [vmem] * (2 + len(near_pieces)),
         out_specs=[vmem] * 4,
         scratch_shapes=[pltpu.VMEM(x_blocks.shape, jnp.float32), pltpu.SemaphoreType.DMA],
         compiler_params=params,
         name="early",
-    )(table, pltpu.with_memory_space_constraint(x_blocks, pltpu.HBM), own_swap, r1, r2, t1, t2, r3)
-    t3 = swap(r3)
-    r4, part = lax.optimization_barrier((r4, part))
-    t4 = swap(r4)
+    )(table, pltpu.with_memory_space_constraint(x_blocks, pltpu.HBM), s0, s1, *near_pieces)
+    r8, part = lax.optimization_barrier((r8, part))
+    t8 = swap(r8)
+    far_pieces = (r5, t5, r6, t6, r7, t7)
     dense = [jax.ShapeDtypeStruct(a.shape, a.dtype) for a in (high, low, part)]
+    first = 1 + len(far_pieces)
     high, low, part = pl.pallas_call(
         functools.partial(middle_kernel, tables),
         out_shape=dense,
-        in_specs=[smem] + [vmem] * 6,
+        in_specs=[smem] + [vmem] * (4 + len(far_pieces)),
         out_specs=[vmem] * 3,
-        input_output_aliases={3: 0, 4: 1, 6: 2},
+        input_output_aliases={first: 0, first + 1: 1, first + 3: 2},
         compiler_params=params,
         name="middle",
-    )(table, r4, t3, *held(high, low, left, part))
+    )(table, *far_pieces, *held(high, low, left, part))
     out, _, _, _ = pl.pallas_call(
         functools.partial(late_kernel, tables),
         out_shape=[jax.ShapeDtypeStruct(x_blocks.shape, jnp.float32)] + dense,
-        in_specs=[smem] + [vmem] * 5,
+        in_specs=[smem] + [vmem] * 6,
         out_specs=[pl.BlockSpec(memory_space=pltpu.HBM)] + [vmem] * 3,
-        input_output_aliases={2: 1, 3: 2, 5: 3},
+        input_output_aliases={3: 1, 4: 2, 6: 3},
         scratch_shapes=[
             pltpu.VMEM((2 * own, order), jnp.bfloat16),
             pltpu.VMEM(x_blocks.shape, jnp.float32),
@@ -340,7 +386,7 @@
         ],
         compiler_params=params,
         name="late",
-    )(table, t4, *held(high, low, left, part))
+    )(table, r8, t8, *held(high, low, left, part))
     return out
 
 
@@ -349,7 +395,7 @@
     rows, slots = columns.shape
     _, chains, panels, lanes = (lax.axis_size(axis) for axis in AXES)
     full = rows <= slots and rows == lanes * width and width % 2 == 0
-    if full and rows <= 8 and edge % 128 == 0 and panels >= 2 and lanes == 2 and chains == 4:
+    if full and rows <= 8 and slab == 2 and edge == 128 and panels >= 2 and lanes == 2 and chains == 4:
         return gather_local(x_blocks, columns)
     return ring_local(x_blocks, columns)
 

time: 34 us -> 39.9 us (1.17)
  waiting for transfers between devices: 11.4 us -> 15.4 us
  other arithmetic: 2.86 us -> 1.61 us
  starting transfers between devices: 11.1 us -> 12.3 us
  local copies, waits for them, and re-layouts: 0 us -> 1.08 us
  Pallas kernels: 8.34 us -> 9.16 us
    ppermute x8 -> x18, waiting for transfers between devices: 8.22 us -> 15.4 us  [move(): return lax.ppermute(block, AXES, route)]
    ppermute x8 -> x18, starting transfers between devices: 7.63 us -> 12.3 us  [move(): return lax.ppermute(block, AXES, route)]
    ppermute x1 -> x0, starting transfers between devices: 3.5 us -> none  [move_only(): return lax.ppermute(block, AXES, route)]
    ppermute x1 -> x0, waiting for transfers between devices: 3.13 us -> none  [move_only(): return lax.ppermute(block, AXES, route)]
    slice x0 -> x1, local copies, waits for them, and re-layouts: none -> 1.08 us  [gather_local(): x0, x1 = (x_blocks[:1], x_blocks[1:])]
    pallas_call x1, Pallas kernels: 1.54 us -> 2.28 us  [gather_local(): pl.pallas_call(functools.partial(middle_kernel, tables), out_shape=dense,...]
    convert_element_type x1, other arithmetic: 0.69 us -> 0.01 us  [slot_table(): count = jnp.sum(here.astype(jnp.int32), axis=1, keepdims=True)]
    select_n x1, other arithmetic: 0.69 us -> 0.01 us  [slot_table(): order = jnp.where(here, slots, filled)]
  transfers between devices with their start and end apart: 9 -> 18, of which waited for: 6 -> 7; matrix products, arithmetic and copies ran while one was open for 8% -> 4% of each run, Pallas kernels for 14% -> 14%
where the time goes in v8:
time: 39.9 us; the launch traced here: 39.7 us
  waiting for transfers between devices  15.4 us (39%)
  starting transfers between devices  12.3 us (31%)
  Pallas kernels  9.16 us (23%)
  other arithmetic  1.61 us (4%)
  local copies, waits for them, and re-layouts  1.08 us (3%)
    ppermute x18, waiting for transfers between devices, move(): return lax.ppermute(block, AXES, route)  15.4 us
    ppermute x18, starting transfers between devices, move(): return lax.ppermute(block, AXES, route)  12.3 us
    pallas_call x1, Pallas kernels, gather_local(): pl.pallas_call(functools.partial(late_kernel, tables), out_shape=[jax.Sha...  3.55 us
    pallas_call x1, Pallas kernels, gather_local(): pl.pallas_call(functools.partial(early_kernel, tables), out_shape=[jax.Sh...  3.33 us
    pallas_call x1, Pallas kernels, gather_local(): pl.pallas_call(functools.partial(middle_kernel, tables), out_shape=dense,...  2.28 us
    slice x1, local copies, waits for them, and re-layouts, gather_local(): x0, x1 = (x_blocks[:1], x_blocks[1:])  1.08 us
    reduce_sum x1, other arithmetic, slot_table(): count = jnp.sum(here.astype(jnp.int32), axis=1, keepdims=True)  0.8 us
  transfers between devices with their start and end apart: 18, of which 7 were waited for; matrix products, arithmetic and copies ran while one was open for 4% of the time, Pallas kernels for 14%

profile of v8, /device:TPU:0, one launch (start us, length us, event | category | flops | bytes accessed | tf_op | source)
XLA Modules:
  0.0 39.7 jit_solution(4202087472326489551)
XLA Ops:
  0.0 1.1 %fusion.2 = (f32[1,4,128,128]{3,2,1,0:T(8,128)S(1)}, f32[1,4,128,128]{3,2,1,0:T(8,128)S(1)}) fusion(f32[2,4,128,128]{3,2,1,0:T(8,128)} %own_hbm.1), kind=kLoop, calls=%fused_computation.15 | loop fusion | bytes 1048576 | tf_op jit(solution)/shard_map/slice | solution.py:329
  1.1 3.1 %collective-permute-start.5 = (f32[1,4,128,128]{3,2,1,0:T(8,128)S(1)}, f32[1,4,128,128]{3,2,1,0:T(8,128)S(1)}, u32[]{:S(2)}, u32[]{:S(2)}) collective-permute-start(f32[1,4,128,128]{3,2,1,0:T(8,128)S(1)} %get-tuple-element.25), channel_id=1, source_target_pairs={{2,0},{0,4},{4,8},{8,12},{12,14},{14,15},{15,13},{13,9},{9,5},{5,1... | collective-permute-start | bytes 786440 | tf_op jit(solution)/shard_map/ppermute | solution.py:285
  4.2 0.0 collective-permute-start.4
  4.2 0.5 %collective-permute-start.1 = (f32[1,4,128,128]{3,2,1,0:T(8,128)S(1)}, f32[1,4,128,128]{3,2,1,0:T(8,128)S(1)}, u32[]{:S(2)}, u32[]{:S(2)}) collective-permute-start(f32[1,4,128,128]{3,2,1,0:T(8,128)S(1)} %get-tuple-element.26), channel_id=1, source_target_pairs={{1,0},{0,1},{17,16},{16,17},{3,2},{2,3},{19,18},{18,19},{5,4},{4,5... | collective-permute-start | bytes 786440 | tf_op jit(solution)/shard_map/ppermute | solution.py:285
  4.7 1.6 %collective-permute-start = (f32[1,4,128,128]{3,2,1,0:T(8,128)S(1)}, f32[1,4,128,128]{3,2,1,0:T(8,128)S(1)}, u32[]{:S(2)}, u32[]{:S(2)}) collective-permute-start(f32[1,4,128,128]{3,2,1,0:T(8,128)S(1)} %get-tuple-element.26), channel_id=1, source_target_pairs={{2,0},{0,4},{4,8},{8,12},{12,14},{14,15},{15,13},{13,9},{9,5},{5,1... | collective-permute-start | bytes 786440 | tf_op jit(solution)/shard_map/ppermute | solution.py:285
  6.3 0.8 %fusion.1 = (s32[8]{0:T(128)S(1)}, s32[8,8]{1,0:T(8,128)S(1)}) fusion(s32[8,16]{1,0:T(8,128)} %param.3), kind=kLoop, calls=%fused_computation.14 | loop fusion | flops 184 | bytes 544 | tf_op jit(solution)/shard_map/reduce_sum | solution.py:251
  7.1 0.1 fusion
  7.2 0.2 convert_reduce_fusion
  7.4 0.1 add_select_fusion
  7.5 1.0 %collective-permute-done.5.refs_0_ = f32[1,4,128,128]{3,2,1,0:T(8,128)S(1)} collective-permute-done((f32[1,4,128,128]{3,2,1,0:T(8,128)S(1)}, f32[1,4,128,128]{3,2,1,0:T(8,128)S(1)}, u32[]{:S(2)}, u32[]{:S(2)}) %collective-permute-start.5) | collective-permute-done | bytes 262176 | tf_op jit(solution)/shard_map/ppermute | solution.py:285
  8.4 0.0 collective-permute-done.4.s0
  8.5 2.2 %collective-permute-start.8 = (f32[1,4,128,128]{3,2,1,0:T(8,128)S(1)}, f32[1,4,128,128]{3,2,1,0:T(8,128)S(1)}, u32[]{:S(2)}, u32[]{:S(2)}) collective-permute-start(f32[1,4,128,128]{3,2,1,0:T(8,128)S(1)} %broadcast_select_fusion.2), channel_id=1, source_target_pairs={{14,0},{0,4},{4,8},{8,12},{12,14},{3,13},{13,9},{9,5},{5,1},{1,3},... | collective-permute-start | bytes 786440 | tf_op jit(solution)/shard_map/ppermute | solution.py:285
  10.6 0.2 select_reduce_fusion
  10.8 0.4 collective-permute-done.refs_2_
  11.3 2.2 %collective-permute-start.2 = (f32[1,4,128,128]{3,2,1,0:T(8,128)S(1)}, f32[1,4,128,128]{3,2,1,0:T(8,128)S(1)}, u32[]{:S(2)}, u32[]{:S(2)}) collective-permute-start(f32[1,4,128,128]{3,2,1,0:T(8,128)S(1)} %broadcast_select_fusion.3), channel_id=1, source_target_pairs={{14,0},{0,4},{4,8},{8,12},{12,14},{3,13},{13,9},{9,5},{5,1},{1,3},... | collective-permute-start | bytes 786440 | tf_op jit(solution)/shard_map/ppermute | solution.py:285
  13.4 0.5 %collective-permute-start.7 = (f32[1,4,128,128]{3,2,1,0:T(8,128)S(1)}, f32[1,4,128,128]{3,2,1,0:T(8,128)S(1)}, u32[]{:S(2)}, u32[]{:S(2)}) collective-permute-start(f32[1,4,128,128]{3,2,1,0:T(8,128)S(1)} %collective-permute-done.refs_2_), channel_id=1, source_target_pairs={{1,0},{0,1},{17,16},{16,17},{3,2},{2,3},{19,18},{18,19},{5,4},{4,5... | collective-permute-start | bytes 786440 | tf_op jit(solution)/shard_map/ppermute | solution.py:285
  13.9 4.0 %collective-permute-done.8.refs_4_ = f32[1,4,128,128]{3,2,1,0:T(8,128)S(1)} collective-permute-done((f32[1,4,128,128]{3,2,1,0:T(8,128)S(1)}, f32[1,4,128,128]{3,2,1,0:T(8,128)S(1)}, u32[]{:S(2)}, u32[]{:S(2)}) %collective-permute-start.8) | collective-permute-done | bytes 262176 | tf_op jit(solution)/shard_map/ppermute | solution.py:285
  18.0 0.1 collective-permute-start.12
  18.1 2.7 %collective-permute-done.2.refs_6_ = f32[1,4,128,128]{3,2,1,0:T(8,128)S(1)} collective-permute-done((f32[1,4,128,128]{3,2,1,0:T(8,128)S(1)}, f32[1,4,128,128]{3,2,1,0:T(8,128)S(1)}, u32[]{:S(2)}, u32[]{:S(2)}) %collective-permute-start.2) | collective-permute-done | bytes 262176 | tf_op jit(solution)/shard_map/ppermute | solution.py:285
  20.8 0.1 collective-permute-start.14
  20.8 0.6 %collective-permute-start.16 = (f32[1,4,128,128]{3,2,1,0:T(8,128)S(1)}, f32[1,4,128,128]{3,2,1,0:T(8,128)S(1)}, u32[]{:S(2)}, u32[]{:S(2)}) collective-permute-start(f32[1,4,128,128]{3,2,1,0:T(8,128)S(1)} %collective-permute-done.8.refs_4_), channel_id=1, source_target_pairs={{1,0},{0,4},{4,8},{8,12},{12,13},{13,9},{9,5},{5,1},{17,16},{16,20... | collective-permute-start | bytes 786440 | tf_op jit(solution)/shard_map/ppermute | solution.py:285
  21.5 0.5 %collective-permute-start.10 = (f32[1,4,128,128]{3,2,1,0:T(8,128)S(1)}, f32[1,4,128,128]{3,2,1,0:T(8,128)S(1)}, u32[]{:S(2)}, u32[]{:S(2)}) collective-permute-start(f32[1,4,128,128]{3,2,1,0:T(8,128)S(1)} %collective-permute-done.2.refs_6_), channel_id=1, source_target_pairs={{1,0},{0,1},{17,16},{16,17},{3,2},{2,3},{19,18},{18,19},{5,4},{4,5... | collective-permute-start | bytes 786440 | tf_op jit(solution)/shard_map/ppermute | solution.py:285
  22.0 5.1 %collective-permute-done.12.refs_0_ = f32[1,4,128,128]{3,2,1,0:T(8,128)S(1)} collective-permute-done((f32[1,4,128,128]{3,2,1,0:T(8,128)S(1)}, f32[1,4,128,128]{3,2,1,0:T(8,128)S(1)}, u32[]{:S(2)}, u32[]{:S(2)}) %collective-permute-start.12) | collective-permute-done | bytes 262176 | tf_op jit(solution)/shard_map/ppermute | solution.py:285
  27.1 0.1 pad_add_fusion.table_ref
  27.2 0.4 collective-permute-done.16.refs_4_
  27.5 0.2 collective-permute-start.13
  27.7 0.4 collective-permute-start.17
  28.0 1.8 %collective-permute-done.14.refs_2_ = f32[1,4,128,128]{3,2,1,0:T(8,128)S(1)} collective-permute-done((f32[1,4,128,128]{3,2,1,0:T(8,128)S(1)}, f32[1,4,128,128]{3,2,1,0:T(8,128)S(1)}, u32[]{:S(2)}, u32[]{:S(2)}) %collective-permute-start.14) | collective-permute-done | bytes 262176 | tf_op jit(solution)/shard_map/ppermute | solution.py:285
  29.9 3.3 %early.1 = (bf16[1024,1024]{1,0:T(8,128)(2,1)S(1)}, bf16[1024,1024]{1,0:T(8,128)(2,1)S(1)}, bf16[512,1024]{1,0:T(8,128)(2,1)S(1)}, f32[256,1024]{1,0:T(8,128)S(1)}) custom-call(s32[8,24]{1,0:T(8,128)S(1)} %pad_add_fusion.table_ref, f32[2,4,128,128]{3,2,1,0:T(8,128)} %own_hbm.1, f32[1,4,128,128]{3,2,1,0:T(8,128)S(1)} %collective-permute-done.4.s0, ...), custom_call_target="tpu_custom_call" | custom-call | tf_op jit(solution)/shard_map/early/pallas_call | solution.py:348
  33.3 0.6 %collective-permute-start.11 = (f32[1,4,128,128]{3,2,1,0:T(8,128)S(1)}, f32[1,4,128,128]{3,2,1,0:T(8,128)S(1)}, u32[]{:S(2)}, u32[]{:S(2)}) collective-permute-start(f32[1,4,128,128]{3,2,1,0:T(8,128)S(1)} %collective-permute-done.3.r8), channel_id=1, source_target_pairs={{1,0},{0,1},{17,16},{16,17},{3,2},{2,3},{19,18},{18,19},{5,4},{4,5... | collective-permute-start | bytes 786440 | tf_op jit(solution)/shard_map/ppermute | solution.py:285
  33.8 2.3 %middle.1 = (bf16[1024,1024]{1,0:T(8,128)(2,1)S(1)}, bf16[1024,1024]{1,0:T(8,128)(2,1)S(1)}, f32[256,1024]{1,0:T(8,128)S(1)}) custom-call(s32[8,24]{1,0:T(8,128)S(1)} %pad_add_fusion.table_ref, f32[1,4,128,128]{3,2,1,0:T(8,128)S(1)} %collective-permute-done.12.refs_0_, ...), custom_call_target="tpu_custom_call", output_to_operand_aliasing={{0}: (7, {}), {1}: (8, {}), {2}: (10, {})} | custom-call | tf_op jit(solution)/shard_map/middle/pallas_call | solution.py:367
  36.1 3.5 %late.1 = (f32[2,4,128,128]{3,2,1,0:T(8,128)}, bf16[1024,1024]{1,0:T(8,128)(2,1)S(1)}, bf16[1024,1024]{1,0:T(8,128)(2,1)S(1)}, f32[256,1024]{1,0:T(8,128)S(1)}) custom-call(s32[8,24]{1,0:T(8,128)S(1)} %pad_add_fusion.table_ref, f32[1,4,128,128]{3,2,1,0:T(8,128)S(1)} %collective-permute-done.3.r8, ...), custom_call_target="tpu_custom_call", output_to_operand_aliasing={{1}: (3, {}), {2}: (4, {}), {3}: (6, {})} | custom-call | tf_op jit(solution)/shard_map/late/pallas_call | solution.py:376
  (23 shorter events, 0.2 us)
Async XLA Ops:
  0.0 18.0 %copy-start = (s32[8,16]{1,0:T(8,128)S(1)}, s32[8,16]{1,0:T(8,128)}, u32[]{:S(2)}) copy-start(s32[8,16]{1,0:T(8,128)} %param.3) | copy-start | bytes 1540
  1.1 7.3 %collective-permute-start.5 = (f32[1,4,128,128]{3,2,1,0:T(8,128)S(1)}, f32[1,4,128,128]{3,2,1,0:T(8,128)S(1)}, u32[]{:S(2)}, u32[]{:S(2)}) collective-permute-start(f32[1,4,128,128]{3,2,1,0:T(8,128)S(1)} %get-tuple-element.25), channel_id=1, source_target_pairs={{2,0},{0,4},{4,8},{8,12},{12,14},{14,15},{15,13},{13,9},{9,5},{5,1... | collective-permute-start | bytes 786440 | tf_op jit(solution)/shard_map/ppermute | solution.py:285
  4.2 4.3 %collective-permute-start.4 = (f32[1,4,128,128]{3,2,1,0:T(8,128)S(1)}, f32[1,4,128,128]{3,2,1,0:T(8,128)S(1)}, u32[]{:S(2)}, u32[]{:S(2)}) collective-permute-start(f32[1,4,128,128]{3,2,1,0:T(8,128)S(1)} %get-tuple-element.25), channel_id=1, source_target_pairs={{1,0},{0,1},{17,16},{16,17},{3,2},{2,3},{19,18},{18,19},{5,4},{4,5... | collective-permute-start | bytes 786440 | tf_op jit(solution)/shard_map/ppermute | solution.py:285
  4.2 6.7 %collective-permute-start.1 = (f32[1,4,128,128]{3,2,1,0:T(8,128)S(1)}, f32[1,4,128,128]{3,2,1,0:T(8,128)S(1)}, u32[]{:S(2)}, u32[]{:S(2)}) collective-permute-start(f32[1,4,128,128]{3,2,1,0:T(8,128)S(1)} %get-tuple-element.26), channel_id=1, source_target_pairs={{1,0},{0,1},{17,16},{16,17},{3,2},{2,3},{19,18},{18,19},{5,4},{4,5... | collective-permute-start | bytes 786440 | tf_op jit(solution)/shard_map/ppermute | solution.py:285
  4.7 6.6 %collective-permute-start = (f32[1,4,128,128]{3,2,1,0:T(8,128)S(1)}, f32[1,4,128,128]{3,2,1,0:T(8,128)S(1)}, u32[]{:S(2)}, u32[]{:S(2)}) collective-permute-start(f32[1,4,128,128]{3,2,1,0:T(8,128)S(1)} %get-tuple-element.26), channel_id=1, source_target_pairs={{2,0},{0,4},{4,8},{8,12},{12,14},{14,15},{15,13},{13,9},{9,5},{5,1... | collective-permute-start | bytes 786440 | tf_op jit(solution)/shard_map/ppermute | solution.py:285
  8.5 9.5 %collective-permute-start.8 = (f32[1,4,128,128]{3,2,1,0:T(8,128)S(1)}, f32[1,4,128,128]{3,2,1,0:T(8,128)S(1)}, u32[]{:S(2)}, u32[]{:S(2)}) collective-permute-start(f32[1,4,128,128]{3,2,1,0:T(8,128)S(1)} %broadcast_select_fusion.2), channel_id=1, source_target_pairs={{14,0},{0,4},{4,8},{8,12},{12,14},{3,13},{13,9},{9,5},{5,1},{1,3},... | collective-permute-start | bytes 786440 | tf_op jit(solution)/shard_map/ppermute | solution.py:285
  11.3 9.5 %collective-permute-start.2 = (f32[1,4,128,128]{3,2,1,0:T(8,128)S(1)}, f32[1,4,128,128]{3,2,1,0:T(8,128)S(1)}, u32[]{:S(2)}, u32[]{:S(2)}) collective-permute-start(f32[1,4,128,128]{3,2,1,0:T(8,128)S(1)} %broadcast_select_fusion.3), channel_id=1, source_target_pairs={{14,0},{0,4},{4,8},{8,12},{12,14},{3,13},{13,9},{9,5},{5,1},{1,3},... | collective-permute-start | bytes 786440 | tf_op jit(solution)/shard_map/ppermute | solution.py:285
  13.4 8.0 %collective-permute-start.6 = (f32[1,4,128,128]{3,2,1,0:T(8,128)S(1)}, f32[1,4,128,128]{3,2,1,0:T(8,128)S(1)}, u32[]{:S(2)}, u32[]{:S(2)}) collective-permute-start(f32[1,4,128,128]{3,2,1,0:T(8,128)S(1)} %collective-permute-done.5.refs_0_), channel_id=1, source_target_pairs={{1,0},{0,1},{17,16},{16,17},{3,2},{2,3},{19,18},{18,19},{5,4},{4,5... | collective-permute-start | bytes 786440 | tf_op jit(solution)/shard_map/ppermute | solution.py:285
  13.4 8.0 %collective-permute-start.7 = (f32[1,4,128,128]{3,2,1,0:T(8,128)S(1)}, f32[1,4,128,128]{3,2,1,0:T(8,128)S(1)}, u32[]{:S(2)}, u32[]{:S(2)}) collective-permute-start(f32[1,4,128,128]{3,2,1,0:T(8,128)S(1)} %collective-permute-done.refs_2_), channel_id=1, source_target_pairs={{1,0},{0,1},{17,16},{16,17},{3,2},{2,3},{19,18},{18,19},{5,4},{4,5... | collective-permute-start | bytes 786440 | tf_op jit(solution)/shard_map/ppermute | solution.py:285
  18.0 9.1 %collective-permute-start.12 = (f32[1,4,128,128]{3,2,1,0:T(8,128)S(1)}, f32[1,4,128,128]{3,2,1,0:T(8,128)S(1)}, u32[]{:S(2)}, u32[]{:S(2)}) collective-permute-start(f32[1,4,128,128]{3,2,1,0:T(8,128)S(1)} %broadcast_select_fusion.1), channel_id=1, source_target_pairs={{14,0},{0,4},{4,8},{8,12},{12,14},{3,13},{13,9},{9,5},{5,1},{1,3},... | collective-permute-start | bytes 786440 | tf_op jit(solution)/shard_map/ppermute | solution.py:285
  20.8 9.1 %collective-permute-start.14 = (f32[1,4,128,128]{3,2,1,0:T(8,128)S(1)}, f32[1,4,128,128]{3,2,1,0:T(8,128)S(1)}, u32[]{:S(2)}, u32[]{:S(2)}) collective-permute-start(f32[1,4,128,128]{3,2,1,0:T(8,128)S(1)} %broadcast_select_fusion), channel_id=1, source_target_pairs={{14,0},{0,4},{4,8},{8,12},{12,14},{3,13},{13,9},{9,5},{5,1},{1,3},... | collective-permute-start | bytes 786440 | tf_op jit(solution)/shard_map/ppermute | solution.py:285
  20.8 6.7 %collective-permute-start.16 = (f32[1,4,128,128]{3,2,1,0:T(8,128)S(1)}, f32[1,4,128,128]{3,2,1,0:T(8,128)S(1)}, u32[]{:S(2)}, u32[]{:S(2)}) collective-permute-start(f32[1,4,128,128]{3,2,1,0:T(8,128)S(1)} %collective-permute-done.8.refs_4_), channel_id=1, source_target_pairs={{1,0},{0,4},{4,8},{8,12},{12,13},{13,9},{9,5},{5,1},{17,16},{16,20... | collective-permute-start | bytes 786440 | tf_op jit(solution)/shard_map/ppermute | solution.py:285
  21.5 6.2 %collective-permute-start.9 = (f32[1,4,128,128]{3,2,1,0:T(8,128)S(1)}, f32[1,4,128,128]{3,2,1,0:T(8,128)S(1)}, u32[]{:S(2)}, u32[]{:S(2)}) collective-permute-start(f32[1,4,128,128]{3,2,1,0:T(8,128)S(1)} %collective-permute-done.8.refs_4_), channel_id=1, source_target_pairs={{1,0},{0,1},{17,16},{16,17},{3,2},{2,3},{19,18},{18,19},{5,4},{4,5... | collective-permute-start | bytes 786440 | tf_op jit(solution)/shard_map/ppermute | solution.py:285
  21.5 8.4 %collective-permute-start.10 = (f32[1,4,128,128]{3,2,1,0:T(8,128)S(1)}, f32[1,4,128,128]{3,2,1,0:T(8,128)S(1)}, u32[]{:S(2)}, u32[]{:S(2)}) collective-permute-start(f32[1,4,128,128]{3,2,1,0:T(8,128)S(1)} %collective-permute-done.2.refs_6_), channel_id=1, source_target_pairs={{1,0},{0,1},{17,16},{16,17},{3,2},{2,3},{19,18},{18,19},{5,4},{4,5... | collective-permute-start | bytes 786440 | tf_op jit(solution)/shard_map/ppermute | solution.py:285
  27.1 6.2 %collective-permute-start.3 = (f32[1,4,128,128]{3,2,1,0:T(8,128)S(1)}, f32[1,4,128,128]{3,2,1,0:T(8,128)S(1)}, u32[]{:S(2)}, u32[]{:S(2)}) collective-permute-start(f32[1,4,128,128]{3,2,1,0:T(8,128)S(1)} %collective-permute-done.2.refs_6_), channel_id=1, source_target_pairs={{1,0},{0,4},{4,8},{8,12},{12,13},{13,9},{9,5},{5,1},{17,16},{16,20... | collective-permute-start | bytes 786440 | tf_op jit(solution)/shard_map/ppermute | solution.py:285
  27.5 6.3 %collective-permute-start.13 = (f32[1,4,128,128]{3,2,1,0:T(8,128)S(1)}, f32[1,4,128,128]{3,2,1,0:T(8,128)S(1)}, u32[]{:S(2)}, u32[]{:S(2)}) collective-permute-start(f32[1,4,128,128]{3,2,1,0:T(8,128)S(1)} %collective-permute-done.12.refs_0_), channel_id=1, source_target_pairs={{1,0},{0,1},{17,16},{16,17},{3,2},{2,3},{19,18},{18,19},{5,4},{4,5... | collective-permute-start | bytes 786440 | tf_op jit(solution)/shard_map/ppermute | solution.py:285
  27.7 6.1 %collective-permute-start.17 = (f32[1,4,128,128]{3,2,1,0:T(8,128)S(1)}, f32[1,4,128,128]{3,2,1,0:T(8,128)S(1)}, u32[]{:S(2)}, u32[]{:S(2)}) collective-permute-start(f32[1,4,128,128]{3,2,1,0:T(8,128)S(1)} %collective-permute-done.16.refs_4_), channel_id=1, source_target_pairs={{1,0},{0,1},{17,16},{16,17},{3,2},{2,3},{19,18},{18,19},{5,4},{4,5... | collective-permute-start | bytes 786440 | tf_op jit(solution)/shard_map/ppermute | solution.py:285
  29.9 3.9 %collective-permute-start.15 = (f32[1,4,128,128]{3,2,1,0:T(8,128)S(1)}, f32[1,4,128,128]{3,2,1,0:T(8,128)S(1)}, u32[]{:S(2)}, u32[]{:S(2)}) collective-permute-start(f32[1,4,128,128]{3,2,1,0:T(8,128)S(1)} %collective-permute-done.14.refs_2_), channel_id=1, source_target_pairs={{1,0},{0,1},{17,16},{16,17},{3,2},{2,3},{19,18},{18,19},{5,4},{4,5... | collective-permute-start | bytes 786440 | tf_op jit(solution)/shard_map/ppermute | solution.py:285
  33.3 2.9 %collective-permute-start.11 = (f32[1,4,128,128]{3,2,1,0:T(8,128)S(1)}, f32[1,4,128,128]{3,2,1,0:T(8,128)S(1)}, u32[]{:S(2)}, u32[]{:S(2)}) collective-permute-start(f32[1,4,128,128]{3,2,1,0:T(8,128)S(1)} %collective-permute-done.3.r8), channel_id=1, source_target_pairs={{1,0},{0,1},{17,16},{16,17},{3,2},{2,3},{19,18},{18,19},{5,4},{4,5... | collective-permute-start | bytes 786440 | tf_op jit(solution)/shard_map/ppermute | solution.py:285

commit v9 on v6

--- a/solution.py
+++ b/solution.py
@@ -110,14 +110,14 @@
     return found
 
 
-def store_piece(piece, plane, group, table_ref, high, low, own=None):
-    slab, width, edge, _ = piece.shape
+def store_piece(piece, plane, group, table_ref, high, low, own=None, slab=2, first=0):
+    count, width, edge, _ = piece.shape
     act = 2 * width
 
     @pl.when(plane >= 0)
     def _():
-        for r in range(slab):
-            row = plane * slab + r
+        for r in range(count):
+            row = plane * slab + first + r
             for w in range(width):
                 slot = group * width + w
                 col = pl.ds(pl.multiple_of(table_ref[row, slot] * edge, edge), edge)
@@ -165,24 +165,26 @@
 
 
 def middle_kernel(
-    tables, table_ref, r4, t3, high_in, low_in, left, part_in, high, low, part_ref
+    tables, table_ref, r4a, r4b, t3, t4a, high_in, low_in, left, part_in, high, low, part_ref
 ):
     place, lane = lax.axis_index("blk"), lax.axis_index("depth")
     far = tables[1]
     here, there = lookup(far, place, lane), lookup(far, place, 1 - lane)
     store_piece(t3, there, 1 - lane, table_ref, high, low)
-    store_piece(r4, here, 1 - lane, table_ref, high, low)
+    store_piece(r4a, here, 1 - lane, table_ref, high, low)
+    store_piece(t4a, there, lane, table_ref, high, low)
+    store_piece(r4b, here, 1 - lane, table_ref, high, low, first=1)
     add_plane(here, left, high, low, part_ref)
 
 
 def late_kernel(
-    tables, table_ref, t4, high_in, low_in, left, part_in,
+    tables, table_ref, t4b, high_in, low_in, left, part_in,
     out_hbm, high, low, square, square_parts, out_ref, out_sem,
 ):
     place, lane = lax.axis_index("blk"), lax.axis_index("depth")
     group = lax.axis_index("panel") * 2 + lane
     there = lookup(tables[1], place, 1 - lane)
-    store_piece(t4, there, lane, table_ref, high, low)
+    store_piece(t4b, there, lane, table_ref, high, low, first=1)
     add_plane(there, left, high, low, square)
     slab, width, edge, _ = out_ref.shape
     act = 2 * width
@@ -289,7 +291,7 @@
     r1, table = lax.optimization_barrier((r1, table))
     r3 = move(r1, second)
     t1 = swap(r1)
-    r4 = move(r2, second)
+    r4a, r4b = move(r2[:1], second), move(r2[1:], second)
     t2 = swap(r2)
 
     order, own = rows * edge, slab * edge
@@ -315,18 +317,20 @@
         name="early",
     )(table, pltpu.with_memory_space_constraint(x_blocks, pltpu.HBM), own_swap, r1, r2, t1, t2, r3)
     t3 = swap(r3)
-    r4, part = lax.optimization_barrier((r4, part))
-    t4 = swap(r4)
+    r4a, part = lax.optimization_barrier((r4a, part))
+    t4a = swap(r4a)
+    r4b, t4a = lax.optimization_barrier((r4b, t4a))
+    t4b = swap(r4b)
     dense = [jax.ShapeDtypeStruct(a.shape, a.dtype) for a in (high, low, part)]
     high, low, part = pl.pallas_call(
         functools.partial(middle_kernel, tables),
         out_shape=dense,
-        in_specs=[smem] + [vmem] * 6,
+        in_specs=[smem] + [vmem] * 8,
         out_specs=[vmem] * 3,
-        input_output_aliases={3: 0, 4: 1, 6: 2},
+        input_output_aliases={5: 0, 6: 1, 8: 2},
         compiler_params=params,
         name="middle",
-    )(table, r4, t3, *held(high, low, left, part))
+    )(table, r4a, r4b, t3, t4a, *held(high, low, left, part))
     out, _, _, _ = pl.pallas_call(
         functools.partial(late_kernel, tables),
         out_shape=[jax.ShapeDtypeStruct(x_blocks.shape, jnp.float32)] + dense,
@@ -340,7 +344,7 @@
         ],
         compiler_params=params,
         name="late",
-    )(table, t4, *held(high, low, left, part))
+    )(table, t4b, *held(high, low, left, part))
     return out
 
 
@@ -349,7 +353,7 @@
     rows, slots = columns.shape
     _, chains, panels, lanes = (lax.axis_size(axis) for axis in AXES)
     full = rows <= slots and rows == lanes * width and width % 2 == 0
-    if full and rows <= 8 and edge % 128 == 0 and panels >= 2 and lanes == 2 and chains == 4:
+    if full and rows <= 8 and slab == 2 and edge == 128 and panels >= 2 and lanes == 2 and chains == 4:
         return gather_local(x_blocks, columns)
     return ring_local(x_blocks, columns)
 

time: 34 us -> 33.8 us (level)
  waiting for transfers between devices: 11.4 us -> 8.85 us
  starting transfers between devices: 11.1 us -> 13.3 us
    ppermute x8 -> x10, waiting for transfers between devices: 8.22 us -> 5.72 us  [move(): return lax.ppermute(block, AXES, route)]
    ppermute x8 -> x10, starting transfers between devices: 7.63 us -> 9.82 us  [move(): return lax.ppermute(block, AXES, route)]
  transfers between devices with their start and end apart: 9 -> 11, of which waited for: 6 -> 5; matrix products, arithmetic and copies ran while one was open for 8% -> 9% of each run, Pallas kernels for 14% -> 14%
where the time goes in v9:
time: 33.8 us; the launch traced here: 33.5 us
  starting transfers between devices  13.3 us (39%)
  waiting for transfers between devices  8.85 us (26%)
  Pallas kernels  8.36 us (25%)
  other arithmetic  2.86 us (8%)
    ppermute x10, starting transfers between devices, move(): return lax.ppermute(block, AXES, route)  9.82 us
    ppermute x10, waiting for transfers between devices, move(): return lax.ppermute(block, AXES, route)  5.72 us
    pallas_call x1, Pallas kernels, gather_local(): pl.pallas_call(functools.partial(late_kernel, tables), out_shape=[jax.Sha...  3.59 us
    ppermute x1, starting transfers between devices, move_only(): return lax.ppermute(block, AXES, route)  3.5 us
    ppermute x1, waiting for transfers between devices, move_only(): return lax.ppermute(block, AXES, route)  3.13 us
    pallas_call x1, Pallas kernels, gather_local(): pl.pallas_call(functools.partial(early_kernel, tables), out_shape=[jax.Sh...  3.13 us
    pallas_call x1, Pallas kernels, gather_local(): pl.pallas_call(functools.partial(middle_kernel, tables), out_shape=dense,...  1.64 us
    reduce_sum x1, other arithmetic, slot_table(): count = jnp.sum(here.astype(jnp.int32), axis=1, keepdims=True)  0.8 us
  transfers between devices with their start and end apart: 11, of which 5 were waited for; matrix products, arithmetic and copies ran while one was open for 9% of the time, Pallas kernels for 14%

profile of v9, /device:TPU:0, one launch (start us, length us, event | category | flops | bytes accessed | tf_op | source)
XLA Modules:
  0.0 33.5 jit_solution(2697338078261816667)
XLA Ops:
  0.0 3.0 %collective-permute-start = (f32[2,4,128,128]{3,2,1,0:T(8,128)}, f32[2,4,128,128]{3,2,1,0:T(8,128)S(1)}, u32[]{:S(2)}, u32[]{:S(2)}) collective-permute-start(f32[2,4,128,128]{3,2,1,0:T(8,128)} %own_hbm.1), channel_id=1, source_target_pairs={{2,0},{0,4},{4,8},{8,12},{12,14},{14,15},{15,13},{13,9},{9,5},{5,1... | collective-permute-start | bytes 1572872 | tf_op jit(solution)/shard_map/ppermute | solution.py:267
  3.0 0.0 collective-permute-start.1
  3.0 0.8 %fusion.1 = (s32[8]{0:T(128)S(1)}, s32[8,8]{1,0:T(8,128)S(1)}) fusion(s32[8,16]{1,0:T(8,128)} %param.3), kind=kLoop, calls=%fused_computation.10 | loop fusion | flops 184 | bytes 544 | tf_op jit(solution)/shard_map/reduce_sum | solution.py:233
  3.8 0.1 fusion
  3.9 0.2 convert_reduce_fusion
  4.2 0.1 add_select_fusion
  4.2 0.2 select_reduce_fusion
  4.4 0.7 %collective-permute-done.1.own_swap = f32[2,4,128,128]{3,2,1,0:T(8,128)S(1)} collective-permute-done((f32[2,4,128,128]{3,2,1,0:T(8,128)}, f32[2,4,128,128]{3,2,1,0:T(8,128)S(1)}, u32[]{:S(2)}, u32[]{:S(2)}) %collective-permute-start.1) | collective-permute-done | bytes 524320 | tf_op jit(solution)/shard_map/ppermute | solution.py:267
  5.1 3.5 %collective-permute-start.2 = (f32[2,4,128,128]{3,2,1,0:T(8,128)S(1)}, f32[2,4,128,128]{3,2,1,0:T(8,128)S(1)}, u32[]{:S(2)}, u32[]{:S(2)}) collective-permute-start(f32[2,4,128,128]{3,2,1,0:T(8,128)S(1)} %collective-permute-done.1.own_swap), channel_id=1, source_target_pairs={{0,4},{4,8},{8,12},{12,14},{13,9},{9,5},{5,1},{1,3},{16,20},{20,24... | collective-permute-start | bytes 1572872 | tf_op jit(solution)/shard_map/ppermute | solution.py:275
  8.7 0.7 %compare_convert_fusion = s32[8,8]{1,0:T(8,128)S(1)} fusion(s32[8,16]{1,0:T(8,128)} %param.3), kind=kLoop, calls=%fused_computation.6 | loop fusion | flops 128 | bytes 512 | tf_op jit(solution)/shard_map/convert_element_type | solution.py:233
  9.3 0.7 %compare_select_fusion = s32[8,8]{1,0:T(8,128)S(1)} fusion(s32[8,8]{1,0:T(8,128)S(1)} %select_reduce_fusion, s32[8,16]{1,0:T(8,128)} %param.3), kind=kLoop, calls=%fused_computation.5 | loop fusion | flops 128 | bytes 768 | tf_op jit(solution)/shard_map/jit(_where)/select_n | solution.py:241
  10.0 0.1 pad_add_fusion.table_ref
  10.1 0.2 collective-permute-done.r1
  10.3 2.1 %collective-permute-start.7 = (f32[2,4,128,128]{3,2,1,0:T(8,128)S(1)}, f32[2,4,128,128]{3,2,1,0:T(8,128)S(1)}, u32[]{:S(2)}, u32[]{:S(2)}) collective-permute-start(f32[2,4,128,128]{3,2,1,0:T(8,128)S(1)} %collective-permute-done.r1), channel_id=1, source_target_pairs={{14,0},{0,4},{4,8},{8,12},{12,14},{3,13},{13,9},{9,5},{5,1},{1,3},... | collective-permute-start | bytes 1572872 | tf_op jit(solution)/shard_map/ppermute | solution.py:267
  12.4 0.0 collective-permute-start.5
  12.4 3.1 %collective-permute-done.2.r2 = f32[2,4,128,128]{3,2,1,0:T(8,128)S(1)} collective-permute-done((f32[2,4,128,128]{3,2,1,0:T(8,128)S(1)}, f32[2,4,128,128]{3,2,1,0:T(8,128)S(1)}, u32[]{:S(2)}, u32[]{:S(2)}) %collective-permute-start.2) | collective-permute-done | bytes 524320 | tf_op jit(solution)/shard_map/ppermute | solution.py:275
  15.6 0.0 collective-permute-start.6
  15.6 2.5 %collective-permute-start.4 = (f32[1,4,128,128]{3,2,1,0:T(8,128)S(1)}, f32[1,4,128,128]{3,2,1,0:T(8,128)S(1)}, u32[]{:S(2)}, u32[]{:S(2)}) collective-permute-start(f32[1,4,128,128]{3,2,1,0:T(8,128)S(1)} %get-tuple-element.33), channel_id=1, source_target_pairs={{14,0},{0,4},{4,8},{8,12},{12,14},{3,13},{13,9},{9,5},{5,1},{1,3},... | collective-permute-start | bytes 786440 | tf_op jit(solution)/shard_map/ppermute | solution.py:267
  18.1 1.6 %collective-permute-start.3 = (f32[1,4,128,128]{3,2,1,0:T(8,128)S(1)}, f32[1,4,128,128]{3,2,1,0:T(8,128)S(1)}, u32[]{:S(2)}, u32[]{:S(2)}) collective-permute-start(f32[1,4,128,128]{3,2,1,0:T(8,128)S(1)} %get-tuple-element.34), channel_id=1, source_target_pairs={{14,0},{0,4},{4,8},{8,12},{12,14},{3,13},{13,9},{9,5},{5,1},{1,3},... | collective-permute-start | bytes 786440 | tf_op jit(solution)/shard_map/ppermute | solution.py:267
  19.7 2.8 %collective-permute-done.7.r3 = f32[2,4,128,128]{3,2,1,0:T(8,128)S(1)} collective-permute-done((f32[2,4,128,128]{3,2,1,0:T(8,128)S(1)}, f32[2,4,128,128]{3,2,1,0:T(8,128)S(1)}, u32[]{:S(2)}, u32[]{:S(2)}) %collective-permute-start.7) | collective-permute-done | bytes 524320 | tf_op jit(solution)/shard_map/ppermute | solution.py:267
  22.5 0.0 collective-permute-start.10
  22.5 0.0 collective-permute-done.5.t1
  22.5 0.0 collective-permute-done.6.t2
  22.5 3.1 %early.1 = (bf16[1024,1024]{1,0:T(8,128)(2,1)S(1)}, bf16[1024,1024]{1,0:T(8,128)(2,1)S(1)}, bf16[512,1024]{1,0:T(8,128)(2,1)S(1)}, f32[256,1024]{1,0:T(8,128)S(1)}) custom-call(s32[8,24]{1,0:T(8,128)S(1)} %pad_add_fusion.table_ref, f32[2,4,128,128]{3,2,1,0:T(8,128)} %own_hbm.1, f32[2,4,128,128]{3,2,1,0:T(8,128)S(1)} %collective-permute-done.1.own_swap, ...), custom_call_target="tpu_custom_call" | custom-call | tf_op jit(solution)/shard_map/early/pallas_call | solution.py:305
  25.7 0.0 collective-permute-done.4.r4a
  25.7 0.6 %collective-permute-start.8 = (f32[1,4,128,128]{3,2,1,0:T(8,128)S(1)}, f32[1,4,128,128]{3,2,1,0:T(8,128)S(1)}, u32[]{:S(2)}, u32[]{:S(2)}) collective-permute-start(f32[1,4,128,128]{3,2,1,0:T(8,128)S(1)} %collective-permute-done.4.r4a), channel_id=1, source_target_pairs={{1,0},{0,1},{17,16},{16,17},{3,2},{2,3},{19,18},{18,19},{5,4},{4,5... | collective-permute-start | bytes 786440 | tf_op jit(solution)/shard_map/ppermute | solution.py:267
  26.3 2.0 %collective-permute-done.3.r4b = f32[1,4,128,128]{3,2,1,0:T(8,128)S(1)} collective-permute-done((f32[1,4,128,128]{3,2,1,0:T(8,128)S(1)}, f32[1,4,128,128]{3,2,1,0:T(8,128)S(1)}, u32[]{:S(2)}, u32[]{:S(2)}) %collective-permute-start.3) | collective-permute-done | bytes 262176 | tf_op jit(solution)/shard_map/ppermute | solution.py:267
  28.2 0.0 collective-permute-done.8.t4a
  28.2 0.0 collective-permute-start.9
  28.3 0.0 collective-permute-done.10.t3
  28.3 1.6 %middle.1 = (bf16[1024,1024]{1,0:T(8,128)(2,1)S(1)}, bf16[1024,1024]{1,0:T(8,128)(2,1)S(1)}, f32[256,1024]{1,0:T(8,128)S(1)}) custom-call(s32[8,24]{1,0:T(8,128)S(1)} %pad_add_fusion.table_ref, f32[1,4,128,128]{3,2,1,0:T(8,128)S(1)} %collective-permute-done.4.r4a, ...), custom_call_target="tpu_custom_call", output_to_operand_aliasing={{0}: (5, {}), {1}: (6, {}), {2}: (8, {})} | custom-call | tf_op jit(solution)/shard_map/middle/pallas_call | solution.py:325
  29.9 3.6 %late.1 = (f32[2,4,128,128]{3,2,1,0:T(8,128)}, bf16[1024,1024]{1,0:T(8,128)(2,1)S(1)}, bf16[1024,1024]{1,0:T(8,128)(2,1)S(1)}, f32[256,1024]{1,0:T(8,128)S(1)}) custom-call(s32[8,24]{1,0:T(8,128)S(1)} %pad_add_fusion.table_ref, f32[1,4,128,128]{3,2,1,0:T(8,128)S(1)} %collective-permute-done.9.t4b, ...), custom_call_target="tpu_custom_call", output_to_operand_aliasing={{1}: (2, {}), {2}: (3, {}), {3}: (5, {})} | custom-call | tf_op jit(solution)/shard_map/late/pallas_call | solution.py:334
  (3 shorter events, 0.0 us)
Async XLA Ops:
  0.0 10.3 %collective-permute-start = (f32[2,4,128,128]{3,2,1,0:T(8,128)}, f32[2,4,128,128]{3,2,1,0:T(8,128)S(1)}, u32[]{:S(2)}, u32[]{:S(2)}) collective-permute-start(f32[2,4,128,128]{3,2,1,0:T(8,128)} %own_hbm.1), channel_id=1, source_target_pairs={{2,0},{0,4},{4,8},{8,12},{12,14},{14,15},{15,13},{13,9},{9,5},{5,1... | collective-permute-start | bytes 1572872 | tf_op jit(solution)/shard_map/ppermute | solution.py:267
  3.0 2.1 %collective-permute-start.1 = (f32[2,4,128,128]{3,2,1,0:T(8,128)}, f32[2,4,128,128]{3,2,1,0:T(8,128)S(1)}, u32[]{:S(2)}, u32[]{:S(2)}) collective-permute-start(f32[2,4,128,128]{3,2,1,0:T(8,128)} %own_hbm.1), channel_id=1, source_target_pairs={{1,0},{0,1},{17,16},{16,17},{3,2},{2,3},{19,18},{18,19},{5,4},{4,5... | collective-permute-start | bytes 1572872 | tf_op jit(solution)/shard_map/ppermute | solution.py:267
  5.1 10.4 %collective-permute-start.2 = (f32[2,4,128,128]{3,2,1,0:T(8,128)S(1)}, f32[2,4,128,128]{3,2,1,0:T(8,128)S(1)}, u32[]{:S(2)}, u32[]{:S(2)}) collective-permute-start(f32[2,4,128,128]{3,2,1,0:T(8,128)S(1)} %collective-permute-done.1.own_swap), channel_id=1, source_target_pairs={{0,4},{4,8},{8,12},{12,14},{13,9},{9,5},{5,1},{1,3},{16,20},{20,24... | collective-permute-start | bytes 1572872 | tf_op jit(solution)/shard_map/ppermute | solution.py:275
  10.3 12.2 %collective-permute-start.7 = (f32[2,4,128,128]{3,2,1,0:T(8,128)S(1)}, f32[2,4,128,128]{3,2,1,0:T(8,128)S(1)}, u32[]{:S(2)}, u32[]{:S(2)}) collective-permute-start(f32[2,4,128,128]{3,2,1,0:T(8,128)S(1)} %collective-permute-done.r1), channel_id=1, source_target_pairs={{14,0},{0,4},{4,8},{8,12},{12,14},{3,13},{13,9},{9,5},{5,1},{1,3},... | collective-permute-start | bytes 1572872 | tf_op jit(solution)/shard_map/ppermute | solution.py:267
  12.4 10.1 %collective-permute-start.5 = (f32[2,4,128,128]{3,2,1,0:T(8,128)S(1)}, f32[2,4,128,128]{3,2,1,0:T(8,128)S(1)}, u32[]{:S(2)}, u32[]{:S(2)}) collective-permute-start(f32[2,4,128,128]{3,2,1,0:T(8,128)S(1)} %collective-permute-done.r1), channel_id=1, source_target_pairs={{1,0},{0,1},{17,16},{16,17},{3,2},{2,3},{19,18},{18,19},{5,4},{4,5... | collective-permute-start | bytes 1572872 | tf_op jit(solution)/shard_map/ppermute | solution.py:267
  15.6 7.0 %collective-permute-start.6 = (f32[2,4,128,128]{3,2,1,0:T(8,128)S(1)}, f32[2,4,128,128]{3,2,1,0:T(8,128)S(1)}, u32[]{:S(2)}, u32[]{:S(2)}) collective-permute-start(f32[2,4,128,128]{3,2,1,0:T(8,128)S(1)} %collective-permute-done.2.r2), channel_id=1, source_target_pairs={{1,0},{0,1},{17,16},{16,17},{3,2},{2,3},{19,18},{18,19},{5,4},{4,5... | collective-permute-start | bytes 1572872 | tf_op jit(solution)/shard_map/ppermute | solution.py:267
  15.6 10.1 %collective-permute-start.4 = (f32[1,4,128,128]{3,2,1,0:T(8,128)S(1)}, f32[1,4,128,128]{3,2,1,0:T(8,128)S(1)}, u32[]{:S(2)}, u32[]{:S(2)}) collective-permute-start(f32[1,4,128,128]{3,2,1,0:T(8,128)S(1)} %get-tuple-element.33), channel_id=1, source_target_pairs={{14,0},{0,4},{4,8},{8,12},{12,14},{3,13},{13,9},{9,5},{5,1},{1,3},... | collective-permute-start | bytes 786440 | tf_op jit(solution)/shard_map/ppermute | solution.py:267
  18.1 10.1 %collective-permute-start.3 = (f32[1,4,128,128]{3,2,1,0:T(8,128)S(1)}, f32[1,4,128,128]{3,2,1,0:T(8,128)S(1)}, u32[]{:S(2)}, u32[]{:S(2)}) collective-permute-start(f32[1,4,128,128]{3,2,1,0:T(8,128)S(1)} %get-tuple-element.34), channel_id=1, source_target_pairs={{14,0},{0,4},{4,8},{8,12},{12,14},{3,13},{13,9},{9,5},{5,1},{1,3},... | collective-permute-start | bytes 786440 | tf_op jit(solution)/shard_map/ppermute | solution.py:267
  22.5 5.7 %collective-permute-start.10 = (f32[2,4,128,128]{3,2,1,0:T(8,128)S(1)}, f32[2,4,128,128]{3,2,1,0:T(8,128)S(1)}, u32[]{:S(2)}, u32[]{:S(2)}) collective-permute-start(f32[2,4,128,128]{3,2,1,0:T(8,128)S(1)} %collective-permute-done.7.r3), channel_id=1, source_target_pairs={{1,0},{0,1},{17,16},{16,17},{3,2},{2,3},{19,18},{18,19},{5,4},{4,5... | collective-permute-start | bytes 1572872 | tf_op jit(solution)/shard_map/ppermute | solution.py:267
  25.7 2.6 %collective-permute-start.8 = (f32[1,4,128,128]{3,2,1,0:T(8,128)S(1)}, f32[1,4,128,128]{3,2,1,0:T(8,128)S(1)}, u32[]{:S(2)}, u32[]{:S(2)}) collective-permute-start(f32[1,4,128,128]{3,2,1,0:T(8,128)S(1)} %collective-permute-done.4.r4a), channel_id=1, source_target_pairs={{1,0},{0,1},{17,16},{16,17},{3,2},{2,3},{19,18},{18,19},{5,4},{4,5... | collective-permute-start | bytes 786440 | tf_op jit(solution)/shard_map/ppermute | solution.py:267
  28.2 1.7 %collective-permute-start.9 = (f32[1,4,128,128]{3,2,1,0:T(8,128)S(1)}, f32[1,4,128,128]{3,2,1,0:T(8,128)S(1)}, u32[]{:S(2)}, u32[]{:S(2)}) collective-permute-start(f32[1,4,128,128]{3,2,1,0:T(8,128)S(1)} %collective-permute-done.3.r4b), channel_id=1, source_target_pairs={{1,0},{0,1},{17,16},{16,17},{3,2},{2,3},{19,18},{18,19},{5,4},{4,5... | collective-permute-start | bytes 786440 | tf_op jit(solution)/shard_map/ppermute | solution.py:267

commit v10 on v9

--- a/solution.py
+++ b/solution.py
@@ -143,7 +143,7 @@
 
 
 def early_kernel(
-    tables, table_ref, own_hbm, own_swap, r1, r2, t1, t2, r3,
+    tables, table_ref, own_hbm, own_swap, r1, r2a, r2b, t1, t2a, t2b, r3,
     high, low, left, part_ref, own_ref, own_sem,
 ):
     place, lane = lax.axis_index("blk"), lax.axis_index("depth")
@@ -154,9 +154,10 @@
     part_ref[...] = jnp.zeros_like(part_ref)
     store_piece(own_swap, place, 1 - lane, table_ref, high, low, left)
     store_piece(r1, here, lane, table_ref, high, low)
-    store_piece(r2, here, 1 - lane, table_ref, high, low)
     store_piece(t1, there, 1 - lane, table_ref, high, low)
-    store_piece(t2, there, lane, table_ref, high, low)
+    for r, (received, swapped) in enumerate(((r2a, t2a), (r2b, t2b))):
+        store_piece(received, here, 1 - lane, table_ref, high, low, first=r)
+        store_piece(swapped, there, lane, table_ref, high, low, first=r)
     store_piece(r3, lookup(far, place, lane), lane, table_ref, high, low)
     own_copy.wait()
     store_piece(own_ref, place, lane, table_ref, high, low, left)
@@ -285,14 +286,14 @@
     tables = (near, far)
 
     table = slot_table(columns, lanes * width)
+    x_late, columns = lax.optimization_barrier((x_blocks, columns))
     r1 = move(x_blocks, first)
-    own_swap = swap(x_blocks)
-    r2 = move_only(own_swap, [up, down])
-    r1, table = lax.optimization_barrier((r1, table))
+    own_swap = swap(x_late)
+    r2a, r2b = [move_only(own_swap[r : r + 1], [up, down]) for r in range(2)]
     r3 = move(r1, second)
     t1 = swap(r1)
-    r4a, r4b = move(r2[:1], second), move(r2[1:], second)
-    t2 = swap(r2)
+    r4a, r4b = move(r2a, second), move(r2b, second)
+    t2a, t2b = swap(r2a), swap(r2b)
 
     order, own = rows * edge, slab * edge
     table = pltpu.with_memory_space_constraint(table, pltpu.SMEM)
@@ -310,12 +311,12 @@
             jax.ShapeDtypeStruct((2 * own, order), jnp.bfloat16),
             jax.ShapeDtypeStruct((own, order), jnp.float32),
         ],
-        in_specs=[smem] + [pl.BlockSpec(memory_space=pltpu.HBM)] + [vmem] * 6,
+        in_specs=[smem] + [pl.BlockSpec(memory_space=pltpu.HBM)] + [vmem] * 8,
         out_specs=[vmem] * 4,
         scratch_shapes=[pltpu.VMEM(x_blocks.shape, jnp.float32), pltpu.SemaphoreType.DMA],
         compiler_params=params,
         name="early",
-    )(table, pltpu.with_memory_space_constraint(x_blocks, pltpu.HBM), own_swap, r1, r2, t1, t2, r3)
+    )(table, pltpu.with_memory_space_constraint(x_blocks, pltpu.HBM), own_swap, r1, r2a, r2b, t1, t2a, t2b, r3)
     t3 = swap(r3)
     r4a, part = lax.optimization_barrier((r4a, part))
     t4a = swap(r4a)

time: 33.8 us -> 35.6 us (1.053)
  starting transfers between devices: 13.3 us -> 15.5 us
  waiting for transfers between devices: 8.85 us -> 8.39 us
    ppermute x1 -> x2, starting transfers between devices: 3.5 us -> 6.98 us  [move_only(): return lax.ppermute(block, AXES, route)]
    ppermute x1 -> x2, waiting for transfers between devices: 3.13 us -> 0.52 us  [move_only(): return lax.ppermute(block, AXES, route)]
    ppermute x10 -> x11, waiting for transfers between devices: 5.72 us -> 7.87 us  [move(): return lax.ppermute(block, AXES, route)]
    ppermute x10 -> x11, starting transfers between devices: 9.82 us -> 8.49 us  [move(): return lax.ppermute(block, AXES, route)]
  transfers between devices with their start and end apart: 11 -> 13, of which waited for: 5 -> 4; matrix products, arithmetic and copies ran while one was open for 9% -> 8% of each run, Pallas kernels for 14% -> 14%
where the time goes in v10:
time: 35.6 us; the launch traced here: 35.2 us
  starting transfers between devices  15.5 us (44%)
  waiting for transfers between devices  8.39 us (24%)
  Pallas kernels  8.38 us (24%)
  other arithmetic  2.86 us (8%)
    ppermute x11, starting transfers between devices, move(): return lax.ppermute(block, AXES, route)  8.49 us
    ppermute x11, waiting for transfers between devices, move(): return lax.ppermute(block, AXES, route)  7.87 us
    ppermute x2, starting transfers between devices, move_only(): return lax.ppermute(block, AXES, route)  6.98 us
    pallas_call x1, Pallas kernels, gather_local(): pl.pallas_call(functools.partial(late_kernel, tables), out_shape=[jax.Sha...  3.61 us
    pallas_call x1, Pallas kernels, gather_local(): pl.pallas_call(functools.partial(early_kernel, tables), out_shape=[jax.Sh...  3.13 us
    pallas_call x1, Pallas kernels, gather_local(): pl.pallas_call(functools.partial(middle_kernel, tables), out_shape=dense,...  1.64 us
    reduce_sum x1, other arithmetic, slot_table(): count = jnp.sum(here.astype(jnp.int32), axis=1, keepdims=True)  0.8 us
  transfers between devices with their start and end apart: 13, of which 4 were waited for; matrix products, arithmetic and copies ran while one was open for 8% of the time, Pallas kernels for 14%

profile of v10, /device:TPU:0, one launch (start us, length us, event | category | flops | bytes accessed | tf_op | source)
XLA Modules:
  0.0 35.2 jit_solution(16877942361648392135)
XLA Ops:
  0.0 3.0 %collective-permute-start.5 = (f32[2,4,128,128]{3,2,1,0:T(8,128)}, f32[2,4,128,128]{3,2,1,0:T(8,128)S(1)}, u32[]{:S(2)}, u32[]{:S(2)}) collective-permute-start(f32[2,4,128,128]{3,2,1,0:T(8,128)} %own_hbm.1), channel_id=1, source_target_pairs={{2,0},{0,4},{4,8},{8,12},{12,14},{14,15},{15,13},{13,9},{9,5},{5,1... | collective-permute-start | bytes 1572872 | tf_op jit(solution)/shard_map/ppermute | solution.py:268
  3.0 0.0 collective-permute-start
  3.0 0.8 %fusion.1 = (s32[8]{0:T(128)S(1)}, s32[8,8]{1,0:T(8,128)S(1)}) fusion(s32[8,16]{1,0:T(8,128)} %param.3), kind=kLoop, calls=%fused_computation.10 | loop fusion | flops 184 | bytes 544 | tf_op jit(solution)/shard_map/reduce_sum | solution.py:234
  3.8 0.1 fusion
  3.9 0.2 convert_reduce_fusion
  4.2 0.1 add_select_fusion
  4.2 0.9 %collective-permute-done.own_swap = f32[2,4,128,128]{3,2,1,0:T(8,128)S(1)} collective-permute-done((f32[2,4,128,128]{3,2,1,0:T(8,128)}, f32[2,4,128,128]{3,2,1,0:T(8,128)S(1)}, u32[]{:S(2)}, u32[]{:S(2)}) %collective-permute-start) | collective-permute-done | bytes 524320 | tf_op jit(solution)/shard_map/ppermute | solution.py:268
  5.2 3.5 %collective-permute-start.3 = (f32[1,4,128,128]{3,2,1,0:T(8,128)S(1)}, f32[1,4,128,128]{3,2,1,0:T(8,128)S(1)}, u32[]{:S(2)}, u32[]{:S(2)}) collective-permute-start(f32[1,4,128,128]{3,2,1,0:T(8,128)S(1)} %get-tuple-element.31), channel_id=1, source_target_pairs={{0,4},{4,8},{8,12},{12,14},{13,9},{9,5},{5,1},{1,3},{16,20},{20,24... | collective-permute-start | bytes 786440 | tf_op jit(solution)/shard_map/ppermute | solution.py:276
  8.7 3.5 %collective-permute-start.1 = (f32[1,4,128,128]{3,2,1,0:T(8,128)S(1)}, f32[1,4,128,128]{3,2,1,0:T(8,128)S(1)}, u32[]{:S(2)}, u32[]{:S(2)}) collective-permute-start(f32[1,4,128,128]{3,2,1,0:T(8,128)S(1)} %get-tuple-element.32), channel_id=1, source_target_pairs={{0,4},{4,8},{8,12},{12,14},{13,9},{9,5},{5,1},{1,3},{16,20},{20,24... | collective-permute-start | bytes 786440 | tf_op jit(solution)/shard_map/ppermute | solution.py:276
  12.2 0.2 select_reduce_fusion
  12.4 0.0 collective-permute-done.5.r1
  12.4 1.5 %collective-permute-start.9 = (f32[2,4,128,128]{3,2,1,0:T(8,128)S(1)}, f32[2,4,128,128]{3,2,1,0:T(8,128)S(1)}, u32[]{:S(2)}, u32[]{:S(2)}) collective-permute-start(f32[2,4,128,128]{3,2,1,0:T(8,128)S(1)} %collective-permute-done.5.r1), channel_id=1, source_target_pairs={{14,0},{0,4},{4,8},{8,12},{12,14},{3,13},{13,9},{9,5},{5,1},{1,3},... | collective-permute-start | bytes 1572872 | tf_op jit(solution)/shard_map/ppermute | solution.py:268
  13.9 0.0 collective-permute-start.6
  13.9 0.7 %compare_select_fusion = s32[8,8]{1,0:T(8,128)S(1)} fusion(s32[8,8]{1,0:T(8,128)S(1)} %select_reduce_fusion, s32[8,16]{1,0:T(8,128)} %param.3), kind=kLoop, calls=%fused_computation.5 | loop fusion | flops 128 | bytes 768 | tf_op jit(solution)/shard_map/jit(_where)/select_n | solution.py:242
  14.6 0.0 collective-permute-done.3.r2a
  14.6 0.5 %collective-permute-start.7 = (f32[1,4,128,128]{3,2,1,0:T(8,128)S(1)}, f32[1,4,128,128]{3,2,1,0:T(8,128)S(1)}, u32[]{:S(2)}, u32[]{:S(2)}) collective-permute-start(f32[1,4,128,128]{3,2,1,0:T(8,128)S(1)} %collective-permute-done.3.r2a), channel_id=1, source_target_pairs={{1,0},{0,1},{17,16},{16,17},{3,2},{2,3},{19,18},{18,19},{5,4},{4,5... | collective-permute-start | bytes 786440 | tf_op jit(solution)/shard_map/ppermute | solution.py:268
  15.1 0.4 %collective-permute-start.4 = (f32[1,4,128,128]{3,2,1,0:T(8,128)S(1)}, f32[1,4,128,128]{3,2,1,0:T(8,128)S(1)}, u32[]{:S(2)}, u32[]{:S(2)}) collective-permute-start(f32[1,4,128,128]{3,2,1,0:T(8,128)S(1)} %collective-permute-done.3.r2a), channel_id=1, source_target_pairs={{14,0},{0,4},{4,8},{8,12},{12,14},{3,13},{13,9},{9,5},{5,1},{1,3},... | collective-permute-start | bytes 786440 | tf_op jit(solution)/shard_map/ppermute | solution.py:268
  15.5 0.5 %collective-permute-done.1.r2b = f32[1,4,128,128]{3,2,1,0:T(8,128)S(1)} collective-permute-done((f32[1,4,128,128]{3,2,1,0:T(8,128)S(1)}, f32[1,4,128,128]{3,2,1,0:T(8,128)S(1)}, u32[]{:S(2)}, u32[]{:S(2)}) %collective-permute-start.1) | collective-permute-done | bytes 262176 | tf_op jit(solution)/shard_map/ppermute | solution.py:276
  16.0 0.0 collective-permute-start.8
  16.0 0.7 %compare_convert_fusion = s32[8,8]{1,0:T(8,128)S(1)} fusion(s32[8,16]{1,0:T(8,128)} %param.3), kind=kLoop, calls=%fused_computation.6 | loop fusion | flops 128 | bytes 512 | tf_op jit(solution)/shard_map/convert_element_type | solution.py:234
  16.7 0.1 pad_add_fusion.table_ref
  16.8 0.0 collective-permute-done.7.t2a
  16.8 2.5 %collective-permute-start.2 = (f32[1,4,128,128]{3,2,1,0:T(8,128)S(1)}, f32[1,4,128,128]{3,2,1,0:T(8,128)S(1)}, u32[]{:S(2)}, u32[]{:S(2)}) collective-permute-start(f32[1,4,128,128]{3,2,1,0:T(8,128)S(1)} %collective-permute-done.1.r2b), channel_id=1, source_target_pairs={{14,0},{0,4},{4,8},{8,12},{12,14},{3,13},{13,9},{9,5},{5,1},{1,3},... | collective-permute-start | bytes 786440 | tf_op jit(solution)/shard_map/ppermute | solution.py:268
  19.3 5.0 %collective-permute-done.9.r3 = f32[2,4,128,128]{3,2,1,0:T(8,128)S(1)} collective-permute-done((f32[2,4,128,128]{3,2,1,0:T(8,128)S(1)}, f32[2,4,128,128]{3,2,1,0:T(8,128)S(1)}, u32[]{:S(2)}, u32[]{:S(2)}) %collective-permute-start.9) | collective-permute-done | bytes 524320 | tf_op jit(solution)/shard_map/ppermute | solution.py:268
  24.3 0.0 collective-permute-start.12
  24.3 0.0 collective-permute-done.8.t2b
  24.3 3.1 %early.1 = (bf16[1024,1024]{1,0:T(8,128)(2,1)S(1)}, bf16[1024,1024]{1,0:T(8,128)(2,1)S(1)}, bf16[512,1024]{1,0:T(8,128)(2,1)S(1)}, f32[256,1024]{1,0:T(8,128)S(1)}) custom-call(s32[8,24]{1,0:T(8,128)S(1)} %pad_add_fusion.table_ref, f32[2,4,128,128]{3,2,1,0:T(8,128)} %own_hbm.1, f32[2,4,128,128]{3,2,1,0:T(8,128)S(1)} %collective-permute-done.own_swap, ...), custom_call_target="tpu_custom_call" | custom-call | tf_op jit(solution)/shard_map/early/pallas_call | solution.py:306
  27.5 0.0 collective-permute-done.4.r4a
  27.5 0.6 %collective-permute-start.10 = (f32[1,4,128,128]{3,2,1,0:T(8,128)S(1)}, f32[1,4,128,128]{3,2,1,0:T(8,128)S(1)}, u32[]{:S(2)}, u32[]{:S(2)}) collective-permute-start(f32[1,4,128,128]{3,2,1,0:T(8,128)S(1)} %collective-permute-done.4.r4a), channel_id=1, source_target_pairs={{1,0},{0,1},{17,16},{16,17},{3,2},{2,3},{19,18},{18,19},{5,4},{4,5... | collective-permute-start | bytes 786440 | tf_op jit(solution)/shard_map/ppermute | solution.py:268
  28.1 1.9 %collective-permute-done.2.r4b = f32[1,4,128,128]{3,2,1,0:T(8,128)S(1)} collective-permute-done((f32[1,4,128,128]{3,2,1,0:T(8,128)S(1)}, f32[1,4,128,128]{3,2,1,0:T(8,128)S(1)}, u32[]{:S(2)}, u32[]{:S(2)}) %collective-permute-start.2) | collective-permute-done | bytes 262176 | tf_op jit(solution)/shard_map/ppermute | solution.py:268
  30.0 1.6 %middle.1 = (bf16[1024,1024]{1,0:T(8,128)(2,1)S(1)}, bf16[1024,1024]{1,0:T(8,128)(2,1)S(1)}, f32[256,1024]{1,0:T(8,128)S(1)}) custom-call(s32[8,24]{1,0:T(8,128)S(1)} %pad_add_fusion.table_ref, f32[1,4,128,128]{3,2,1,0:T(8,128)S(1)} %collective-permute-done.4.r4a, ...), custom_call_target="tpu_custom_call", output_to_operand_aliasing={{0}: (5, {}), {1}: (6, {}), {2}: (8, {})} | custom-call | tf_op jit(solution)/shard_map/middle/pallas_call | solution.py:326
  31.6 3.6 %late.1 = (f32[2,4,128,128]{3,2,1,0:T(8,128)}, bf16[1024,1024]{1,0:T(8,128)(2,1)S(1)}, bf16[1024,1024]{1,0:T(8,128)(2,1)S(1)}, f32[256,1024]{1,0:T(8,128)S(1)}) custom-call(s32[8,24]{1,0:T(8,128)S(1)} %pad_add_fusion.table_ref, f32[1,4,128,128]{3,2,1,0:T(8,128)S(1)} %collective-permute-done.11.t4b, ...), custom_call_target="tpu_custom_call", output_to_operand_aliasing={{1}: (2, {}), {2}: (3, {}), {3}: (5, {})} | custom-call | tf_op jit(solution)/shard_map/late/pallas_call | solution.py:335
  (7 shorter events, 0.1 us)
Async XLA Ops:
  0.0 12.4 %collective-permute-start.5 = (f32[2,4,128,128]{3,2,1,0:T(8,128)}, f32[2,4,128,128]{3,2,1,0:T(8,128)S(1)}, u32[]{:S(2)}, u32[]{:S(2)}) collective-permute-start(f32[2,4,128,128]{3,2,1,0:T(8,128)} %own_hbm.1), channel_id=1, source_target_pairs={{2,0},{0,4},{4,8},{8,12},{12,14},{14,15},{15,13},{13,9},{9,5},{5,1... | collective-permute-start | bytes 1572872 | tf_op jit(solution)/shard_map/ppermute | solution.py:268
  3.0 2.1 %collective-permute-start = (f32[2,4,128,128]{3,2,1,0:T(8,128)}, f32[2,4,128,128]{3,2,1,0:T(8,128)S(1)}, u32[]{:S(2)}, u32[]{:S(2)}) collective-permute-start(f32[2,4,128,128]{3,2,1,0:T(8,128)} %own_hbm.1), channel_id=1, source_target_pairs={{1,0},{0,1},{17,16},{16,17},{3,2},{2,3},{19,18},{18,19},{5,4},{4,5... | collective-permute-start | bytes 1572872 | tf_op jit(solution)/shard_map/ppermute | solution.py:268
  5.2 9.4 %collective-permute-start.3 = (f32[1,4,128,128]{3,2,1,0:T(8,128)S(1)}, f32[1,4,128,128]{3,2,1,0:T(8,128)S(1)}, u32[]{:S(2)}, u32[]{:S(2)}) collective-permute-start(f32[1,4,128,128]{3,2,1,0:T(8,128)S(1)} %get-tuple-element.31), channel_id=1, source_target_pairs={{0,4},{4,8},{8,12},{12,14},{13,9},{9,5},{5,1},{1,3},{16,20},{20,24... | collective-permute-start | bytes 786440 | tf_op jit(solution)/shard_map/ppermute | solution.py:276
  8.7 7.3 %collective-permute-start.1 = (f32[1,4,128,128]{3,2,1,0:T(8,128)S(1)}, f32[1,4,128,128]{3,2,1,0:T(8,128)S(1)}, u32[]{:S(2)}, u32[]{:S(2)}) collective-permute-start(f32[1,4,128,128]{3,2,1,0:T(8,128)S(1)} %get-tuple-element.32), channel_id=1, source_target_pairs={{0,4},{4,8},{8,12},{12,14},{13,9},{9,5},{5,1},{1,3},{16,20},{20,24... | collective-permute-start | bytes 786440 | tf_op jit(solution)/shard_map/ppermute | solution.py:276
  12.4 11.9 %collective-permute-start.9 = (f32[2,4,128,128]{3,2,1,0:T(8,128)S(1)}, f32[2,4,128,128]{3,2,1,0:T(8,128)S(1)}, u32[]{:S(2)}, u32[]{:S(2)}) collective-permute-start(f32[2,4,128,128]{3,2,1,0:T(8,128)S(1)} %collective-permute-done.5.r1), channel_id=1, source_target_pairs={{14,0},{0,4},{4,8},{8,12},{12,14},{3,13},{13,9},{9,5},{5,1},{1,3},... | collective-permute-start | bytes 1572872 | tf_op jit(solution)/shard_map/ppermute | solution.py:268
  13.9 10.4 %collective-permute-start.6 = (f32[2,4,128,128]{3,2,1,0:T(8,128)S(1)}, f32[2,4,128,128]{3,2,1,0:T(8,128)S(1)}, u32[]{:S(2)}, u32[]{:S(2)}) collective-permute-start(f32[2,4,128,128]{3,2,1,0:T(8,128)S(1)} %collective-permute-done.5.r1), channel_id=1, source_target_pairs={{1,0},{0,1},{17,16},{16,17},{3,2},{2,3},{19,18},{18,19},{5,4},{4,5... | collective-permute-start | bytes 1572872 | tf_op jit(solution)/shard_map/ppermute | solution.py:268
  14.6 2.2 %collective-permute-start.7 = (f32[1,4,128,128]{3,2,1,0:T(8,128)S(1)}, f32[1,4,128,128]{3,2,1,0:T(8,128)S(1)}, u32[]{:S(2)}, u32[]{:S(2)}) collective-permute-start(f32[1,4,128,128]{3,2,1,0:T(8,128)S(1)} %collective-permute-done.3.r2a), channel_id=1, source_target_pairs={{1,0},{0,1},{17,16},{16,17},{3,2},{2,3},{19,18},{18,19},{5,4},{4,5... | collective-permute-start | bytes 786440 | tf_op jit(solution)/shard_map/ppermute | solution.py:268
  15.1 12.3 %collective-permute-start.4 = (f32[1,4,128,128]{3,2,1,0:T(8,128)S(1)}, f32[1,4,128,128]{3,2,1,0:T(8,128)S(1)}, u32[]{:S(2)}, u32[]{:S(2)}) collective-permute-start(f32[1,4,128,128]{3,2,1,0:T(8,128)S(1)} %collective-permute-done.3.r2a), channel_id=1, source_target_pairs={{14,0},{0,4},{4,8},{8,12},{12,14},{3,13},{13,9},{9,5},{5,1},{1,3},... | collective-permute-start | bytes 786440 | tf_op jit(solution)/shard_map/ppermute | solution.py:268
  16.0 8.3 %collective-permute-start.8 = (f32[1,4,128,128]{3,2,1,0:T(8,128)S(1)}, f32[1,4,128,128]{3,2,1,0:T(8,128)S(1)}, u32[]{:S(2)}, u32[]{:S(2)}) collective-permute-start(f32[1,4,128,128]{3,2,1,0:T(8,128)S(1)} %collective-permute-done.1.r2b), channel_id=1, source_target_pairs={{1,0},{0,1},{17,16},{16,17},{3,2},{2,3},{19,18},{18,19},{5,4},{4,5... | collective-permute-start | bytes 786440 | tf_op jit(solution)/shard_map/ppermute | solution.py:268
  16.8 13.1 %collective-permute-start.2 = (f32[1,4,128,128]{3,2,1,0:T(8,128)S(1)}, f32[1,4,128,128]{3,2,1,0:T(8,128)S(1)}, u32[]{:S(2)}, u32[]{:S(2)}) collective-permute-start(f32[1,4,128,128]{3,2,1,0:T(8,128)S(1)} %collective-permute-done.1.r2b), channel_id=1, source_target_pairs={{14,0},{0,4},{4,8},{8,12},{12,14},{3,13},{13,9},{9,5},{5,1},{1,3},... | collective-permute-start | bytes 786440 | tf_op jit(solution)/shard_map/ppermute | solution.py:268
  24.3 5.6 %collective-permute-start.12 = (f32[2,4,128,128]{3,2,1,0:T(8,128)S(1)}, f32[2,4,128,128]{3,2,1,0:T(8,128)S(1)}, u32[]{:S(2)}, u32[]{:S(2)}) collective-permute-start(f32[2,4,128,128]{3,2,1,0:T(8,128)S(1)} %collective-permute-done.9.r3), channel_id=1, source_target_pairs={{1,0},{0,1},{17,16},{16,17},{3,2},{2,3},{19,18},{18,19},{5,4},{4,5... | collective-permute-start | bytes 1572872 | tf_op jit(solution)/shard_map/ppermute | solution.py:268
  27.5 2.5 %collective-permute-start.10 = (f32[1,4,128,128]{3,2,1,0:T(8,128)S(1)}, f32[1,4,128,128]{3,2,1,0:T(8,128)S(1)}, u32[]{:S(2)}, u32[]{:S(2)}) collective-permute-start(f32[1,4,128,128]{3,2,1,0:T(8,128)S(1)} %collective-permute-done.4.r4a), channel_id=1, source_target_pairs={{1,0},{0,1},{17,16},{16,17},{3,2},{2,3},{19,18},{18,19},{5,4},{4,5... | collective-permute-start | bytes 786440 | tf_op jit(solution)/shard_map/ppermute | solution.py:268
  30.0 1.7 %collective-permute-start.11 = (f32[1,4,128,128]{3,2,1,0:T(8,128)S(1)}, f32[1,4,128,128]{3,2,1,0:T(8,128)S(1)}, u32[]{:S(2)}, u32[]{:S(2)}) collective-permute-start(f32[1,4,128,128]{3,2,1,0:T(8,128)S(1)} %collective-permute-done.2.r4b), channel_id=1, source_target_pairs={{1,0},{0,1},{17,16},{16,17},{3,2},{2,3},{19,18},{18,19},{5,4},{4,5... | collective-permute-start | bytes 786440 | tf_op jit(solution)/shard_map/ppermute | solution.py:268

commit v11 on v9

--- a/solution.py
+++ b/solution.py
@@ -131,15 +131,27 @@
                     own[pl.ds((slab + r) * edge, edge), col] = block_low
 
 
+def add_rows(first, depth, left, high, low, part_ref):
+    rows, tile = pl.ds(pl.multiple_of(first, depth), depth), 256
+    for n in range(part_ref.shape[1] // tile):
+        cols = pl.ds(n * tile, tile)
+        part_ref[:, cols] += stacked_dot(left[:, rows], high[rows, cols], low[rows, cols])
+
+
 def add_plane(plane, left, high, low, part_ref):
-    depth, tile = part_ref.shape[0], 256
+    depth = part_ref.shape[0]
 
     @pl.when(plane >= 0)
     def _():
-        rows = pl.ds(pl.multiple_of(plane * depth, depth), depth)
-        for n in range(part_ref.shape[1] // tile):
-            cols = pl.ds(n * tile, tile)
-            part_ref[:, cols] += stacked_dot(left[:, rows], high[rows, cols], low[rows, cols])
+        add_rows(plane * depth, depth, left, high, low, part_ref)
+
+
+def add_row(plane, r, left, high, low, part_ref):
+    depth = part_ref.shape[0] // 2
+
+    @pl.when(plane >= 0)
+    def _():
+        add_rows((plane * 2 + r) * depth, depth, left, high, low, part_ref)
 
 
 def early_kernel(
@@ -164,17 +176,26 @@
         add_plane(plane, left, high, low, part_ref)
 
 
+def waiting_kernel(
+    tables, table_ref, r4a, high_in, low_in, left, part_in, high, low, part_ref
+):
+    place, lane = lax.axis_index("blk"), lax.axis_index("depth")
+    here = lookup(tables[1], place, lane)
+    store_piece(r4a, here, 1 - lane, table_ref, high, low)
+    add_row(here, 0, left, high, low, part_ref)
+
+
 def middle_kernel(
-    tables, table_ref, r4a, r4b, t3, t4a, high_in, low_in, left, part_in, high, low, part_ref
+    tables, table_ref, r4b, t3, t4a, high_in, low_in, left, part_in, high, low, part_ref
 ):
     place, lane = lax.axis_index("blk"), lax.axis_index("depth")
     far = tables[1]
     here, there = lookup(far, place, lane), lookup(far, place, 1 - lane)
     store_piece(t3, there, 1 - lane, table_ref, high, low)
-    store_piece(r4a, here, 1 - lane, table_ref, high, low)
     store_piece(t4a, there, lane, table_ref, high, low)
     store_piece(r4b, here, 1 - lane, table_ref, high, low, first=1)
-    add_plane(here, left, high, low, part_ref)
+    add_row(there, 0, left, high, low, part_ref)
+    add_row(here, 1, left, high, low, part_ref)
 
 
 def late_kernel(
@@ -183,19 +204,25 @@
 ):
     place, lane = lax.axis_index("blk"), lax.axis_index("depth")
     group = lax.axis_index("panel") * 2 + lane
+    slab, width, edge, _ = out_ref.shape
+    act, tile = 2 * width, 256
     there = lookup(tables[1], place, 1 - lane)
     store_piece(t4b, there, lane, table_ref, high, low, first=1)
-    add_plane(there, left, high, low, square)
-    slab, width, edge, _ = out_ref.shape
-    act = 2 * width
-    for r in range(slab):
-        for c in range(square.shape[1] // edge):
-            kept = table_ref[place * slab + r, 2 * act + c] > 0
-            col = pl.ds(c * edge, edge)
-            block = jnp.where(kept, square[pl.ds(r * edge, edge), col], 0.0)
-            block_high, block_low = split(block)
-            square_parts[pl.ds(2 * r * edge, edge), col] = block_high
-            square_parts[pl.ds((2 * r + 1) * edge, edge), col] = block_low
+    rows = pl.ds(pl.multiple_of((jnp.maximum(there, 0) * 2 + 1) * edge, edge), edge)
+    for n in range(square.shape[1] // tile):
+        cols = pl.ds(n * tile, tile)
+        more = stacked_dot(left[:, rows], high[rows, cols], low[rows, cols])
+        total = square[:, cols] + jnp.where(there >= 0, more, 0.0)
+        square[:, cols] = total
+        for r in range(slab):
+            for k in range(tile // edge):
+                c = n * (tile // edge) + k
+                kept = table_ref[place * slab + r, 2 * act + c] > 0
+                block = total[r * edge : (r + 1) * edge, k * edge : (k + 1) * edge]
+                block_high, block_low = split(jnp.where(kept, block, 0.0))
+                col = pl.ds(c * edge, edge)
+                square_parts[pl.ds(2 * r * edge, edge), col] = block_high
+                square_parts[pl.ds((2 * r + 1) * edge, edge), col] = block_low
     copies = []
     for r in range(slab):
         row = place * slab + r
@@ -319,18 +346,24 @@
     t3 = swap(r3)
     r4a, part = lax.optimization_barrier((r4a, part))
     t4a = swap(r4a)
-    r4b, t4a = lax.optimization_barrier((r4b, t4a))
+    dense = [jax.ShapeDtypeStruct(a.shape, a.dtype) for a in (high, low, part)]
+
+    def add_to_square(kernel, name, *pieces):
+        first = 1 + len(pieces)
+        return pl.pallas_call(
+            functools.partial(kernel, tables),
+            out_shape=dense,
+            in_specs=[smem] + [vmem] * (4 + len(pieces)),
+            out_specs=[vmem] * 3,
+            input_output_aliases={first: 0, first + 1: 1, first + 3: 2},
+            compiler_params=params,
+            name=name,
+        )(table, *pieces, *held(high, low, left, part))
+
+    high, low, part = add_to_square(waiting_kernel, "waiting", r4a)
+    r4b, t4a, part = lax.optimization_barrier((r4b, t4a, part))
     t4b = swap(r4b)
-    dense = [jax.ShapeDtypeStruct(a.shape, a.dtype) for a in (high, low, part)]
-    high, low, part = pl.pallas_call(
-        functools.partial(middle_kernel, tables),
-        out_shape=dense,
-        in_specs=[smem] + [vmem] * 8,
-        out_specs=[vmem] * 3,
-        input_output_aliases={5: 0, 6: 1, 8: 2},
-        compiler_params=params,
-        name="middle",
-    )(table, r4a, r4b, t3, t4a, *held(high, low, left, part))
+    high, low, part = add_to_square(middle_kernel, "middle", r4b, t3, t4a)
     out, _, _, _ = pl.pallas_call(
         functools.partial(late_kernel, tables),
         out_shape=[jax.ShapeDtypeStruct(x_blocks.shape, jnp.float32)] + dense,

time: 33.8 us -> 34.3 us (1.015)
  Pallas kernels: 8.36 us -> 10 us
  waiting for transfers between devices: 8.85 us -> 7.6 us
    pallas_call x1 -> x2, Pallas kernels: 1.64 us -> 3.37 us  [add_to_square(): pl.pallas_call(functools.partial(kernel, tables), out_shape=dense, in_spe...]
    ppermute x10, waiting for transfers between devices: 5.72 us -> 4.47 us  [move(): return lax.ppermute(block, AXES, route)]
  transfers between devices with their start and end apart: 11 -> 11, of which waited for: 5 -> 5; matrix products, arithmetic and copies ran while one was open for 9% -> 9% of each run, Pallas kernels for 14% -> 19%
where the time goes in v11:
time: 34.3 us; the launch traced here: 34 us
  starting transfers between devices  13.3 us (39%)
  Pallas kernels  10 us (29%)
  waiting for transfers between devices  7.6 us (22%)
  other arithmetic  2.86 us (8%)
    ppermute x10, starting transfers between devices, move(): return lax.ppermute(block, AXES, route)  9.82 us
    ppermute x10, waiting for transfers between devices, move(): return lax.ppermute(block, AXES, route)  4.47 us
    pallas_call x1, Pallas kernels, gather_local(): pl.pallas_call(functools.partial(late_kernel, tables), out_shape=[jax.Sha...  3.54 us
    ppermute x1, starting transfers between devices, move_only(): return lax.ppermute(block, AXES, route)  3.5 us
    pallas_call x2, Pallas kernels, add_to_square(): pl.pallas_call(functools.partial(kernel, tables), out_shape=dense, in_spe...  3.37 us
    ppermute x1, waiting for transfers between devices, move_only(): return lax.ppermute(block, AXES, route)  3.13 us
    pallas_call x1, Pallas kernels, gather_local(): pl.pallas_call(functools.partial(early_kernel, tables), out_shape=[jax.Sh...  3.13 us
    reduce_sum x1, other arithmetic, slot_table(): count = jnp.sum(here.astype(jnp.int32), axis=1, keepdims=True)  0.8 us
  transfers between devices with their start and end apart: 11, of which 5 were waited for; matrix products, arithmetic and copies ran while one was open for 9% of the time, Pallas kernels for 19%

profile of v11, /device:TPU:0, one launch (start us, length us, event | category | flops | bytes accessed | tf_op | source)
XLA Modules:
  0.0 34.0 jit_solution(12760712907935505157)
XLA Ops:
  0.0 3.0 %collective-permute-start = (f32[2,4,128,128]{3,2,1,0:T(8,128)}, f32[2,4,128,128]{3,2,1,0:T(8,128)S(1)}, u32[]{:S(2)}, u32[]{:S(2)}) collective-permute-start(f32[2,4,128,128]{3,2,1,0:T(8,128)} %own_hbm.1), channel_id=1, source_target_pairs={{2,0},{0,4},{4,8},{8,12},{12,14},{14,15},{15,13},{13,9},{9,5},{5,1... | collective-permute-start | bytes 1572872 | tf_op jit(solution)/shard_map/ppermute | solution.py:294
  3.0 0.0 collective-permute-start.1
  3.0 0.8 %fusion.1 = (s32[8]{0:T(128)S(1)}, s32[8,8]{1,0:T(8,128)S(1)}) fusion(s32[8,16]{1,0:T(8,128)} %param.3), kind=kLoop, calls=%fused_computation.10 | loop fusion | flops 184 | bytes 544 | tf_op jit(solution)/shard_map/reduce_sum | solution.py:260
  3.8 0.1 fusion
  3.9 0.2 convert_reduce_fusion
  4.2 0.1 add_select_fusion
  4.2 0.2 select_reduce_fusion
  4.4 0.7 %collective-permute-done.1.own_swap = f32[2,4,128,128]{3,2,1,0:T(8,128)S(1)} collective-permute-done((f32[2,4,128,128]{3,2,1,0:T(8,128)}, f32[2,4,128,128]{3,2,1,0:T(8,128)S(1)}, u32[]{:S(2)}, u32[]{:S(2)}) %collective-permute-start.1) | collective-permute-done | bytes 524320 | tf_op jit(solution)/shard_map/ppermute | solution.py:294
  5.1 3.5 %collective-permute-start.2 = (f32[2,4,128,128]{3,2,1,0:T(8,128)S(1)}, f32[2,4,128,128]{3,2,1,0:T(8,128)S(1)}, u32[]{:S(2)}, u32[]{:S(2)}) collective-permute-start(f32[2,4,128,128]{3,2,1,0:T(8,128)S(1)} %collective-permute-done.1.own_swap), channel_id=1, source_target_pairs={{0,4},{4,8},{8,12},{12,14},{13,9},{9,5},{5,1},{1,3},{16,20},{20,24... | collective-permute-start | bytes 1572872 | tf_op jit(solution)/shard_map/ppermute | solution.py:302
  8.7 0.7 %compare_convert_fusion = s32[8,8]{1,0:T(8,128)S(1)} fusion(s32[8,16]{1,0:T(8,128)} %param.3), kind=kLoop, calls=%fused_computation.6 | loop fusion | flops 128 | bytes 512 | tf_op jit(solution)/shard_map/convert_element_type | solution.py:260
  9.3 0.7 %compare_select_fusion = s32[8,8]{1,0:T(8,128)S(1)} fusion(s32[8,8]{1,0:T(8,128)S(1)} %select_reduce_fusion, s32[8,16]{1,0:T(8,128)} %param.3), kind=kLoop, calls=%fused_computation.5 | loop fusion | flops 128 | bytes 768 | tf_op jit(solution)/shard_map/jit(_where)/select_n | solution.py:268
  10.0 0.1 pad_add_fusion.table_ref
  10.1 0.2 collective-permute-done.r1
  10.3 2.1 %collective-permute-start.7 = (f32[2,4,128,128]{3,2,1,0:T(8,128)S(1)}, f32[2,4,128,128]{3,2,1,0:T(8,128)S(1)}, u32[]{:S(2)}, u32[]{:S(2)}) collective-permute-start(f32[2,4,128,128]{3,2,1,0:T(8,128)S(1)} %collective-permute-done.r1), channel_id=1, source_target_pairs={{14,0},{0,4},{4,8},{8,12},{12,14},{3,13},{13,9},{9,5},{5,1},{1,3},... | collective-permute-start | bytes 1572872 | tf_op jit(solution)/shard_map/ppermute | solution.py:294
  12.4 3.1 %collective-permute-done.2.r2 = f32[2,4,128,128]{3,2,1,0:T(8,128)S(1)} collective-permute-done((f32[2,4,128,128]{3,2,1,0:T(8,128)S(1)}, f32[2,4,128,128]{3,2,1,0:T(8,128)S(1)}, u32[]{:S(2)}, u32[]{:S(2)}) %collective-permute-start.2) | collective-permute-done | bytes 524320 | tf_op jit(solution)/shard_map/ppermute | solution.py:302
  15.6 0.0 collective-permute-start.6
  15.6 2.5 %collective-permute-start.4 = (f32[1,4,128,128]{3,2,1,0:T(8,128)S(1)}, f32[1,4,128,128]{3,2,1,0:T(8,128)S(1)}, u32[]{:S(2)}, u32[]{:S(2)}) collective-permute-start(f32[1,4,128,128]{3,2,1,0:T(8,128)S(1)} %get-tuple-element.41), channel_id=1, source_target_pairs={{14,0},{0,4},{4,8},{8,12},{12,14},{3,13},{13,9},{9,5},{5,1},{1,3},... | collective-permute-start | bytes 786440 | tf_op jit(solution)/shard_map/ppermute | solution.py:294
  18.1 1.6 %collective-permute-start.3 = (f32[1,4,128,128]{3,2,1,0:T(8,128)S(1)}, f32[1,4,128,128]{3,2,1,0:T(8,128)S(1)}, u32[]{:S(2)}, u32[]{:S(2)}) collective-permute-start(f32[1,4,128,128]{3,2,1,0:T(8,128)S(1)} %get-tuple-element.42), channel_id=1, source_target_pairs={{14,0},{0,4},{4,8},{8,12},{12,14},{3,13},{13,9},{9,5},{5,1},{1,3},... | collective-permute-start | bytes 786440 | tf_op jit(solution)/shard_map/ppermute | solution.py:294
  19.7 2.8 %collective-permute-done.7.r3 = f32[2,4,128,128]{3,2,1,0:T(8,128)S(1)} collective-permute-done((f32[2,4,128,128]{3,2,1,0:T(8,128)S(1)}, f32[2,4,128,128]{3,2,1,0:T(8,128)S(1)}, u32[]{:S(2)}, u32[]{:S(2)}) %collective-permute-start.7) | collective-permute-done | bytes 524320 | tf_op jit(solution)/shard_map/ppermute | solution.py:294
  22.5 0.0 collective-permute-start.10
  22.5 0.0 collective-permute-done.5.t1
  22.5 0.0 collective-permute-done.6.t2
  22.5 3.1 %early.1 = (bf16[1024,1024]{1,0:T(8,128)(2,1)S(1)}, bf16[1024,1024]{1,0:T(8,128)(2,1)S(1)}, bf16[512,1024]{1,0:T(8,128)(2,1)S(1)}, f32[256,1024]{1,0:T(8,128)S(1)}) custom-call(s32[8,24]{1,0:T(8,128)S(1)} %pad_add_fusion.table_ref, f32[2,4,128,128]{3,2,1,0:T(8,128)} %own_hbm.1, f32[2,4,128,128]{3,2,1,0:T(8,128)S(1)} %collective-permute-done.1.own_swap, ...), custom_call_target="tpu_custom_call" | custom-call | tf_op jit(solution)/shard_map/early/pallas_call | solution.py:332
  25.7 0.6 %collective-permute-start.8 = (f32[1,4,128,128]{3,2,1,0:T(8,128)S(1)}, f32[1,4,128,128]{3,2,1,0:T(8,128)S(1)}, u32[]{:S(2)}, u32[]{:S(2)}) collective-permute-start(f32[1,4,128,128]{3,2,1,0:T(8,128)S(1)} %collective-permute-done.4.r4a), channel_id=1, source_target_pairs={{1,0},{0,1},{17,16},{16,17},{3,2},{2,3},{19,18},{18,19},{5,4},{4,5... | collective-permute-start | bytes 786440 | tf_op jit(solution)/shard_map/ppermute | solution.py:294
  26.3 1.2 %waiting.1 = (bf16[1024,1024]{1,0:T(8,128)(2,1)S(1)}, bf16[1024,1024]{1,0:T(8,128)(2,1)S(1)}, f32[256,1024]{1,0:T(8,128)S(1)}) custom-call(s32[8,24]{1,0:T(8,128)S(1)} %pad_add_fusion.table_ref, f32[1,4,128,128]{3,2,1,0:T(8,128)S(1)} %collective-permute-done.4.r4a, ...), custom_call_target="tpu_custom_call", output_to_operand_aliasing={{0}: (2, {}), {1}: (3, {}), {2}: (5, {})} | custom-call | tf_op jit(solution)/shard_map/waiting/pallas_call | solution.py:353
  27.5 0.7 %collective-permute-done.3.r4b = f32[1,4,128,128]{3,2,1,0:T(8,128)S(1)} collective-permute-done((f32[1,4,128,128]{3,2,1,0:T(8,128)S(1)}, f32[1,4,128,128]{3,2,1,0:T(8,128)S(1)}, u32[]{:S(2)}, u32[]{:S(2)}) %collective-permute-start.3) | collective-permute-done | bytes 262176 | tf_op jit(solution)/shard_map/ppermute | solution.py:294
  28.2 0.0 collective-permute-done.8.t4a
  28.2 0.0 collective-permute-start.9
  28.3 0.0 collective-permute-done.10.t3
  28.3 2.1 %middle.1 = (bf16[1024,1024]{1,0:T(8,128)(2,1)S(1)}, bf16[1024,1024]{1,0:T(8,128)(2,1)S(1)}, f32[256,1024]{1,0:T(8,128)S(1)}) custom-call(s32[8,24]{1,0:T(8,128)S(1)} %pad_add_fusion.table_ref, f32[1,4,128,128]{3,2,1,0:T(8,128)S(1)} %collective-permute-done.3.r4b, ...), custom_call_target="tpu_custom_call", output_to_operand_aliasing={{0}: (4, {}), {1}: (5, {}), {2}: (7, {})} | custom-call | tf_op jit(solution)/shard_map/middle/pallas_call | solution.py:353
  30.4 0.0 collective-permute-done.9.t4b
  30.4 3.5 %late.1 = (f32[2,4,128,128]{3,2,1,0:T(8,128)}, bf16[1024,1024]{1,0:T(8,128)(2,1)S(1)}, bf16[1024,1024]{1,0:T(8,128)(2,1)S(1)}, f32[256,1024]{1,0:T(8,128)S(1)}) custom-call(s32[8,24]{1,0:T(8,128)S(1)} %pad_add_fusion.table_ref, f32[1,4,128,128]{3,2,1,0:T(8,128)S(1)} %collective-permute-done.9.t4b, ...), custom_call_target="tpu_custom_call", output_to_operand_aliasing={{1}: (2, {}), {2}: (3, {}), {3}: (5, {})} | custom-call | tf_op jit(solution)/shard_map/late/pallas_call | solution.py:367
  (4 shorter events, 0.0 us)
Async XLA Ops:
  0.0 10.3 %collective-permute-start = (f32[2,4,128,128]{3,2,1,0:T(8,128)}, f32[2,4,128,128]{3,2,1,0:T(8,128)S(1)}, u32[]{:S(2)}, u32[]{:S(2)}) collective-permute-start(f32[2,4,128,128]{3,2,1,0:T(8,128)} %own_hbm.1), channel_id=1, source_target_pairs={{2,0},{0,4},{4,8},{8,12},{12,14},{14,15},{15,13},{13,9},{9,5},{5,1... | collective-permute-start | bytes 1572872 | tf_op jit(solution)/shard_map/ppermute | solution.py:294
  3.0 2.1 %collective-permute-start.1 = (f32[2,4,128,128]{3,2,1,0:T(8,128)}, f32[2,4,128,128]{3,2,1,0:T(8,128)S(1)}, u32[]{:S(2)}, u32[]{:S(2)}) collective-permute-start(f32[2,4,128,128]{3,2,1,0:T(8,128)} %own_hbm.1), channel_id=1, source_target_pairs={{1,0},{0,1},{17,16},{16,17},{3,2},{2,3},{19,18},{18,19},{5,4},{4,5... | collective-permute-start | bytes 1572872 | tf_op jit(solution)/shard_map/ppermute | solution.py:294
  5.1 10.4 %collective-permute-start.2 = (f32[2,4,128,128]{3,2,1,0:T(8,128)S(1)}, f32[2,4,128,128]{3,2,1,0:T(8,128)S(1)}, u32[]{:S(2)}, u32[]{:S(2)}) collective-permute-start(f32[2,4,128,128]{3,2,1,0:T(8,128)S(1)} %collective-permute-done.1.own_swap), channel_id=1, source_target_pairs={{0,4},{4,8},{8,12},{12,14},{13,9},{9,5},{5,1},{1,3},{16,20},{20,24... | collective-permute-start | bytes 1572872 | tf_op jit(solution)/shard_map/ppermute | solution.py:302
  10.3 12.2 %collective-permute-start.7 = (f32[2,4,128,128]{3,2,1,0:T(8,128)S(1)}, f32[2,4,128,128]{3,2,1,0:T(8,128)S(1)}, u32[]{:S(2)}, u32[]{:S(2)}) collective-permute-start(f32[2,4,128,128]{3,2,1,0:T(8,128)S(1)} %collective-permute-done.r1), channel_id=1, source_target_pairs={{14,0},{0,4},{4,8},{8,12},{12,14},{3,13},{13,9},{9,5},{5,1},{1,3},... | collective-permute-start | bytes 1572872 | tf_op jit(solution)/shard_map/ppermute | solution.py:294
  12.4 10.1 %collective-permute-start.5 = (f32[2,4,128,128]{3,2,1,0:T(8,128)S(1)}, f32[2,4,128,128]{3,2,1,0:T(8,128)S(1)}, u32[]{:S(2)}, u32[]{:S(2)}) collective-permute-start(f32[2,4,128,128]{3,2,1,0:T(8,128)S(1)} %collective-permute-done.r1), channel_id=1, source_target_pairs={{1,0},{0,1},{17,16},{16,17},{3,2},{2,3},{19,18},{18,19},{5,4},{4,5... | collective-permute-start | bytes 1572872 | tf_op jit(solution)/shard_map/ppermute | solution.py:294
  15.6 7.0 %collective-permute-start.6 = (f32[2,4,128,128]{3,2,1,0:T(8,128)S(1)}, f32[2,4,128,128]{3,2,1,0:T(8,128)S(1)}, u32[]{:S(2)}, u32[]{:S(2)}) collective-permute-start(f32[2,4,128,128]{3,2,1,0:T(8,128)S(1)} %collective-permute-done.2.r2), channel_id=1, source_target_pairs={{1,0},{0,1},{17,16},{16,17},{3,2},{2,3},{19,18},{18,19},{5,4},{4,5... | collective-permute-start | bytes 1572872 | tf_op jit(solution)/shard_map/ppermute | solution.py:294
  15.6 10.1 %collective-permute-start.4 = (f32[1,4,128,128]{3,2,1,0:T(8,128)S(1)}, f32[1,4,128,128]{3,2,1,0:T(8,128)S(1)}, u32[]{:S(2)}, u32[]{:S(2)}) collective-permute-start(f32[1,4,128,128]{3,2,1,0:T(8,128)S(1)} %get-tuple-element.41), channel_id=1, source_target_pairs={{14,0},{0,4},{4,8},{8,12},{12,14},{3,13},{13,9},{9,5},{5,1},{1,3},... | collective-permute-start | bytes 786440 | tf_op jit(solution)/shard_map/ppermute | solution.py:294
  18.1 10.1 %collective-permute-start.3 = (f32[1,4,128,128]{3,2,1,0:T(8,128)S(1)}, f32[1,4,128,128]{3,2,1,0:T(8,128)S(1)}, u32[]{:S(2)}, u32[]{:S(2)}) collective-permute-start(f32[1,4,128,128]{3,2,1,0:T(8,128)S(1)} %get-tuple-element.42), channel_id=1, source_target_pairs={{14,0},{0,4},{4,8},{8,12},{12,14},{3,13},{13,9},{9,5},{5,1},{1,3},... | collective-permute-start | bytes 786440 | tf_op jit(solution)/shard_map/ppermute | solution.py:294
  22.5 5.7 %collective-permute-start.10 = (f32[2,4,128,128]{3,2,1,0:T(8,128)S(1)}, f32[2,4,128,128]{3,2,1,0:T(8,128)S(1)}, u32[]{:S(2)}, u32[]{:S(2)}) collective-permute-start(f32[2,4,128,128]{3,2,1,0:T(8,128)S(1)} %collective-permute-done.7.r3), channel_id=1, source_target_pairs={{1,0},{0,1},{17,16},{16,17},{3,2},{2,3},{19,18},{18,19},{5,4},{4,5... | collective-permute-start | bytes 1572872 | tf_op jit(solution)/shard_map/ppermute | solution.py:294
  25.7 2.6 %collective-permute-start.8 = (f32[1,4,128,128]{3,2,1,0:T(8,128)S(1)}, f32[1,4,128,128]{3,2,1,0:T(8,128)S(1)}, u32[]{:S(2)}, u32[]{:S(2)}) collective-permute-start(f32[1,4,128,128]{3,2,1,0:T(8,128)S(1)} %collective-permute-done.4.r4a), channel_id=1, source_target_pairs={{1,0},{0,1},{17,16},{16,17},{3,2},{2,3},{19,18},{18,19},{5,4},{4,5... | collective-permute-start | bytes 786440 | tf_op jit(solution)/shard_map/ppermute | solution.py:294
  28.2 2.2 %collective-permute-start.9 = (f32[1,4,128,128]{3,2,1,0:T(8,128)S(1)}, f32[1,4,128,128]{3,2,1,0:T(8,128)S(1)}, u32[]{:S(2)}, u32[]{:S(2)}) collective-permute-start(f32[1,4,128,128]{3,2,1,0:T(8,128)S(1)} %collective-permute-done.3.r4b), channel_id=1, source_target_pairs={{1,0},{0,1},{17,16},{16,17},{3,2},{2,3},{19,18},{18,19},{5,4},{4,5... | collective-permute-start | bytes 786440 | tf_op jit(solution)/shard_map/ppermute | solution.py:294

commit v12 on v9

--- a/solution.py
+++ b/solution.py
@@ -274,14 +274,14 @@
         route = [(index(g, a), index(g, b)) for g in range(groups) for a, b in pairs]
         return lax.ppermute(block, AXES, route)
 
-    up = [(z, 0, 0) for z in range(chains)] + [(last, 1, 0)]
-    down = [(z, 0, 1) for z in reversed(range(chains))] + [(0, 1, 1)]
-    first = [up + [(last, 1, 1)] + down + [(0, 1, 0)]]
+    up = [(z, 0, 1) for z in range(chains)] + [(last, 1, 1)]
+    down = [(z, 0, 0) for z in reversed(range(chains))] + [(0, 1, 0)]
+    first = [up + [(last, 1, 0)] + down + [(0, 1, 1)]]
     second = [up, down]
-    near = [(z - 1, z + 1 if z < last else -1) for z in range(chains)]
-    far = [(z - 2 if z >= 2 else -1, z + 2 if z + 2 < chains else -1) for z in range(chains)]
-    far[0] = (last, far[0][1])
-    far[last] = (far[last][0], 0)
+    near = [(z + 1 if z < last else -1, z - 1) for z in range(chains)]
+    far = [(z + 2 if z + 2 < chains else -1, z - 2 if z >= 2 else -1) for z in range(chains)]
+    far[0] = (far[0][0], last)
+    far[last] = (0, far[last][1])
     tables = (near, far)
 
     table = slot_table(columns, lanes * width)

time: 33.8 us -> 33.1 us (0.979)
  starting transfers between devices: 13.3 us -> 12 us
  waiting for transfers between devices: 8.85 us -> 9.42 us
    ppermute x1, starting transfers between devices: 3.5 us -> 2.28 us  [move_only(): return lax.ppermute(block, AXES, route)]
    ppermute x1, waiting for transfers between devices: 3.13 us -> 3.79 us  [move_only(): return lax.ppermute(block, AXES, route)]
  transfers between devices with their start and end apart: 11 -> 11, of which waited for: 5 -> 5; matrix products, arithmetic and copies ran while one was open for 9% -> 9% of each run, Pallas kernels for 14% -> 15%
where the time goes in v12:
time: 33.1 us; the launch traced here: 32.7 us
  starting transfers between devices  12 us (36%)
  waiting for transfers between devices  9.42 us (28%)
  Pallas kernels  8.36 us (25%)
  other arithmetic  2.86 us (9%)
    ppermute x10, starting transfers between devices, move(): return lax.ppermute(block, AXES, route)  9.68 us
    ppermute x10, waiting for transfers between devices, move(): return lax.ppermute(block, AXES, route)  5.63 us
    ppermute x1, waiting for transfers between devices, move_only(): return lax.ppermute(block, AXES, route)  3.79 us
    pallas_call x1, Pallas kernels, gather_local(): pl.pallas_call(functools.partial(late_kernel, tables), out_shape=[jax.Sha...  3.61 us
    pallas_call x1, Pallas kernels, gather_local(): pl.pallas_call(functools.partial(early_kernel, tables), out_shape=[jax.Sh...  3.13 us
    ppermute x1, starting transfers between devices, move_only(): return lax.ppermute(block, AXES, route)  2.28 us
    pallas_call x1, Pallas kernels, gather_local(): pl.pallas_call(functools.partial(middle_kernel, tables), out_shape=dense,...  1.63 us
    reduce_sum x1, other arithmetic, slot_table(): count = jnp.sum(here.astype(jnp.int32), axis=1, keepdims=True)  0.8 us
  transfers between devices with their start and end apart: 11, of which 5 were waited for; matrix products, arithmetic and copies ran while one was open for 9% of the time, Pallas kernels for 15%

profile of v12, /device:TPU:0, one launch (start us, length us, event | category | flops | bytes accessed | tf_op | source)
XLA Modules:
  0.0 32.7 jit_solution(191802869439106948)
XLA Ops:
  0.0 2.9 %collective-permute-start = (f32[2,4,128,128]{3,2,1,0:T(8,128)}, f32[2,4,128,128]{3,2,1,0:T(8,128)S(1)}, u32[]{:S(2)}, u32[]{:S(2)}) collective-permute-start(f32[2,4,128,128]{3,2,1,0:T(8,128)} %own_hbm.1), channel_id=1, source_target_pairs={{3,1},{1,5},{5,9},{9,13},{13,15},{15,14},{14,12},{12,8},{8,4},{4,0... | collective-permute-start | bytes 1572872 | tf_op jit(solution)/shard_map/ppermute | solution.py:267
  2.9 0.0 collective-permute-start.1
  2.9 0.8 %fusion.1 = (s32[8]{0:T(128)S(1)}, s32[8,8]{1,0:T(8,128)S(1)}) fusion(s32[8,16]{1,0:T(8,128)} %param.3), kind=kLoop, calls=%fused_computation.10 | loop fusion | flops 184 | bytes 544 | tf_op jit(solution)/shard_map/reduce_sum | solution.py:233
  3.7 0.1 fusion
  3.9 0.2 convert_reduce_fusion
  4.1 0.1 add_select_fusion
  4.1 0.2 select_reduce_fusion
  4.4 0.7 %collective-permute-done.1.own_swap = f32[2,4,128,128]{3,2,1,0:T(8,128)S(1)} collective-permute-done((f32[2,4,128,128]{3,2,1,0:T(8,128)}, f32[2,4,128,128]{3,2,1,0:T(8,128)S(1)}, u32[]{:S(2)}, u32[]{:S(2)}) %collective-permute-start.1) | collective-permute-done | bytes 524320 | tf_op jit(solution)/shard_map/ppermute | solution.py:267
  5.1 2.3 %collective-permute-start.2 = (f32[2,4,128,128]{3,2,1,0:T(8,128)S(1)}, f32[2,4,128,128]{3,2,1,0:T(8,128)S(1)}, u32[]{:S(2)}, u32[]{:S(2)}) collective-permute-start(f32[2,4,128,128]{3,2,1,0:T(8,128)S(1)} %collective-permute-done.1.own_swap), channel_id=1, source_target_pairs={{1,5},{5,9},{9,13},{13,15},{12,8},{8,4},{4,0},{0,2},{17,21},{21,25... | collective-permute-start | bytes 1572872 | tf_op jit(solution)/shard_map/ppermute | solution.py:275
  7.3 0.7 %compare_convert_fusion = s32[8,8]{1,0:T(8,128)S(1)} fusion(s32[8,16]{1,0:T(8,128)} %param.3), kind=kLoop, calls=%fused_computation.6 | loop fusion | flops 128 | bytes 512 | tf_op jit(solution)/shard_map/convert_element_type | solution.py:233
  8.0 0.7 %compare_select_fusion = s32[8,8]{1,0:T(8,128)S(1)} fusion(s32[8,8]{1,0:T(8,128)S(1)} %select_reduce_fusion, s32[8,16]{1,0:T(8,128)} %param.3), kind=kLoop, calls=%fused_computation.5 | loop fusion | flops 128 | bytes 768 | tf_op jit(solution)/shard_map/jit(_where)/select_n | solution.py:241
  8.7 0.1 pad_add_fusion.table_ref
  8.8 1.6 %collective-permute-done.r1 = f32[2,4,128,128]{3,2,1,0:T(8,128)S(1)} collective-permute-done((f32[2,4,128,128]{3,2,1,0:T(8,128)}, f32[2,4,128,128]{3,2,1,0:T(8,128)S(1)}, u32[]{:S(2)}, u32[]{:S(2)}) %collective-permute-start) | collective-permute-done | bytes 524320 | tf_op jit(solution)/shard_map/ppermute | solution.py:267
  10.4 1.9 %collective-permute-start.7 = (f32[2,4,128,128]{3,2,1,0:T(8,128)S(1)}, f32[2,4,128,128]{3,2,1,0:T(8,128)S(1)}, u32[]{:S(2)}, u32[]{:S(2)}) collective-permute-start(f32[2,4,128,128]{3,2,1,0:T(8,128)S(1)} %collective-permute-done.r1), channel_id=1, source_target_pairs={{15,1},{1,5},{5,9},{9,13},{13,15},{2,12},{12,8},{8,4},{4,0},{0,2},... | collective-permute-start | bytes 1572872 | tf_op jit(solution)/shard_map/ppermute | solution.py:267
  12.3 0.0 collective-permute-start.5
  12.3 3.8 %collective-permute-done.2.r2 = f32[2,4,128,128]{3,2,1,0:T(8,128)S(1)} collective-permute-done((f32[2,4,128,128]{3,2,1,0:T(8,128)S(1)}, f32[2,4,128,128]{3,2,1,0:T(8,128)S(1)}, u32[]{:S(2)}, u32[]{:S(2)}) %collective-permute-start.2) | collective-permute-done | bytes 524320 | tf_op jit(solution)/shard_map/ppermute | solution.py:275
  16.1 0.0 collective-permute-start.6
  16.2 1.9 %collective-permute-start.4 = (f32[1,4,128,128]{3,2,1,0:T(8,128)S(1)}, f32[1,4,128,128]{3,2,1,0:T(8,128)S(1)}, u32[]{:S(2)}, u32[]{:S(2)}) collective-permute-start(f32[1,4,128,128]{3,2,1,0:T(8,128)S(1)} %get-tuple-element.33), channel_id=1, source_target_pairs={{15,1},{1,5},{5,9},{9,13},{13,15},{2,12},{12,8},{8,4},{4,0},{0,2},... | collective-permute-start | bytes 786440 | tf_op jit(solution)/shard_map/ppermute | solution.py:267
  18.0 2.3 %collective-permute-start.3 = (f32[1,4,128,128]{3,2,1,0:T(8,128)S(1)}, f32[1,4,128,128]{3,2,1,0:T(8,128)S(1)}, u32[]{:S(2)}, u32[]{:S(2)}) collective-permute-start(f32[1,4,128,128]{3,2,1,0:T(8,128)S(1)} %get-tuple-element.34), channel_id=1, source_target_pairs={{15,1},{1,5},{5,9},{9,13},{13,15},{2,12},{12,8},{8,4},{4,0},{0,2},... | collective-permute-start | bytes 786440 | tf_op jit(solution)/shard_map/ppermute | solution.py:267
  20.3 1.4 %collective-permute-done.7.r3 = f32[2,4,128,128]{3,2,1,0:T(8,128)S(1)} collective-permute-done((f32[2,4,128,128]{3,2,1,0:T(8,128)S(1)}, f32[2,4,128,128]{3,2,1,0:T(8,128)S(1)}, u32[]{:S(2)}, u32[]{:S(2)}) %collective-permute-start.7) | collective-permute-done | bytes 524320 | tf_op jit(solution)/shard_map/ppermute | solution.py:267
  21.7 0.0 collective-permute-start.10
  21.7 0.0 collective-permute-done.5.t1
  21.7 0.0 collective-permute-done.6.t2
  21.8 3.1 %early.1 = (bf16[1024,1024]{1,0:T(8,128)(2,1)S(1)}, bf16[1024,1024]{1,0:T(8,128)(2,1)S(1)}, bf16[512,1024]{1,0:T(8,128)(2,1)S(1)}, f32[256,1024]{1,0:T(8,128)S(1)}) custom-call(s32[8,24]{1,0:T(8,128)S(1)} %pad_add_fusion.table_ref, f32[2,4,128,128]{3,2,1,0:T(8,128)} %own_hbm.1, f32[2,4,128,128]{3,2,1,0:T(8,128)S(1)} %collective-permute-done.1.own_swap, ...), custom_call_target="tpu_custom_call" | custom-call | tf_op jit(solution)/shard_map/early/pallas_call | solution.py:305
  24.9 0.0 collective-permute-done.4.r4a
  24.9 0.6 %collective-permute-start.8 = (f32[1,4,128,128]{3,2,1,0:T(8,128)S(1)}, f32[1,4,128,128]{3,2,1,0:T(8,128)S(1)}, u32[]{:S(2)}, u32[]{:S(2)}) collective-permute-start(f32[1,4,128,128]{3,2,1,0:T(8,128)S(1)} %collective-permute-done.4.r4a), channel_id=1, source_target_pairs={{1,0},{0,1},{17,16},{16,17},{3,2},{2,3},{19,18},{18,19},{5,4},{4,5... | collective-permute-start | bytes 786440 | tf_op jit(solution)/shard_map/ppermute | solution.py:267
  25.5 1.9 %collective-permute-done.3.r4b = f32[1,4,128,128]{3,2,1,0:T(8,128)S(1)} collective-permute-done((f32[1,4,128,128]{3,2,1,0:T(8,128)S(1)}, f32[1,4,128,128]{3,2,1,0:T(8,128)S(1)}, u32[]{:S(2)}, u32[]{:S(2)}) %collective-permute-start.3) | collective-permute-done | bytes 262176 | tf_op jit(solution)/shard_map/ppermute | solution.py:267
  27.4 0.0 collective-permute-done.8.t4a
  27.4 0.1 collective-permute-start.9
  27.5 0.0 collective-permute-done.10.t3
  27.5 1.6 %middle.1 = (bf16[1024,1024]{1,0:T(8,128)(2,1)S(1)}, bf16[1024,1024]{1,0:T(8,128)(2,1)S(1)}, f32[256,1024]{1,0:T(8,128)S(1)}) custom-call(s32[8,24]{1,0:T(8,128)S(1)} %pad_add_fusion.table_ref, f32[1,4,128,128]{3,2,1,0:T(8,128)S(1)} %collective-permute-done.4.r4a, ...), custom_call_target="tpu_custom_call", output_to_operand_aliasing={{0}: (5, {}), {1}: (6, {}), {2}: (8, {})} | custom-call | tf_op jit(solution)/shard_map/middle/pallas_call | solution.py:325
  29.1 3.6 %late.1 = (f32[2,4,128,128]{3,2,1,0:T(8,128)}, bf16[1024,1024]{1,0:T(8,128)(2,1)S(1)}, bf16[1024,1024]{1,0:T(8,128)(2,1)S(1)}, f32[256,1024]{1,0:T(8,128)S(1)}) custom-call(s32[8,24]{1,0:T(8,128)S(1)} %pad_add_fusion.table_ref, f32[1,4,128,128]{3,2,1,0:T(8,128)S(1)} %collective-permute-done.9.t4b, ...), custom_call_target="tpu_custom_call", output_to_operand_aliasing={{1}: (2, {}), {2}: (3, {}), {3}: (5, {})} | custom-call | tf_op jit(solution)/shard_map/late/pallas_call | solution.py:334
  (3 shorter events, 0.0 us)
Async XLA Ops:
  0.0 10.4 %collective-permute-start = (f32[2,4,128,128]{3,2,1,0:T(8,128)}, f32[2,4,128,128]{3,2,1,0:T(8,128)S(1)}, u32[]{:S(2)}, u32[]{:S(2)}) collective-permute-start(f32[2,4,128,128]{3,2,1,0:T(8,128)} %own_hbm.1), channel_id=1, source_target_pairs={{3,1},{1,5},{5,9},{9,13},{13,15},{15,14},{14,12},{12,8},{8,4},{4,0... | collective-permute-start | bytes 1572872 | tf_op jit(solution)/shard_map/ppermute | solution.py:267
  2.9 2.1 %collective-permute-start.1 = (f32[2,4,128,128]{3,2,1,0:T(8,128)}, f32[2,4,128,128]{3,2,1,0:T(8,128)S(1)}, u32[]{:S(2)}, u32[]{:S(2)}) collective-permute-start(f32[2,4,128,128]{3,2,1,0:T(8,128)} %own_hbm.1), channel_id=1, source_target_pairs={{1,0},{0,1},{17,16},{16,17},{3,2},{2,3},{19,18},{18,19},{5,4},{4,5... | collective-permute-start | bytes 1572872 | tf_op jit(solution)/shard_map/ppermute | solution.py:267
  5.1 11.1 %collective-permute-start.2 = (f32[2,4,128,128]{3,2,1,0:T(8,128)S(1)}, f32[2,4,128,128]{3,2,1,0:T(8,128)S(1)}, u32[]{:S(2)}, u32[]{:S(2)}) collective-permute-start(f32[2,4,128,128]{3,2,1,0:T(8,128)S(1)} %collective-permute-done.1.own_swap), channel_id=1, source_target_pairs={{1,5},{5,9},{9,13},{13,15},{12,8},{8,4},{4,0},{0,2},{17,21},{21,25... | collective-permute-start | bytes 1572872 | tf_op jit(solution)/shard_map/ppermute | solution.py:275
  10.4 11.3 %collective-permute-start.7 = (f32[2,4,128,128]{3,2,1,0:T(8,128)S(1)}, f32[2,4,128,128]{3,2,1,0:T(8,128)S(1)}, u32[]{:S(2)}, u32[]{:S(2)}) collective-permute-start(f32[2,4,128,128]{3,2,1,0:T(8,128)S(1)} %collective-permute-done.r1), channel_id=1, source_target_pairs={{15,1},{1,5},{5,9},{9,13},{13,15},{2,12},{12,8},{8,4},{4,0},{0,2},... | collective-permute-start | bytes 1572872 | tf_op jit(solution)/shard_map/ppermute | solution.py:267
  12.3 9.4 %collective-permute-start.5 = (f32[2,4,128,128]{3,2,1,0:T(8,128)S(1)}, f32[2,4,128,128]{3,2,1,0:T(8,128)S(1)}, u32[]{:S(2)}, u32[]{:S(2)}) collective-permute-start(f32[2,4,128,128]{3,2,1,0:T(8,128)S(1)} %collective-permute-done.r1), channel_id=1, source_target_pairs={{1,0},{0,1},{17,16},{16,17},{3,2},{2,3},{19,18},{18,19},{5,4},{4,5... | collective-permute-start | bytes 1572872 | tf_op jit(solution)/shard_map/ppermute | solution.py:267
  16.1 5.6 %collective-permute-start.6 = (f32[2,4,128,128]{3,2,1,0:T(8,128)S(1)}, f32[2,4,128,128]{3,2,1,0:T(8,128)S(1)}, u32[]{:S(2)}, u32[]{:S(2)}) collective-permute-start(f32[2,4,128,128]{3,2,1,0:T(8,128)S(1)} %collective-permute-done.2.r2), channel_id=1, source_target_pairs={{1,0},{0,1},{17,16},{16,17},{3,2},{2,3},{19,18},{18,19},{5,4},{4,5... | collective-permute-start | bytes 1572872 | tf_op jit(solution)/shard_map/ppermute | solution.py:267
  16.2 8.7 %collective-permute-start.4 = (f32[1,4,128,128]{3,2,1,0:T(8,128)S(1)}, f32[1,4,128,128]{3,2,1,0:T(8,128)S(1)}, u32[]{:S(2)}, u32[]{:S(2)}) collective-permute-start(f32[1,4,128,128]{3,2,1,0:T(8,128)S(1)} %get-tuple-element.33), channel_id=1, source_target_pairs={{15,1},{1,5},{5,9},{9,13},{13,15},{2,12},{12,8},{8,4},{4,0},{0,2},... | collective-permute-start | bytes 786440 | tf_op jit(solution)/shard_map/ppermute | solution.py:267
  18.0 9.3 %collective-permute-start.3 = (f32[1,4,128,128]{3,2,1,0:T(8,128)S(1)}, f32[1,4,128,128]{3,2,1,0:T(8,128)S(1)}, u32[]{:S(2)}, u32[]{:S(2)}) collective-permute-start(f32[1,4,128,128]{3,2,1,0:T(8,128)S(1)} %get-tuple-element.34), channel_id=1, source_target_pairs={{15,1},{1,5},{5,9},{9,13},{13,15},{2,12},{12,8},{8,4},{4,0},{0,2},... | collective-permute-start | bytes 786440 | tf_op jit(solution)/shard_map/ppermute | solution.py:267
  21.7 5.7 %collective-permute-start.10 = (f32[2,4,128,128]{3,2,1,0:T(8,128)S(1)}, f32[2,4,128,128]{3,2,1,0:T(8,128)S(1)}, u32[]{:S(2)}, u32[]{:S(2)}) collective-permute-start(f32[2,4,128,128]{3,2,1,0:T(8,128)S(1)} %collective-permute-done.7.r3), channel_id=1, source_target_pairs={{1,0},{0,1},{17,16},{16,17},{3,2},{2,3},{19,18},{18,19},{5,4},{4,5... | collective-permute-start | bytes 1572872 | tf_op jit(solution)/shard_map/ppermute | solution.py:267
  24.9 2.5 %collective-permute-start.8 = (f32[1,4,128,128]{3,2,1,0:T(8,128)S(1)}, f32[1,4,128,128]{3,2,1,0:T(8,128)S(1)}, u32[]{:S(2)}, u32[]{:S(2)}) collective-permute-start(f32[1,4,128,128]{3,2,1,0:T(8,128)S(1)} %collective-permute-done.4.r4a), channel_id=1, source_target_pairs={{1,0},{0,1},{17,16},{16,17},{3,2},{2,3},{19,18},{18,19},{5,4},{4,5... | collective-permute-start | bytes 786440 | tf_op jit(solution)/shard_map/ppermute | solution.py:267
  27.4 1.7 %collective-permute-start.9 = (f32[1,4,128,128]{3,2,1,0:T(8,128)S(1)}, f32[1,4,128,128]{3,2,1,0:T(8,128)S(1)}, u32[]{:S(2)}, u32[]{:S(2)}) collective-permute-start(f32[1,4,128,128]{3,2,1,0:T(8,128)S(1)} %collective-permute-done.3.r4b), channel_id=1, source_target_pairs={{1,0},{0,1},{17,16},{16,17},{3,2},{2,3},{19,18},{18,19},{5,4},{4,5... | collective-permute-start | bytes 786440 | tf_op jit(solution)/shard_map/ppermute | solution.py:267

commit v13 on v12

--- a/solution.py
+++ b/solution.py
@@ -278,20 +278,31 @@
     down = [(z, 0, 0) for z in reversed(range(chains))] + [(0, 1, 0)]
     first = [up + [(last, 1, 0)] + down + [(0, 1, 1)]]
     second = [up, down]
+    inside = [up[:-1] + down[:-1]]
     near = [(z + 1 if z < last else -1, z - 1) for z in range(chains)]
     far = [(z + 2 if z + 2 < chains else -1, z - 2 if z >= 2 else -1) for z in range(chains)]
     far[0] = (far[0][0], last)
     far[last] = (0, far[last][1])
     tables = (near, far)
 
+    helper = functools.reduce(
+        jnp.logical_or,
+        [
+            (lax.axis_index("blk") == z) & (lax.axis_index("panel") == x) & (lane == c)
+            for lane in (lax.axis_index("depth"),)
+            for z, x, c in (up[-1], down[-1])
+        ],
+    )
+
     table = slot_table(columns, lanes * width)
     r1 = move(x_blocks, first)
     own_swap = swap(x_blocks)
-    r2 = move_only(own_swap, [up, down])
+    r2 = move(own_swap, inside)
+    crossed = [move_only(own_swap[r : r + 1], [up[-2:], down[-2:]]) for r in range(2)]
     r1, table = lax.optimization_barrier((r1, table))
     r3 = move(r1, second)
     t1 = swap(r1)
-    r4a, r4b = move(r2[:1], second), move(r2[1:], second)
+    r4a, r4b = [move(jnp.where(helper, crossed[r], r2[r : r + 1]), second) for r in range(2)]
     t2 = swap(r2)
 
     order, own = rows * edge, slab * edge

time: 33.1 us -> 33.5 us (1.012)
  waiting for transfers between devices: 9.42 us -> 6.89 us
  starting transfers between devices: 12 us -> 14.1 us
  local copies, waits for them, and re-layouts: 0.03 us -> 0.82 us
    ppermute x1 -> x2, waiting for transfers between devices: 3.79 us -> 0.01 us  [move_only(): return lax.ppermute(block, AXES, route)]
    ppermute x1 -> x2, starting transfers between devices: 2.28 us -> 4.16 us  [move_only(): return lax.ppermute(block, AXES, route)]
    ppermute x10 -> x11, waiting for transfers between devices: 5.63 us -> 6.88 us  [move(): return lax.ppermute(block, AXES, route)]
    slice x1, local copies, waits for them, and re-layouts: 0.03 us -> 0.82 us  [gather_local(): own_swap[r:r + 1]]
    ppermute x10 -> x11, starting transfers between devices: 9.68 us -> 9.97 us  [move(): return lax.ppermute(block, AXES, route)]
  transfers between devices with their start and end apart: 11 -> 13, of which waited for: 5 -> 3; matrix products, arithmetic and copies ran while one was open for 9% -> 11% of each run, Pallas kernels for 15% -> 14%
where the time goes in v13:
time: 33.5 us; the launch traced here: 33.2 us
  starting transfers between devices  14.1 us (42%)
  Pallas kernels  8.35 us (25%)
  waiting for transfers between devices  6.89 us (21%)
  other arithmetic  2.94 us (9%)
  local copies, waits for them, and re-layouts  0.82 us (2%)
    ppermute x11, starting transfers between devices, move(): return lax.ppermute(block, AXES, route)  9.97 us
    ppermute x11, waiting for transfers between devices, move(): return lax.ppermute(block, AXES, route)  6.88 us
    ppermute x2, starting transfers between devices, move_only(): return lax.ppermute(block, AXES, route)  4.16 us
    pallas_call x1, Pallas kernels, gather_local(): pl.pallas_call(functools.partial(late_kernel, tables), out_shape=[jax.Sha...  3.61 us
    pallas_call x1, Pallas kernels, gather_local(): pl.pallas_call(functools.partial(early_kernel, tables), out_shape=[jax.Sh...  3.12 us
    pallas_call x1, Pallas kernels, gather_local(): pl.pallas_call(functools.partial(middle_kernel, tables), out_shape=dense,...  1.62 us
    slice x1, local copies, waits for them, and re-layouts, gather_local(): own_swap[r:r + 1]  0.82 us
    reduce_sum x1, other arithmetic, slot_table(): count = jnp.sum(here.astype(jnp.int32), axis=1, keepdims=True)  0.8 us
  transfers between devices with their start and end apart: 13, of which 3 were waited for; matrix products, arithmetic and copies ran while one was open for 11% of the time, Pallas kernels for 14%

profile of v13, /device:TPU:0, one launch (start us, length us, event | category | flops | bytes accessed | tf_op | source)
XLA Modules:
  0.0 33.2 jit_solution(13960458930261336982)
XLA Ops:
  0.0 2.9 %collective-permute-start = (f32[2,4,128,128]{3,2,1,0:T(8,128)}, f32[2,4,128,128]{3,2,1,0:T(8,128)S(1)}, u32[]{:S(2)}, u32[]{:S(2)}) collective-permute-start(f32[2,4,128,128]{3,2,1,0:T(8,128)} %own_hbm.1), channel_id=1, source_target_pairs={{3,1},{1,5},{5,9},{9,13},{13,15},{15,14},{14,12},{12,8},{8,4},{4,0... | collective-permute-start | bytes 1572872 | tf_op jit(solution)/shard_map/ppermute | solution.py:267
  2.9 0.0 collective-permute-start.1
  2.9 0.8 %fusion.1 = (s32[8]{0:T(128)S(1)}, s32[8,8]{1,0:T(8,128)S(1)}) fusion(s32[8,16]{1,0:T(8,128)} %param.3), kind=kLoop, calls=%fused_computation.12 | loop fusion | flops 184 | bytes 544 | tf_op jit(solution)/shard_map/reduce_sum | solution.py:233
  3.7 0.1 fusion
  3.9 0.2 convert_reduce_fusion
  4.1 0.1 add_select_fusion
  4.1 0.2 select_reduce_fusion
  4.4 0.7 %compare_select_fusion = s32[8,8]{1,0:T(8,128)S(1)} fusion(s32[8,8]{1,0:T(8,128)S(1)} %select_reduce_fusion, s32[8,16]{1,0:T(8,128)} %param.3), kind=kLoop, calls=%fused_computation.7 | loop fusion | flops 128 | bytes 768 | tf_op jit(solution)/shard_map/jit(_where)/select_n | solution.py:241
  5.1 0.5 %collective-permute-start.3 = (f32[2,4,128,128]{3,2,1,0:T(8,128)S(1)}, f32[2,4,128,128]{3,2,1,0:T(8,128)S(1)}, u32[]{:S(2)}, u32[]{:S(2)}) collective-permute-start(f32[2,4,128,128]{3,2,1,0:T(8,128)S(1)} %collective-permute-done.1.own_swap), channel_id=1, source_target_pairs={{0,1},{1,5},{5,9},{9,13},{13,12},{12,8},{8,4},{4,0},{16,17},{17,21... | collective-permute-start | bytes 1572872 | tf_op jit(solution)/shard_map/ppermute | solution.py:267
  5.6 0.8 %fusion.2 = (f32[1,4,128,128]{3,2,1,0:T(8,128)}, f32[1,4,128,128]{3,2,1,0:T(8,128)}) fusion(f32[2,4,128,128]{3,2,1,0:T(8,128)S(1)} %collective-permute-done.1.own_swap), kind=kLoop, calls=%fused_computation.13 | loop fusion | bytes 1048576 | tf_op jit(solution)/shard_map/slice | solution.py:301
  6.4 2.2 %collective-permute-start.5 = (f32[1,4,128,128]{3,2,1,0:T(8,128)}, f32[1,4,128,128]{3,2,1,0:T(8,128)S(1)}, u32[]{:S(2)}, u32[]{:S(2)}) collective-permute-start(f32[1,4,128,128]{3,2,1,0:T(8,128)} %get-tuple-element.35), channel_id=1, source_target_pairs={{13,15},{0,2},{29,31},{16,18}} | collective-permute-start | bytes 786440 | tf_op jit(solution)/shard_map/ppermute | solution.py:275
  8.5 2.0 %collective-permute-start.2 = (f32[1,4,128,128]{3,2,1,0:T(8,128)}, f32[1,4,128,128]{3,2,1,0:T(8,128)}, u32[]{:S(2)}, u32[]{:S(2)}) collective-permute-start(f32[1,4,128,128]{3,2,1,0:T(8,128)} %get-tuple-element.36), channel_id=1, source_target_pairs={{13,15},{0,2},{29,31},{16,18}} | collective-permute-start | bytes 786440 | tf_op jit(solution)/shard_map/ppermute | solution.py:275
  10.6 0.7 %compare_convert_fusion = s32[8,8]{1,0:T(8,128)S(1)} fusion(s32[8,16]{1,0:T(8,128)} %param.3), kind=kLoop, calls=%fused_computation.8 | loop fusion | flops 128 | bytes 512 | tf_op jit(solution)/shard_map/convert_element_type | solution.py:233
  11.2 0.1 pad_add_fusion.table_ref
  11.3 0.0 collective-permute-done.r1
  11.3 1.0 %collective-permute-start.9 = (f32[2,4,128,128]{3,2,1,0:T(8,128)S(1)}, f32[2,4,128,128]{3,2,1,0:T(8,128)S(1)}, u32[]{:S(2)}, u32[]{:S(2)}) collective-permute-start(f32[2,4,128,128]{3,2,1,0:T(8,128)S(1)} %collective-permute-done.r1), channel_id=1, source_target_pairs={{15,1},{1,5},{5,9},{9,13},{13,15},{2,12},{12,8},{8,4},{4,0},{0,2},... | collective-permute-start | bytes 1572872 | tf_op jit(solution)/shard_map/ppermute | solution.py:267
  12.3 0.0 collective-permute-start.7
  12.3 3.7 %collective-permute-done.3.r2 = f32[2,4,128,128]{3,2,1,0:T(8,128)S(1)} collective-permute-done((f32[2,4,128,128]{3,2,1,0:T(8,128)S(1)}, f32[2,4,128,128]{3,2,1,0:T(8,128)S(1)}, u32[]{:S(2)}, u32[]{:S(2)}) %collective-permute-start.3) | collective-permute-done | bytes 524320 | tf_op jit(solution)/shard_map/ppermute | solution.py:267
  16.0 0.0 collective-permute-start.8
  16.0 0.0 collective-permute-done.5
  16.0 0.1 slice_select_fusion
  16.1 3.0 %collective-permute-start.6 = (f32[1,4,128,128]{3,2,1,0:T(8,128)S(1)}, f32[1,4,128,128]{3,2,1,0:T(8,128)S(1)}, u32[]{:S(2)}, u32[]{:S(2)}) collective-permute-start(f32[1,4,128,128]{3,2,1,0:T(8,128)S(1)} %get-tuple-element.33), channel_id=1, source_target_pairs={{15,1},{1,5},{5,9},{9,13},{13,15},{2,12},{12,8},{8,4},{4,0},{0,2},... | collective-permute-start | bytes 786440 | tf_op jit(solution)/shard_map/ppermute | solution.py:267
  19.1 1.2 %collective-permute-start.4 = (f32[1,4,128,128]{3,2,1,0:T(8,128)S(1)}, f32[1,4,128,128]{3,2,1,0:T(8,128)S(1)}, u32[]{:S(2)}, u32[]{:S(2)}) collective-permute-start(f32[1,4,128,128]{3,2,1,0:T(8,128)S(1)} %get-tuple-element.34), channel_id=1, source_target_pairs={{15,1},{1,5},{5,9},{9,13},{13,15},{2,12},{12,8},{8,4},{4,0},{0,2},... | collective-permute-start | bytes 786440 | tf_op jit(solution)/shard_map/ppermute | solution.py:267
  20.3 1.3 %collective-permute-done.9.r3 = f32[2,4,128,128]{3,2,1,0:T(8,128)S(1)} collective-permute-done((f32[2,4,128,128]{3,2,1,0:T(8,128)S(1)}, f32[2,4,128,128]{3,2,1,0:T(8,128)S(1)}, u32[]{:S(2)}, u32[]{:S(2)}) %collective-permute-start.9) | collective-permute-done | bytes 524320 | tf_op jit(solution)/shard_map/ppermute | solution.py:267
  21.6 0.0 collective-permute-done.7.t1
  21.6 0.0 collective-permute-done.8.t2
  21.6 3.1 %early.1 = (bf16[1024,1024]{1,0:T(8,128)(2,1)S(1)}, bf16[1024,1024]{1,0:T(8,128)(2,1)S(1)}, bf16[512,1024]{1,0:T(8,128)(2,1)S(1)}, f32[256,1024]{1,0:T(8,128)S(1)}) custom-call(s32[8,24]{1,0:T(8,128)S(1)} %pad_add_fusion.table_ref, f32[2,4,128,128]{3,2,1,0:T(8,128)} %own_hbm.1, f32[2,4,128,128]{3,2,1,0:T(8,128)S(1)} %collective-permute-done.1.own_swap, ...), custom_call_target="tpu_custom_call" | custom-call | tf_op jit(solution)/shard_map/early/pallas_call | solution.py:316
  24.8 0.6 %collective-permute-start.10 = (f32[1,4,128,128]{3,2,1,0:T(8,128)S(1)}, f32[1,4,128,128]{3,2,1,0:T(8,128)S(1)}, u32[]{:S(2)}, u32[]{:S(2)}) collective-permute-start(f32[1,4,128,128]{3,2,1,0:T(8,128)S(1)} %collective-permute-done.6.r4a), channel_id=1, source_target_pairs={{1,0},{0,1},{17,16},{16,17},{3,2},{2,3},{19,18},{18,19},{5,4},{4,5... | collective-permute-start | bytes 786440 | tf_op jit(solution)/shard_map/ppermute | solution.py:267
  25.3 1.9 %collective-permute-done.4.r4b = f32[1,4,128,128]{3,2,1,0:T(8,128)S(1)} collective-permute-done((f32[1,4,128,128]{3,2,1,0:T(8,128)S(1)}, f32[1,4,128,128]{3,2,1,0:T(8,128)S(1)}, u32[]{:S(2)}, u32[]{:S(2)}) %collective-permute-start.4) | collective-permute-done | bytes 262176 | tf_op jit(solution)/shard_map/ppermute | solution.py:267
  27.2 0.7 %collective-permute-start.11 = (f32[1,4,128,128]{3,2,1,0:T(8,128)S(1)}, f32[1,4,128,128]{3,2,1,0:T(8,128)S(1)}, u32[]{:S(2)}, u32[]{:S(2)}) collective-permute-start(f32[1,4,128,128]{3,2,1,0:T(8,128)S(1)} %collective-permute-done.4.r4b), channel_id=1, source_target_pairs={{1,0},{0,1},{17,16},{16,17},{3,2},{2,3},{19,18},{18,19},{5,4},{4,5... | collective-permute-start | bytes 786440 | tf_op jit(solution)/shard_map/ppermute | solution.py:267
  28.0 1.6 %middle.1 = (bf16[1024,1024]{1,0:T(8,128)(2,1)S(1)}, bf16[1024,1024]{1,0:T(8,128)(2,1)S(1)}, f32[256,1024]{1,0:T(8,128)S(1)}) custom-call(s32[8,24]{1,0:T(8,128)S(1)} %pad_add_fusion.table_ref, f32[1,4,128,128]{3,2,1,0:T(8,128)S(1)} %collective-permute-done.6.r4a, ...), custom_call_target="tpu_custom_call", output_to_operand_aliasing={{0}: (5, {}), {1}: (6, {}), {2}: (8, {})} | custom-call | tf_op jit(solution)/shard_map/middle/pallas_call | solution.py:336
  29.6 3.6 %late.1 = (f32[2,4,128,128]{3,2,1,0:T(8,128)}, bf16[1024,1024]{1,0:T(8,128)(2,1)S(1)}, bf16[1024,1024]{1,0:T(8,128)(2,1)S(1)}, f32[256,1024]{1,0:T(8,128)S(1)}) custom-call(s32[8,24]{1,0:T(8,128)S(1)} %pad_add_fusion.table_ref, f32[1,4,128,128]{3,2,1,0:T(8,128)S(1)} %collective-permute-done.11.t4b, ...), custom_call_target="tpu_custom_call", output_to_operand_aliasing={{1}: (2, {}), {2}: (3, {}), {3}: (5, {})} | custom-call | tf_op jit(solution)/shard_map/late/pallas_call | solution.py:345
  (8 shorter events, 0.0 us)
Async XLA Ops:
  0.0 11.3 %collective-permute-start = (f32[2,4,128,128]{3,2,1,0:T(8,128)}, f32[2,4,128,128]{3,2,1,0:T(8,128)S(1)}, u32[]{:S(2)}, u32[]{:S(2)}) collective-permute-start(f32[2,4,128,128]{3,2,1,0:T(8,128)} %own_hbm.1), channel_id=1, source_target_pairs={{3,1},{1,5},{5,9},{9,13},{13,15},{15,14},{14,12},{12,8},{8,4},{4,0... | collective-permute-start | bytes 1572872 | tf_op jit(solution)/shard_map/ppermute | solution.py:267
  2.9 2.1 %collective-permute-start.1 = (f32[2,4,128,128]{3,2,1,0:T(8,128)}, f32[2,4,128,128]{3,2,1,0:T(8,128)S(1)}, u32[]{:S(2)}, u32[]{:S(2)}) collective-permute-start(f32[2,4,128,128]{3,2,1,0:T(8,128)} %own_hbm.1), channel_id=1, source_target_pairs={{1,0},{0,1},{17,16},{16,17},{3,2},{2,3},{19,18},{18,19},{5,4},{4,5... | collective-permute-start | bytes 1572872 | tf_op jit(solution)/shard_map/ppermute | solution.py:267
  5.1 10.9 %collective-permute-start.3 = (f32[2,4,128,128]{3,2,1,0:T(8,128)S(1)}, f32[2,4,128,128]{3,2,1,0:T(8,128)S(1)}, u32[]{:S(2)}, u32[]{:S(2)}) collective-permute-start(f32[2,4,128,128]{3,2,1,0:T(8,128)S(1)} %collective-permute-done.1.own_swap), channel_id=1, source_target_pairs={{0,1},{1,5},{5,9},{9,13},{13,12},{12,8},{8,4},{4,0},{16,17},{17,21... | collective-permute-start | bytes 1572872 | tf_op jit(solution)/shard_map/ppermute | solution.py:267
  6.4 9.6 %collective-permute-start.5 = (f32[1,4,128,128]{3,2,1,0:T(8,128)}, f32[1,4,128,128]{3,2,1,0:T(8,128)S(1)}, u32[]{:S(2)}, u32[]{:S(2)}) collective-permute-start(f32[1,4,128,128]{3,2,1,0:T(8,128)} %get-tuple-element.35), channel_id=1, source_target_pairs={{13,15},{0,2},{29,31},{16,18}} | collective-permute-start | bytes 786440 | tf_op jit(solution)/shard_map/ppermute | solution.py:275
  8.5 7.5 %collective-permute-start.2 = (f32[1,4,128,128]{3,2,1,0:T(8,128)}, f32[1,4,128,128]{3,2,1,0:T(8,128)}, u32[]{:S(2)}, u32[]{:S(2)}) collective-permute-start(f32[1,4,128,128]{3,2,1,0:T(8,128)} %get-tuple-element.36), channel_id=1, source_target_pairs={{13,15},{0,2},{29,31},{16,18}} | collective-permute-start | bytes 786440 | tf_op jit(solution)/shard_map/ppermute | solution.py:275
  11.3 10.3 %collective-permute-start.9 = (f32[2,4,128,128]{3,2,1,0:T(8,128)S(1)}, f32[2,4,128,128]{3,2,1,0:T(8,128)S(1)}, u32[]{:S(2)}, u32[]{:S(2)}) collective-permute-start(f32[2,4,128,128]{3,2,1,0:T(8,128)S(1)} %collective-permute-done.r1), channel_id=1, source_target_pairs={{15,1},{1,5},{5,9},{9,13},{13,15},{2,12},{12,8},{8,4},{4,0},{0,2},... | collective-permute-start | bytes 1572872 | tf_op jit(solution)/shard_map/ppermute | solution.py:267
  12.3 9.3 %collective-permute-start.7 = (f32[2,4,128,128]{3,2,1,0:T(8,128)S(1)}, f32[2,4,128,128]{3,2,1,0:T(8,128)S(1)}, u32[]{:S(2)}, u32[]{:S(2)}) collective-permute-start(f32[2,4,128,128]{3,2,1,0:T(8,128)S(1)} %collective-permute-done.r1), channel_id=1, source_target_pairs={{1,0},{0,1},{17,16},{16,17},{3,2},{2,3},{19,18},{18,19},{5,4},{4,5... | collective-permute-start | bytes 1572872 | tf_op jit(solution)/shard_map/ppermute | solution.py:267
  16.0 5.6 %collective-permute-start.8 = (f32[2,4,128,128]{3,2,1,0:T(8,128)S(1)}, f32[2,4,128,128]{3,2,1,0:T(8,128)S(1)}, u32[]{:S(2)}, u32[]{:S(2)}) collective-permute-start(f32[2,4,128,128]{3,2,1,0:T(8,128)S(1)} %collective-permute-done.3.r2), channel_id=1, source_target_pairs={{1,0},{0,1},{17,16},{16,17},{3,2},{2,3},{19,18},{18,19},{5,4},{4,5... | collective-permute-start | bytes 1572872 | tf_op jit(solution)/shard_map/ppermute | solution.py:267
  16.1 8.7 %collective-permute-start.6 = (f32[1,4,128,128]{3,2,1,0:T(8,128)S(1)}, f32[1,4,128,128]{3,2,1,0:T(8,128)S(1)}, u32[]{:S(2)}, u32[]{:S(2)}) collective-permute-start(f32[1,4,128,128]{3,2,1,0:T(8,128)S(1)} %get-tuple-element.33), channel_id=1, source_target_pairs={{15,1},{1,5},{5,9},{9,13},{13,15},{2,12},{12,8},{8,4},{4,0},{0,2},... | collective-permute-start | bytes 786440 | tf_op jit(solution)/shard_map/ppermute | solution.py:267
  19.1 8.1 %collective-permute-start.4 = (f32[1,4,128,128]{3,2,1,0:T(8,128)S(1)}, f32[1,4,128,128]{3,2,1,0:T(8,128)S(1)}, u32[]{:S(2)}, u32[]{:S(2)}) collective-permute-start(f32[1,4,128,128]{3,2,1,0:T(8,128)S(1)} %get-tuple-element.34), channel_id=1, source_target_pairs={{15,1},{1,5},{5,9},{9,13},{13,15},{2,12},{12,8},{8,4},{4,0},{0,2},... | collective-permute-start | bytes 786440 | tf_op jit(solution)/shard_map/ppermute | solution.py:267
  21.6 6.3 %collective-permute-start.12 = (f32[2,4,128,128]{3,2,1,0:T(8,128)S(1)}, f32[2,4,128,128]{3,2,1,0:T(8,128)S(1)}, u32[]{:S(2)}, u32[]{:S(2)}) collective-permute-start(f32[2,4,128,128]{3,2,1,0:T(8,128)S(1)} %collective-permute-done.9.r3), channel_id=1, source_target_pairs={{1,0},{0,1},{17,16},{16,17},{3,2},{2,3},{19,18},{18,19},{5,4},{4,5... | collective-permute-start | bytes 1572872 | tf_op jit(solution)/shard_map/ppermute | solution.py:267
  24.8 2.5 %collective-permute-start.10 = (f32[1,4,128,128]{3,2,1,0:T(8,128)S(1)}, f32[1,4,128,128]{3,2,1,0:T(8,128)S(1)}, u32[]{:S(2)}, u32[]{:S(2)}) collective-permute-start(f32[1,4,128,128]{3,2,1,0:T(8,128)S(1)} %collective-permute-done.6.r4a), channel_id=1, source_target_pairs={{1,0},{0,1},{17,16},{16,17},{3,2},{2,3},{19,18},{18,19},{5,4},{4,5... | collective-permute-start | bytes 786440 | tf_op jit(solution)/shard_map/ppermute | solution.py:267
  27.2 2.3 %collective-permute-start.11 = (f32[1,4,128,128]{3,2,1,0:T(8,128)S(1)}, f32[1,4,128,128]{3,2,1,0:T(8,128)S(1)}, u32[]{:S(2)}, u32[]{:S(2)}) collective-permute-start(f32[1,4,128,128]{3,2,1,0:T(8,128)S(1)} %collective-permute-done.4.r4b), channel_id=1, source_target_pairs={{1,0},{0,1},{17,16},{16,17},{3,2},{2,3},{19,18},{18,19},{5,4},{4,5... | collective-permute-start | bytes 786440 | tf_op jit(solution)/shard_map/ppermute | solution.py:267

commit v14 on v6

--- a/solution.py
+++ b/solution.py
@@ -272,14 +272,14 @@
         route = [(index(g, a), index(g, b)) for g in range(groups) for a, b in pairs]
         return lax.ppermute(block, AXES, route)
 
-    up = [(z, 0, 0) for z in range(chains)] + [(last, 1, 0)]
-    down = [(z, 0, 1) for z in reversed(range(chains))] + [(0, 1, 1)]
-    first = [up + [(last, 1, 1)] + down + [(0, 1, 0)]]
+    up = [(z, 0, 1) for z in range(chains)] + [(last, 1, 1)]
+    down = [(z, 0, 0) for z in reversed(range(chains))] + [(0, 1, 0)]
+    first = [up + [(last, 1, 0)] + down + [(0, 1, 1)]]
     second = [up, down]
-    near = [(z - 1, z + 1 if z < last else -1) for z in range(chains)]
-    far = [(z - 2 if z >= 2 else -1, z + 2 if z + 2 < chains else -1) for z in range(chains)]
-    far[0] = (last, far[0][1])
-    far[last] = (far[last][0], 0)
+    near = [(z + 1 if z < last else -1, z - 1) for z in range(chains)]
+    far = [(z + 2 if z + 2 < chains else -1, z - 2 if z >= 2 else -1) for z in range(chains)]
+    far[0] = (far[0][0], last)
+    far[last] = (0, far[last][1])
     tables = (near, far)
 
     table = slot_table(columns, lanes * width)

time: 34 us -> 33.2 us (0.976)
  starting transfers between devices: 11.1 us -> 8.99 us
  waiting for transfers between devices: 11.4 us -> 12.7 us
    ppermute x1, starting transfers between devices: 3.5 us -> 2.28 us  [move_only(): return lax.ppermute(block, AXES, route)]
    ppermute x8, starting transfers between devices: 7.63 us -> 6.72 us  [move(): return lax.ppermute(block, AXES, route)]
    ppermute x8, waiting for transfers between devices: 8.22 us -> 8.91 us  [move(): return lax.ppermute(block, AXES, route)]
    ppermute x1, waiting for transfers between devices: 3.13 us -> 3.79 us  [move_only(): return lax.ppermute(block, AXES, route)]
  transfers between devices with their start and end apart: 9 -> 9, of which waited for: 6 -> 6; matrix products, arithmetic and copies ran while one was open for 8% -> 9% of each run, Pallas kernels for 14% -> 14%
where the time goes in v14:
time: 33.2 us; the launch traced here: 32.9 us
  waiting for transfers between devices  12.7 us (38%)
  starting transfers between devices  8.99 us (27%)
  Pallas kernels  8.32 us (25%)
  other arithmetic  2.86 us (9%)
    ppermute x8, waiting for transfers between devices, move(): return lax.ppermute(block, AXES, route)  8.91 us
    ppermute x8, starting transfers between devices, move(): return lax.ppermute(block, AXES, route)  6.72 us
    ppermute x1, waiting for transfers between devices, move_only(): return lax.ppermute(block, AXES, route)  3.79 us
    pallas_call x1, Pallas kernels, gather_local(): pl.pallas_call(functools.partial(late_kernel, tables), out_shape=[jax.Sha...  3.66 us
    pallas_call x1, Pallas kernels, gather_local(): pl.pallas_call(functools.partial(early_kernel, tables), out_shape=[jax.Sh...  3.13 us
    ppermute x1, starting transfers between devices, move_only(): return lax.ppermute(block, AXES, route)  2.28 us
    pallas_call x1, Pallas kernels, gather_local(): pl.pallas_call(functools.partial(middle_kernel, tables), out_shape=dense,...  1.54 us
    reduce_sum x1, other arithmetic, slot_table(): count = jnp.sum(here.astype(jnp.int32), axis=1, keepdims=True)  0.8 us
  transfers between devices with their start and end apart: 9, of which 6 were waited for; matrix products, arithmetic and copies ran while one was open for 9% of the time, Pallas kernels for 14%

profile of v14, /device:TPU:0, one launch (start us, length us, event | category | flops | bytes accessed | tf_op | source)
XLA Modules:
  0.0 32.9 jit_solution(8817645816292429122)
XLA Ops:
  0.0 2.9 %collective-permute-start = (f32[2,4,128,128]{3,2,1,0:T(8,128)}, f32[2,4,128,128]{3,2,1,0:T(8,128)S(1)}, u32[]{:S(2)}, u32[]{:S(2)}) collective-permute-start(f32[2,4,128,128]{3,2,1,0:T(8,128)} %own_hbm.1), channel_id=1, source_target_pairs={{3,1},{1,5},{5,9},{9,13},{13,15},{15,14},{14,12},{12,8},{8,4},{4,0... | collective-permute-start | bytes 1572872 | tf_op jit(solution)/shard_map/ppermute | solution.py:265
  2.9 0.0 collective-permute-start.1
  2.9 0.8 %fusion.1 = (s32[8]{0:T(128)S(1)}, s32[8,8]{1,0:T(8,128)S(1)}) fusion(s32[8,16]{1,0:T(8,128)} %param.3), kind=kLoop, calls=%fused_computation.10 | loop fusion | flops 184 | bytes 544 | tf_op jit(solution)/shard_map/reduce_sum | solution.py:231
  3.7 0.1 fusion
  3.9 0.2 convert_reduce_fusion
  4.1 0.1 add_select_fusion
  4.1 0.2 select_reduce_fusion
  4.4 0.7 %collective-permute-done.1.own_swap = f32[2,4,128,128]{3,2,1,0:T(8,128)S(1)} collective-permute-done((f32[2,4,128,128]{3,2,1,0:T(8,128)}, f32[2,4,128,128]{3,2,1,0:T(8,128)S(1)}, u32[]{:S(2)}, u32[]{:S(2)}) %collective-permute-start.1) | collective-permute-done | bytes 524320 | tf_op jit(solution)/shard_map/ppermute | solution.py:265
  5.1 2.3 %collective-permute-start.2 = (f32[2,4,128,128]{3,2,1,0:T(8,128)S(1)}, f32[2,4,128,128]{3,2,1,0:T(8,128)S(1)}, u32[]{:S(2)}, u32[]{:S(2)}) collective-permute-start(f32[2,4,128,128]{3,2,1,0:T(8,128)S(1)} %collective-permute-done.1.own_swap), channel_id=1, source_target_pairs={{1,5},{5,9},{9,13},{13,15},{12,8},{8,4},{4,0},{0,2},{17,21},{21,25... | collective-permute-start | bytes 1572872 | tf_op jit(solution)/shard_map/ppermute | solution.py:273
  7.3 0.7 %compare_convert_fusion = s32[8,8]{1,0:T(8,128)S(1)} fusion(s32[8,16]{1,0:T(8,128)} %param.3), kind=kLoop, calls=%fused_computation.6 | loop fusion | flops 128 | bytes 512 | tf_op jit(solution)/shard_map/convert_element_type | solution.py:231
  8.0 0.7 %compare_select_fusion = s32[8,8]{1,0:T(8,128)S(1)} fusion(s32[8,8]{1,0:T(8,128)S(1)} %select_reduce_fusion, s32[8,16]{1,0:T(8,128)} %param.3), kind=kLoop, calls=%fused_computation.5 | loop fusion | flops 128 | bytes 768 | tf_op jit(solution)/shard_map/jit(_where)/select_n | solution.py:239
  8.7 0.1 pad_add_fusion.table_ref
  8.8 1.6 %collective-permute-done.r1 = f32[2,4,128,128]{3,2,1,0:T(8,128)S(1)} collective-permute-done((f32[2,4,128,128]{3,2,1,0:T(8,128)}, f32[2,4,128,128]{3,2,1,0:T(8,128)S(1)}, u32[]{:S(2)}, u32[]{:S(2)}) %collective-permute-start) | collective-permute-done | bytes 524320 | tf_op jit(solution)/shard_map/ppermute | solution.py:265
  10.4 1.9 %collective-permute-start.6 = (f32[2,4,128,128]{3,2,1,0:T(8,128)S(1)}, f32[2,4,128,128]{3,2,1,0:T(8,128)S(1)}, u32[]{:S(2)}, u32[]{:S(2)}) collective-permute-start(f32[2,4,128,128]{3,2,1,0:T(8,128)S(1)} %collective-permute-done.r1), channel_id=1, source_target_pairs={{15,1},{1,5},{5,9},{9,13},{13,15},{2,12},{12,8},{8,4},{4,0},{0,2},... | collective-permute-start | bytes 1572872 | tf_op jit(solution)/shard_map/ppermute | solution.py:265
  12.3 0.0 collective-permute-start.4
  12.3 3.8 %collective-permute-done.2.r2 = f32[2,4,128,128]{3,2,1,0:T(8,128)S(1)} collective-permute-done((f32[2,4,128,128]{3,2,1,0:T(8,128)S(1)}, f32[2,4,128,128]{3,2,1,0:T(8,128)S(1)}, u32[]{:S(2)}, u32[]{:S(2)}) %collective-permute-start.2) | collective-permute-done | bytes 524320 | tf_op jit(solution)/shard_map/ppermute | solution.py:273
  16.1 0.0 collective-permute-start.5
  16.1 1.8 %collective-permute-start.3 = (f32[2,4,128,128]{3,2,1,0:T(8,128)S(1)}, f32[2,4,128,128]{3,2,1,0:T(8,128)S(1)}, u32[]{:S(2)}, u32[]{:S(2)}) collective-permute-start(f32[2,4,128,128]{3,2,1,0:T(8,128)S(1)} %collective-permute-done.2.r2), channel_id=1, source_target_pairs={{15,1},{1,5},{5,9},{9,13},{13,15},{2,12},{12,8},{8,4},{4,0},{0,2},... | collective-permute-start | bytes 1572872 | tf_op jit(solution)/shard_map/ppermute | solution.py:265
  18.0 3.8 %collective-permute-done.6.r3 = f32[2,4,128,128]{3,2,1,0:T(8,128)S(1)} collective-permute-done((f32[2,4,128,128]{3,2,1,0:T(8,128)S(1)}, f32[2,4,128,128]{3,2,1,0:T(8,128)S(1)}, u32[]{:S(2)}, u32[]{:S(2)}) %collective-permute-start.6) | collective-permute-done | bytes 524320 | tf_op jit(solution)/shard_map/ppermute | solution.py:265
  21.7 0.0 collective-permute-start.8
  21.7 0.0 collective-permute-done.4.t1
  21.7 0.0 collective-permute-done.5.t2
  21.8 3.1 %early.1 = (bf16[1024,1024]{1,0:T(8,128)(2,1)S(1)}, bf16[1024,1024]{1,0:T(8,128)(2,1)S(1)}, bf16[512,1024]{1,0:T(8,128)(2,1)S(1)}, f32[256,1024]{1,0:T(8,128)S(1)}) custom-call(s32[8,24]{1,0:T(8,128)S(1)} %pad_add_fusion.table_ref, f32[2,4,128,128]{3,2,1,0:T(8,128)} %own_hbm.1, f32[2,4,128,128]{3,2,1,0:T(8,128)S(1)} %collective-permute-done.1.own_swap, ...), custom_call_target="tpu_custom_call" | custom-call | tf_op jit(solution)/shard_map/early/pallas_call | solution.py:303
  24.9 2.5 %collective-permute-done.3.r4 = f32[2,4,128,128]{3,2,1,0:T(8,128)S(1)} collective-permute-done((f32[2,4,128,128]{3,2,1,0:T(8,128)S(1)}, f32[2,4,128,128]{3,2,1,0:T(8,128)S(1)}, u32[]{:S(2)}, u32[]{:S(2)}) %collective-permute-start.3) | collective-permute-done | bytes 524320 | tf_op jit(solution)/shard_map/ppermute | solution.py:265
  27.4 0.0 collective-permute-start.7
  27.4 0.0 collective-permute-done.8.t3
  27.4 1.5 %middle.1 = (bf16[1024,1024]{1,0:T(8,128)(2,1)S(1)}, bf16[1024,1024]{1,0:T(8,128)(2,1)S(1)}, f32[256,1024]{1,0:T(8,128)S(1)}) custom-call(s32[8,24]{1,0:T(8,128)S(1)} %pad_add_fusion.table_ref, f32[2,4,128,128]{3,2,1,0:T(8,128)S(1)} %collective-permute-done.3.r4, ...), custom_call_target="tpu_custom_call", output_to_operand_aliasing={{0}: (3, {}), {1}: (4, {}), {2}: (6, {})} | custom-call | tf_op jit(solution)/shard_map/middle/pallas_call | solution.py:321
  28.9 0.4 %collective-permute-done.7.t4 = f32[2,4,128,128]{3,2,1,0:T(8,128)S(1)} collective-permute-done((f32[2,4,128,128]{3,2,1,0:T(8,128)S(1)}, f32[2,4,128,128]{3,2,1,0:T(8,128)S(1)}, u32[]{:S(2)}, u32[]{:S(2)}) %collective-permute-start.7) | collective-permute-done | bytes 524320 | tf_op jit(solution)/shard_map/ppermute | solution.py:265
  29.3 3.7 %late.1 = (f32[2,4,128,128]{3,2,1,0:T(8,128)}, bf16[1024,1024]{1,0:T(8,128)(2,1)S(1)}, bf16[1024,1024]{1,0:T(8,128)(2,1)S(1)}, f32[256,1024]{1,0:T(8,128)S(1)}) custom-call(s32[8,24]{1,0:T(8,128)S(1)} %pad_add_fusion.table_ref, f32[2,4,128,128]{3,2,1,0:T(8,128)S(1)} %collective-permute-done.7.t4, ...), custom_call_target="tpu_custom_call", output_to_operand_aliasing={{1}: (2, {}), {2}: (3, {}), {3}: (5, {})} | custom-call | tf_op jit(solution)/shard_map/late/pallas_call | solution.py:330
  (1 shorter events, 0.0 us)
Async XLA Ops:
  0.0 10.4 %collective-permute-start = (f32[2,4,128,128]{3,2,1,0:T(8,128)}, f32[2,4,128,128]{3,2,1,0:T(8,128)S(1)}, u32[]{:S(2)}, u32[]{:S(2)}) collective-permute-start(f32[2,4,128,128]{3,2,1,0:T(8,128)} %own_hbm.1), channel_id=1, source_target_pairs={{3,1},{1,5},{5,9},{9,13},{13,15},{15,14},{14,12},{12,8},{8,4},{4,0... | collective-permute-start | bytes 1572872 | tf_op jit(solution)/shard_map/ppermute | solution.py:265
  2.9 2.1 %collective-permute-start.1 = (f32[2,4,128,128]{3,2,1,0:T(8,128)}, f32[2,4,128,128]{3,2,1,0:T(8,128)S(1)}, u32[]{:S(2)}, u32[]{:S(2)}) collective-permute-start(f32[2,4,128,128]{3,2,1,0:T(8,128)} %own_hbm.1), channel_id=1, source_target_pairs={{1,0},{0,1},{17,16},{16,17},{3,2},{2,3},{19,18},{18,19},{5,4},{4,5... | collective-permute-start | bytes 1572872 | tf_op jit(solution)/shard_map/ppermute | solution.py:265
  5.1 11.1 %collective-permute-start.2 = (f32[2,4,128,128]{3,2,1,0:T(8,128)S(1)}, f32[2,4,128,128]{3,2,1,0:T(8,128)S(1)}, u32[]{:S(2)}, u32[]{:S(2)}) collective-permute-start(f32[2,4,128,128]{3,2,1,0:T(8,128)S(1)} %collective-permute-done.1.own_swap), channel_id=1, source_target_pairs={{1,5},{5,9},{9,13},{13,15},{12,8},{8,4},{4,0},{0,2},{17,21},{21,25... | collective-permute-start | bytes 1572872 | tf_op jit(solution)/shard_map/ppermute | solution.py:273
  10.4 11.3 %collective-permute-start.6 = (f32[2,4,128,128]{3,2,1,0:T(8,128)S(1)}, f32[2,4,128,128]{3,2,1,0:T(8,128)S(1)}, u32[]{:S(2)}, u32[]{:S(2)}) collective-permute-start(f32[2,4,128,128]{3,2,1,0:T(8,128)S(1)} %collective-permute-done.r1), channel_id=1, source_target_pairs={{15,1},{1,5},{5,9},{9,13},{13,15},{2,12},{12,8},{8,4},{4,0},{0,2},... | collective-permute-start | bytes 1572872 | tf_op jit(solution)/shard_map/ppermute | solution.py:265
  12.3 9.4 %collective-permute-start.4 = (f32[2,4,128,128]{3,2,1,0:T(8,128)S(1)}, f32[2,4,128,128]{3,2,1,0:T(8,128)S(1)}, u32[]{:S(2)}, u32[]{:S(2)}) collective-permute-start(f32[2,4,128,128]{3,2,1,0:T(8,128)S(1)} %collective-permute-done.r1), channel_id=1, source_target_pairs={{1,0},{0,1},{17,16},{16,17},{3,2},{2,3},{19,18},{18,19},{5,4},{4,5... | collective-permute-start | bytes 1572872 | tf_op jit(solution)/shard_map/ppermute | solution.py:265
  16.1 5.6 %collective-permute-start.5 = (f32[2,4,128,128]{3,2,1,0:T(8,128)S(1)}, f32[2,4,128,128]{3,2,1,0:T(8,128)S(1)}, u32[]{:S(2)}, u32[]{:S(2)}) collective-permute-start(f32[2,4,128,128]{3,2,1,0:T(8,128)S(1)} %collective-permute-done.2.r2), channel_id=1, source_target_pairs={{1,0},{0,1},{17,16},{16,17},{3,2},{2,3},{19,18},{18,19},{5,4},{4,5... | collective-permute-start | bytes 1572872 | tf_op jit(solution)/shard_map/ppermute | solution.py:265
  16.1 11.2 %collective-permute-start.3 = (f32[2,4,128,128]{3,2,1,0:T(8,128)S(1)}, f32[2,4,128,128]{3,2,1,0:T(8,128)S(1)}, u32[]{:S(2)}, u32[]{:S(2)}) collective-permute-start(f32[2,4,128,128]{3,2,1,0:T(8,128)S(1)} %collective-permute-done.2.r2), channel_id=1, source_target_pairs={{15,1},{1,5},{5,9},{9,13},{13,15},{2,12},{12,8},{8,4},{4,0},{0,2},... | collective-permute-start | bytes 1572872 | tf_op jit(solution)/shard_map/ppermute | solution.py:265
  21.7 5.6 %collective-permute-start.8 = (f32[2,4,128,128]{3,2,1,0:T(8,128)S(1)}, f32[2,4,128,128]{3,2,1,0:T(8,128)S(1)}, u32[]{:S(2)}, u32[]{:S(2)}) collective-permute-start(f32[2,4,128,128]{3,2,1,0:T(8,128)S(1)} %collective-permute-done.6.r3), channel_id=1, source_target_pairs={{1,0},{0,1},{17,16},{16,17},{3,2},{2,3},{19,18},{18,19},{5,4},{4,5... | collective-permute-start | bytes 1572872 | tf_op jit(solution)/shard_map/ppermute | solution.py:265
  27.4 1.9 %collective-permute-start.7 = (f32[2,4,128,128]{3,2,1,0:T(8,128)S(1)}, f32[2,4,128,128]{3,2,1,0:T(8,128)S(1)}, u32[]{:S(2)}, u32[]{:S(2)}) collective-permute-start(f32[2,4,128,128]{3,2,1,0:T(8,128)S(1)} %collective-permute-done.3.r4), channel_id=1, source_target_pairs={{1,0},{0,1},{17,16},{16,17},{3,2},{2,3},{19,18},{18,19},{5,4},{4,5... | collective-permute-start | bytes 1572872 | tf_op jit(solution)/shard_map/ppermute | solution.py:265

commit v15 on v14

--- a/solution.py
+++ b/solution.py
@@ -110,7 +110,7 @@
     return found
 
 
-def store_piece(piece, plane, group, table_ref, high, low, own=None):
+def store_piece(piece, plane, code_of, high, low, own=None):
     slab, width, edge, _ = piece.shape
     act = 2 * width
 
@@ -119,9 +119,9 @@
         for r in range(slab):
             row = plane * slab + r
             for w in range(width):
-                slot = group * width + w
-                col = pl.ds(pl.multiple_of(table_ref[row, slot] * edge, edge), edge)
-                block = jnp.where(table_ref[row, act + slot] > 0, piece[r, w], 0.0)
+                code = code_of(r, w)
+                col = pl.ds(pl.multiple_of(code % act * edge, edge), edge)
+                block = jnp.where(code < act, piece[r, w], 0.0)
                 block_high, block_low = split(block)
                 at = pl.ds(pl.multiple_of(row * edge, edge), edge)
                 high[at, col] = block_high
@@ -131,6 +131,18 @@
                     own[pl.ds((slab + r) * edge, edge), col] = block_low
 
 
+def table_codes(table_ref, plane, group, slab, width):
+    row = jnp.maximum(plane, 0) * slab
+    return lambda r, w: table_ref[row + r, group * width + w]
+
+
+T3, R4, T4, OWN, KEPT = 0, 1, 2, 3, 4
+
+
+def noted_codes(notes, kind, slab, width):
+    return lambda r, w: notes[0, (kind * slab + r) * width + w]
+
+
 def add_plane(plane, left, high, low, part_ref):
     depth, tile = part_ref.shape[0], 256
 
@@ -144,51 +156,76 @@
 
 def early_kernel(
     tables, table_ref, own_hbm, own_swap, r1, r2, t1, t2, r3,
-    high, low, left, part_ref, own_ref, own_sem,
+    high, low, left, part_ref, notes_ref, own_ref, own_sem,
 ):
     place, lane = lax.axis_index("blk"), lax.axis_index("depth")
     near, far = tables
+    slab, width = own_swap.shape[:2]
+    act = 2 * width
     own_copy = pltpu.make_async_copy(own_hbm, own_ref, own_sem)
     own_copy.start()
     here, there = lookup(near, place, lane), lookup(near, place, 1 - lane)
+    far_here, far_there = lookup(far, place, lane), lookup(far, place, 1 - lane)
     part_ref[...] = jnp.zeros_like(part_ref)
-    store_piece(own_swap, place, 1 - lane, table_ref, high, low, left)
-    store_piece(r1, here, lane, table_ref, high, low)
-    store_piece(r2, here, 1 - lane, table_ref, high, low)
-    store_piece(t1, there, 1 - lane, table_ref, high, low)
-    store_piece(t2, there, lane, table_ref, high, low)
-    store_piece(r3, lookup(far, place, lane), lane, table_ref, high, low)
+
+    def codes(plane, group):
+        return table_codes(table_ref, plane, group, slab, width)
+
+    kinds = ((far_there, 1 - lane), (far_here, 1 - lane), (far_there, lane), (place, lane))
+    notes = jnp.zeros(notes_ref.shape, jnp.int32)
+    index = lax.broadcasted_iota(jnp.int32, notes.shape, 1)
+    for kind, (plane, group) in enumerate(kinds):
+        for r in range(slab):
+            for w in range(width):
+                at = (kind * slab + r) * width + w
+                notes = jnp.where(index == at, codes(plane, group)(r, w), notes)
+    for r in range(slab):
+        notes = jnp.where(
+            index == KEPT * slab * width + r, table_ref[place * slab + r, act], notes
+        )
+    notes_ref[...] = notes
+
+    store_piece(own_swap, place, codes(place, 1 - lane), high, low, left)
+    store_piece(r1, here, codes(here, lane), high, low)
+    store_piece(r2, here, codes(here, 1 - lane), high, low)
+    store_piece(t1, there, codes(there, 1 - lane), high, low)
+    store_piece(t2, there, codes(there, lane), high, low)
+    store_piece(r3, far_here, codes(far_here, lane), high, low)
     own_copy.wait()
-    store_piece(own_ref, place, lane, table_ref, high, low, left)
+    store_piece(own_ref, place, codes(place, lane), high, low, left)
     for plane in (place, here, there):
         add_plane(plane, left, high, low, part_ref)
 
 
 def middle_kernel(
-    tables, table_ref, r4, t3, high_in, low_in, left, part_in, high, low, part_ref
+    tables, notes_ref, r4, t3, high_in, low_in, left, part_in, high, low, part_ref
 ):
     place, lane = lax.axis_index("blk"), lax.axis_index("depth")
-    far = tables[1]
-    here, there = lookup(far, place, lane), lookup(far, place, 1 - lane)
-    store_piece(t3, there, 1 - lane, table_ref, high, low)
-    store_piece(r4, here, 1 - lane, table_ref, high, low)
+    here, there = lookup(tables[1], place, lane), lookup(tables[1], place, 1 - lane)
+    slab, width = r4.shape[:2]
+    notes = notes_ref[...]
+    store_piece(t3, there, noted_codes(notes, T3, slab, width), high, low)
+    store_piece(r4, here, noted_codes(notes, R4, slab, width), high, low)
     add_plane(here, left, high, low, part_ref)
 
 
 def late_kernel(
-    tables, table_ref, t4, high_in, low_in, left, part_in,
+    tables, notes_ref, t4, high_in, low_in, left, part_in,
     out_hbm, high, low, square, square_parts, out_ref, out_sem,
 ):
     place, lane = lax.axis_index("blk"), lax.axis_index("depth")
-    group = lax.axis_index("panel") * 2 + lane
     there = lookup(tables[1], place, 1 - lane)
-    store_piece(t4, there, lane, table_ref, high, low)
-    add_plane(there, left, high, low, square)
     slab, width, edge, _ = out_ref.shape
     act = 2 * width
+    holds = lax.axis_index("panel") == 0
+    notes = notes_ref[...]
+    own_codes = noted_codes(notes, OWN, slab, width)
+    store_piece(t4, there, noted_codes(notes, T4, slab, width), high, low)
+    add_plane(there, left, high, low, square)
     for r in range(slab):
+        flags = notes[0, KEPT * slab * width + r]
         for c in range(square.shape[1] // edge):
-            kept = table_ref[place * slab + r, 2 * act + c] > 0
+            kept = (flags >> c) % 2 > 0
             col = pl.ds(c * edge, edge)
             block = jnp.where(kept, square[pl.ds(r * edge, edge), col], 0.0)
             block_high, block_low = split(block)
@@ -196,23 +233,19 @@
             square_parts[pl.ds((2 * r + 1) * edge, edge), col] = block_low
     copies = []
     for r in range(slab):
-        row = place * slab + r
         left_parts = square_parts[pl.ds(2 * r * edge, 2 * edge), :]
         for w in range(0, width, 2):
-            slots = [jnp.minimum(group * width + w + k, act - 1) for k in range(2)]
-            cols = [
-                pl.ds(pl.multiple_of(table_ref[row, slot] * edge, edge), edge) for slot in slots
-            ]
+            codes = [own_codes(r, w + k) for k in range(2)]
+            cols = [pl.ds(pl.multiple_of(code % act * edge, edge), edge) for code in codes]
             cube = stacked_dot(
                 left_parts,
                 jnp.concatenate([high[:, col] for col in cols], axis=1),
                 jnp.concatenate([low[:, col] for col in cols], axis=1),
             )
             for k in range(2):
-                there = (group * width + w + k < act) & (table_ref[row, act + slots[k]] > 0)
                 value = 3.0 * square[pl.ds(r * edge, edge), cols[k]]
                 value = value - 2.0 * cube[:, k * edge : (k + 1) * edge]
-                out_ref[r, w + k] = jnp.where(there, value, 0.0)
+                out_ref[r, w + k] = jnp.where(holds & (codes[k] < act), value, 0.0)
             ready = (r, pl.ds(w, 2))
             copies.append(
                 pltpu.make_async_copy(out_ref.at[ready], out_hbm.at[ready], out_sem.at[len(copies)])
@@ -236,8 +269,9 @@
     filled = jnp.sum(
         jnp.where(at[:, None, :] == jnp.arange(act, dtype=jnp.int32)[None, :, None], ids, 0), axis=2
     )
-    order = jnp.where(here, slots, filled)
-    return jnp.concatenate([order, here.astype(jnp.int32), taken.astype(jnp.int32)], axis=1)
+    codes = jnp.where(here, slots, filled + act)
+    kept = jnp.sum(jnp.where(taken, 1 << ids, 0), axis=1, keepdims=True)
+    return jnp.concatenate([codes, kept], axis=1).astype(jnp.int32)
 
 
 def gather_local(x_blocks, columns):
@@ -300,16 +334,17 @@
     def held(*arrays):
         return [pltpu.with_memory_space_constraint(a, pltpu.VMEM) for a in arrays]
 
-    high, low, left, part = pl.pallas_call(
+    high, low, left, part, notes = pl.pallas_call(
         functools.partial(early_kernel, tables),
         out_shape=[
             jax.ShapeDtypeStruct((order, order), jnp.bfloat16),
             jax.ShapeDtypeStruct((order, order), jnp.bfloat16),
             jax.ShapeDtypeStruct((2 * own, order), jnp.bfloat16),
             jax.ShapeDtypeStruct((own, order), jnp.float32),
+            jax.ShapeDtypeStruct((8, 128), jnp.int32),
         ],
         in_specs=[smem] + [pl.BlockSpec(memory_space=pltpu.HBM)] + [vmem] * 6,
-        out_specs=[vmem] * 4,
+        out_specs=[vmem] * 5,
         scratch_shapes=[pltpu.VMEM(x_blocks.shape, jnp.float32), pltpu.SemaphoreType.DMA],
         compiler_params=params,
         name="early",
@@ -321,16 +356,16 @@
     high, low, part = pl.pallas_call(
         functools.partial(middle_kernel, tables),
         out_shape=dense,
-        in_specs=[smem] + [vmem] * 6,
+        in_specs=[vmem] * 7,
         out_specs=[vmem] * 3,
         input_output_aliases={3: 0, 4: 1, 6: 2},
         compiler_params=params,
         name="middle",
-    )(table, r4, t3, *held(high, low, left, part))
+    )(notes, r4, t3, *held(high, low, left, part))
     out, _, _, _ = pl.pallas_call(
         functools.partial(late_kernel, tables),
         out_shape=[jax.ShapeDtypeStruct(x_blocks.shape, jnp.float32)] + dense,
-        in_specs=[smem] + [vmem] * 5,
+        in_specs=[vmem] * 6,
         out_specs=[pl.BlockSpec(memory_space=pltpu.HBM)] + [vmem] * 3,
         input_output_aliases={2: 1, 3: 2, 5: 3},
         scratch_shapes=[
@@ -340,7 +375,7 @@
         ],
         compiler_params=params,
         name="late",
-    )(table, t4, *held(high, low, left, part))
+    )(notes, t4, *held(high, low, left, part))
     return out
 
 
@@ -349,7 +384,7 @@
     rows, slots = columns.shape
     _, chains, panels, lanes = (lax.axis_size(axis) for axis in AXES)
     full = rows <= slots and rows == lanes * width and width % 2 == 0
-    if full and rows <= 8 and edge % 128 == 0 and panels >= 2 and lanes == 2 and chains == 4:
+    if full and rows <= 8 and slab == 2 and edge == 128 and panels >= 2 and lanes == 2 and chains == 4:
         return gather_local(x_blocks, columns)
     return ring_local(x_blocks, columns)
 

time: 33.2 us -> 32.7 us (0.985)
  waiting for transfers between devices: 12.7 us -> 13.7 us
  Pallas kernels: 8.32 us -> 7.36 us
  other arithmetic: 2.86 us -> 2.24 us
    ppermute x8, waiting for transfers between devices: 8.91 us -> 9.95 us  [move(): return lax.ppermute(block, AXES, route)]
    convert_element_type x1 -> x0, other arithmetic: 0.69 us -> none  [slot_table(): count = jnp.sum(here.astype(jnp.int32), axis=1, keepdims=True)]
    pallas_call x1, Pallas kernels: 1.54 us -> 1.06 us  [gather_local(): pl.pallas_call(functools.partial(middle_kernel, tables), out_shape=dense,...]
    pallas_call x1, Pallas kernels: 3.66 us -> 3.21 us  [gather_local(): pl.pallas_call(functools.partial(late_kernel, tables), out_shape=[jax.Sha...]
  transfers between devices with their start and end apart: 9 -> 9, of which waited for: 6 -> 6; matrix products, arithmetic and copies ran while one was open for 9% -> 7% of each run, Pallas kernels for 14% -> 13%
where the time goes in v15:
time: 32.7 us; the launch traced here: 32.5 us
  waiting for transfers between devices  13.7 us (42%)
  starting transfers between devices  8.99 us (27%)
  Pallas kernels  7.36 us (23%)
  other arithmetic  2.24 us (7%)
    ppermute x8, waiting for transfers between devices, move(): return lax.ppermute(block, AXES, route)  9.95 us
    ppermute x8, starting transfers between devices, move(): return lax.ppermute(block, AXES, route)  6.72 us
    ppermute x1, waiting for transfers between devices, move_only(): return lax.ppermute(block, AXES, route)  3.79 us
    pallas_call x1, Pallas kernels, gather_local(): pl.pallas_call(functools.partial(late_kernel, tables), out_shape=[jax.Sha...  3.21 us
    pallas_call x1, Pallas kernels, gather_local(): pl.pallas_call(functools.partial(early_kernel, tables), out_shape=[jax.Sh...  3.1 us
    ppermute x1, starting transfers between devices, move_only(): return lax.ppermute(block, AXES, route)  2.28 us
    pallas_call x1, Pallas kernels, gather_local(): pl.pallas_call(functools.partial(middle_kernel, tables), out_shape=dense,...  1.06 us
    reduce_sum x1, other arithmetic, slot_table(): count = jnp.sum(here.astype(jnp.int32), axis=1, keepdims=True)  0.8 us
  transfers between devices with their start and end apart: 9, of which 6 were waited for; matrix products, arithmetic and copies ran while one was open for 7% of the time, Pallas kernels for 13%

profile of v15, /device:TPU:0, one launch (start us, length us, event | category | flops | bytes accessed | tf_op | source)
XLA Modules:
  0.0 32.5 jit_solution(18321571770874358040)
XLA Ops:
  0.0 2.9 %collective-permute-start = (f32[2,4,128,128]{3,2,1,0:T(8,128)}, f32[2,4,128,128]{3,2,1,0:T(8,128)S(1)}, u32[]{:S(2)}, u32[]{:S(2)}) collective-permute-start(f32[2,4,128,128]{3,2,1,0:T(8,128)} %own_hbm.1), channel_id=1, source_target_pairs={{3,1},{1,5},{5,9},{9,13},{13,15},{15,14},{14,12},{12,8},{8,4},{4,0... | collective-permute-start | bytes 1572872 | tf_op jit(solution)/shard_map/ppermute | solution.py:299
  2.9 0.0 collective-permute-start.1
  2.9 0.8 %fusion.1 = (s32[8]{0:T(128)S(1)}, s32[8,8]{1,0:T(8,128)S(1)}) fusion(s32[8,16]{1,0:T(8,128)} %param.3), kind=kLoop, calls=%fused_computation.7 | loop fusion | flops 184 | bytes 544 | tf_op jit(solution)/shard_map/reduce_sum | solution.py:264
  3.7 0.1 fusion
  3.9 0.2 convert_reduce_fusion
  4.1 1.0 %collective-permute-done.1.own_swap = f32[2,4,128,128]{3,2,1,0:T(8,128)S(1)} collective-permute-done((f32[2,4,128,128]{3,2,1,0:T(8,128)}, f32[2,4,128,128]{3,2,1,0:T(8,128)S(1)}, u32[]{:S(2)}, u32[]{:S(2)}) %collective-permute-start.1) | collective-permute-done | bytes 524320 | tf_op jit(solution)/shard_map/ppermute | solution.py:299
  5.1 2.3 %collective-permute-start.2 = (f32[2,4,128,128]{3,2,1,0:T(8,128)S(1)}, f32[2,4,128,128]{3,2,1,0:T(8,128)S(1)}, u32[]{:S(2)}, u32[]{:S(2)}) collective-permute-start(f32[2,4,128,128]{3,2,1,0:T(8,128)S(1)} %collective-permute-done.1.own_swap), channel_id=1, source_target_pairs={{1,5},{5,9},{9,13},{13,15},{12,8},{8,4},{4,0},{0,2},{17,21},{21,25... | collective-permute-start | bytes 1572872 | tf_op jit(solution)/shard_map/ppermute | solution.py:307
  7.3 0.1 add_select_fusion
  7.5 0.1 copy.10
  7.5 0.2 select_reduce_fusion
  7.8 0.7 %compare_select_fusion = s32[8,8]{1,0:T(8,128)S(1)} fusion(s32[8,8]{1,0:T(8,128)S(1)} %select_reduce_fusion, s32[8,16]{1,0:T(8,128)} %param.3), kind=kLoop, calls=%fused_computation.5 | loop fusion | flops 192 | bytes 768 | tf_op jit(solution)/shard_map/jit(_where)/select_n | solution.py:272
  8.5 0.1 pad_add_fusion.table_ref
  8.5 1.9 %collective-permute-done.r1 = f32[2,4,128,128]{3,2,1,0:T(8,128)S(1)} collective-permute-done((f32[2,4,128,128]{3,2,1,0:T(8,128)}, f32[2,4,128,128]{3,2,1,0:T(8,128)S(1)}, u32[]{:S(2)}, u32[]{:S(2)}) %collective-permute-start) | collective-permute-done | bytes 524320 | tf_op jit(solution)/shard_map/ppermute | solution.py:299
  10.4 1.9 %collective-permute-start.5 = (f32[2,4,128,128]{3,2,1,0:T(8,128)S(1)}, f32[2,4,128,128]{3,2,1,0:T(8,128)S(1)}, u32[]{:S(2)}, u32[]{:S(2)}) collective-permute-start(f32[2,4,128,128]{3,2,1,0:T(8,128)S(1)} %collective-permute-done.r1), channel_id=1, source_target_pairs={{15,1},{1,5},{5,9},{9,13},{13,15},{2,12},{12,8},{8,4},{4,0},{0,2},... | collective-permute-start | bytes 1572872 | tf_op jit(solution)/shard_map/ppermute | solution.py:299
  12.3 0.0 collective-permute-start.3
  12.3 3.8 %collective-permute-done.2.r2 = f32[2,4,128,128]{3,2,1,0:T(8,128)S(1)} collective-permute-done((f32[2,4,128,128]{3,2,1,0:T(8,128)S(1)}, f32[2,4,128,128]{3,2,1,0:T(8,128)S(1)}, u32[]{:S(2)}, u32[]{:S(2)}) %collective-permute-start.2) | collective-permute-done | bytes 524320 | tf_op jit(solution)/shard_map/ppermute | solution.py:307
  16.1 0.0 collective-permute-start.4
  16.1 1.8 %collective-permute-start.6 = (f32[2,4,128,128]{3,2,1,0:T(8,128)S(1)}, f32[2,4,128,128]{3,2,1,0:T(8,128)S(1)}, u32[]{:S(2)}, u32[]{:S(2)}) collective-permute-start(f32[2,4,128,128]{3,2,1,0:T(8,128)S(1)} %collective-permute-done.2.r2), channel_id=1, source_target_pairs={{15,1},{1,5},{5,9},{9,13},{13,15},{2,12},{12,8},{8,4},{4,0},{0,2},... | collective-permute-start | bytes 1572872 | tf_op jit(solution)/shard_map/ppermute | solution.py:299
  18.0 3.8 %collective-permute-done.5.r3 = f32[2,4,128,128]{3,2,1,0:T(8,128)S(1)} collective-permute-done((f32[2,4,128,128]{3,2,1,0:T(8,128)S(1)}, f32[2,4,128,128]{3,2,1,0:T(8,128)S(1)}, u32[]{:S(2)}, u32[]{:S(2)}) %collective-permute-start.5) | collective-permute-done | bytes 524320 | tf_op jit(solution)/shard_map/ppermute | solution.py:299
  21.7 0.0 collective-permute-start.8
  21.7 0.0 collective-permute-done.3.t1
  21.7 0.0 collective-permute-done.4.t2
  21.8 3.1 %early.1 = (bf16[1024,1024]{1,0:T(8,128)(2,1)S(1)}, bf16[1024,1024]{1,0:T(8,128)(2,1)S(1)}, bf16[512,1024]{1,0:T(8,128)(2,1)S(1)}, f32[256,1024]{1,0:T(8,128)S(1)}, s32[8,128]{1,0:T(8,128)S(1)}) custom-call(s32[8,9]{1,0:T(8,128)S(1)} %pad_add_fusion.table_ref, f32[2,4,128,128]{3,2,1,0:T(8,128)} %own_hbm.1, ...), custom_call_target="tpu_custom_call" | custom-call | tf_op jit(solution)/shard_map/early/pallas_call | solution.py:337
  24.9 2.5 %collective-permute-done.6.r4 = f32[2,4,128,128]{3,2,1,0:T(8,128)S(1)} collective-permute-done((f32[2,4,128,128]{3,2,1,0:T(8,128)S(1)}, f32[2,4,128,128]{3,2,1,0:T(8,128)S(1)}, u32[]{:S(2)}, u32[]{:S(2)}) %collective-permute-start.6) | collective-permute-done | bytes 524320 | tf_op jit(solution)/shard_map/ppermute | solution.py:299
  27.4 0.0 collective-permute-start.7
  27.4 0.0 collective-permute-done.8.t3
  27.4 1.1 %middle.1 = (bf16[1024,1024]{1,0:T(8,128)(2,1)S(1)}, bf16[1024,1024]{1,0:T(8,128)(2,1)S(1)}, f32[256,1024]{1,0:T(8,128)S(1)}) custom-call(s32[8,128]{1,0:T(8,128)S(1)} %get-tuple-element.20.notes_ref, f32[2,4,128,128]{3,2,1,0:T(8,128)S(1)} %collective-permute-done.6.r4, ...), custom_call_target="tpu_custom_call", output_to_operand_aliasing={{0}: (3, {}), {1}: (4, {}), {2}: (6, {})} | custom-call | tf_op jit(solution)/shard_map/middle/pallas_call | solution.py:356
  28.4 0.8 %collective-permute-done.7.t4 = f32[2,4,128,128]{3,2,1,0:T(8,128)S(1)} collective-permute-done((f32[2,4,128,128]{3,2,1,0:T(8,128)S(1)}, f32[2,4,128,128]{3,2,1,0:T(8,128)S(1)}, u32[]{:S(2)}, u32[]{:S(2)}) %collective-permute-start.7) | collective-permute-done | bytes 524320 | tf_op jit(solution)/shard_map/ppermute | solution.py:299
  29.3 3.2 %late.1 = (f32[2,4,128,128]{3,2,1,0:T(8,128)}, bf16[1024,1024]{1,0:T(8,128)(2,1)S(1)}, bf16[1024,1024]{1,0:T(8,128)(2,1)S(1)}, f32[256,1024]{1,0:T(8,128)S(1)}) custom-call(s32[8,128]{1,0:T(8,128)S(1)} %get-tuple-element.20.notes_ref, f32[2,4,128,128]{3,2,1,0:T(8,128)S(1)} %collective-permute-done.7.t4, ...), custom_call_target="tpu_custom_call", output_to_operand_aliasing={{1}: (2, {}), {2}: (3, {}), {3}: (5, {})} | custom-call | tf_op jit(solution)/shard_map/late/pallas_call | solution.py:365
  (3 shorter events, 0.0 us)
Async XLA Ops:
  0.0 10.4 %collective-permute-start = (f32[2,4,128,128]{3,2,1,0:T(8,128)}, f32[2,4,128,128]{3,2,1,0:T(8,128)S(1)}, u32[]{:S(2)}, u32[]{:S(2)}) collective-permute-start(f32[2,4,128,128]{3,2,1,0:T(8,128)} %own_hbm.1), channel_id=1, source_target_pairs={{3,1},{1,5},{5,9},{9,13},{13,15},{15,14},{14,12},{12,8},{8,4},{4,0... | collective-permute-start | bytes 1572872 | tf_op jit(solution)/shard_map/ppermute | solution.py:299
  2.9 2.1 %collective-permute-start.1 = (f32[2,4,128,128]{3,2,1,0:T(8,128)}, f32[2,4,128,128]{3,2,1,0:T(8,128)S(1)}, u32[]{:S(2)}, u32[]{:S(2)}) collective-permute-start(f32[2,4,128,128]{3,2,1,0:T(8,128)} %own_hbm.1), channel_id=1, source_target_pairs={{1,0},{0,1},{17,16},{16,17},{3,2},{2,3},{19,18},{18,19},{5,4},{4,5... | collective-permute-start | bytes 1572872 | tf_op jit(solution)/shard_map/ppermute | solution.py:299
  5.1 11.1 %collective-permute-start.2 = (f32[2,4,128,128]{3,2,1,0:T(8,128)S(1)}, f32[2,4,128,128]{3,2,1,0:T(8,128)S(1)}, u32[]{:S(2)}, u32[]{:S(2)}) collective-permute-start(f32[2,4,128,128]{3,2,1,0:T(8,128)S(1)} %collective-permute-done.1.own_swap), channel_id=1, source_target_pairs={{1,5},{5,9},{9,13},{13,15},{12,8},{8,4},{4,0},{0,2},{17,21},{21,25... | collective-permute-start | bytes 1572872 | tf_op jit(solution)/shard_map/ppermute | solution.py:307
  10.4 11.3 %collective-permute-start.5 = (f32[2,4,128,128]{3,2,1,0:T(8,128)S(1)}, f32[2,4,128,128]{3,2,1,0:T(8,128)S(1)}, u32[]{:S(2)}, u32[]{:S(2)}) collective-permute-start(f32[2,4,128,128]{3,2,1,0:T(8,128)S(1)} %collective-permute-done.r1), channel_id=1, source_target_pairs={{15,1},{1,5},{5,9},{9,13},{13,15},{2,12},{12,8},{8,4},{4,0},{0,2},... | collective-permute-start | bytes 1572872 | tf_op jit(solution)/shard_map/ppermute | solution.py:299
  12.3 9.4 %collective-permute-start.3 = (f32[2,4,128,128]{3,2,1,0:T(8,128)S(1)}, f32[2,4,128,128]{3,2,1,0:T(8,128)S(1)}, u32[]{:S(2)}, u32[]{:S(2)}) collective-permute-start(f32[2,4,128,128]{3,2,1,0:T(8,128)S(1)} %collective-permute-done.r1), channel_id=1, source_target_pairs={{1,0},{0,1},{17,16},{16,17},{3,2},{2,3},{19,18},{18,19},{5,4},{4,5... | collective-permute-start | bytes 1572872 | tf_op jit(solution)/shard_map/ppermute | solution.py:299
  16.1 5.6 %collective-permute-start.4 = (f32[2,4,128,128]{3,2,1,0:T(8,128)S(1)}, f32[2,4,128,128]{3,2,1,0:T(8,128)S(1)}, u32[]{:S(2)}, u32[]{:S(2)}) collective-permute-start(f32[2,4,128,128]{3,2,1,0:T(8,128)S(1)} %collective-permute-done.2.r2), channel_id=1, source_target_pairs={{1,0},{0,1},{17,16},{16,17},{3,2},{2,3},{19,18},{18,19},{5,4},{4,5... | collective-permute-start | bytes 1572872 | tf_op jit(solution)/shard_map/ppermute | solution.py:299
  16.1 11.2 %collective-permute-start.6 = (f32[2,4,128,128]{3,2,1,0:T(8,128)S(1)}, f32[2,4,128,128]{3,2,1,0:T(8,128)S(1)}, u32[]{:S(2)}, u32[]{:S(2)}) collective-permute-start(f32[2,4,128,128]{3,2,1,0:T(8,128)S(1)} %collective-permute-done.2.r2), channel_id=1, source_target_pairs={{15,1},{1,5},{5,9},{9,13},{13,15},{2,12},{12,8},{8,4},{4,0},{0,2},... | collective-permute-start | bytes 1572872 | tf_op jit(solution)/shard_map/ppermute | solution.py:299
  21.7 5.6 %collective-permute-start.8 = (f32[2,4,128,128]{3,2,1,0:T(8,128)S(1)}, f32[2,4,128,128]{3,2,1,0:T(8,128)S(1)}, u32[]{:S(2)}, u32[]{:S(2)}) collective-permute-start(f32[2,4,128,128]{3,2,1,0:T(8,128)S(1)} %collective-permute-done.5.r3), channel_id=1, source_target_pairs={{1,0},{0,1},{17,16},{16,17},{3,2},{2,3},{19,18},{18,19},{5,4},{4,5... | collective-permute-start | bytes 1572872 | tf_op jit(solution)/shard_map/ppermute | solution.py:299
  27.4 1.9 %collective-permute-start.7 = (f32[2,4,128,128]{3,2,1,0:T(8,128)S(1)}, f32[2,4,128,128]{3,2,1,0:T(8,128)S(1)}, u32[]{:S(2)}, u32[]{:S(2)}) collective-permute-start(f32[2,4,128,128]{3,2,1,0:T(8,128)S(1)} %collective-permute-done.6.r4), channel_id=1, source_target_pairs={{1,0},{0,1},{17,16},{16,17},{3,2},{2,3},{19,18},{18,19},{5,4},{4,5... | collective-permute-start | bytes 1572872 | tf_op jit(solution)/shard_map/ppermute | solution.py:299

commit v16 on v15

--- a/solution.py
+++ b/solution.py
@@ -110,16 +110,16 @@
     return found
 
 
-def store_piece(piece, plane, code_of, high, low, own=None):
-    slab, width, edge, _ = piece.shape
+def store_piece(piece, plane, code_of, high, low, own=None, slab=2, first=0):
+    count, width, edge, _ = piece.shape
     act = 2 * width
 
     @pl.when(plane >= 0)
     def _():
-        for r in range(slab):
-            row = plane * slab + r
+        for r in range(count):
+            row = plane * slab + first + r
             for w in range(width):
-                code = code_of(r, w)
+                code = code_of(first + r, w)
                 col = pl.ds(pl.multiple_of(code % act * edge, edge), edge)
                 block = jnp.where(code < act, piece[r, w], 0.0)
                 block_high, block_low = split(block)
@@ -198,19 +198,21 @@
 
 
 def middle_kernel(
-    tables, notes_ref, r4, t3, high_in, low_in, left, part_in, high, low, part_ref
+    tables, notes_ref, r4a, r4b, t3, t4a, high_in, low_in, left, part_in, high, low, part_ref
 ):
     place, lane = lax.axis_index("blk"), lax.axis_index("depth")
     here, there = lookup(tables[1], place, lane), lookup(tables[1], place, 1 - lane)
-    slab, width = r4.shape[:2]
+    slab, width = t3.shape[:2]
     notes = notes_ref[...]
     store_piece(t3, there, noted_codes(notes, T3, slab, width), high, low)
-    store_piece(r4, here, noted_codes(notes, R4, slab, width), high, low)
+    store_piece(r4a, here, noted_codes(notes, R4, slab, width), high, low)
+    store_piece(t4a, there, noted_codes(notes, T4, slab, width), high, low)
+    store_piece(r4b, here, noted_codes(notes, R4, slab, width), high, low, first=1)
     add_plane(here, left, high, low, part_ref)
 
 
 def late_kernel(
-    tables, notes_ref, t4, high_in, low_in, left, part_in,
+    tables, notes_ref, t4b, high_in, low_in, left, part_in,
     out_hbm, high, low, square, square_parts, out_ref, out_sem,
 ):
     place, lane = lax.axis_index("blk"), lax.axis_index("depth")
@@ -220,7 +222,7 @@
     holds = lax.axis_index("panel") == 0
     notes = notes_ref[...]
     own_codes = noted_codes(notes, OWN, slab, width)
-    store_piece(t4, there, noted_codes(notes, T4, slab, width), high, low)
+    store_piece(t4b, there, noted_codes(notes, T4, slab, width), high, low, first=1)
     add_plane(there, left, high, low, square)
     for r in range(slab):
         flags = notes[0, KEPT * slab * width + r]
@@ -323,7 +325,7 @@
     r1, table = lax.optimization_barrier((r1, table))
     r3 = move(r1, second)
     t1 = swap(r1)
-    r4 = move(r2, second)
+    r4a, r4b = move(r2[:1], second), move(r2[1:], second)
     t2 = swap(r2)
 
     order, own = rows * edge, slab * edge
@@ -350,18 +352,20 @@
         name="early",
     )(table, pltpu.with_memory_space_constraint(x_blocks, pltpu.HBM), own_swap, r1, r2, t1, t2, r3)
     t3 = swap(r3)
-    r4, part = lax.optimization_barrier((r4, part))
-    t4 = swap(r4)
+    r4a, part = lax.optimization_barrier((r4a, part))
+    t4a = swap(r4a)
+    r4b, t4a = lax.optimization_barrier((r4b, t4a))
+    t4b = swap(r4b)
     dense = [jax.ShapeDtypeStruct(a.shape, a.dtype) for a in (high, low, part)]
     high, low, part = pl.pallas_call(
         functools.partial(middle_kernel, tables),
         out_shape=dense,
-        in_specs=[vmem] * 7,
+        in_specs=[vmem] * 9,
         out_specs=[vmem] * 3,
-        input_output_aliases={3: 0, 4: 1, 6: 2},
+        input_output_aliases={5: 0, 6: 1, 8: 2},
         compiler_params=params,
         name="middle",
-    )(notes, r4, t3, *held(high, low, left, part))
+    )(notes, r4a, r4b, t3, t4a, *held(high, low, left, part))
     out, _, _, _ = pl.pallas_call(
         functools.partial(late_kernel, tables),
         out_shape=[jax.ShapeDtypeStruct(x_blocks.shape, jnp.float32)] + dense,
@@ -375,7 +379,7 @@
         ],
         compiler_params=params,
         name="late",
-    )(notes, t4, *held(high, low, left, part))
+    )(notes, t4b, *held(high, low, left, part))
     return out
 
 

time: 32.7 us -> 32.3 us (0.988)
  waiting for transfers between devices: 13.7 us -> 10 us
  starting transfers between devices: 8.99 us -> 11.9 us
    ppermute x8 -> x10, waiting for transfers between devices: 9.95 us -> 6.25 us  [move(): return lax.ppermute(block, AXES, route)]
    ppermute x8 -> x10, starting transfers between devices: 6.72 us -> 9.67 us  [move(): return lax.ppermute(block, AXES, route)]
  transfers between devices with their start and end apart: 9 -> 11, of which waited for: 6 -> 6; matrix products, arithmetic and copies ran while one was open for 7% -> 7% of each run, Pallas kernels for 13% -> 14%
where the time goes in v16:
time: 32.3 us; the launch traced here: 32 us
  starting transfers between devices  11.9 us (37%)
  waiting for transfers between devices  10 us (31%)
  Pallas kernels  7.62 us (24%)
  other arithmetic  2.24 us (7%)
    ppermute x10, starting transfers between devices, move(): return lax.ppermute(block, AXES, route)  9.67 us
    ppermute x10, waiting for transfers between devices, move(): return lax.ppermute(block, AXES, route)  6.25 us
    ppermute x1, waiting for transfers between devices, move_only(): return lax.ppermute(block, AXES, route)  3.79 us
    pallas_call x1, Pallas kernels, gather_local(): pl.pallas_call(functools.partial(early_kernel, tables), out_shape=[jax.Sh...  3.14 us
    pallas_call x1, Pallas kernels, gather_local(): pl.pallas_call(functools.partial(late_kernel, tables), out_shape=[jax.Sha...  3.13 us
    ppermute x1, starting transfers between devices, move_only(): return lax.ppermute(block, AXES, route)  2.28 us
    pallas_call x1, Pallas kernels, gather_local(): pl.pallas_call(functools.partial(middle_kernel, tables), out_shape=dense,...  1.34 us
    reduce_sum x1, other arithmetic, slot_table(): count = jnp.sum(here.astype(jnp.int32), axis=1, keepdims=True)  0.8 us
  transfers between devices with their start and end apart: 11, of which 6 were waited for; matrix products, arithmetic and copies ran while one was open for 7% of the time, Pallas kernels for 14%

profile of v16, /device:TPU:0, one launch (start us, length us, event | category | flops | bytes accessed | tf_op | source)
XLA Modules:
  0.0 32.0 jit_solution(2048467945887015866)
XLA Ops:
  0.0 2.9 %collective-permute-start = (f32[2,4,128,128]{3,2,1,0:T(8,128)}, f32[2,4,128,128]{3,2,1,0:T(8,128)S(1)}, u32[]{:S(2)}, u32[]{:S(2)}) collective-permute-start(f32[2,4,128,128]{3,2,1,0:T(8,128)} %own_hbm.1), channel_id=1, source_target_pairs={{3,1},{1,5},{5,9},{9,13},{13,15},{15,14},{14,12},{12,8},{8,4},{4,0... | collective-permute-start | bytes 1572872 | tf_op jit(solution)/shard_map/ppermute | solution.py:301
  2.9 0.0 collective-permute-start.1
  2.9 0.8 %fusion.1 = (s32[8]{0:T(128)S(1)}, s32[8,8]{1,0:T(8,128)S(1)}) fusion(s32[8,16]{1,0:T(8,128)} %param.3), kind=kLoop, calls=%fused_computation.7 | loop fusion | flops 184 | bytes 544 | tf_op jit(solution)/shard_map/reduce_sum | solution.py:266
  3.7 0.1 fusion
  3.9 0.2 convert_reduce_fusion
  4.1 1.0 %collective-permute-done.1.own_swap = f32[2,4,128,128]{3,2,1,0:T(8,128)S(1)} collective-permute-done((f32[2,4,128,128]{3,2,1,0:T(8,128)}, f32[2,4,128,128]{3,2,1,0:T(8,128)S(1)}, u32[]{:S(2)}, u32[]{:S(2)}) %collective-permute-start.1) | collective-permute-done | bytes 524320 | tf_op jit(solution)/shard_map/ppermute | solution.py:301
  5.1 2.3 %collective-permute-start.2 = (f32[2,4,128,128]{3,2,1,0:T(8,128)S(1)}, f32[2,4,128,128]{3,2,1,0:T(8,128)S(1)}, u32[]{:S(2)}, u32[]{:S(2)}) collective-permute-start(f32[2,4,128,128]{3,2,1,0:T(8,128)S(1)} %collective-permute-done.1.own_swap), channel_id=1, source_target_pairs={{1,5},{5,9},{9,13},{13,15},{12,8},{8,4},{4,0},{0,2},{17,21},{21,25... | collective-permute-start | bytes 1572872 | tf_op jit(solution)/shard_map/ppermute | solution.py:309
  7.3 0.1 add_select_fusion
  7.5 0.1 copy.10
  7.5 0.2 select_reduce_fusion
  7.8 0.7 %compare_select_fusion = s32[8,8]{1,0:T(8,128)S(1)} fusion(s32[8,8]{1,0:T(8,128)S(1)} %select_reduce_fusion, s32[8,16]{1,0:T(8,128)} %param.3), kind=kLoop, calls=%fused_computation.5 | loop fusion | flops 192 | bytes 768 | tf_op jit(solution)/shard_map/jit(_where)/select_n | solution.py:274
  8.5 0.1 pad_add_fusion.table_ref
  8.5 1.9 %collective-permute-done.r1 = f32[2,4,128,128]{3,2,1,0:T(8,128)S(1)} collective-permute-done((f32[2,4,128,128]{3,2,1,0:T(8,128)}, f32[2,4,128,128]{3,2,1,0:T(8,128)S(1)}, u32[]{:S(2)}, u32[]{:S(2)}) %collective-permute-start) | collective-permute-done | bytes 524320 | tf_op jit(solution)/shard_map/ppermute | solution.py:301
  10.4 1.9 %collective-permute-start.5 = (f32[2,4,128,128]{3,2,1,0:T(8,128)S(1)}, f32[2,4,128,128]{3,2,1,0:T(8,128)S(1)}, u32[]{:S(2)}, u32[]{:S(2)}) collective-permute-start(f32[2,4,128,128]{3,2,1,0:T(8,128)S(1)} %collective-permute-done.r1), channel_id=1, source_target_pairs={{15,1},{1,5},{5,9},{9,13},{13,15},{2,12},{12,8},{8,4},{4,0},{0,2},... | collective-permute-start | bytes 1572872 | tf_op jit(solution)/shard_map/ppermute | solution.py:301
  12.3 0.0 collective-permute-start.3
  12.3 3.8 %collective-permute-done.2.r2 = f32[2,4,128,128]{3,2,1,0:T(8,128)S(1)} collective-permute-done((f32[2,4,128,128]{3,2,1,0:T(8,128)S(1)}, f32[2,4,128,128]{3,2,1,0:T(8,128)S(1)}, u32[]{:S(2)}, u32[]{:S(2)}) %collective-permute-start.2) | collective-permute-done | bytes 524320 | tf_op jit(solution)/shard_map/ppermute | solution.py:309
  16.1 0.0 collective-permute-start.4
  16.2 1.9 %collective-permute-start.7 = (f32[1,4,128,128]{3,2,1,0:T(8,128)S(1)}, f32[1,4,128,128]{3,2,1,0:T(8,128)S(1)}, u32[]{:S(2)}, u32[]{:S(2)}) collective-permute-start(f32[1,4,128,128]{3,2,1,0:T(8,128)S(1)} %get-tuple-element.35), channel_id=1, source_target_pairs={{15,1},{1,5},{5,9},{9,13},{13,15},{2,12},{12,8},{8,4},{4,0},{0,2},... | collective-permute-start | bytes 786440 | tf_op jit(solution)/shard_map/ppermute | solution.py:301
  18.0 2.3 %collective-permute-start.6 = (f32[1,4,128,128]{3,2,1,0:T(8,128)S(1)}, f32[1,4,128,128]{3,2,1,0:T(8,128)S(1)}, u32[]{:S(2)}, u32[]{:S(2)}) collective-permute-start(f32[1,4,128,128]{3,2,1,0:T(8,128)S(1)} %get-tuple-element.36), channel_id=1, source_target_pairs={{15,1},{1,5},{5,9},{9,13},{13,15},{2,12},{12,8},{8,4},{4,0},{0,2},... | collective-permute-start | bytes 786440 | tf_op jit(solution)/shard_map/ppermute | solution.py:301
  20.3 1.4 %collective-permute-done.5.r3 = f32[2,4,128,128]{3,2,1,0:T(8,128)S(1)} collective-permute-done((f32[2,4,128,128]{3,2,1,0:T(8,128)S(1)}, f32[2,4,128,128]{3,2,1,0:T(8,128)S(1)}, u32[]{:S(2)}, u32[]{:S(2)}) %collective-permute-start.5) | collective-permute-done | bytes 524320 | tf_op jit(solution)/shard_map/ppermute | solution.py:301
  21.7 0.0 collective-permute-done.3.t1
  21.7 0.0 collective-permute-done.4.t2
  21.8 3.1 %early.1 = (bf16[1024,1024]{1,0:T(8,128)(2,1)S(1)}, bf16[1024,1024]{1,0:T(8,128)(2,1)S(1)}, bf16[512,1024]{1,0:T(8,128)(2,1)S(1)}, f32[256,1024]{1,0:T(8,128)S(1)}, s32[8,128]{1,0:T(8,128)S(1)}) custom-call(s32[8,9]{1,0:T(8,128)S(1)} %pad_add_fusion.table_ref, f32[2,4,128,128]{3,2,1,0:T(8,128)} %own_hbm.1, ...), custom_call_target="tpu_custom_call" | custom-call | tf_op jit(solution)/shard_map/early/pallas_call | solution.py:339
  24.9 0.0 collective-permute-done.7.r4a
  24.9 0.6 %collective-permute-start.8 = (f32[1,4,128,128]{3,2,1,0:T(8,128)S(1)}, f32[1,4,128,128]{3,2,1,0:T(8,128)S(1)}, u32[]{:S(2)}, u32[]{:S(2)}) collective-permute-start(f32[1,4,128,128]{3,2,1,0:T(8,128)S(1)} %collective-permute-done.7.r4a), channel_id=1, source_target_pairs={{1,0},{0,1},{17,16},{16,17},{3,2},{2,3},{19,18},{18,19},{5,4},{4,5... | collective-permute-start | bytes 786440 | tf_op jit(solution)/shard_map/ppermute | solution.py:301
  25.5 1.9 %collective-permute-done.6.r4b = f32[1,4,128,128]{3,2,1,0:T(8,128)S(1)} collective-permute-done((f32[1,4,128,128]{3,2,1,0:T(8,128)S(1)}, f32[1,4,128,128]{3,2,1,0:T(8,128)S(1)}, u32[]{:S(2)}, u32[]{:S(2)}) %collective-permute-start.6) | collective-permute-done | bytes 262176 | tf_op jit(solution)/shard_map/ppermute | solution.py:301
  27.4 0.0 collective-permute-done.8.t4a
  27.4 0.1 collective-permute-start.9
  27.5 0.0 collective-permute-done.10.t3
  27.5 1.3 %middle.1 = (bf16[1024,1024]{1,0:T(8,128)(2,1)S(1)}, bf16[1024,1024]{1,0:T(8,128)(2,1)S(1)}, f32[256,1024]{1,0:T(8,128)S(1)}) custom-call(s32[8,128]{1,0:T(8,128)S(1)} %get-tuple-element.22.notes_ref, f32[1,4,128,128]{3,2,1,0:T(8,128)S(1)} %collective-permute-done.7.r4a, ...), custom_call_target="tpu_custom_call", output_to_operand_aliasing={{0}: (5, {}), {1}: (6, {}), {2}: (8, {})} | custom-call | tf_op jit(solution)/shard_map/middle/pallas_call | solution.py:360
  28.8 0.1 collective-permute-done.9.t4b
  28.9 3.1 %late.1 = (f32[2,4,128,128]{3,2,1,0:T(8,128)}, bf16[1024,1024]{1,0:T(8,128)(2,1)S(1)}, bf16[1024,1024]{1,0:T(8,128)(2,1)S(1)}, f32[256,1024]{1,0:T(8,128)S(1)}) custom-call(s32[8,128]{1,0:T(8,128)S(1)} %get-tuple-element.22.notes_ref, f32[1,4,128,128]{3,2,1,0:T(8,128)S(1)} %collective-permute-done.9.t4b, ...), custom_call_target="tpu_custom_call", output_to_operand_aliasing={{1}: (2, {}), {2}: (3, {}), {3}: (5, {})} | custom-call | tf_op jit(solution)/shard_map/late/pallas_call | solution.py:369
  (5 shorter events, 0.1 us)
Async XLA Ops:
  0.0 10.4 %collective-permute-start = (f32[2,4,128,128]{3,2,1,0:T(8,128)}, f32[2,4,128,128]{3,2,1,0:T(8,128)S(1)}, u32[]{:S(2)}, u32[]{:S(2)}) collective-permute-start(f32[2,4,128,128]{3,2,1,0:T(8,128)} %own_hbm.1), channel_id=1, source_target_pairs={{3,1},{1,5},{5,9},{9,13},{13,15},{15,14},{14,12},{12,8},{8,4},{4,0... | collective-permute-start | bytes 1572872 | tf_op jit(solution)/shard_map/ppermute | solution.py:301
  2.9 2.1 %collective-permute-start.1 = (f32[2,4,128,128]{3,2,1,0:T(8,128)}, f32[2,4,128,128]{3,2,1,0:T(8,128)S(1)}, u32[]{:S(2)}, u32[]{:S(2)}) collective-permute-start(f32[2,4,128,128]{3,2,1,0:T(8,128)} %own_hbm.1), channel_id=1, source_target_pairs={{1,0},{0,1},{17,16},{16,17},{3,2},{2,3},{19,18},{18,19},{5,4},{4,5... | collective-permute-start | bytes 1572872 | tf_op jit(solution)/shard_map/ppermute | solution.py:301
  5.1 11.1 %collective-permute-start.2 = (f32[2,4,128,128]{3,2,1,0:T(8,128)S(1)}, f32[2,4,128,128]{3,2,1,0:T(8,128)S(1)}, u32[]{:S(2)}, u32[]{:S(2)}) collective-permute-start(f32[2,4,128,128]{3,2,1,0:T(8,128)S(1)} %collective-permute-done.1.own_swap), channel_id=1, source_target_pairs={{1,5},{5,9},{9,13},{13,15},{12,8},{8,4},{4,0},{0,2},{17,21},{21,25... | collective-permute-start | bytes 1572872 | tf_op jit(solution)/shard_map/ppermute | solution.py:309
  10.4 11.3 %collective-permute-start.5 = (f32[2,4,128,128]{3,2,1,0:T(8,128)S(1)}, f32[2,4,128,128]{3,2,1,0:T(8,128)S(1)}, u32[]{:S(2)}, u32[]{:S(2)}) collective-permute-start(f32[2,4,128,128]{3,2,1,0:T(8,128)S(1)} %collective-permute-done.r1), channel_id=1, source_target_pairs={{15,1},{1,5},{5,9},{9,13},{13,15},{2,12},{12,8},{8,4},{4,0},{0,2},... | collective-permute-start | bytes 1572872 | tf_op jit(solution)/shard_map/ppermute | solution.py:301
  12.3 9.4 %collective-permute-start.3 = (f32[2,4,128,128]{3,2,1,0:T(8,128)S(1)}, f32[2,4,128,128]{3,2,1,0:T(8,128)S(1)}, u32[]{:S(2)}, u32[]{:S(2)}) collective-permute-start(f32[2,4,128,128]{3,2,1,0:T(8,128)S(1)} %collective-permute-done.r1), channel_id=1, source_target_pairs={{1,0},{0,1},{17,16},{16,17},{3,2},{2,3},{19,18},{18,19},{5,4},{4,5... | collective-permute-start | bytes 1572872 | tf_op jit(solution)/shard_map/ppermute | solution.py:301
  16.1 5.6 %collective-permute-start.4 = (f32[2,4,128,128]{3,2,1,0:T(8,128)S(1)}, f32[2,4,128,128]{3,2,1,0:T(8,128)S(1)}, u32[]{:S(2)}, u32[]{:S(2)}) collective-permute-start(f32[2,4,128,128]{3,2,1,0:T(8,128)S(1)} %collective-permute-done.2.r2), channel_id=1, source_target_pairs={{1,0},{0,1},{17,16},{16,17},{3,2},{2,3},{19,18},{18,19},{5,4},{4,5... | collective-permute-start | bytes 1572872 | tf_op jit(solution)/shard_map/ppermute | solution.py:301
  16.2 8.7 %collective-permute-start.7 = (f32[1,4,128,128]{3,2,1,0:T(8,128)S(1)}, f32[1,4,128,128]{3,2,1,0:T(8,128)S(1)}, u32[]{:S(2)}, u32[]{:S(2)}) collective-permute-start(f32[1,4,128,128]{3,2,1,0:T(8,128)S(1)} %get-tuple-element.35), channel_id=1, source_target_pairs={{15,1},{1,5},{5,9},{9,13},{13,15},{2,12},{12,8},{8,4},{4,0},{0,2},... | collective-permute-start | bytes 786440 | tf_op jit(solution)/shard_map/ppermute | solution.py:301
  18.0 9.3 %collective-permute-start.6 = (f32[1,4,128,128]{3,2,1,0:T(8,128)S(1)}, f32[1,4,128,128]{3,2,1,0:T(8,128)S(1)}, u32[]{:S(2)}, u32[]{:S(2)}) collective-permute-start(f32[1,4,128,128]{3,2,1,0:T(8,128)S(1)} %get-tuple-element.36), channel_id=1, source_target_pairs={{15,1},{1,5},{5,9},{9,13},{13,15},{2,12},{12,8},{8,4},{4,0},{0,2},... | collective-permute-start | bytes 786440 | tf_op jit(solution)/shard_map/ppermute | solution.py:301
  21.7 5.7 %collective-permute-start.10 = (f32[2,4,128,128]{3,2,1,0:T(8,128)S(1)}, f32[2,4,128,128]{3,2,1,0:T(8,128)S(1)}, u32[]{:S(2)}, u32[]{:S(2)}) collective-permute-start(f32[2,4,128,128]{3,2,1,0:T(8,128)S(1)} %collective-permute-done.5.r3), channel_id=1, source_target_pairs={{1,0},{0,1},{17,16},{16,17},{3,2},{2,3},{19,18},{18,19},{5,4},{4,5... | collective-permute-start | bytes 1572872 | tf_op jit(solution)/shard_map/ppermute | solution.py:301
  24.9 2.4 %collective-permute-start.8 = (f32[1,4,128,128]{3,2,1,0:T(8,128)S(1)}, f32[1,4,128,128]{3,2,1,0:T(8,128)S(1)}, u32[]{:S(2)}, u32[]{:S(2)}) collective-permute-start(f32[1,4,128,128]{3,2,1,0:T(8,128)S(1)} %collective-permute-done.7.r4a), channel_id=1, source_target_pairs={{1,0},{0,1},{17,16},{16,17},{3,2},{2,3},{19,18},{18,19},{5,4},{4,5... | collective-permute-start | bytes 786440 | tf_op jit(solution)/shard_map/ppermute | solution.py:301
  27.4 1.5 %collective-permute-start.9 = (f32[1,4,128,128]{3,2,1,0:T(8,128)S(1)}, f32[1,4,128,128]{3,2,1,0:T(8,128)S(1)}, u32[]{:S(2)}, u32[]{:S(2)}) collective-permute-start(f32[1,4,128,128]{3,2,1,0:T(8,128)S(1)} %collective-permute-done.6.r4b), channel_id=1, source_target_pairs={{1,0},{0,1},{17,16},{16,17},{3,2},{2,3},{19,18},{18,19},{5,4},{4,5... | collective-permute-start | bytes 786440 | tf_op jit(solution)/shard_map/ppermute | solution.py:301

commit v17 on v16

--- a/solution.py
+++ b/solution.py
@@ -310,7 +310,7 @@
 
     up = [(z, 0, 1) for z in range(chains)] + [(last, 1, 1)]
     down = [(z, 0, 0) for z in reversed(range(chains))] + [(0, 1, 0)]
-    first = [up + [(last, 1, 0)] + down + [(0, 1, 1)]]
+    first = [up + down]
     second = [up, down]
     near = [(z + 1 if z < last else -1, z - 1) for z in range(chains)]
     far = [(z + 2 if z + 2 < chains else -1, z - 2 if z >= 2 else -1) for z in range(chains)]

time: 32.3 us -> 32.3 us (level)
  starting transfers between devices: 11.9 us -> 12.3 us
where the time goes in v17:
time: 32.3 us; the launch traced here: 32 us
  starting transfers between devices  12.3 us (38%)
  waiting for transfers between devices  9.72 us (30%)
  Pallas kernels  7.59 us (23%)
  other arithmetic  2.24 us (7%)
    ppermute x10, starting transfers between devices, move(): return lax.ppermute(block, AXES, route)  9.68 us
    ppermute x10, waiting for transfers between devices, move(): return lax.ppermute(block, AXES, route)  5.93 us
    ppermute x1, waiting for transfers between devices, move_only(): return lax.ppermute(block, AXES, route)  3.79 us
    pallas_call x1, Pallas kernels, gather_local(): pl.pallas_call(functools.partial(early_kernel, tables), out_shape=[jax.Sh...  3.13 us
    pallas_call x1, Pallas kernels, gather_local(): pl.pallas_call(functools.partial(late_kernel, tables), out_shape=[jax.Sha...  3.12 us
    ppermute x1, starting transfers between devices, move_only(): return lax.ppermute(block, AXES, route)  2.6 us
    pallas_call x1, Pallas kernels, gather_local(): pl.pallas_call(functools.partial(middle_kernel, tables), out_shape=dense,...  1.34 us
    reduce_sum x1, other arithmetic, slot_table(): count = jnp.sum(here.astype(jnp.int32), axis=1, keepdims=True)  0.8 us
  transfers between devices with their start and end apart: 11, of which 6 were waited for; matrix products, arithmetic and copies ran while one was open for 7% of the time, Pallas kernels for 14%

profile of v17, /device:TPU:0, one launch (start us, length us, event | category | flops | bytes accessed | tf_op | source)
XLA Modules:
  0.0 32.0 jit_solution(14421958145264276116)
XLA Ops:
  0.0 2.9 %collective-permute-start = (f32[2,4,128,128]{3,2,1,0:T(8,128)}, f32[2,4,128,128]{3,2,1,0:T(8,128)S(1)}, u32[]{:S(2)}, u32[]{:S(2)}) collective-permute-start(f32[2,4,128,128]{3,2,1,0:T(8,128)} %own_hbm.1), channel_id=1, source_target_pairs={{2,1},{1,5},{5,9},{9,13},{13,15},{15,12},{12,8},{8,4},{4,0},{0,2},... | collective-permute-start | bytes 1572872 | tf_op jit(solution)/shard_map/ppermute | solution.py:301
  2.9 0.0 collective-permute-start.1
  2.9 0.8 %fusion.1 = (s32[8]{0:T(128)S(1)}, s32[8,8]{1,0:T(8,128)S(1)}) fusion(s32[8,16]{1,0:T(8,128)} %param.3), kind=kLoop, calls=%fused_computation.7 | loop fusion | flops 184 | bytes 544 | tf_op jit(solution)/shard_map/reduce_sum | solution.py:266
  3.7 0.1 fusion
  3.9 0.2 convert_reduce_fusion
  4.1 1.0 %collective-permute-done.1.own_swap = f32[2,4,128,128]{3,2,1,0:T(8,128)S(1)} collective-permute-done((f32[2,4,128,128]{3,2,1,0:T(8,128)}, f32[2,4,128,128]{3,2,1,0:T(8,128)S(1)}, u32[]{:S(2)}, u32[]{:S(2)}) %collective-permute-start.1) | collective-permute-done | bytes 524320 | tf_op jit(solution)/shard_map/ppermute | solution.py:301
  5.1 2.6 %collective-permute-start.2 = (f32[2,4,128,128]{3,2,1,0:T(8,128)S(1)}, f32[2,4,128,128]{3,2,1,0:T(8,128)S(1)}, u32[]{:S(2)}, u32[]{:S(2)}) collective-permute-start(f32[2,4,128,128]{3,2,1,0:T(8,128)S(1)} %collective-permute-done.1.own_swap), channel_id=1, source_target_pairs={{1,5},{5,9},{9,13},{13,15},{12,8},{8,4},{4,0},{0,2},{17,21},{21,25... | collective-permute-start | bytes 1572872 | tf_op jit(solution)/shard_map/ppermute | solution.py:309
  7.7 0.1 add_select_fusion
  7.8 0.1 copy.10
  7.9 0.2 select_reduce_fusion
  8.1 0.7 %compare_select_fusion = s32[8,8]{1,0:T(8,128)S(1)} fusion(s32[8,8]{1,0:T(8,128)S(1)} %select_reduce_fusion, s32[8,16]{1,0:T(8,128)} %param.3), kind=kLoop, calls=%fused_computation.5 | loop fusion | flops 192 | bytes 768 | tf_op jit(solution)/shard_map/jit(_where)/select_n | solution.py:274
  8.8 0.1 pad_add_fusion.table_ref
  8.9 1.5 %collective-permute-done.r1 = f32[2,4,128,128]{3,2,1,0:T(8,128)S(1)} collective-permute-done((f32[2,4,128,128]{3,2,1,0:T(8,128)}, f32[2,4,128,128]{3,2,1,0:T(8,128)S(1)}, u32[]{:S(2)}, u32[]{:S(2)}) %collective-permute-start) | collective-permute-done | bytes 524320 | tf_op jit(solution)/shard_map/ppermute | solution.py:301
  10.4 1.9 %collective-permute-start.5 = (f32[2,4,128,128]{3,2,1,0:T(8,128)S(1)}, f32[2,4,128,128]{3,2,1,0:T(8,128)S(1)}, u32[]{:S(2)}, u32[]{:S(2)}) collective-permute-start(f32[2,4,128,128]{3,2,1,0:T(8,128)S(1)} %collective-permute-done.r1), channel_id=1, source_target_pairs={{15,1},{1,5},{5,9},{9,13},{13,15},{2,12},{12,8},{8,4},{4,0},{0,2},... | collective-permute-start | bytes 1572872 | tf_op jit(solution)/shard_map/ppermute | solution.py:301
  12.3 0.0 collective-permute-start.3
  12.3 3.8 %collective-permute-done.2.r2 = f32[2,4,128,128]{3,2,1,0:T(8,128)S(1)} collective-permute-done((f32[2,4,128,128]{3,2,1,0:T(8,128)S(1)}, f32[2,4,128,128]{3,2,1,0:T(8,128)S(1)}, u32[]{:S(2)}, u32[]{:S(2)}) %collective-permute-start.2) | collective-permute-done | bytes 524320 | tf_op jit(solution)/shard_map/ppermute | solution.py:309
  16.1 0.0 collective-permute-start.4
  16.2 1.9 %collective-permute-start.7 = (f32[1,4,128,128]{3,2,1,0:T(8,128)S(1)}, f32[1,4,128,128]{3,2,1,0:T(8,128)S(1)}, u32[]{:S(2)}, u32[]{:S(2)}) collective-permute-start(f32[1,4,128,128]{3,2,1,0:T(8,128)S(1)} %get-tuple-element.35), channel_id=1, source_target_pairs={{15,1},{1,5},{5,9},{9,13},{13,15},{2,12},{12,8},{8,4},{4,0},{0,2},... | collective-permute-start | bytes 786440 | tf_op jit(solution)/shard_map/ppermute | solution.py:301
  18.0 2.3 %collective-permute-start.6 = (f32[1,4,128,128]{3,2,1,0:T(8,128)S(1)}, f32[1,4,128,128]{3,2,1,0:T(8,128)S(1)}, u32[]{:S(2)}, u32[]{:S(2)}) collective-permute-start(f32[1,4,128,128]{3,2,1,0:T(8,128)S(1)} %get-tuple-element.36), channel_id=1, source_target_pairs={{15,1},{1,5},{5,9},{9,13},{13,15},{2,12},{12,8},{8,4},{4,0},{0,2},... | collective-permute-start | bytes 786440 | tf_op jit(solution)/shard_map/ppermute | solution.py:301
  20.3 1.4 %collective-permute-done.5.r3 = f32[2,4,128,128]{3,2,1,0:T(8,128)S(1)} collective-permute-done((f32[2,4,128,128]{3,2,1,0:T(8,128)S(1)}, f32[2,4,128,128]{3,2,1,0:T(8,128)S(1)}, u32[]{:S(2)}, u32[]{:S(2)}) %collective-permute-start.5) | collective-permute-done | bytes 524320 | tf_op jit(solution)/shard_map/ppermute | solution.py:301
  21.7 0.0 collective-permute-start.10
  21.7 0.0 collective-permute-done.3.t1
  21.7 0.0 collective-permute-done.4.t2
  21.8 3.1 %early.1 = (bf16[1024,1024]{1,0:T(8,128)(2,1)S(1)}, bf16[1024,1024]{1,0:T(8,128)(2,1)S(1)}, bf16[512,1024]{1,0:T(8,128)(2,1)S(1)}, f32[256,1024]{1,0:T(8,128)S(1)}, s32[8,128]{1,0:T(8,128)S(1)}) custom-call(s32[8,9]{1,0:T(8,128)S(1)} %pad_add_fusion.table_ref, f32[2,4,128,128]{3,2,1,0:T(8,128)} %own_hbm.1, ...), custom_call_target="tpu_custom_call" | custom-call | tf_op jit(solution)/shard_map/early/pallas_call | solution.py:339
  24.9 0.6 %collective-permute-start.8 = (f32[1,4,128,128]{3,2,1,0:T(8,128)S(1)}, f32[1,4,128,128]{3,2,1,0:T(8,128)S(1)}, u32[]{:S(2)}, u32[]{:S(2)}) collective-permute-start(f32[1,4,128,128]{3,2,1,0:T(8,128)S(1)} %collective-permute-done.7.r4a), channel_id=1, source_target_pairs={{1,0},{0,1},{17,16},{16,17},{3,2},{2,3},{19,18},{18,19},{5,4},{4,5... | collective-permute-start | bytes 786440 | tf_op jit(solution)/shard_map/ppermute | solution.py:301
  25.5 1.9 %collective-permute-done.6.r4b = f32[1,4,128,128]{3,2,1,0:T(8,128)S(1)} collective-permute-done((f32[1,4,128,128]{3,2,1,0:T(8,128)S(1)}, f32[1,4,128,128]{3,2,1,0:T(8,128)S(1)}, u32[]{:S(2)}, u32[]{:S(2)}) %collective-permute-start.6) | collective-permute-done | bytes 262176 | tf_op jit(solution)/shard_map/ppermute | solution.py:301
  27.4 0.0 collective-permute-done.8.t4a
  27.4 0.1 collective-permute-start.9
  27.5 0.0 collective-permute-done.10.t3
  27.5 1.3 %middle.1 = (bf16[1024,1024]{1,0:T(8,128)(2,1)S(1)}, bf16[1024,1024]{1,0:T(8,128)(2,1)S(1)}, f32[256,1024]{1,0:T(8,128)S(1)}) custom-call(s32[8,128]{1,0:T(8,128)S(1)} %get-tuple-element.22.notes_ref, f32[1,4,128,128]{3,2,1,0:T(8,128)S(1)} %collective-permute-done.7.r4a, ...), custom_call_target="tpu_custom_call", output_to_operand_aliasing={{0}: (5, {}), {1}: (6, {}), {2}: (8, {})} | custom-call | tf_op jit(solution)/shard_map/middle/pallas_call | solution.py:360
  28.8 0.1 collective-permute-done.9.t4b
  28.9 3.1 %late.1 = (f32[2,4,128,128]{3,2,1,0:T(8,128)}, bf16[1024,1024]{1,0:T(8,128)(2,1)S(1)}, bf16[1024,1024]{1,0:T(8,128)(2,1)S(1)}, f32[256,1024]{1,0:T(8,128)S(1)}) custom-call(s32[8,128]{1,0:T(8,128)S(1)} %get-tuple-element.22.notes_ref, f32[1,4,128,128]{3,2,1,0:T(8,128)S(1)} %collective-permute-done.9.t4b, ...), custom_call_target="tpu_custom_call", output_to_operand_aliasing={{1}: (2, {}), {2}: (3, {}), {3}: (5, {})} | custom-call | tf_op jit(solution)/shard_map/late/pallas_call | solution.py:369
  (5 shorter events, 0.1 us)
Async XLA Ops:
  0.0 10.4 %collective-permute-start = (f32[2,4,128,128]{3,2,1,0:T(8,128)}, f32[2,4,128,128]{3,2,1,0:T(8,128)S(1)}, u32[]{:S(2)}, u32[]{:S(2)}) collective-permute-start(f32[2,4,128,128]{3,2,1,0:T(8,128)} %own_hbm.1), channel_id=1, source_target_pairs={{2,1},{1,5},{5,9},{9,13},{13,15},{15,12},{12,8},{8,4},{4,0},{0,2},... | collective-permute-start | bytes 1572872 | tf_op jit(solution)/shard_map/ppermute | solution.py:301
  2.9 2.1 %collective-permute-start.1 = (f32[2,4,128,128]{3,2,1,0:T(8,128)}, f32[2,4,128,128]{3,2,1,0:T(8,128)S(1)}, u32[]{:S(2)}, u32[]{:S(2)}) collective-permute-start(f32[2,4,128,128]{3,2,1,0:T(8,128)} %own_hbm.1), channel_id=1, source_target_pairs={{1,0},{0,1},{17,16},{16,17},{3,2},{2,3},{19,18},{18,19},{5,4},{4,5... | collective-permute-start | bytes 1572872 | tf_op jit(solution)/shard_map/ppermute | solution.py:301
  5.1 11.1 %collective-permute-start.2 = (f32[2,4,128,128]{3,2,1,0:T(8,128)S(1)}, f32[2,4,128,128]{3,2,1,0:T(8,128)S(1)}, u32[]{:S(2)}, u32[]{:S(2)}) collective-permute-start(f32[2,4,128,128]{3,2,1,0:T(8,128)S(1)} %collective-permute-done.1.own_swap), channel_id=1, source_target_pairs={{1,5},{5,9},{9,13},{13,15},{12,8},{8,4},{4,0},{0,2},{17,21},{21,25... | collective-permute-start | bytes 1572872 | tf_op jit(solution)/shard_map/ppermute | solution.py:309
  10.4 11.3 %collective-permute-start.5 = (f32[2,4,128,128]{3,2,1,0:T(8,128)S(1)}, f32[2,4,128,128]{3,2,1,0:T(8,128)S(1)}, u32[]{:S(2)}, u32[]{:S(2)}) collective-permute-start(f32[2,4,128,128]{3,2,1,0:T(8,128)S(1)} %collective-permute-done.r1), channel_id=1, source_target_pairs={{15,1},{1,5},{5,9},{9,13},{13,15},{2,12},{12,8},{8,4},{4,0},{0,2},... | collective-permute-start | bytes 1572872 | tf_op jit(solution)/shard_map/ppermute | solution.py:301
  12.3 9.4 %collective-permute-start.3 = (f32[2,4,128,128]{3,2,1,0:T(8,128)S(1)}, f32[2,4,128,128]{3,2,1,0:T(8,128)S(1)}, u32[]{:S(2)}, u32[]{:S(2)}) collective-permute-start(f32[2,4,128,128]{3,2,1,0:T(8,128)S(1)} %collective-permute-done.r1), channel_id=1, source_target_pairs={{1,0},{0,1},{17,16},{16,17},{3,2},{2,3},{19,18},{18,19},{5,4},{4,5... | collective-permute-start | bytes 1572872 | tf_op jit(solution)/shard_map/ppermute | solution.py:301
  16.1 5.6 %collective-permute-start.4 = (f32[2,4,128,128]{3,2,1,0:T(8,128)S(1)}, f32[2,4,128,128]{3,2,1,0:T(8,128)S(1)}, u32[]{:S(2)}, u32[]{:S(2)}) collective-permute-start(f32[2,4,128,128]{3,2,1,0:T(8,128)S(1)} %collective-permute-done.2.r2), channel_id=1, source_target_pairs={{1,0},{0,1},{17,16},{16,17},{3,2},{2,3},{19,18},{18,19},{5,4},{4,5... | collective-permute-start | bytes 1572872 | tf_op jit(solution)/shard_map/ppermute | solution.py:301
  16.2 8.7 %collective-permute-start.7 = (f32[1,4,128,128]{3,2,1,0:T(8,128)S(1)}, f32[1,4,128,128]{3,2,1,0:T(8,128)S(1)}, u32[]{:S(2)}, u32[]{:S(2)}) collective-permute-start(f32[1,4,128,128]{3,2,1,0:T(8,128)S(1)} %get-tuple-element.35), channel_id=1, source_target_pairs={{15,1},{1,5},{5,9},{9,13},{13,15},{2,12},{12,8},{8,4},{4,0},{0,2},... | collective-permute-start | bytes 786440 | tf_op jit(solution)/shard_map/ppermute | solution.py:301
  18.0 9.3 %collective-permute-start.6 = (f32[1,4,128,128]{3,2,1,0:T(8,128)S(1)}, f32[1,4,128,128]{3,2,1,0:T(8,128)S(1)}, u32[]{:S(2)}, u32[]{:S(2)}) collective-permute-start(f32[1,4,128,128]{3,2,1,0:T(8,128)S(1)} %get-tuple-element.36), channel_id=1, source_target_pairs={{15,1},{1,5},{5,9},{9,13},{13,15},{2,12},{12,8},{8,4},{4,0},{0,2},... | collective-permute-start | bytes 786440 | tf_op jit(solution)/shard_map/ppermute | solution.py:301
  21.7 5.7 %collective-permute-start.10 = (f32[2,4,128,128]{3,2,1,0:T(8,128)S(1)}, f32[2,4,128,128]{3,2,1,0:T(8,128)S(1)}, u32[]{:S(2)}, u32[]{:S(2)}) collective-permute-start(f32[2,4,128,128]{3,2,1,0:T(8,128)S(1)} %collective-permute-done.5.r3), channel_id=1, source_target_pairs={{1,0},{0,1},{17,16},{16,17},{3,2},{2,3},{19,18},{18,19},{5,4},{4,5... | collective-permute-start | bytes 1572872 | tf_op jit(solution)/shard_map/ppermute | solution.py:301
  24.9 2.5 %collective-permute-start.8 = (f32[1,4,128,128]{3,2,1,0:T(8,128)S(1)}, f32[1,4,128,128]{3,2,1,0:T(8,128)S(1)}, u32[]{:S(2)}, u32[]{:S(2)}) collective-permute-start(f32[1,4,128,128]{3,2,1,0:T(8,128)S(1)} %collective-permute-done.7.r4a), channel_id=1, source_target_pairs={{1,0},{0,1},{17,16},{16,17},{3,2},{2,3},{19,18},{18,19},{5,4},{4,5... | collective-permute-start | bytes 786440 | tf_op jit(solution)/shard_map/ppermute | solution.py:301
  27.4 1.5 %collective-permute-start.9 = (f32[1,4,128,128]{3,2,1,0:T(8,128)S(1)}, f32[1,4,128,128]{3,2,1,0:T(8,128)S(1)}, u32[]{:S(2)}, u32[]{:S(2)}) collective-permute-start(f32[1,4,128,128]{3,2,1,0:T(8,128)S(1)} %collective-permute-done.6.r4b), channel_id=1, source_target_pairs={{1,0},{0,1},{17,16},{16,17},{3,2},{2,3},{19,18},{18,19},{5,4},{4,5... | collective-permute-start | bytes 786440 | tf_op jit(solution)/shard_map/ppermute | solution.py:301

commit v18 on v16

--- a/solution.py
+++ b/solution.py
@@ -144,7 +144,7 @@
 
 
 def add_plane(plane, left, high, low, part_ref):
-    depth, tile = part_ref.shape[0], 256
+    depth, tile = part_ref.shape[0], 512
 
     @pl.when(plane >= 0)
     def _():
@@ -236,23 +236,19 @@
     copies = []
     for r in range(slab):
         left_parts = square_parts[pl.ds(2 * r * edge, 2 * edge), :]
-        for w in range(0, width, 2):
-            codes = [own_codes(r, w + k) for k in range(2)]
-            cols = [pl.ds(pl.multiple_of(code % act * edge, edge), edge) for code in codes]
-            cube = stacked_dot(
-                left_parts,
-                jnp.concatenate([high[:, col] for col in cols], axis=1),
-                jnp.concatenate([low[:, col] for col in cols], axis=1),
-            )
-            for k in range(2):
-                value = 3.0 * square[pl.ds(r * edge, edge), cols[k]]
-                value = value - 2.0 * cube[:, k * edge : (k + 1) * edge]
-                out_ref[r, w + k] = jnp.where(holds & (codes[k] < act), value, 0.0)
-            ready = (r, pl.ds(w, 2))
-            copies.append(
-                pltpu.make_async_copy(out_ref.at[ready], out_hbm.at[ready], out_sem.at[len(copies)])
-            )
-            copies[-1].start()
+        codes = [own_codes(r, w) for w in range(width)]
+        cols = [pl.ds(pl.multiple_of(code % act * edge, edge), edge) for code in codes]
+        cube = stacked_dot(
+            left_parts,
+            jnp.concatenate([high[:, col] for col in cols], axis=1),
+            jnp.concatenate([low[:, col] for col in cols], axis=1),
+        )
+        for w in range(width):
+            value = 3.0 * square[pl.ds(r * edge, edge), cols[w]]
+            value = value - 2.0 * cube[:, w * edge : (w + 1) * edge]
+            out_ref[r, w] = jnp.where(holds & (codes[w] < act), value, 0.0)
+        copies.append(pltpu.make_async_copy(out_ref.at[r], out_hbm.at[r], out_sem.at[r]))
+        copies[-1].start()
     for copy in copies:
         copy.wait()
 
@@ -375,7 +371,7 @@
         scratch_shapes=[
             pltpu.VMEM((2 * own, order), jnp.bfloat16),
             pltpu.VMEM(x_blocks.shape, jnp.float32),
-            pltpu.SemaphoreType.DMA((slab * width // 2,)),
+            pltpu.SemaphoreType.DMA((slab,)),
         ],
         compiler_params=params,
         name="late",

time: 32.3 us -> 32.3 us (level)
  no operation moved by 1% of the time
where the time goes in v18:
time: 32.3 us; the launch traced here: 32 us
  starting transfers between devices  12 us (37%)
  waiting for transfers between devices  10.1 us (31%)
  Pallas kernels  7.56 us (23%)
  other arithmetic  2.24 us (7%)
    ppermute x10, starting transfers between devices, move(): return lax.ppermute(block, AXES, route)  9.68 us
    ppermute x10, waiting for transfers between devices, move(): return lax.ppermute(block, AXES, route)  6.3 us
    ppermute x1, waiting for transfers between devices, move_only(): return lax.ppermute(block, AXES, route)  3.79 us
    pallas_call x1, Pallas kernels, gather_local(): pl.pallas_call(functools.partial(late_kernel, tables), out_shape=[jax.Sha...  3.14 us
    pallas_call x1, Pallas kernels, gather_local(): pl.pallas_call(functools.partial(early_kernel, tables), out_shape=[jax.Sh...  3.08 us
    ppermute x1, starting transfers between devices, move_only(): return lax.ppermute(block, AXES, route)  2.28 us
    pallas_call x1, Pallas kernels, gather_local(): pl.pallas_call(functools.partial(middle_kernel, tables), out_shape=dense,...  1.34 us
    reduce_sum x1, other arithmetic, slot_table(): count = jnp.sum(here.astype(jnp.int32), axis=1, keepdims=True)  0.8 us
  transfers between devices with their start and end apart: 11, of which 6 were waited for; matrix products, arithmetic and copies ran while one was open for 7% of the time, Pallas kernels for 14%

profile of v18, /device:TPU:0, one launch (start us, length us, event | category | flops | bytes accessed | tf_op | source)
XLA Modules:
  0.0 32.0 jit_solution(18289695982753012926)
XLA Ops:
  0.0 2.9 %collective-permute-start = (f32[2,4,128,128]{3,2,1,0:T(8,128)}, f32[2,4,128,128]{3,2,1,0:T(8,128)S(1)}, u32[]{:S(2)}, u32[]{:S(2)}) collective-permute-start(f32[2,4,128,128]{3,2,1,0:T(8,128)} %own_hbm.1), channel_id=1, source_target_pairs={{3,1},{1,5},{5,9},{9,13},{13,15},{15,14},{14,12},{12,8},{8,4},{4,0... | collective-permute-start | bytes 1572872 | tf_op jit(solution)/shard_map/ppermute | solution.py:297
  2.9 0.0 collective-permute-start.1
  2.9 0.8 %fusion.1 = (s32[8]{0:T(128)S(1)}, s32[8,8]{1,0:T(8,128)S(1)}) fusion(s32[8,16]{1,0:T(8,128)} %param.3), kind=kLoop, calls=%fused_computation.7 | loop fusion | flops 184 | bytes 544 | tf_op jit(solution)/shard_map/reduce_sum | solution.py:262
  3.7 0.1 fusion
  3.9 0.2 convert_reduce_fusion
  4.1 1.0 %collective-permute-done.1.own_swap = f32[2,4,128,128]{3,2,1,0:T(8,128)S(1)} collective-permute-done((f32[2,4,128,128]{3,2,1,0:T(8,128)}, f32[2,4,128,128]{3,2,1,0:T(8,128)S(1)}, u32[]{:S(2)}, u32[]{:S(2)}) %collective-permute-start.1) | collective-permute-done | bytes 524320 | tf_op jit(solution)/shard_map/ppermute | solution.py:297
  5.1 2.3 %collective-permute-start.2 = (f32[2,4,128,128]{3,2,1,0:T(8,128)S(1)}, f32[2,4,128,128]{3,2,1,0:T(8,128)S(1)}, u32[]{:S(2)}, u32[]{:S(2)}) collective-permute-start(f32[2,4,128,128]{3,2,1,0:T(8,128)S(1)} %collective-permute-done.1.own_swap), channel_id=1, source_target_pairs={{1,5},{5,9},{9,13},{13,15},{12,8},{8,4},{4,0},{0,2},{17,21},{21,25... | collective-permute-start | bytes 1572872 | tf_op jit(solution)/shard_map/ppermute | solution.py:305
  7.3 0.1 add_select_fusion
  7.5 0.1 copy.10
  7.5 0.2 select_reduce_fusion
  7.8 0.7 %compare_select_fusion = s32[8,8]{1,0:T(8,128)S(1)} fusion(s32[8,8]{1,0:T(8,128)S(1)} %select_reduce_fusion, s32[8,16]{1,0:T(8,128)} %param.3), kind=kLoop, calls=%fused_computation.5 | loop fusion | flops 192 | bytes 768 | tf_op jit(solution)/shard_map/jit(_where)/select_n | solution.py:270
  8.5 0.1 pad_add_fusion.table_ref
  8.5 1.9 %collective-permute-done.r1 = f32[2,4,128,128]{3,2,1,0:T(8,128)S(1)} collective-permute-done((f32[2,4,128,128]{3,2,1,0:T(8,128)}, f32[2,4,128,128]{3,2,1,0:T(8,128)S(1)}, u32[]{:S(2)}, u32[]{:S(2)}) %collective-permute-start) | collective-permute-done | bytes 524320 | tf_op jit(solution)/shard_map/ppermute | solution.py:297
  10.4 1.9 %collective-permute-start.5 = (f32[2,4,128,128]{3,2,1,0:T(8,128)S(1)}, f32[2,4,128,128]{3,2,1,0:T(8,128)S(1)}, u32[]{:S(2)}, u32[]{:S(2)}) collective-permute-start(f32[2,4,128,128]{3,2,1,0:T(8,128)S(1)} %collective-permute-done.r1), channel_id=1, source_target_pairs={{15,1},{1,5},{5,9},{9,13},{13,15},{2,12},{12,8},{8,4},{4,0},{0,2},... | collective-permute-start | bytes 1572872 | tf_op jit(solution)/shard_map/ppermute | solution.py:297
  12.3 0.0 collective-permute-start.3
  12.3 3.8 %collective-permute-done.2.r2 = f32[2,4,128,128]{3,2,1,0:T(8,128)S(1)} collective-permute-done((f32[2,4,128,128]{3,2,1,0:T(8,128)S(1)}, f32[2,4,128,128]{3,2,1,0:T(8,128)S(1)}, u32[]{:S(2)}, u32[]{:S(2)}) %collective-permute-start.2) | collective-permute-done | bytes 524320 | tf_op jit(solution)/shard_map/ppermute | solution.py:305
  16.1 0.0 collective-permute-start.4
  16.2 1.9 %collective-permute-start.7 = (f32[1,4,128,128]{3,2,1,0:T(8,128)S(1)}, f32[1,4,128,128]{3,2,1,0:T(8,128)S(1)}, u32[]{:S(2)}, u32[]{:S(2)}) collective-permute-start(f32[1,4,128,128]{3,2,1,0:T(8,128)S(1)} %get-tuple-element.35), channel_id=1, source_target_pairs={{15,1},{1,5},{5,9},{9,13},{13,15},{2,12},{12,8},{8,4},{4,0},{0,2},... | collective-permute-start | bytes 786440 | tf_op jit(solution)/shard_map/ppermute | solution.py:297
  18.0 2.3 %collective-permute-start.6 = (f32[1,4,128,128]{3,2,1,0:T(8,128)S(1)}, f32[1,4,128,128]{3,2,1,0:T(8,128)S(1)}, u32[]{:S(2)}, u32[]{:S(2)}) collective-permute-start(f32[1,4,128,128]{3,2,1,0:T(8,128)S(1)} %get-tuple-element.36), channel_id=1, source_target_pairs={{15,1},{1,5},{5,9},{9,13},{13,15},{2,12},{12,8},{8,4},{4,0},{0,2},... | collective-permute-start | bytes 786440 | tf_op jit(solution)/shard_map/ppermute | solution.py:297
  20.3 1.4 %collective-permute-done.5.r3 = f32[2,4,128,128]{3,2,1,0:T(8,128)S(1)} collective-permute-done((f32[2,4,128,128]{3,2,1,0:T(8,128)S(1)}, f32[2,4,128,128]{3,2,1,0:T(8,128)S(1)}, u32[]{:S(2)}, u32[]{:S(2)}) %collective-permute-start.5) | collective-permute-done | bytes 524320 | tf_op jit(solution)/shard_map/ppermute | solution.py:297
  21.7 0.0 collective-permute-start.10
  21.7 0.0 collective-permute-done.3.t1
  21.8 3.1 %early.1 = (bf16[1024,1024]{1,0:T(8,128)(2,1)S(1)}, bf16[1024,1024]{1,0:T(8,128)(2,1)S(1)}, bf16[512,1024]{1,0:T(8,128)(2,1)S(1)}, f32[256,1024]{1,0:T(8,128)S(1)}, s32[8,128]{1,0:T(8,128)S(1)}) custom-call(s32[8,9]{1,0:T(8,128)S(1)} %pad_add_fusion.table_ref, f32[2,4,128,128]{3,2,1,0:T(8,128)} %own_hbm.1, ...), custom_call_target="tpu_custom_call" | custom-call | tf_op jit(solution)/shard_map/early/pallas_call | solution.py:335
  24.8 0.0 collective-permute-done.7.r4a
  24.9 0.6 %collective-permute-start.8 = (f32[1,4,128,128]{3,2,1,0:T(8,128)S(1)}, f32[1,4,128,128]{3,2,1,0:T(8,128)S(1)}, u32[]{:S(2)}, u32[]{:S(2)}) collective-permute-start(f32[1,4,128,128]{3,2,1,0:T(8,128)S(1)} %collective-permute-done.7.r4a), channel_id=1, source_target_pairs={{1,0},{0,1},{17,16},{16,17},{3,2},{2,3},{19,18},{18,19},{5,4},{4,5... | collective-permute-start | bytes 786440 | tf_op jit(solution)/shard_map/ppermute | solution.py:297
  25.4 1.9 %collective-permute-done.6.r4b = f32[1,4,128,128]{3,2,1,0:T(8,128)S(1)} collective-permute-done((f32[1,4,128,128]{3,2,1,0:T(8,128)S(1)}, f32[1,4,128,128]{3,2,1,0:T(8,128)S(1)}, u32[]{:S(2)}, u32[]{:S(2)}) %collective-permute-start.6) | collective-permute-done | bytes 262176 | tf_op jit(solution)/shard_map/ppermute | solution.py:297
  27.4 0.0 collective-permute-done.8.t4a
  27.4 0.1 collective-permute-start.9
  27.5 0.0 collective-permute-done.10.t3
  27.5 1.3 %middle.1 = (bf16[1024,1024]{1,0:T(8,128)(2,1)S(1)}, bf16[1024,1024]{1,0:T(8,128)(2,1)S(1)}, f32[256,1024]{1,0:T(8,128)S(1)}) custom-call(s32[8,128]{1,0:T(8,128)S(1)} %get-tuple-element.22.notes_ref, f32[1,4,128,128]{3,2,1,0:T(8,128)S(1)} %collective-permute-done.7.r4a, ...), custom_call_target="tpu_custom_call", output_to_operand_aliasing={{0}: (5, {}), {1}: (6, {}), {2}: (8, {})} | custom-call | tf_op jit(solution)/shard_map/middle/pallas_call | solution.py:356
  28.8 0.1 collective-permute-done.9.t4b
  28.9 3.1 %late.1 = (f32[2,4,128,128]{3,2,1,0:T(8,128)}, bf16[1024,1024]{1,0:T(8,128)(2,1)S(1)}, bf16[1024,1024]{1,0:T(8,128)(2,1)S(1)}, f32[256,1024]{1,0:T(8,128)S(1)}) custom-call(s32[8,128]{1,0:T(8,128)S(1)} %get-tuple-element.22.notes_ref, f32[1,4,128,128]{3,2,1,0:T(8,128)S(1)} %collective-permute-done.9.t4b, ...), custom_call_target="tpu_custom_call", output_to_operand_aliasing={{1}: (2, {}), {2}: (3, {}), {3}: (5, {})} | custom-call | tf_op jit(solution)/shard_map/late/pallas_call | solution.py:365
  (5 shorter events, 0.1 us)
Async XLA Ops:
  0.0 10.4 %collective-permute-start = (f32[2,4,128,128]{3,2,1,0:T(8,128)}, f32[2,4,128,128]{3,2,1,0:T(8,128)S(1)}, u32[]{:S(2)}, u32[]{:S(2)}) collective-permute-start(f32[2,4,128,128]{3,2,1,0:T(8,128)} %own_hbm.1), channel_id=1, source_target_pairs={{3,1},{1,5},{5,9},{9,13},{13,15},{15,14},{14,12},{12,8},{8,4},{4,0... | collective-permute-start | bytes 1572872 | tf_op jit(solution)/shard_map/ppermute | solution.py:297
  2.9 2.1 %collective-permute-start.1 = (f32[2,4,128,128]{3,2,1,0:T(8,128)}, f32[2,4,128,128]{3,2,1,0:T(8,128)S(1)}, u32[]{:S(2)}, u32[]{:S(2)}) collective-permute-start(f32[2,4,128,128]{3,2,1,0:T(8,128)} %own_hbm.1), channel_id=1, source_target_pairs={{1,0},{0,1},{17,16},{16,17},{3,2},{2,3},{19,18},{18,19},{5,4},{4,5... | collective-permute-start | bytes 1572872 | tf_op jit(solution)/shard_map/ppermute | solution.py:297
  5.1 11.1 %collective-permute-start.2 = (f32[2,4,128,128]{3,2,1,0:T(8,128)S(1)}, f32[2,4,128,128]{3,2,1,0:T(8,128)S(1)}, u32[]{:S(2)}, u32[]{:S(2)}) collective-permute-start(f32[2,4,128,128]{3,2,1,0:T(8,128)S(1)} %collective-permute-done.1.own_swap), channel_id=1, source_target_pairs={{1,5},{5,9},{9,13},{13,15},{12,8},{8,4},{4,0},{0,2},{17,21},{21,25... | collective-permute-start | bytes 1572872 | tf_op jit(solution)/shard_map/ppermute | solution.py:305
  10.4 11.3 %collective-permute-start.5 = (f32[2,4,128,128]{3,2,1,0:T(8,128)S(1)}, f32[2,4,128,128]{3,2,1,0:T(8,128)S(1)}, u32[]{:S(2)}, u32[]{:S(2)}) collective-permute-start(f32[2,4,128,128]{3,2,1,0:T(8,128)S(1)} %collective-permute-done.r1), channel_id=1, source_target_pairs={{15,1},{1,5},{5,9},{9,13},{13,15},{2,12},{12,8},{8,4},{4,0},{0,2},... | collective-permute-start | bytes 1572872 | tf_op jit(solution)/shard_map/ppermute | solution.py:297
  12.3 9.4 %collective-permute-start.3 = (f32[2,4,128,128]{3,2,1,0:T(8,128)S(1)}, f32[2,4,128,128]{3,2,1,0:T(8,128)S(1)}, u32[]{:S(2)}, u32[]{:S(2)}) collective-permute-start(f32[2,4,128,128]{3,2,1,0:T(8,128)S(1)} %collective-permute-done.r1), channel_id=1, source_target_pairs={{1,0},{0,1},{17,16},{16,17},{3,2},{2,3},{19,18},{18,19},{5,4},{4,5... | collective-permute-start | bytes 1572872 | tf_op jit(solution)/shard_map/ppermute | solution.py:297
  16.1 5.6 %collective-permute-start.4 = (f32[2,4,128,128]{3,2,1,0:T(8,128)S(1)}, f32[2,4,128,128]{3,2,1,0:T(8,128)S(1)}, u32[]{:S(2)}, u32[]{:S(2)}) collective-permute-start(f32[2,4,128,128]{3,2,1,0:T(8,128)S(1)} %collective-permute-done.2.r2), channel_id=1, source_target_pairs={{1,0},{0,1},{17,16},{16,17},{3,2},{2,3},{19,18},{18,19},{5,4},{4,5... | collective-permute-start | bytes 1572872 | tf_op jit(solution)/shard_map/ppermute | solution.py:297
  16.2 8.7 %collective-permute-start.7 = (f32[1,4,128,128]{3,2,1,0:T(8,128)S(1)}, f32[1,4,128,128]{3,2,1,0:T(8,128)S(1)}, u32[]{:S(2)}, u32[]{:S(2)}) collective-permute-start(f32[1,4,128,128]{3,2,1,0:T(8,128)S(1)} %get-tuple-element.35), channel_id=1, source_target_pairs={{15,1},{1,5},{5,9},{9,13},{13,15},{2,12},{12,8},{8,4},{4,0},{0,2},... | collective-permute-start | bytes 786440 | tf_op jit(solution)/shard_map/ppermute | solution.py:297
  18.0 9.3 %collective-permute-start.6 = (f32[1,4,128,128]{3,2,1,0:T(8,128)S(1)}, f32[1,4,128,128]{3,2,1,0:T(8,128)S(1)}, u32[]{:S(2)}, u32[]{:S(2)}) collective-permute-start(f32[1,4,128,128]{3,2,1,0:T(8,128)S(1)} %get-tuple-element.36), channel_id=1, source_target_pairs={{15,1},{1,5},{5,9},{9,13},{13,15},{2,12},{12,8},{8,4},{4,0},{0,2},... | collective-permute-start | bytes 786440 | tf_op jit(solution)/shard_map/ppermute | solution.py:297
  21.7 5.7 %collective-permute-start.10 = (f32[2,4,128,128]{3,2,1,0:T(8,128)S(1)}, f32[2,4,128,128]{3,2,1,0:T(8,128)S(1)}, u32[]{:S(2)}, u32[]{:S(2)}) collective-permute-start(f32[2,4,128,128]{3,2,1,0:T(8,128)S(1)} %collective-permute-done.5.r3), channel_id=1, source_target_pairs={{1,0},{0,1},{17,16},{16,17},{3,2},{2,3},{19,18},{18,19},{5,4},{4,5... | collective-permute-start | bytes 1572872 | tf_op jit(solution)/shard_map/ppermute | solution.py:297
  24.9 2.5 %collective-permute-start.8 = (f32[1,4,128,128]{3,2,1,0:T(8,128)S(1)}, f32[1,4,128,128]{3,2,1,0:T(8,128)S(1)}, u32[]{:S(2)}, u32[]{:S(2)}) collective-permute-start(f32[1,4,128,128]{3,2,1,0:T(8,128)S(1)} %collective-permute-done.7.r4a), channel_id=1, source_target_pairs={{1,0},{0,1},{17,16},{16,17},{3,2},{2,3},{19,18},{18,19},{5,4},{4,5... | collective-permute-start | bytes 786440 | tf_op jit(solution)/shard_map/ppermute | solution.py:297
  27.4 1.5 %collective-permute-start.9 = (f32[1,4,128,128]{3,2,1,0:T(8,128)S(1)}, f32[1,4,128,128]{3,2,1,0:T(8,128)S(1)}, u32[]{:S(2)}, u32[]{:S(2)}) collective-permute-start(f32[1,4,128,128]{3,2,1,0:T(8,128)S(1)} %collective-permute-done.6.r4b), channel_id=1, source_target_pairs={{1,0},{0,1},{17,16},{16,17},{3,2},{2,3},{19,18},{18,19},{5,4},{4,5... | collective-permute-start | bytes 786440 | tf_op jit(solution)/shard_map/ppermute | solution.py:297

commit v19 on v16

--- a/solution.py
+++ b/solution.py
@@ -311,7 +311,10 @@
     up = [(z, 0, 1) for z in range(chains)] + [(last, 1, 1)]
     down = [(z, 0, 0) for z in reversed(range(chains))] + [(0, 1, 0)]
     first = [up + [(last, 1, 0)] + down + [(0, 1, 1)]]
-    second = [up, down]
+    second = [
+        up[:-1] + [(last, 1, 0), up[-1]],
+        down[:-1] + [(0, 1, 1), down[-1]],
+    ]
     near = [(z + 1 if z < last else -1, z - 1) for z in range(chains)]
     far = [(z + 2 if z + 2 < chains else -1, z - 2 if z >= 2 else -1) for z in range(chains)]
     far[0] = (far[0][0], last)

time: 32.3 us -> 32.3 us (level)
  waiting for transfers between devices: 10 us -> 13.3 us
  starting transfers between devices: 11.9 us -> 8.67 us
    ppermute x10, starting transfers between devices: 9.67 us -> 6.4 us  [move(): return lax.ppermute(block, AXES, route)]
    ppermute x10, waiting for transfers between devices: 6.25 us -> 8.32 us  [move(): return lax.ppermute(block, AXES, route)]
    ppermute x1, waiting for transfers between devices: 3.79 us -> 5.01 us  [move_only(): return lax.ppermute(block, AXES, route)]
where the time goes in v19:
time: 32.3 us; the launch traced here: 32 us
  waiting for transfers between devices  13.3 us (41%)
  starting transfers between devices  8.67 us (27%)
  Pallas kernels  7.59 us (23%)
  other arithmetic  2.24 us (7%)
    ppermute x10, waiting for transfers between devices, move(): return lax.ppermute(block, AXES, route)  8.32 us
    ppermute x10, starting transfers between devices, move(): return lax.ppermute(block, AXES, route)  6.4 us
    ppermute x1, waiting for transfers between devices, move_only(): return lax.ppermute(block, AXES, route)  5.01 us
    pallas_call x1, Pallas kernels, gather_local(): pl.pallas_call(functools.partial(early_kernel, tables), out_shape=[jax.Sh...  3.13 us
    pallas_call x1, Pallas kernels, gather_local(): pl.pallas_call(functools.partial(late_kernel, tables), out_shape=[jax.Sha...  3.13 us
    ppermute x1, starting transfers between devices, move_only(): return lax.ppermute(block, AXES, route)  2.28 us
    pallas_call x1, Pallas kernels, gather_local(): pl.pallas_call(functools.partial(middle_kernel, tables), out_shape=dense,...  1.33 us
    reduce_sum x1, other arithmetic, slot_table(): count = jnp.sum(here.astype(jnp.int32), axis=1, keepdims=True)  0.8 us
  transfers between devices with their start and end apart: 11, of which 6 were waited for; matrix products, arithmetic and copies ran while one was open for 7% of the time, Pallas kernels for 14%

profile of v19, /device:TPU:0, one launch (start us, length us, event | category | flops | bytes accessed | tf_op | source)
XLA Modules:
  0.0 32.0 jit_solution(10659906029491851038)
XLA Ops:
  0.0 2.9 %collective-permute-start = (f32[2,4,128,128]{3,2,1,0:T(8,128)}, f32[2,4,128,128]{3,2,1,0:T(8,128)S(1)}, u32[]{:S(2)}, u32[]{:S(2)}) collective-permute-start(f32[2,4,128,128]{3,2,1,0:T(8,128)} %own_hbm.1), channel_id=1, source_target_pairs={{3,1},{1,5},{5,9},{9,13},{13,15},{15,14},{14,12},{12,8},{8,4},{4,0... | collective-permute-start | bytes 1572872 | tf_op jit(solution)/shard_map/ppermute | solution.py:301
  2.9 0.0 collective-permute-start.1
  2.9 0.8 %fusion.1 = (s32[8]{0:T(128)S(1)}, s32[8,8]{1,0:T(8,128)S(1)}) fusion(s32[8,16]{1,0:T(8,128)} %param.3), kind=kLoop, calls=%fused_computation.7 | loop fusion | flops 184 | bytes 544 | tf_op jit(solution)/shard_map/reduce_sum | solution.py:266
  3.7 0.1 fusion
  3.9 0.2 convert_reduce_fusion
  4.1 1.0 %collective-permute-done.1.own_swap = f32[2,4,128,128]{3,2,1,0:T(8,128)S(1)} collective-permute-done((f32[2,4,128,128]{3,2,1,0:T(8,128)}, f32[2,4,128,128]{3,2,1,0:T(8,128)S(1)}, u32[]{:S(2)}, u32[]{:S(2)}) %collective-permute-start.1) | collective-permute-done | bytes 524320 | tf_op jit(solution)/shard_map/ppermute | solution.py:301
  5.1 2.3 %collective-permute-start.2 = (f32[2,4,128,128]{3,2,1,0:T(8,128)S(1)}, f32[2,4,128,128]{3,2,1,0:T(8,128)S(1)}, u32[]{:S(2)}, u32[]{:S(2)}) collective-permute-start(f32[2,4,128,128]{3,2,1,0:T(8,128)S(1)} %collective-permute-done.1.own_swap), channel_id=1, source_target_pairs={{1,5},{5,9},{9,13},{13,15},{12,8},{8,4},{4,0},{0,2},{17,21},{21,25... | collective-permute-start | bytes 1572872 | tf_op jit(solution)/shard_map/ppermute | solution.py:309
  7.3 0.1 add_select_fusion
  7.5 0.1 copy.10
  7.5 0.2 select_reduce_fusion
  7.8 0.7 %compare_select_fusion = s32[8,8]{1,0:T(8,128)S(1)} fusion(s32[8,8]{1,0:T(8,128)S(1)} %select_reduce_fusion, s32[8,16]{1,0:T(8,128)} %param.3), kind=kLoop, calls=%fused_computation.5 | loop fusion | flops 192 | bytes 768 | tf_op jit(solution)/shard_map/jit(_where)/select_n | solution.py:274
  8.5 0.1 pad_add_fusion.table_ref
  8.5 1.9 %collective-permute-done.r1 = f32[2,4,128,128]{3,2,1,0:T(8,128)S(1)} collective-permute-done((f32[2,4,128,128]{3,2,1,0:T(8,128)}, f32[2,4,128,128]{3,2,1,0:T(8,128)S(1)}, u32[]{:S(2)}, u32[]{:S(2)}) %collective-permute-start) | collective-permute-done | bytes 524320 | tf_op jit(solution)/shard_map/ppermute | solution.py:301
  10.4 0.0 collective-permute-start.5
  10.4 0.7 %collective-permute-start.3 = (f32[2,4,128,128]{3,2,1,0:T(8,128)S(1)}, f32[2,4,128,128]{3,2,1,0:T(8,128)S(1)}, u32[]{:S(2)}, u32[]{:S(2)}) collective-permute-start(f32[2,4,128,128]{3,2,1,0:T(8,128)S(1)} %collective-permute-done.r1), channel_id=1, source_target_pairs={{1,0},{0,1},{17,16},{16,17},{3,2},{2,3},{19,18},{18,19},{5,4},{4,5... | collective-permute-start | bytes 1572872 | tf_op jit(solution)/shard_map/ppermute | solution.py:301
  11.1 5.0 %collective-permute-done.2.r2 = f32[2,4,128,128]{3,2,1,0:T(8,128)S(1)} collective-permute-done((f32[2,4,128,128]{3,2,1,0:T(8,128)S(1)}, f32[2,4,128,128]{3,2,1,0:T(8,128)S(1)}, u32[]{:S(2)}, u32[]{:S(2)}) %collective-permute-start.2) | collective-permute-done | bytes 524320 | tf_op jit(solution)/shard_map/ppermute | solution.py:309
  16.1 0.0 collective-permute-start.4
  16.2 2.0 %collective-permute-start.7 = (f32[1,4,128,128]{3,2,1,0:T(8,128)S(1)}, f32[1,4,128,128]{3,2,1,0:T(8,128)S(1)}, u32[]{:S(2)}, u32[]{:S(2)}) collective-permute-start(f32[1,4,128,128]{3,2,1,0:T(8,128)S(1)} %get-tuple-element.35), channel_id=1, source_target_pairs={{15,1},{1,5},{5,9},{9,13},{13,14},{14,15},{2,12},{12,8},{8,4},{4,0... | collective-permute-start | bytes 786440 | tf_op jit(solution)/shard_map/ppermute | solution.py:301
  18.2 0.1 collective-permute-start.6
  18.2 3.5 %collective-permute-done.5.r3 = f32[2,4,128,128]{3,2,1,0:T(8,128)S(1)} collective-permute-done((f32[2,4,128,128]{3,2,1,0:T(8,128)S(1)}, f32[2,4,128,128]{3,2,1,0:T(8,128)S(1)}, u32[]{:S(2)}, u32[]{:S(2)}) %collective-permute-start.5) | collective-permute-done | bytes 524320 | tf_op jit(solution)/shard_map/ppermute | solution.py:301
  21.7 0.0 collective-permute-start.10
  21.7 0.0 collective-permute-done.3.t1
  21.7 0.0 collective-permute-done.4.t2
  21.8 3.1 %early.1 = (bf16[1024,1024]{1,0:T(8,128)(2,1)S(1)}, bf16[1024,1024]{1,0:T(8,128)(2,1)S(1)}, bf16[512,1024]{1,0:T(8,128)(2,1)S(1)}, f32[256,1024]{1,0:T(8,128)S(1)}, s32[8,128]{1,0:T(8,128)S(1)}) custom-call(s32[8,9]{1,0:T(8,128)S(1)} %pad_add_fusion.table_ref, f32[2,4,128,128]{3,2,1,0:T(8,128)} %own_hbm.1, ...), custom_call_target="tpu_custom_call" | custom-call | tf_op jit(solution)/shard_map/early/pallas_call | solution.py:342
  24.9 0.0 collective-permute-done.7.r4a
  24.9 0.6 %collective-permute-start.8 = (f32[1,4,128,128]{3,2,1,0:T(8,128)S(1)}, f32[1,4,128,128]{3,2,1,0:T(8,128)S(1)}, u32[]{:S(2)}, u32[]{:S(2)}) collective-permute-start(f32[1,4,128,128]{3,2,1,0:T(8,128)S(1)} %collective-permute-done.7.r4a), channel_id=1, source_target_pairs={{1,0},{0,1},{17,16},{16,17},{3,2},{2,3},{19,18},{18,19},{5,4},{4,5... | collective-permute-start | bytes 786440 | tf_op jit(solution)/shard_map/ppermute | solution.py:301
  25.5 1.9 %collective-permute-done.6.r4b = f32[1,4,128,128]{3,2,1,0:T(8,128)S(1)} collective-permute-done((f32[1,4,128,128]{3,2,1,0:T(8,128)S(1)}, f32[1,4,128,128]{3,2,1,0:T(8,128)S(1)}, u32[]{:S(2)}, u32[]{:S(2)}) %collective-permute-start.6) | collective-permute-done | bytes 262176 | tf_op jit(solution)/shard_map/ppermute | solution.py:301
  27.4 0.0 collective-permute-done.8.t4a
  27.4 0.1 collective-permute-start.9
  27.5 1.3 %middle.1 = (bf16[1024,1024]{1,0:T(8,128)(2,1)S(1)}, bf16[1024,1024]{1,0:T(8,128)(2,1)S(1)}, f32[256,1024]{1,0:T(8,128)S(1)}) custom-call(s32[8,128]{1,0:T(8,128)S(1)} %get-tuple-element.22.notes_ref, f32[1,4,128,128]{3,2,1,0:T(8,128)S(1)} %collective-permute-done.7.r4a, ...), custom_call_target="tpu_custom_call", output_to_operand_aliasing={{0}: (5, {}), {1}: (6, {}), {2}: (8, {})} | custom-call | tf_op jit(solution)/shard_map/middle/pallas_call | solution.py:363
  28.8 0.1 collective-permute-done.9.t4b
  28.9 3.1 %late.1 = (f32[2,4,128,128]{3,2,1,0:T(8,128)}, bf16[1024,1024]{1,0:T(8,128)(2,1)S(1)}, bf16[1024,1024]{1,0:T(8,128)(2,1)S(1)}, f32[256,1024]{1,0:T(8,128)S(1)}) custom-call(s32[8,128]{1,0:T(8,128)S(1)} %get-tuple-element.22.notes_ref, f32[1,4,128,128]{3,2,1,0:T(8,128)S(1)} %collective-permute-done.9.t4b, ...), custom_call_target="tpu_custom_call", output_to_operand_aliasing={{1}: (2, {}), {2}: (3, {}), {3}: (5, {})} | custom-call | tf_op jit(solution)/shard_map/late/pallas_call | solution.py:372
  (5 shorter events, 0.1 us)
Async XLA Ops:
  0.0 10.4 %collective-permute-start = (f32[2,4,128,128]{3,2,1,0:T(8,128)}, f32[2,4,128,128]{3,2,1,0:T(8,128)S(1)}, u32[]{:S(2)}, u32[]{:S(2)}) collective-permute-start(f32[2,4,128,128]{3,2,1,0:T(8,128)} %own_hbm.1), channel_id=1, source_target_pairs={{3,1},{1,5},{5,9},{9,13},{13,15},{15,14},{14,12},{12,8},{8,4},{4,0... | collective-permute-start | bytes 1572872 | tf_op jit(solution)/shard_map/ppermute | solution.py:301
  2.9 2.1 %collective-permute-start.1 = (f32[2,4,128,128]{3,2,1,0:T(8,128)}, f32[2,4,128,128]{3,2,1,0:T(8,128)S(1)}, u32[]{:S(2)}, u32[]{:S(2)}) collective-permute-start(f32[2,4,128,128]{3,2,1,0:T(8,128)} %own_hbm.1), channel_id=1, source_target_pairs={{1,0},{0,1},{17,16},{16,17},{3,2},{2,3},{19,18},{18,19},{5,4},{4,5... | collective-permute-start | bytes 1572872 | tf_op jit(solution)/shard_map/ppermute | solution.py:301
  5.1 11.1 %collective-permute-start.2 = (f32[2,4,128,128]{3,2,1,0:T(8,128)S(1)}, f32[2,4,128,128]{3,2,1,0:T(8,128)S(1)}, u32[]{:S(2)}, u32[]{:S(2)}) collective-permute-start(f32[2,4,128,128]{3,2,1,0:T(8,128)S(1)} %collective-permute-done.1.own_swap), channel_id=1, source_target_pairs={{1,5},{5,9},{9,13},{13,15},{12,8},{8,4},{4,0},{0,2},{17,21},{21,25... | collective-permute-start | bytes 1572872 | tf_op jit(solution)/shard_map/ppermute | solution.py:309
  10.4 11.3 %collective-permute-start.5 = (f32[2,4,128,128]{3,2,1,0:T(8,128)S(1)}, f32[2,4,128,128]{3,2,1,0:T(8,128)S(1)}, u32[]{:S(2)}, u32[]{:S(2)}) collective-permute-start(f32[2,4,128,128]{3,2,1,0:T(8,128)S(1)} %collective-permute-done.r1), channel_id=1, source_target_pairs={{15,1},{1,5},{5,9},{9,13},{13,14},{14,15},{2,12},{12,8},{8,4},{4,0... | collective-permute-start | bytes 1572872 | tf_op jit(solution)/shard_map/ppermute | solution.py:301
  10.4 11.4 %collective-permute-start.3 = (f32[2,4,128,128]{3,2,1,0:T(8,128)S(1)}, f32[2,4,128,128]{3,2,1,0:T(8,128)S(1)}, u32[]{:S(2)}, u32[]{:S(2)}) collective-permute-start(f32[2,4,128,128]{3,2,1,0:T(8,128)S(1)} %collective-permute-done.r1), channel_id=1, source_target_pairs={{1,0},{0,1},{17,16},{16,17},{3,2},{2,3},{19,18},{18,19},{5,4},{4,5... | collective-permute-start | bytes 1572872 | tf_op jit(solution)/shard_map/ppermute | solution.py:301
  16.1 5.6 %collective-permute-start.4 = (f32[2,4,128,128]{3,2,1,0:T(8,128)S(1)}, f32[2,4,128,128]{3,2,1,0:T(8,128)S(1)}, u32[]{:S(2)}, u32[]{:S(2)}) collective-permute-start(f32[2,4,128,128]{3,2,1,0:T(8,128)S(1)} %collective-permute-done.2.r2), channel_id=1, source_target_pairs={{1,0},{0,1},{17,16},{16,17},{3,2},{2,3},{19,18},{18,19},{5,4},{4,5... | collective-permute-start | bytes 1572872 | tf_op jit(solution)/shard_map/ppermute | solution.py:301
  16.2 8.7 %collective-permute-start.7 = (f32[1,4,128,128]{3,2,1,0:T(8,128)S(1)}, f32[1,4,128,128]{3,2,1,0:T(8,128)S(1)}, u32[]{:S(2)}, u32[]{:S(2)}) collective-permute-start(f32[1,4,128,128]{3,2,1,0:T(8,128)S(1)} %get-tuple-element.35), channel_id=1, source_target_pairs={{15,1},{1,5},{5,9},{9,13},{13,14},{14,15},{2,12},{12,8},{8,4},{4,0... | collective-permute-start | bytes 786440 | tf_op jit(solution)/shard_map/ppermute | solution.py:301
  18.2 9.2 %collective-permute-start.6 = (f32[1,4,128,128]{3,2,1,0:T(8,128)S(1)}, f32[1,4,128,128]{3,2,1,0:T(8,128)S(1)}, u32[]{:S(2)}, u32[]{:S(2)}) collective-permute-start(f32[1,4,128,128]{3,2,1,0:T(8,128)S(1)} %get-tuple-element.36), channel_id=1, source_target_pairs={{15,1},{1,5},{5,9},{9,13},{13,14},{14,15},{2,12},{12,8},{8,4},{4,0... | collective-permute-start | bytes 786440 | tf_op jit(solution)/shard_map/ppermute | solution.py:301
  21.7 5.7 %collective-permute-start.10 = (f32[2,4,128,128]{3,2,1,0:T(8,128)S(1)}, f32[2,4,128,128]{3,2,1,0:T(8,128)S(1)}, u32[]{:S(2)}, u32[]{:S(2)}) collective-permute-start(f32[2,4,128,128]{3,2,1,0:T(8,128)S(1)} %collective-permute-done.5.r3), channel_id=1, source_target_pairs={{1,0},{0,1},{17,16},{16,17},{3,2},{2,3},{19,18},{18,19},{5,4},{4,5... | collective-permute-start | bytes 1572872 | tf_op jit(solution)/shard_map/ppermute | solution.py:301
  24.9 2.5 %collective-permute-start.8 = (f32[1,4,128,128]{3,2,1,0:T(8,128)S(1)}, f32[1,4,128,128]{3,2,1,0:T(8,128)S(1)}, u32[]{:S(2)}, u32[]{:S(2)}) collective-permute-start(f32[1,4,128,128]{3,2,1,0:T(8,128)S(1)} %collective-permute-done.7.r4a), channel_id=1, source_target_pairs={{1,0},{0,1},{17,16},{16,17},{3,2},{2,3},{19,18},{18,19},{5,4},{4,5... | collective-permute-start | bytes 786440 | tf_op jit(solution)/shard_map/ppermute | solution.py:301
  27.4 1.5 %collective-permute-start.9 = (f32[1,4,128,128]{3,2,1,0:T(8,128)S(1)}, f32[1,4,128,128]{3,2,1,0:T(8,128)S(1)}, u32[]{:S(2)}, u32[]{:S(2)}) collective-permute-start(f32[1,4,128,128]{3,2,1,0:T(8,128)S(1)} %collective-permute-done.6.r4b), channel_id=1, source_target_pairs={{1,0},{0,1},{17,16},{16,17},{3,2},{2,3},{19,18},{18,19},{5,4},{4,5... | collective-permute-start | bytes 786440 | tf_op jit(solution)/shard_map/ppermute | solution.py:301

commit v20 on v18

--- a/solution.py
+++ b/solution.py
@@ -159,19 +159,26 @@
     high, low, left, part_ref, notes_ref, own_ref, own_sem,
 ):
     place, lane = lax.axis_index("blk"), lax.axis_index("depth")
-    near, far = tables
+    (near, near_senders), (far, far_senders) = tables
     slab, width = own_swap.shape[:2]
     act = 2 * width
     own_copy = pltpu.make_async_copy(own_hbm, own_ref, own_sem)
     own_copy.start()
     here, there = lookup(near, place, lane), lookup(near, place, 1 - lane)
     far_here, far_there = lookup(far, place, lane), lookup(far, place, 1 - lane)
+    sender, other_sender = [lookup(near_senders, place, c) for c in (lane, 1 - lane)]
+    far_sender, far_other = [lookup(far_senders, place, c) for c in (lane, 1 - lane)]
     part_ref[...] = jnp.zeros_like(part_ref)
 
     def codes(plane, group):
         return table_codes(table_ref, plane, group, slab, width)
 
-    kinds = ((far_there, 1 - lane), (far_here, 1 - lane), (far_there, lane), (place, lane))
+    kinds = (
+        (far_there, far_other),
+        (far_here, 1 - far_sender),
+        (far_there, 1 - far_other),
+        (place, lane),
+    )
     notes = jnp.zeros(notes_ref.shape, jnp.int32)
     index = lax.broadcasted_iota(jnp.int32, notes.shape, 1)
     for kind, (plane, group) in enumerate(kinds):
@@ -186,11 +193,11 @@
     notes_ref[...] = notes
 
     store_piece(own_swap, place, codes(place, 1 - lane), high, low, left)
-    store_piece(r1, here, codes(here, lane), high, low)
-    store_piece(r2, here, codes(here, 1 - lane), high, low)
-    store_piece(t1, there, codes(there, 1 - lane), high, low)
-    store_piece(t2, there, codes(there, lane), high, low)
-    store_piece(r3, far_here, codes(far_here, lane), high, low)
+    store_piece(r1, here, codes(here, sender), high, low)
+    store_piece(r2, here, codes(here, 1 - sender), high, low)
+    store_piece(t1, there, codes(there, other_sender), high, low)
+    store_piece(t2, there, codes(there, 1 - other_sender), high, low)
+    store_piece(r3, far_here, codes(far_here, far_sender), high, low)
     own_copy.wait()
     store_piece(own_ref, place, codes(place, lane), high, low, left)
     for plane in (place, here, there):
@@ -201,7 +208,7 @@
     tables, notes_ref, r4a, r4b, t3, t4a, high_in, low_in, left, part_in, high, low, part_ref
 ):
     place, lane = lax.axis_index("blk"), lax.axis_index("depth")
-    here, there = lookup(tables[1], place, lane), lookup(tables[1], place, 1 - lane)
+    here, there = [lookup(tables[1][0], place, c) for c in (lane, 1 - lane)]
     slab, width = t3.shape[:2]
     notes = notes_ref[...]
     store_piece(t3, there, noted_codes(notes, T3, slab, width), high, low)
@@ -216,7 +223,7 @@
     out_hbm, high, low, square, square_parts, out_ref, out_sem,
 ):
     place, lane = lax.axis_index("blk"), lax.axis_index("depth")
-    there = lookup(tables[1], place, 1 - lane)
+    there = lookup(tables[1][0], place, 1 - lane)
     slab, width, edge, _ = out_ref.shape
     act = 2 * width
     holds = lax.axis_index("panel") == 0
@@ -304,15 +311,27 @@
         route = [(index(g, a), index(g, b)) for g in range(groups) for a, b in pairs]
         return lax.ppermute(block, AXES, route)
 
-    up = [(z, 0, 1) for z in range(chains)] + [(last, 1, 1)]
-    down = [(z, 0, 0) for z in reversed(range(chains))] + [(0, 1, 0)]
-    first = [up + [(last, 1, 0)] + down + [(0, 1, 1)]]
+    down_lane = [1 if z == 1 else 0 for z in range(chains)]
+    up_lane = [1 - c for c in down_lane]
+    up = [(z, 0, up_lane[z]) for z in range(chains)] + [(last, 1, up_lane[last])]
+    down = [(z, 0, down_lane[z]) for z in reversed(range(chains))] + [(0, 1, down_lane[0])]
+    first = [up + [(last, 1, down_lane[last])] + down + [(0, 1, up_lane[0])]]
     second = [up, down]
-    near = [(z + 1 if z < last else -1, z - 1) for z in range(chains)]
-    far = [(z + 2 if z + 2 < chains else -1, z - 2 if z >= 2 else -1) for z in range(chains)]
-    far[0] = (far[0][0], last)
-    far[last] = (0, far[last][1])
-    tables = (near, far)
+
+    def received(hops):
+        planes, senders = [], []
+        for z in range(chains):
+            below = z - hops if z >= hops else -1
+            above = z + hops if z + hops < chains else -1
+            if hops == 2:
+                below, above = last if z == 0 else below, 0 if z == last else above
+            row = [above, below] if down_lane[z] == 0 else [below, above]
+            lane_of = [down_lane, up_lane] if down_lane[z] == 0 else [up_lane, down_lane]
+            planes.append(row)
+            senders.append([lanes_of[plane] for plane, lanes_of in zip(row, lane_of)])
+        return planes, senders
+
+    tables = received(1), received(2)
 
     table = slot_table(columns, lanes * width)
     r1 = move(x_blocks, first)

time: 32.3 us -> 32.3 us (level)
  the two profiles are of different devices: /device:TPU:0 before, /device:TPU:25 now
where the time goes in v20:
time: 32.3 us; the launch traced here: 32.1 us
  starting transfers between devices  11.4 us (35%)
  waiting for transfers between devices  10.7 us (33%)
  Pallas kernels  7.56 us (23%)
  other arithmetic  2.24 us (7%)
    ppermute x10, starting transfers between devices, move(): return lax.ppermute(block, AXES, route)  8.48 us
    ppermute x10, waiting for transfers between devices, move(): return lax.ppermute(block, AXES, route)  7.32 us
    ppermute x1, waiting for transfers between devices, move_only(): return lax.ppermute(block, AXES, route)  3.34 us
    pallas_call x1, Pallas kernels, gather_local(): pl.pallas_call(functools.partial(late_kernel, tables), out_shape=[jax.Sha...  3.15 us
    pallas_call x1, Pallas kernels, gather_local(): pl.pallas_call(functools.partial(early_kernel, tables), out_shape=[jax.Sh...  3.07 us
    ppermute x1, starting transfers between devices, move_only(): return lax.ppermute(block, AXES, route)  2.95 us
    pallas_call x1, Pallas kernels, gather_local(): pl.pallas_call(functools.partial(middle_kernel, tables), out_shape=dense,...  1.34 us
    reduce_sum x1, other arithmetic, slot_table(): count = jnp.sum(here.astype(jnp.int32), axis=1, keepdims=True)  0.8 us
  transfers between devices with their start and end apart: 11, of which 6 were waited for; matrix products, arithmetic and copies ran while one was open for 7% of the time, Pallas kernels for 14%

profile of v20, /device:TPU:25, one launch (start us, length us, event | category | flops | bytes accessed | tf_op | source)
XLA Modules:
  0.0 32.1 jit_solution(16635634111643406650)
XLA Ops:
  0.0 1.2 %collective-permute-start = (f32[2,4,128,128]{3,2,1,0:T(8,128)}, f32[2,4,128,128]{3,2,1,0:T(8,128)S(1)}, u32[]{:S(2)}, u32[]{:S(2)}) collective-permute-start(f32[2,4,128,128]{3,2,1,0:T(8,128)} %own_hbm.1), channel_id=1, source_target_pairs={{3,1},{1,4},{4,9},{9,13},{13,15},{15,14},{14,12},{12,8},{8,5},{5,0... | collective-permute-start | bytes 1572872 | tf_op jit(solution)/shard_map/ppermute | solution.py:304
  1.2 0.0 collective-permute-start.1
  1.2 0.8 %fusion.1 = (s32[8]{0:T(128)S(1)}, s32[8,8]{1,0:T(8,128)S(1)}) fusion(s32[8,16]{1,0:T(8,128)} %param.3), kind=kLoop, calls=%fused_computation.7 | loop fusion | flops 184 | bytes 544 | tf_op jit(solution)/shard_map/reduce_sum | solution.py:269
  2.0 0.1 fusion
  2.1 0.2 convert_reduce_fusion
  2.4 1.0 %collective-permute-done.1.own_swap = f32[2,4,128,128]{3,2,1,0:T(8,128)S(1)} collective-permute-done((f32[2,4,128,128]{3,2,1,0:T(8,128)}, f32[2,4,128,128]{3,2,1,0:T(8,128)S(1)}, u32[]{:S(2)}, u32[]{:S(2)}) %collective-permute-start.1) | collective-permute-done | bytes 524320 | tf_op jit(solution)/shard_map/ppermute | solution.py:304
  3.3 2.9 %collective-permute-start.2 = (f32[2,4,128,128]{3,2,1,0:T(8,128)S(1)}, f32[2,4,128,128]{3,2,1,0:T(8,128)S(1)}, u32[]{:S(2)}, u32[]{:S(2)}) collective-permute-start(f32[2,4,128,128]{3,2,1,0:T(8,128)S(1)} %collective-permute-done.1.own_swap), channel_id=1, source_target_pairs={{1,4},{4,9},{9,13},{13,15},{12,8},{8,5},{5,0},{0,2},{17,20},{20,25... | collective-permute-start | bytes 1572872 | tf_op jit(solution)/shard_map/ppermute | solution.py:312
  6.3 0.1 add_select_fusion
  6.4 0.1 copy.10
  6.5 0.2 select_reduce_fusion
  6.7 0.7 %compare_select_fusion = s32[8,8]{1,0:T(8,128)S(1)} fusion(s32[8,8]{1,0:T(8,128)S(1)} %select_reduce_fusion, s32[8,16]{1,0:T(8,128)} %param.3), kind=kLoop, calls=%fused_computation.5 | loop fusion | flops 192 | bytes 768 | tf_op jit(solution)/shard_map/jit(_where)/select_n | solution.py:277
  7.4 0.1 pad_add_fusion.table_ref
  7.5 1.1 %collective-permute-done.r1 = f32[2,4,128,128]{3,2,1,0:T(8,128)S(1)} collective-permute-done((f32[2,4,128,128]{3,2,1,0:T(8,128)}, f32[2,4,128,128]{3,2,1,0:T(8,128)S(1)}, u32[]{:S(2)}, u32[]{:S(2)}) %collective-permute-start) | collective-permute-done | bytes 524320 | tf_op jit(solution)/shard_map/ppermute | solution.py:304
  8.5 0.9 %collective-permute-start.5 = (f32[2,4,128,128]{3,2,1,0:T(8,128)S(1)}, f32[2,4,128,128]{3,2,1,0:T(8,128)S(1)}, u32[]{:S(2)}, u32[]{:S(2)}) collective-permute-start(f32[2,4,128,128]{3,2,1,0:T(8,128)S(1)} %collective-permute-done.r1), channel_id=1, source_target_pairs={{15,1},{1,4},{4,9},{9,13},{13,15},{2,12},{12,8},{8,5},{5,0},{0,2},... | collective-permute-start | bytes 1572872 | tf_op jit(solution)/shard_map/ppermute | solution.py:304
  9.5 1.1 %collective-permute-start.3 = (f32[2,4,128,128]{3,2,1,0:T(8,128)S(1)}, f32[2,4,128,128]{3,2,1,0:T(8,128)S(1)}, u32[]{:S(2)}, u32[]{:S(2)}) collective-permute-start(f32[2,4,128,128]{3,2,1,0:T(8,128)S(1)} %collective-permute-done.r1), channel_id=1, source_target_pairs={{1,0},{0,1},{17,16},{16,17},{3,2},{2,3},{19,18},{18,19},{5,4},{4,5... | collective-permute-start | bytes 1572872 | tf_op jit(solution)/shard_map/ppermute | solution.py:304
  10.5 3.3 %collective-permute-done.2.r2 = f32[2,4,128,128]{3,2,1,0:T(8,128)S(1)} collective-permute-done((f32[2,4,128,128]{3,2,1,0:T(8,128)S(1)}, f32[2,4,128,128]{3,2,1,0:T(8,128)S(1)}, u32[]{:S(2)}, u32[]{:S(2)}) %collective-permute-start.2) | collective-permute-done | bytes 524320 | tf_op jit(solution)/shard_map/ppermute | solution.py:312
  13.9 0.0 collective-permute-start.4
  13.9 1.6 %collective-permute-start.7 = (f32[1,4,128,128]{3,2,1,0:T(8,128)S(1)}, f32[1,4,128,128]{3,2,1,0:T(8,128)S(1)}, u32[]{:S(2)}, u32[]{:S(2)}) collective-permute-start(f32[1,4,128,128]{3,2,1,0:T(8,128)S(1)} %get-tuple-element.35), channel_id=1, source_target_pairs={{15,1},{1,4},{4,9},{9,13},{13,15},{2,12},{12,8},{8,5},{5,0},{0,2},... | collective-permute-start | bytes 786440 | tf_op jit(solution)/shard_map/ppermute | solution.py:304
  15.5 0.5 %collective-permute-start.6 = (f32[1,4,128,128]{3,2,1,0:T(8,128)S(1)}, f32[1,4,128,128]{3,2,1,0:T(8,128)S(1)}, u32[]{:S(2)}, u32[]{:S(2)}) collective-permute-start(f32[1,4,128,128]{3,2,1,0:T(8,128)S(1)} %get-tuple-element.36), channel_id=1, source_target_pairs={{15,1},{1,4},{4,9},{9,13},{13,15},{2,12},{12,8},{8,5},{5,0},{0,2},... | collective-permute-start | bytes 786440 | tf_op jit(solution)/shard_map/ppermute | solution.py:304
  16.0 3.8 %collective-permute-done.5.r3 = f32[2,4,128,128]{3,2,1,0:T(8,128)S(1)} collective-permute-done((f32[2,4,128,128]{3,2,1,0:T(8,128)S(1)}, f32[2,4,128,128]{3,2,1,0:T(8,128)S(1)}, u32[]{:S(2)}, u32[]{:S(2)}) %collective-permute-start.5) | collective-permute-done | bytes 524320 | tf_op jit(solution)/shard_map/ppermute | solution.py:304
  19.8 2.2 %collective-permute-start.10 = (f32[2,4,128,128]{3,2,1,0:T(8,128)S(1)}, f32[2,4,128,128]{3,2,1,0:T(8,128)S(1)}, u32[]{:S(2)}, u32[]{:S(2)}) collective-permute-start(f32[2,4,128,128]{3,2,1,0:T(8,128)S(1)} %collective-permute-done.5.r3), channel_id=1, source_target_pairs={{1,0},{0,1},{17,16},{16,17},{3,2},{2,3},{19,18},{18,19},{5,4},{4,5... | collective-permute-start | bytes 1572872 | tf_op jit(solution)/shard_map/ppermute | solution.py:304
  21.9 0.0 collective-permute-done.3.t1
  21.9 0.0 collective-permute-done.4.t2
  22.0 3.1 %early.1 = (bf16[1024,1024]{1,0:T(8,128)(2,1)S(1)}, bf16[1024,1024]{1,0:T(8,128)(2,1)S(1)}, bf16[512,1024]{1,0:T(8,128)(2,1)S(1)}, f32[256,1024]{1,0:T(8,128)S(1)}, s32[8,128]{1,0:T(8,128)S(1)}) custom-call(s32[8,9]{1,0:T(8,128)S(1)} %pad_add_fusion.table_ref, f32[2,4,128,128]{3,2,1,0:T(8,128)} %own_hbm.1, ...), custom_call_target="tpu_custom_call" | custom-call | tf_op jit(solution)/shard_map/early/pallas_call | solution.py:354
  25.0 0.0 collective-permute-done.7.r4a
  25.0 0.1 collective-permute-start.8
  25.1 0.3 collective-permute-done.6.r4b
  25.4 1.2 %collective-permute-done.8.t4a = f32[1,4,128,128]{3,2,1,0:T(8,128)S(1)} collective-permute-done((f32[1,4,128,128]{3,2,1,0:T(8,128)S(1)}, f32[1,4,128,128]{3,2,1,0:T(8,128)S(1)}, u32[]{:S(2)}, u32[]{:S(2)}) %collective-permute-start.8) | collective-permute-done | bytes 262176 | tf_op jit(solution)/shard_map/ppermute | solution.py:304
  26.6 0.9 %collective-permute-start.9 = (f32[1,4,128,128]{3,2,1,0:T(8,128)S(1)}, f32[1,4,128,128]{3,2,1,0:T(8,128)S(1)}, u32[]{:S(2)}, u32[]{:S(2)}) collective-permute-start(f32[1,4,128,128]{3,2,1,0:T(8,128)S(1)} %collective-permute-done.6.r4b), channel_id=1, source_target_pairs={{1,0},{0,1},{17,16},{16,17},{3,2},{2,3},{19,18},{18,19},{5,4},{4,5... | collective-permute-start | bytes 786440 | tf_op jit(solution)/shard_map/ppermute | solution.py:304
  27.6 0.0 collective-permute-done.10.t3
  27.6 1.3 %middle.1 = (bf16[1024,1024]{1,0:T(8,128)(2,1)S(1)}, bf16[1024,1024]{1,0:T(8,128)(2,1)S(1)}, f32[256,1024]{1,0:T(8,128)S(1)}) custom-call(s32[8,128]{1,0:T(8,128)S(1)} %get-tuple-element.22.notes_ref, f32[1,4,128,128]{3,2,1,0:T(8,128)S(1)} %collective-permute-done.7.r4a, ...), custom_call_target="tpu_custom_call", output_to_operand_aliasing={{0}: (5, {}), {1}: (6, {}), {2}: (8, {})} | custom-call | tf_op jit(solution)/shard_map/middle/pallas_call | solution.py:375
  28.9 3.2 %late.1 = (f32[2,4,128,128]{3,2,1,0:T(8,128)}, bf16[1024,1024]{1,0:T(8,128)(2,1)S(1)}, bf16[1024,1024]{1,0:T(8,128)(2,1)S(1)}, f32[256,1024]{1,0:T(8,128)S(1)}) custom-call(s32[8,128]{1,0:T(8,128)S(1)} %get-tuple-element.22.notes_ref, f32[1,4,128,128]{3,2,1,0:T(8,128)S(1)} %collective-permute-done.9.t4b, ...), custom_call_target="tpu_custom_call", output_to_operand_aliasing={{1}: (2, {}), {2}: (3, {}), {3}: (5, {})} | custom-call | tf_op jit(solution)/shard_map/late/pallas_call | solution.py:384
  (5 shorter events, 0.1 us)
Async XLA Ops:
  0.0 8.5 %collective-permute-start = (f32[2,4,128,128]{3,2,1,0:T(8,128)}, f32[2,4,128,128]{3,2,1,0:T(8,128)S(1)}, u32[]{:S(2)}, u32[]{:S(2)}) collective-permute-start(f32[2,4,128,128]{3,2,1,0:T(8,128)} %own_hbm.1), channel_id=1, source_target_pairs={{3,1},{1,4},{4,9},{9,13},{13,15},{15,14},{14,12},{12,8},{8,5},{5,0... | collective-permute-start | bytes 1572872 | tf_op jit(solution)/shard_map/ppermute | solution.py:304
  1.2 2.1 %collective-permute-start.1 = (f32[2,4,128,128]{3,2,1,0:T(8,128)}, f32[2,4,128,128]{3,2,1,0:T(8,128)S(1)}, u32[]{:S(2)}, u32[]{:S(2)}) collective-permute-start(f32[2,4,128,128]{3,2,1,0:T(8,128)} %own_hbm.1), channel_id=1, source_target_pairs={{1,0},{0,1},{17,16},{16,17},{3,2},{2,3},{19,18},{18,19},{5,4},{4,5... | collective-permute-start | bytes 1572872 | tf_op jit(solution)/shard_map/ppermute | solution.py:304
  3.3 10.5 %collective-permute-start.2 = (f32[2,4,128,128]{3,2,1,0:T(8,128)S(1)}, f32[2,4,128,128]{3,2,1,0:T(8,128)S(1)}, u32[]{:S(2)}, u32[]{:S(2)}) collective-permute-start(f32[2,4,128,128]{3,2,1,0:T(8,128)S(1)} %collective-permute-done.1.own_swap), channel_id=1, source_target_pairs={{1,4},{4,9},{9,13},{13,15},{12,8},{8,5},{5,0},{0,2},{17,20},{20,25... | collective-permute-start | bytes 1572872 | tf_op jit(solution)/shard_map/ppermute | solution.py:312
  8.5 11.2 %collective-permute-start.5 = (f32[2,4,128,128]{3,2,1,0:T(8,128)S(1)}, f32[2,4,128,128]{3,2,1,0:T(8,128)S(1)}, u32[]{:S(2)}, u32[]{:S(2)}) collective-permute-start(f32[2,4,128,128]{3,2,1,0:T(8,128)S(1)} %collective-permute-done.r1), channel_id=1, source_target_pairs={{15,1},{1,4},{4,9},{9,13},{13,15},{2,12},{12,8},{8,5},{5,0},{0,2},... | collective-permute-start | bytes 1572872 | tf_op jit(solution)/shard_map/ppermute | solution.py:304
  9.5 12.5 %collective-permute-start.3 = (f32[2,4,128,128]{3,2,1,0:T(8,128)S(1)}, f32[2,4,128,128]{3,2,1,0:T(8,128)S(1)}, u32[]{:S(2)}, u32[]{:S(2)}) collective-permute-start(f32[2,4,128,128]{3,2,1,0:T(8,128)S(1)} %collective-permute-done.r1), channel_id=1, source_target_pairs={{1,0},{0,1},{17,16},{16,17},{3,2},{2,3},{19,18},{18,19},{5,4},{4,5... | collective-permute-start | bytes 1572872 | tf_op jit(solution)/shard_map/ppermute | solution.py:304
  13.9 8.1 %collective-permute-start.4 = (f32[2,4,128,128]{3,2,1,0:T(8,128)S(1)}, f32[2,4,128,128]{3,2,1,0:T(8,128)S(1)}, u32[]{:S(2)}, u32[]{:S(2)}) collective-permute-start(f32[2,4,128,128]{3,2,1,0:T(8,128)S(1)} %collective-permute-done.2.r2), channel_id=1, source_target_pairs={{1,0},{0,1},{17,16},{16,17},{3,2},{2,3},{19,18},{18,19},{5,4},{4,5... | collective-permute-start | bytes 1572872 | tf_op jit(solution)/shard_map/ppermute | solution.py:304
  13.9 11.1 %collective-permute-start.7 = (f32[1,4,128,128]{3,2,1,0:T(8,128)S(1)}, f32[1,4,128,128]{3,2,1,0:T(8,128)S(1)}, u32[]{:S(2)}, u32[]{:S(2)}) collective-permute-start(f32[1,4,128,128]{3,2,1,0:T(8,128)S(1)} %get-tuple-element.35), channel_id=1, source_target_pairs={{15,1},{1,4},{4,9},{9,13},{13,15},{2,12},{12,8},{8,5},{5,0},{0,2},... | collective-permute-start | bytes 786440 | tf_op jit(solution)/shard_map/ppermute | solution.py:304
  15.5 9.9 %collective-permute-start.6 = (f32[1,4,128,128]{3,2,1,0:T(8,128)S(1)}, f32[1,4,128,128]{3,2,1,0:T(8,128)S(1)}, u32[]{:S(2)}, u32[]{:S(2)}) collective-permute-start(f32[1,4,128,128]{3,2,1,0:T(8,128)S(1)} %get-tuple-element.36), channel_id=1, source_target_pairs={{15,1},{1,4},{4,9},{9,13},{13,15},{2,12},{12,8},{8,5},{5,0},{0,2},... | collective-permute-start | bytes 786440 | tf_op jit(solution)/shard_map/ppermute | solution.py:304
  19.8 7.8 %collective-permute-start.10 = (f32[2,4,128,128]{3,2,1,0:T(8,128)S(1)}, f32[2,4,128,128]{3,2,1,0:T(8,128)S(1)}, u32[]{:S(2)}, u32[]{:S(2)}) collective-permute-start(f32[2,4,128,128]{3,2,1,0:T(8,128)S(1)} %collective-permute-done.5.r3), channel_id=1, source_target_pairs={{1,0},{0,1},{17,16},{16,17},{3,2},{2,3},{19,18},{18,19},{5,4},{4,5... | collective-permute-start | bytes 1572872 | tf_op jit(solution)/shard_map/ppermute | solution.py:304
  25.0 1.6 %collective-permute-start.8 = (f32[1,4,128,128]{3,2,1,0:T(8,128)S(1)}, f32[1,4,128,128]{3,2,1,0:T(8,128)S(1)}, u32[]{:S(2)}, u32[]{:S(2)}) collective-permute-start(f32[1,4,128,128]{3,2,1,0:T(8,128)S(1)} %collective-permute-done.7.r4a), channel_id=1, source_target_pairs={{1,0},{0,1},{17,16},{16,17},{3,2},{2,3},{19,18},{18,19},{5,4},{4,5... | collective-permute-start | bytes 786440 | tf_op jit(solution)/shard_map/ppermute | solution.py:304
  26.6 2.3 %collective-permute-start.9 = (f32[1,4,128,128]{3,2,1,0:T(8,128)S(1)}, f32[1,4,128,128]{3,2,1,0:T(8,128)S(1)}, u32[]{:S(2)}, u32[]{:S(2)}) collective-permute-start(f32[1,4,128,128]{3,2,1,0:T(8,128)S(1)} %collective-permute-done.6.r4b), channel_id=1, source_target_pairs={{1,0},{0,1},{17,16},{16,17},{3,2},{2,3},{19,18},{18,19},{5,4},{4,5... | collective-permute-start | bytes 786440 | tf_op jit(solution)/shard_map/ppermute | solution.py:304

commit v21 on v20

--- a/solution.py
+++ b/solution.py
@@ -159,13 +159,15 @@
     high, low, left, part_ref, notes_ref, own_ref, own_sem,
 ):
     place, lane = lax.axis_index("blk"), lax.axis_index("depth")
-    (near, near_senders), (far, far_senders) = tables
+    (hop1, hop1_senders), (near, near_senders), (far, far_senders) = tables
     slab, width = own_swap.shape[:2]
     act = 2 * width
     own_copy = pltpu.make_async_copy(own_hbm, own_ref, own_sem)
     own_copy.start()
     here, there = lookup(near, place, lane), lookup(near, place, 1 - lane)
     far_here, far_there = lookup(far, place, lane), lookup(far, place, 1 - lane)
+    first_here, first_there = [lookup(hop1, place, c) for c in (lane, 1 - lane)]
+    first_sender, first_other = [lookup(hop1_senders, place, c) for c in (lane, 1 - lane)]
     sender, other_sender = [lookup(near_senders, place, c) for c in (lane, 1 - lane)]
     far_sender, far_other = [lookup(far_senders, place, c) for c in (lane, 1 - lane)]
     part_ref[...] = jnp.zeros_like(part_ref)
@@ -193,9 +195,9 @@
     notes_ref[...] = notes
 
     store_piece(own_swap, place, codes(place, 1 - lane), high, low, left)
-    store_piece(r1, here, codes(here, sender), high, low)
+    store_piece(r1, first_here, codes(first_here, first_sender), high, low)
     store_piece(r2, here, codes(here, 1 - sender), high, low)
-    store_piece(t1, there, codes(there, other_sender), high, low)
+    store_piece(t1, first_there, codes(first_there, first_other), high, low)
     store_piece(t2, there, codes(there, 1 - other_sender), high, low)
     store_piece(r3, far_here, codes(far_here, far_sender), high, low)
     own_copy.wait()
@@ -208,7 +210,7 @@
     tables, notes_ref, r4a, r4b, t3, t4a, high_in, low_in, left, part_in, high, low, part_ref
 ):
     place, lane = lax.axis_index("blk"), lax.axis_index("depth")
-    here, there = [lookup(tables[1][0], place, c) for c in (lane, 1 - lane)]
+    here, there = [lookup(tables[-1][0], place, c) for c in (lane, 1 - lane)]
     slab, width = t3.shape[:2]
     notes = notes_ref[...]
     store_piece(t3, there, noted_codes(notes, T3, slab, width), high, low)
@@ -223,7 +225,7 @@
     out_hbm, high, low, square, square_parts, out_ref, out_sem,
 ):
     place, lane = lax.axis_index("blk"), lax.axis_index("depth")
-    there = lookup(tables[1][0], place, 1 - lane)
+    there = lookup(tables[-1][0], place, 1 - lane)
     slab, width, edge, _ = out_ref.shape
     act = 2 * width
     holds = lax.axis_index("panel") == 0
@@ -315,7 +317,10 @@
     up_lane = [1 - c for c in down_lane]
     up = [(z, 0, up_lane[z]) for z in range(chains)] + [(last, 1, up_lane[last])]
     down = [(z, 0, down_lane[z]) for z in reversed(range(chains))] + [(0, 1, down_lane[0])]
-    first = [up + [(last, 1, down_lane[last])] + down + [(0, 1, up_lane[0])]]
+    first = [
+        up[:last] + down + [(0, 1, up_lane[0])],
+        [up[last], up[-1], (last, 1, down_lane[last])],
+    ]
     second = [up, down]
 
     def received(hops):
@@ -331,7 +336,9 @@
             senders.append([lanes_of[plane] for plane, lanes_of in zip(row, lane_of)])
         return planes, senders
 
-    tables = received(1), received(2)
+    near, far = received(1), received(2)
+    hop1 = [rows[:last] + [rows[last][::-1]] for rows in near]
+    tables = hop1, near, far
 
     table = slot_table(columns, lanes * width)
     r1 = move(x_blocks, first)

time: 32.3 us -> 31.8 us (0.985)
  the two profiles are of different devices: /device:TPU:25 before, /device:TPU:0 now
where the time goes in v21:
time: 31.8 us; the launch traced here: 31.5 us
  starting transfers between devices  13.7 us (43%)
  waiting for transfers between devices  7.74 us (24%)
  Pallas kernels  7.56 us (24%)
  other arithmetic  2.24 us (7%)
    ppermute x10, starting transfers between devices, move(): return lax.ppermute(block, AXES, route)  11.5 us
    ppermute x10, waiting for transfers between devices, move(): return lax.ppermute(block, AXES, route)  4.53 us
    ppermute x1, waiting for transfers between devices, move_only(): return lax.ppermute(block, AXES, route)  3.21 us
    pallas_call x1, Pallas kernels, gather_local(): pl.pallas_call(functools.partial(late_kernel, tables), out_shape=[jax.Sha...  3.14 us
    pallas_call x1, Pallas kernels, gather_local(): pl.pallas_call(functools.partial(early_kernel, tables), out_shape=[jax.Sh...  3.08 us
    ppermute x1, starting transfers between devices, move_only(): return lax.ppermute(block, AXES, route)  2.28 us
    pallas_call x1, Pallas kernels, gather_local(): pl.pallas_call(functools.partial(middle_kernel, tables), out_shape=dense,...  1.34 us
    reduce_sum x1, other arithmetic, slot_table(): count = jnp.sum(here.astype(jnp.int32), axis=1, keepdims=True)  0.8 us
  transfers between devices with their start and end apart: 11, of which 6 were waited for; matrix products, arithmetic and copies ran while one was open for 7% of the time, Pallas kernels for 14%

profile of v21, /device:TPU:0, one launch (start us, length us, event | category | flops | bytes accessed | tf_op | source)
XLA Modules:
  0.0 31.5 jit_solution(4575298759586247306)
XLA Ops:
  0.0 2.9 %collective-permute-start = (f32[2,4,128,128]{3,2,1,0:T(8,128)}, f32[2,4,128,128]{3,2,1,0:T(8,128)S(1)}, u32[]{:S(2)}, u32[]{:S(2)}) collective-permute-start(f32[2,4,128,128]{3,2,1,0:T(8,128)} %own_hbm.1), channel_id=1, source_target_pairs={{3,1},{1,4},{4,9},{9,12},{12,8},{8,5},{5,0},{0,2},{2,3},{14,13},{1... | collective-permute-start | bytes 1572872 | tf_op jit(solution)/shard_map/ppermute | solution.py:306
  2.9 0.2 collective-permute-start.1
  3.1 0.8 %fusion.1 = (s32[8]{0:T(128)S(1)}, s32[8,8]{1,0:T(8,128)S(1)}) fusion(s32[8,16]{1,0:T(8,128)} %param.3), kind=kLoop, calls=%fused_computation.7 | loop fusion | flops 184 | bytes 544 | tf_op jit(solution)/shard_map/reduce_sum | solution.py:271
  3.9 0.1 fusion
  4.1 0.2 convert_reduce_fusion
  4.3 0.8 %collective-permute-done.1.own_swap = f32[2,4,128,128]{3,2,1,0:T(8,128)S(1)} collective-permute-done((f32[2,4,128,128]{3,2,1,0:T(8,128)}, f32[2,4,128,128]{3,2,1,0:T(8,128)S(1)}, u32[]{:S(2)}, u32[]{:S(2)}) %collective-permute-start.1) | collective-permute-done | bytes 524320 | tf_op jit(solution)/shard_map/ppermute | solution.py:306
  5.1 2.3 %collective-permute-start.2 = (f32[2,4,128,128]{3,2,1,0:T(8,128)S(1)}, f32[2,4,128,128]{3,2,1,0:T(8,128)S(1)}, u32[]{:S(2)}, u32[]{:S(2)}) collective-permute-start(f32[2,4,128,128]{3,2,1,0:T(8,128)S(1)} %collective-permute-done.1.own_swap), channel_id=1, source_target_pairs={{1,4},{4,9},{9,13},{13,15},{12,8},{8,5},{5,0},{0,2},{17,20},{20,25... | collective-permute-start | bytes 1572872 | tf_op jit(solution)/shard_map/ppermute | solution.py:314
  7.3 0.1 add_select_fusion
  7.5 0.1 copy.10
  7.5 0.2 select_reduce_fusion
  7.8 0.7 %compare_select_fusion = s32[8,8]{1,0:T(8,128)S(1)} fusion(s32[8,8]{1,0:T(8,128)S(1)} %select_reduce_fusion, s32[8,16]{1,0:T(8,128)} %param.3), kind=kLoop, calls=%fused_computation.5 | loop fusion | flops 192 | bytes 768 | tf_op jit(solution)/shard_map/jit(_where)/select_n | solution.py:279
  8.5 0.1 pad_add_fusion.table_ref
  8.5 1.4 %collective-permute-done.r1 = f32[2,4,128,128]{3,2,1,0:T(8,128)S(1)} collective-permute-done((f32[2,4,128,128]{3,2,1,0:T(8,128)}, f32[2,4,128,128]{3,2,1,0:T(8,128)S(1)}, u32[]{:S(2)}, u32[]{:S(2)}) %collective-permute-start) | collective-permute-done | bytes 524320 | tf_op jit(solution)/shard_map/ppermute | solution.py:306
  10.0 2.4 %collective-permute-start.5 = (f32[2,4,128,128]{3,2,1,0:T(8,128)S(1)}, f32[2,4,128,128]{3,2,1,0:T(8,128)S(1)}, u32[]{:S(2)}, u32[]{:S(2)}) collective-permute-start(f32[2,4,128,128]{3,2,1,0:T(8,128)S(1)} %collective-permute-done.r1), channel_id=1, source_target_pairs={{15,1},{1,4},{4,9},{9,13},{13,15},{2,12},{12,8},{8,5},{5,0},{0,2},... | collective-permute-start | bytes 1572872 | tf_op jit(solution)/shard_map/ppermute | solution.py:306
  12.3 0.0 collective-permute-start.3
  12.3 3.2 %collective-permute-done.2.r2 = f32[2,4,128,128]{3,2,1,0:T(8,128)S(1)} collective-permute-done((f32[2,4,128,128]{3,2,1,0:T(8,128)S(1)}, f32[2,4,128,128]{3,2,1,0:T(8,128)S(1)}, u32[]{:S(2)}, u32[]{:S(2)}) %collective-permute-start.2) | collective-permute-done | bytes 524320 | tf_op jit(solution)/shard_map/ppermute | solution.py:314
  15.6 0.0 collective-permute-start.4
  15.6 2.5 %collective-permute-start.7 = (f32[1,4,128,128]{3,2,1,0:T(8,128)S(1)}, f32[1,4,128,128]{3,2,1,0:T(8,128)S(1)}, u32[]{:S(2)}, u32[]{:S(2)}) collective-permute-start(f32[1,4,128,128]{3,2,1,0:T(8,128)S(1)} %get-tuple-element.35), channel_id=1, source_target_pairs={{15,1},{1,4},{4,9},{9,13},{13,15},{2,12},{12,8},{8,5},{5,0},{0,2},... | collective-permute-start | bytes 786440 | tf_op jit(solution)/shard_map/ppermute | solution.py:306
  18.0 2.8 %collective-permute-start.6 = (f32[1,4,128,128]{3,2,1,0:T(8,128)S(1)}, f32[1,4,128,128]{3,2,1,0:T(8,128)S(1)}, u32[]{:S(2)}, u32[]{:S(2)}) collective-permute-start(f32[1,4,128,128]{3,2,1,0:T(8,128)S(1)} %get-tuple-element.36), channel_id=1, source_target_pairs={{15,1},{1,4},{4,9},{9,13},{13,15},{2,12},{12,8},{8,5},{5,0},{0,2},... | collective-permute-start | bytes 786440 | tf_op jit(solution)/shard_map/ppermute | solution.py:306
  20.9 0.3 collective-permute-done.5.r3
  21.2 0.0 collective-permute-start.10
  21.2 0.0 collective-permute-done.3.t1
  21.2 0.0 collective-permute-done.4.t2
  21.2 3.1 %early.1 = (bf16[1024,1024]{1,0:T(8,128)(2,1)S(1)}, bf16[1024,1024]{1,0:T(8,128)(2,1)S(1)}, bf16[512,1024]{1,0:T(8,128)(2,1)S(1)}, f32[256,1024]{1,0:T(8,128)S(1)}, s32[8,128]{1,0:T(8,128)S(1)}) custom-call(s32[8,9]{1,0:T(8,128)S(1)} %pad_add_fusion.table_ref, f32[2,4,128,128]{3,2,1,0:T(8,128)} %own_hbm.1, ...), custom_call_target="tpu_custom_call" | custom-call | tf_op jit(solution)/shard_map/early/pallas_call | solution.py:361
  24.3 0.0 collective-permute-done.7.r4a
  24.3 0.6 %collective-permute-start.8 = (f32[1,4,128,128]{3,2,1,0:T(8,128)S(1)}, f32[1,4,128,128]{3,2,1,0:T(8,128)S(1)}, u32[]{:S(2)}, u32[]{:S(2)}) collective-permute-start(f32[1,4,128,128]{3,2,1,0:T(8,128)S(1)} %collective-permute-done.7.r4a), channel_id=1, source_target_pairs={{1,0},{0,1},{17,16},{16,17},{3,2},{2,3},{19,18},{18,19},{5,4},{4,5... | collective-permute-start | bytes 786440 | tf_op jit(solution)/shard_map/ppermute | solution.py:306
  24.8 1.9 %collective-permute-done.6.r4b = f32[1,4,128,128]{3,2,1,0:T(8,128)S(1)} collective-permute-done((f32[1,4,128,128]{3,2,1,0:T(8,128)S(1)}, f32[1,4,128,128]{3,2,1,0:T(8,128)S(1)}, u32[]{:S(2)}, u32[]{:S(2)}) %collective-permute-start.6) | collective-permute-done | bytes 262176 | tf_op jit(solution)/shard_map/ppermute | solution.py:306
  26.8 0.0 collective-permute-done.8.t4a
  26.8 0.1 collective-permute-start.9
  26.9 1.3 %middle.1 = (bf16[1024,1024]{1,0:T(8,128)(2,1)S(1)}, bf16[1024,1024]{1,0:T(8,128)(2,1)S(1)}, f32[256,1024]{1,0:T(8,128)S(1)}) custom-call(s32[8,128]{1,0:T(8,128)S(1)} %get-tuple-element.22.notes_ref, f32[1,4,128,128]{3,2,1,0:T(8,128)S(1)} %collective-permute-done.7.r4a, ...), custom_call_target="tpu_custom_call", output_to_operand_aliasing={{0}: (5, {}), {1}: (6, {}), {2}: (8, {})} | custom-call | tf_op jit(solution)/shard_map/middle/pallas_call | solution.py:382
  28.2 0.1 collective-permute-done.9.t4b
  28.3 3.1 %late.1 = (f32[2,4,128,128]{3,2,1,0:T(8,128)}, bf16[1024,1024]{1,0:T(8,128)(2,1)S(1)}, bf16[1024,1024]{1,0:T(8,128)(2,1)S(1)}, f32[256,1024]{1,0:T(8,128)S(1)}) custom-call(s32[8,128]{1,0:T(8,128)S(1)} %get-tuple-element.22.notes_ref, f32[1,4,128,128]{3,2,1,0:T(8,128)S(1)} %collective-permute-done.9.t4b, ...), custom_call_target="tpu_custom_call", output_to_operand_aliasing={{1}: (2, {}), {2}: (3, {}), {3}: (5, {})} | custom-call | tf_op jit(solution)/shard_map/late/pallas_call | solution.py:391
  (5 shorter events, 0.1 us)
Async XLA Ops:
  0.0 10.0 %collective-permute-start = (f32[2,4,128,128]{3,2,1,0:T(8,128)}, f32[2,4,128,128]{3,2,1,0:T(8,128)S(1)}, u32[]{:S(2)}, u32[]{:S(2)}) collective-permute-start(f32[2,4,128,128]{3,2,1,0:T(8,128)} %own_hbm.1), channel_id=1, source_target_pairs={{3,1},{1,4},{4,9},{9,12},{12,8},{8,5},{5,0},{0,2},{2,3},{14,13},{1... | collective-permute-start | bytes 1572872 | tf_op jit(solution)/shard_map/ppermute | solution.py:306
  2.9 2.1 %collective-permute-start.1 = (f32[2,4,128,128]{3,2,1,0:T(8,128)}, f32[2,4,128,128]{3,2,1,0:T(8,128)S(1)}, u32[]{:S(2)}, u32[]{:S(2)}) collective-permute-start(f32[2,4,128,128]{3,2,1,0:T(8,128)} %own_hbm.1), channel_id=1, source_target_pairs={{1,0},{0,1},{17,16},{16,17},{3,2},{2,3},{19,18},{18,19},{5,4},{4,5... | collective-permute-start | bytes 1572872 | tf_op jit(solution)/shard_map/ppermute | solution.py:306
  5.1 10.5 %collective-permute-start.2 = (f32[2,4,128,128]{3,2,1,0:T(8,128)S(1)}, f32[2,4,128,128]{3,2,1,0:T(8,128)S(1)}, u32[]{:S(2)}, u32[]{:S(2)}) collective-permute-start(f32[2,4,128,128]{3,2,1,0:T(8,128)S(1)} %collective-permute-done.1.own_swap), channel_id=1, source_target_pairs={{1,4},{4,9},{9,13},{13,15},{12,8},{8,5},{5,0},{0,2},{17,20},{20,25... | collective-permute-start | bytes 1572872 | tf_op jit(solution)/shard_map/ppermute | solution.py:314
  10.0 11.2 %collective-permute-start.5 = (f32[2,4,128,128]{3,2,1,0:T(8,128)S(1)}, f32[2,4,128,128]{3,2,1,0:T(8,128)S(1)}, u32[]{:S(2)}, u32[]{:S(2)}) collective-permute-start(f32[2,4,128,128]{3,2,1,0:T(8,128)S(1)} %collective-permute-done.r1), channel_id=1, source_target_pairs={{15,1},{1,4},{4,9},{9,13},{13,15},{2,12},{12,8},{8,5},{5,0},{0,2},... | collective-permute-start | bytes 1572872 | tf_op jit(solution)/shard_map/ppermute | solution.py:306
  12.3 8.8 %collective-permute-start.3 = (f32[2,4,128,128]{3,2,1,0:T(8,128)S(1)}, f32[2,4,128,128]{3,2,1,0:T(8,128)S(1)}, u32[]{:S(2)}, u32[]{:S(2)}) collective-permute-start(f32[2,4,128,128]{3,2,1,0:T(8,128)S(1)} %collective-permute-done.r1), channel_id=1, source_target_pairs={{1,0},{0,1},{17,16},{16,17},{3,2},{2,3},{19,18},{18,19},{5,4},{4,5... | collective-permute-start | bytes 1572872 | tf_op jit(solution)/shard_map/ppermute | solution.py:306
  15.6 5.6 %collective-permute-start.4 = (f32[2,4,128,128]{3,2,1,0:T(8,128)S(1)}, f32[2,4,128,128]{3,2,1,0:T(8,128)S(1)}, u32[]{:S(2)}, u32[]{:S(2)}) collective-permute-start(f32[2,4,128,128]{3,2,1,0:T(8,128)S(1)} %collective-permute-done.2.r2), channel_id=1, source_target_pairs={{1,0},{0,1},{17,16},{16,17},{3,2},{2,3},{19,18},{18,19},{5,4},{4,5... | collective-permute-start | bytes 1572872 | tf_op jit(solution)/shard_map/ppermute | solution.py:306
  15.6 8.7 %collective-permute-start.7 = (f32[1,4,128,128]{3,2,1,0:T(8,128)S(1)}, f32[1,4,128,128]{3,2,1,0:T(8,128)S(1)}, u32[]{:S(2)}, u32[]{:S(2)}) collective-permute-start(f32[1,4,128,128]{3,2,1,0:T(8,128)S(1)} %get-tuple-element.35), channel_id=1, source_target_pairs={{15,1},{1,4},{4,9},{9,13},{13,15},{2,12},{12,8},{8,5},{5,0},{0,2},... | collective-permute-start | bytes 786440 | tf_op jit(solution)/shard_map/ppermute | solution.py:306
  18.0 8.7 %collective-permute-start.6 = (f32[1,4,128,128]{3,2,1,0:T(8,128)S(1)}, f32[1,4,128,128]{3,2,1,0:T(8,128)S(1)}, u32[]{:S(2)}, u32[]{:S(2)}) collective-permute-start(f32[1,4,128,128]{3,2,1,0:T(8,128)S(1)} %get-tuple-element.36), channel_id=1, source_target_pairs={{15,1},{1,4},{4,9},{9,13},{13,15},{2,12},{12,8},{8,5},{5,0},{0,2},... | collective-permute-start | bytes 786440 | tf_op jit(solution)/shard_map/ppermute | solution.py:306
  21.2 5.7 %collective-permute-start.10 = (f32[2,4,128,128]{3,2,1,0:T(8,128)S(1)}, f32[2,4,128,128]{3,2,1,0:T(8,128)S(1)}, u32[]{:S(2)}, u32[]{:S(2)}) collective-permute-start(f32[2,4,128,128]{3,2,1,0:T(8,128)S(1)} %collective-permute-done.5.r3), channel_id=1, source_target_pairs={{1,0},{0,1},{17,16},{16,17},{3,2},{2,3},{19,18},{18,19},{5,4},{4,5... | collective-permute-start | bytes 1572872 | tf_op jit(solution)/shard_map/ppermute | solution.py:306
  24.3 2.5 %collective-permute-start.8 = (f32[1,4,128,128]{3,2,1,0:T(8,128)S(1)}, f32[1,4,128,128]{3,2,1,0:T(8,128)S(1)}, u32[]{:S(2)}, u32[]{:S(2)}) collective-permute-start(f32[1,4,128,128]{3,2,1,0:T(8,128)S(1)} %collective-permute-done.7.r4a), channel_id=1, source_target_pairs={{1,0},{0,1},{17,16},{16,17},{3,2},{2,3},{19,18},{18,19},{5,4},{4,5... | collective-permute-start | bytes 786440 | tf_op jit(solution)/shard_map/ppermute | solution.py:306
  26.8 1.5 %collective-permute-start.9 = (f32[1,4,128,128]{3,2,1,0:T(8,128)S(1)}, f32[1,4,128,128]{3,2,1,0:T(8,128)S(1)}, u32[]{:S(2)}, u32[]{:S(2)}) collective-permute-start(f32[1,4,128,128]{3,2,1,0:T(8,128)S(1)} %collective-permute-done.6.r4b), channel_id=1, source_target_pairs={{1,0},{0,1},{17,16},{16,17},{3,2},{2,3},{19,18},{18,19},{5,4},{4,5... | collective-permute-start | bytes 786440 | tf_op jit(solution)/shard_map/ppermute | solution.py:306

commit v22 on v21

--- a/solution.py
+++ b/solution.py
@@ -152,6 +152,43 @@
         for n in range(part_ref.shape[1] // tile):
             cols = pl.ds(n * tile, tile)
             part_ref[:, cols] += stacked_dot(left[:, rows], high[rows, cols], low[rows, cols])
+
+
+def clear_row(plane, r, code_of, width, high, low):
+    edge = high.shape[0] // (2 * width)
+
+    @pl.when(plane >= 0)
+    def _():
+        at = pl.ds(pl.multiple_of((plane * 2 + r) * edge, edge), edge)
+        for w in range(width):
+            col = pl.ds(pl.multiple_of(code_of(r, w) % (2 * width) * edge, edge), edge)
+            high[at, col] = jnp.zeros((edge, edge), jnp.bfloat16)
+            low[at, col] = jnp.zeros((edge, edge), jnp.bfloat16)
+
+
+def add_row_blocks(piece, plane, r, code_of, left, high, low, part_ref):
+    _, width, edge, _ = piece.shape
+    act = 2 * width
+
+    @pl.when(plane >= 0)
+    def _():
+        at = pl.ds(pl.multiple_of((plane * 2 + r) * edge, edge), edge)
+        for w in range(0, width, 2):
+            codes = [code_of(r, w + k) for k in range(2)]
+            cols = [pl.ds(pl.multiple_of(code % act * edge, edge), edge) for code in codes]
+            parts = [
+                split(jnp.where(code < act, piece[0, w + k], 0.0)) for k, code in enumerate(codes)
+            ]
+            for col, (block_high, block_low) in zip(cols, parts):
+                high[at, col] = block_high
+                low[at, col] = block_low
+            more = stacked_dot(
+                left[:, at],
+                jnp.concatenate([block_high for block_high, _ in parts], axis=1),
+                jnp.concatenate([block_low for _, block_low in parts], axis=1),
+            )
+            for k, col in enumerate(cols):
+                part_ref[:, col] += more[:, k * edge : (k + 1) * edge]
 
 
 def early_kernel(
@@ -206,18 +243,31 @@
         add_plane(plane, left, high, low, part_ref)
 
 
+def waiting_kernel(tables, notes_ref, r4a, high_in, low_in, left, part_in, high, low, part_ref):
+    place, lane = lax.axis_index("blk"), lax.axis_index("depth")
+    here = lookup(tables[-1][0], place, lane)
+    width = r4a.shape[1]
+    codes = noted_codes(notes_ref[...], R4, 2, width)
+    store_piece(r4a, here, codes, high, low)
+    clear_row(here, 1, codes, width, high, low)
+    add_plane(here, left, high, low, part_ref)
+
+
 def middle_kernel(
-    tables, notes_ref, r4a, r4b, t3, t4a, high_in, low_in, left, part_in, high, low, part_ref
+    tables, notes_ref, r4b, t3, t4a, high_in, low_in, left, part_in, high, low, part_ref
 ):
     place, lane = lax.axis_index("blk"), lax.axis_index("depth")
     here, there = [lookup(tables[-1][0], place, c) for c in (lane, 1 - lane)]
     slab, width = t3.shape[:2]
     notes = notes_ref[...]
+    codes = noted_codes(notes, T4, slab, width)
     store_piece(t3, there, noted_codes(notes, T3, slab, width), high, low)
-    store_piece(r4a, here, noted_codes(notes, R4, slab, width), high, low)
-    store_piece(t4a, there, noted_codes(notes, T4, slab, width), high, low)
-    store_piece(r4b, here, noted_codes(notes, R4, slab, width), high, low, first=1)
-    add_plane(here, left, high, low, part_ref)
+    store_piece(t4a, there, codes, high, low)
+    clear_row(there, 1, codes, width, high, low)
+    add_plane(there, left, high, low, part_ref)
+    add_row_blocks(
+        r4b, here, 1, noted_codes(notes, R4, slab, width), left, high, low, part_ref
+    )
 
 
 def late_kernel(
@@ -231,8 +281,9 @@
     holds = lax.axis_index("panel") == 0
     notes = notes_ref[...]
     own_codes = noted_codes(notes, OWN, slab, width)
-    store_piece(t4b, there, noted_codes(notes, T4, slab, width), high, low, first=1)
-    add_plane(there, left, high, low, square)
+    add_row_blocks(
+        t4b, there, 1, noted_codes(notes, T4, slab, width), left, high, low, square
+    )
     for r in range(slab):
         flags = notes[0, KEPT * slab * width + r]
         for c in range(square.shape[1] // edge):
@@ -376,18 +427,24 @@
     t3 = swap(r3)
     r4a, part = lax.optimization_barrier((r4a, part))
     t4a = swap(r4a)
-    r4b, t4a = lax.optimization_barrier((r4b, t4a))
+    dense = [jax.ShapeDtypeStruct(a.shape, a.dtype) for a in (high, low, part)]
+
+    def add_to_square(kernel, name, *pieces):
+        at = 1 + len(pieces)
+        return pl.pallas_call(
+            functools.partial(kernel, tables),
+            out_shape=dense,
+            in_specs=[vmem] * (at + 4),
+            out_specs=[vmem] * 3,
+            input_output_aliases={at: 0, at + 1: 1, at + 3: 2},
+            compiler_params=params,
+            name=name,
+        )(notes, *pieces, *held(high, low, left, part))
+
+    high, low, part = add_to_square(waiting_kernel, "waiting", r4a)
+    r4b, t4a, part = lax.optimization_barrier((r4b, t4a, part))
     t4b = swap(r4b)
-    dense = [jax.ShapeDtypeStruct(a.shape, a.dtype) for a in (high, low, part)]
-    high, low, part = pl.pallas_call(
-        functools.partial(middle_kernel, tables),
-        out_shape=dense,
-        in_specs=[vmem] * 9,
-        out_specs=[vmem] * 3,
-        input_output_aliases={5: 0, 6: 1, 8: 2},
-        compiler_params=params,
-        name="middle",
-    )(notes, r4a, r4b, t3, t4a, *held(high, low, left, part))
+    high, low, part = add_to_square(middle_kernel, "middle", r4b, t3, t4a)
     out, _, _, _ = pl.pallas_call(
         functools.partial(late_kernel, tables),
         out_shape=[jax.ShapeDtypeStruct(x_blocks.shape, jnp.float32)] + dense,

time: 31.8 us -> 31.8 us (level)
  waiting for transfers between devices: 7.74 us -> 6.89 us
  Pallas kernels: 7.56 us -> 8.33 us
    pallas_call x1 -> x2, Pallas kernels: 1.34 us -> 2.33 us  [add_to_square(): pl.pallas_call(functools.partial(kernel, tables), out_shape=dense, in_spe...]
    ppermute x10, waiting for transfers between devices: 4.53 us -> 3.68 us  [move(): return lax.ppermute(block, AXES, route)]
  transfers between devices with their start and end apart: 11 -> 11, of which waited for: 6 -> 5; matrix products, arithmetic and copies ran while one was open for 7% -> 7% of each run, Pallas kernels for 14% -> 17%
where the time goes in v22:
time: 31.8 us; the launch traced here: 31.4 us
  starting transfers between devices  13.7 us (43%)
  Pallas kernels  8.33 us (26%)
  waiting for transfers between devices  6.89 us (22%)
  other arithmetic  2.24 us (7%)
    ppermute x10, starting transfers between devices, move(): return lax.ppermute(block, AXES, route)  11.5 us
    ppermute x10, waiting for transfers between devices, move(): return lax.ppermute(block, AXES, route)  3.68 us
    ppermute x1, waiting for transfers between devices, move_only(): return lax.ppermute(block, AXES, route)  3.21 us
    pallas_call x1, Pallas kernels, gather_local(): pl.pallas_call(functools.partial(early_kernel, tables), out_shape=[jax.Sh...  3.03 us
    pallas_call x1, Pallas kernels, gather_local(): pl.pallas_call(functools.partial(late_kernel, tables), out_shape=[jax.Sha...  2.97 us
    pallas_call x2, Pallas kernels, add_to_square(): pl.pallas_call(functools.partial(kernel, tables), out_shape=dense, in_spe...  2.33 us
    ppermute x1, starting transfers between devices, move_only(): return lax.ppermute(block, AXES, route)  2.28 us
    reduce_sum x1, other arithmetic, slot_table(): count = jnp.sum(here.astype(jnp.int32), axis=1, keepdims=True)  0.8 us
  transfers between devices with their start and end apart: 11, of which 5 were waited for; matrix products, arithmetic and copies ran while one was open for 7% of the time, Pallas kernels for 17%

profile of v22, /device:TPU:0, one launch (start us, length us, event | category | flops | bytes accessed | tf_op | source)
XLA Modules:
  0.0 31.4 jit_solution(14365599978863142544)
XLA Ops:
  0.0 2.9 %collective-permute-start = (f32[2,4,128,128]{3,2,1,0:T(8,128)}, f32[2,4,128,128]{3,2,1,0:T(8,128)S(1)}, u32[]{:S(2)}, u32[]{:S(2)}) collective-permute-start(f32[2,4,128,128]{3,2,1,0:T(8,128)} %own_hbm.1), channel_id=1, source_target_pairs={{3,1},{1,4},{4,9},{9,12},{12,8},{8,5},{5,0},{0,2},{2,3},{14,13},{1... | collective-permute-start | bytes 1572872 | tf_op jit(solution)/shard_map/ppermute | solution.py:357
  2.9 0.2 collective-permute-start.1
  3.1 0.8 %fusion.1 = (s32[8]{0:T(128)S(1)}, s32[8,8]{1,0:T(8,128)S(1)}) fusion(s32[8,16]{1,0:T(8,128)} %param.3), kind=kLoop, calls=%fused_computation.7 | loop fusion | flops 184 | bytes 544 | tf_op jit(solution)/shard_map/reduce_sum | solution.py:322
  3.9 0.1 fusion
  4.1 0.2 convert_reduce_fusion
  4.3 0.8 %collective-permute-done.1.own_swap = f32[2,4,128,128]{3,2,1,0:T(8,128)S(1)} collective-permute-done((f32[2,4,128,128]{3,2,1,0:T(8,128)}, f32[2,4,128,128]{3,2,1,0:T(8,128)S(1)}, u32[]{:S(2)}, u32[]{:S(2)}) %collective-permute-start.1) | collective-permute-done | bytes 524320 | tf_op jit(solution)/shard_map/ppermute | solution.py:357
  5.1 2.3 %collective-permute-start.2 = (f32[2,4,128,128]{3,2,1,0:T(8,128)S(1)}, f32[2,4,128,128]{3,2,1,0:T(8,128)S(1)}, u32[]{:S(2)}, u32[]{:S(2)}) collective-permute-start(f32[2,4,128,128]{3,2,1,0:T(8,128)S(1)} %collective-permute-done.1.own_swap), channel_id=1, source_target_pairs={{1,4},{4,9},{9,13},{13,15},{12,8},{8,5},{5,0},{0,2},{17,20},{20,25... | collective-permute-start | bytes 1572872 | tf_op jit(solution)/shard_map/ppermute | solution.py:365
  7.3 0.1 add_select_fusion
  7.5 0.1 copy.13
  7.5 0.2 select_reduce_fusion
  7.8 0.7 %compare_select_fusion = s32[8,8]{1,0:T(8,128)S(1)} fusion(s32[8,8]{1,0:T(8,128)S(1)} %select_reduce_fusion, s32[8,16]{1,0:T(8,128)} %param.3), kind=kLoop, calls=%fused_computation.5 | loop fusion | flops 192 | bytes 768 | tf_op jit(solution)/shard_map/jit(_where)/select_n | solution.py:330
  8.5 0.1 pad_add_fusion.table_ref
  8.5 1.4 %collective-permute-done.r1 = f32[2,4,128,128]{3,2,1,0:T(8,128)S(1)} collective-permute-done((f32[2,4,128,128]{3,2,1,0:T(8,128)}, f32[2,4,128,128]{3,2,1,0:T(8,128)S(1)}, u32[]{:S(2)}, u32[]{:S(2)}) %collective-permute-start) | collective-permute-done | bytes 524320 | tf_op jit(solution)/shard_map/ppermute | solution.py:357
  10.0 2.4 %collective-permute-start.5 = (f32[2,4,128,128]{3,2,1,0:T(8,128)S(1)}, f32[2,4,128,128]{3,2,1,0:T(8,128)S(1)}, u32[]{:S(2)}, u32[]{:S(2)}) collective-permute-start(f32[2,4,128,128]{3,2,1,0:T(8,128)S(1)} %collective-permute-done.r1), channel_id=1, source_target_pairs={{15,1},{1,4},{4,9},{9,13},{13,15},{2,12},{12,8},{8,5},{5,0},{0,2},... | collective-permute-start | bytes 1572872 | tf_op jit(solution)/shard_map/ppermute | solution.py:357
  12.3 0.0 collective-permute-start.3
  12.3 3.2 %collective-permute-done.2.r2 = f32[2,4,128,128]{3,2,1,0:T(8,128)S(1)} collective-permute-done((f32[2,4,128,128]{3,2,1,0:T(8,128)S(1)}, f32[2,4,128,128]{3,2,1,0:T(8,128)S(1)}, u32[]{:S(2)}, u32[]{:S(2)}) %collective-permute-start.2) | collective-permute-done | bytes 524320 | tf_op jit(solution)/shard_map/ppermute | solution.py:365
  15.6 0.0 collective-permute-start.4
  15.6 2.5 %collective-permute-start.7 = (f32[1,4,128,128]{3,2,1,0:T(8,128)S(1)}, f32[1,4,128,128]{3,2,1,0:T(8,128)S(1)}, u32[]{:S(2)}, u32[]{:S(2)}) collective-permute-start(f32[1,4,128,128]{3,2,1,0:T(8,128)S(1)} %get-tuple-element.43), channel_id=1, source_target_pairs={{15,1},{1,4},{4,9},{9,13},{13,15},{2,12},{12,8},{8,5},{5,0},{0,2},... | collective-permute-start | bytes 786440 | tf_op jit(solution)/shard_map/ppermute | solution.py:357
  18.0 2.8 %collective-permute-start.6 = (f32[1,4,128,128]{3,2,1,0:T(8,128)S(1)}, f32[1,4,128,128]{3,2,1,0:T(8,128)S(1)}, u32[]{:S(2)}, u32[]{:S(2)}) collective-permute-start(f32[1,4,128,128]{3,2,1,0:T(8,128)S(1)} %get-tuple-element.44), channel_id=1, source_target_pairs={{15,1},{1,4},{4,9},{9,13},{13,15},{2,12},{12,8},{8,5},{5,0},{0,2},... | collective-permute-start | bytes 786440 | tf_op jit(solution)/shard_map/ppermute | solution.py:357
  20.9 0.3 collective-permute-done.5.r3
  21.2 0.0 collective-permute-start.10
  21.2 0.0 collective-permute-done.3.t1
  21.2 0.0 collective-permute-done.4.t2
  21.2 3.0 %early.1 = (bf16[1024,1024]{1,0:T(8,128)(2,1)S(1)}, bf16[1024,1024]{1,0:T(8,128)(2,1)S(1)}, bf16[512,1024]{1,0:T(8,128)(2,1)S(1)}, f32[256,1024]{1,0:T(8,128)S(1)}, s32[8,128]{1,0:T(8,128)S(1)}) custom-call(s32[8,9]{1,0:T(8,128)S(1)} %pad_add_fusion.table_ref, f32[2,4,128,128]{3,2,1,0:T(8,128)} %own_hbm.1, ...), custom_call_target="tpu_custom_call" | custom-call | tf_op jit(solution)/shard_map/early/pallas_call | solution.py:412
  24.2 0.0 collective-permute-done.7.r4a
  24.2 0.6 %collective-permute-start.8 = (f32[1,4,128,128]{3,2,1,0:T(8,128)S(1)}, f32[1,4,128,128]{3,2,1,0:T(8,128)S(1)}, u32[]{:S(2)}, u32[]{:S(2)}) collective-permute-start(f32[1,4,128,128]{3,2,1,0:T(8,128)S(1)} %collective-permute-done.7.r4a), channel_id=1, source_target_pairs={{1,0},{0,1},{17,16},{16,17},{3,2},{2,3},{19,18},{18,19},{5,4},{4,5... | collective-permute-start | bytes 786440 | tf_op jit(solution)/shard_map/ppermute | solution.py:357
  24.8 0.8 %waiting.1 = (bf16[1024,1024]{1,0:T(8,128)(2,1)S(1)}, bf16[1024,1024]{1,0:T(8,128)(2,1)S(1)}, f32[256,1024]{1,0:T(8,128)S(1)}) custom-call(s32[8,128]{1,0:T(8,128)S(1)} %get-tuple-element.26.notes_ref, f32[1,4,128,128]{3,2,1,0:T(8,128)S(1)} %collective-permute-done.7.r4a, ...), custom_call_target="tpu_custom_call", output_to_operand_aliasing={{0}: (2, {}), {1}: (3, {}), {2}: (5, {})} | custom-call | tf_op jit(solution)/shard_map/waiting/pallas_call | solution.py:434
  25.6 1.2 %collective-permute-done.6.r4b = f32[1,4,128,128]{3,2,1,0:T(8,128)S(1)} collective-permute-done((f32[1,4,128,128]{3,2,1,0:T(8,128)S(1)}, f32[1,4,128,128]{3,2,1,0:T(8,128)S(1)}, u32[]{:S(2)}, u32[]{:S(2)}) %collective-permute-start.6) | collective-permute-done | bytes 262176 | tf_op jit(solution)/shard_map/ppermute | solution.py:357
  26.8 0.1 collective-permute-start.9
  26.9 1.5 %middle.1 = (bf16[1024,1024]{1,0:T(8,128)(2,1)S(1)}, bf16[1024,1024]{1,0:T(8,128)(2,1)S(1)}, f32[256,1024]{1,0:T(8,128)S(1)}) custom-call(s32[8,128]{1,0:T(8,128)S(1)} %get-tuple-element.26.notes_ref, f32[1,4,128,128]{3,2,1,0:T(8,128)S(1)} %collective-permute-done.6.r4b, ...), custom_call_target="tpu_custom_call", output_to_operand_aliasing={{0}: (4, {}), {1}: (5, {}), {2}: (7, {})} | custom-call | tf_op jit(solution)/shard_map/middle/pallas_call | solution.py:434
  28.4 0.0 collective-permute-done.9.t4b
  28.4 3.0 %late.1 = (f32[2,4,128,128]{3,2,1,0:T(8,128)}, bf16[1024,1024]{1,0:T(8,128)(2,1)S(1)}, bf16[1024,1024]{1,0:T(8,128)(2,1)S(1)}, f32[256,1024]{1,0:T(8,128)S(1)}) custom-call(s32[8,128]{1,0:T(8,128)S(1)} %get-tuple-element.26.notes_ref, f32[1,4,128,128]{3,2,1,0:T(8,128)S(1)} %collective-permute-done.9.t4b, ...), custom_call_target="tpu_custom_call", output_to_operand_aliasing={{1}: (2, {}), {2}: (3, {}), {3}: (5, {})} | custom-call | tf_op jit(solution)/shard_map/late/pallas_call | solution.py:448
  (6 shorter events, 0.1 us)
Async XLA Ops:
  0.0 10.0 %collective-permute-start = (f32[2,4,128,128]{3,2,1,0:T(8,128)}, f32[2,4,128,128]{3,2,1,0:T(8,128)S(1)}, u32[]{:S(2)}, u32[]{:S(2)}) collective-permute-start(f32[2,4,128,128]{3,2,1,0:T(8,128)} %own_hbm.1), channel_id=1, source_target_pairs={{3,1},{1,4},{4,9},{9,12},{12,8},{8,5},{5,0},{0,2},{2,3},{14,13},{1... | collective-permute-start | bytes 1572872 | tf_op jit(solution)/shard_map/ppermute | solution.py:357
  2.9 2.1 %collective-permute-start.1 = (f32[2,4,128,128]{3,2,1,0:T(8,128)}, f32[2,4,128,128]{3,2,1,0:T(8,128)S(1)}, u32[]{:S(2)}, u32[]{:S(2)}) collective-permute-start(f32[2,4,128,128]{3,2,1,0:T(8,128)} %own_hbm.1), channel_id=1, source_target_pairs={{1,0},{0,1},{17,16},{16,17},{3,2},{2,3},{19,18},{18,19},{5,4},{4,5... | collective-permute-start | bytes 1572872 | tf_op jit(solution)/shard_map/ppermute | solution.py:357
  5.1 10.5 %collective-permute-start.2 = (f32[2,4,128,128]{3,2,1,0:T(8,128)S(1)}, f32[2,4,128,128]{3,2,1,0:T(8,128)S(1)}, u32[]{:S(2)}, u32[]{:S(2)}) collective-permute-start(f32[2,4,128,128]{3,2,1,0:T(8,128)S(1)} %collective-permute-done.1.own_swap), channel_id=1, source_target_pairs={{1,4},{4,9},{9,13},{13,15},{12,8},{8,5},{5,0},{0,2},{17,20},{20,25... | collective-permute-start | bytes 1572872 | tf_op jit(solution)/shard_map/ppermute | solution.py:365
  10.0 11.2 %collective-permute-start.5 = (f32[2,4,128,128]{3,2,1,0:T(8,128)S(1)}, f32[2,4,128,128]{3,2,1,0:T(8,128)S(1)}, u32[]{:S(2)}, u32[]{:S(2)}) collective-permute-start(f32[2,4,128,128]{3,2,1,0:T(8,128)S(1)} %collective-permute-done.r1), channel_id=1, source_target_pairs={{15,1},{1,4},{4,9},{9,13},{13,15},{2,12},{12,8},{8,5},{5,0},{0,2},... | collective-permute-start | bytes 1572872 | tf_op jit(solution)/shard_map/ppermute | solution.py:357
  12.3 8.8 %collective-permute-start.3 = (f32[2,4,128,128]{3,2,1,0:T(8,128)S(1)}, f32[2,4,128,128]{3,2,1,0:T(8,128)S(1)}, u32[]{:S(2)}, u32[]{:S(2)}) collective-permute-start(f32[2,4,128,128]{3,2,1,0:T(8,128)S(1)} %collective-permute-done.r1), channel_id=1, source_target_pairs={{1,0},{0,1},{17,16},{16,17},{3,2},{2,3},{19,18},{18,19},{5,4},{4,5... | collective-permute-start | bytes 1572872 | tf_op jit(solution)/shard_map/ppermute | solution.py:357
  15.6 5.6 %collective-permute-start.4 = (f32[2,4,128,128]{3,2,1,0:T(8,128)S(1)}, f32[2,4,128,128]{3,2,1,0:T(8,128)S(1)}, u32[]{:S(2)}, u32[]{:S(2)}) collective-permute-start(f32[2,4,128,128]{3,2,1,0:T(8,128)S(1)} %collective-permute-done.2.r2), channel_id=1, source_target_pairs={{1,0},{0,1},{17,16},{16,17},{3,2},{2,3},{19,18},{18,19},{5,4},{4,5... | collective-permute-start | bytes 1572872 | tf_op jit(solution)/shard_map/ppermute | solution.py:357
  15.6 8.6 %collective-permute-start.7 = (f32[1,4,128,128]{3,2,1,0:T(8,128)S(1)}, f32[1,4,128,128]{3,2,1,0:T(8,128)S(1)}, u32[]{:S(2)}, u32[]{:S(2)}) collective-permute-start(f32[1,4,128,128]{3,2,1,0:T(8,128)S(1)} %get-tuple-element.43), channel_id=1, source_target_pairs={{15,1},{1,4},{4,9},{9,13},{13,15},{2,12},{12,8},{8,5},{5,0},{0,2},... | collective-permute-start | bytes 786440 | tf_op jit(solution)/shard_map/ppermute | solution.py:357
  18.0 8.7 %collective-permute-start.6 = (f32[1,4,128,128]{3,2,1,0:T(8,128)S(1)}, f32[1,4,128,128]{3,2,1,0:T(8,128)S(1)}, u32[]{:S(2)}, u32[]{:S(2)}) collective-permute-start(f32[1,4,128,128]{3,2,1,0:T(8,128)S(1)} %get-tuple-element.44), channel_id=1, source_target_pairs={{15,1},{1,4},{4,9},{9,13},{13,15},{2,12},{12,8},{8,5},{5,0},{0,2},... | collective-permute-start | bytes 786440 | tf_op jit(solution)/shard_map/ppermute | solution.py:357
  21.2 5.7 %collective-permute-start.10 = (f32[2,4,128,128]{3,2,1,0:T(8,128)S(1)}, f32[2,4,128,128]{3,2,1,0:T(8,128)S(1)}, u32[]{:S(2)}, u32[]{:S(2)}) collective-permute-start(f32[2,4,128,128]{3,2,1,0:T(8,128)S(1)} %collective-permute-done.5.r3), channel_id=1, source_target_pairs={{1,0},{0,1},{17,16},{16,17},{3,2},{2,3},{19,18},{18,19},{5,4},{4,5... | collective-permute-start | bytes 1572872 | tf_op jit(solution)/shard_map/ppermute | solution.py:357
  24.2 2.6 %collective-permute-start.8 = (f32[1,4,128,128]{3,2,1,0:T(8,128)S(1)}, f32[1,4,128,128]{3,2,1,0:T(8,128)S(1)}, u32[]{:S(2)}, u32[]{:S(2)}) collective-permute-start(f32[1,4,128,128]{3,2,1,0:T(8,128)S(1)} %collective-permute-done.7.r4a), channel_id=1, source_target_pairs={{1,0},{0,1},{17,16},{16,17},{3,2},{2,3},{19,18},{18,19},{5,4},{4,5... | collective-permute-start | bytes 786440 | tf_op jit(solution)/shard_map/ppermute | solution.py:357
  26.8 1.6 %collective-permute-start.9 = (f32[1,4,128,128]{3,2,1,0:T(8,128)S(1)}, f32[1,4,128,128]{3,2,1,0:T(8,128)S(1)}, u32[]{:S(2)}, u32[]{:S(2)}) collective-permute-start(f32[1,4,128,128]{3,2,1,0:T(8,128)S(1)} %collective-permute-done.6.r4b), channel_id=1, source_target_pairs={{1,0},{0,1},{17,16},{16,17},{3,2},{2,3},{19,18},{18,19},{5,4},{4,5... | collective-permute-start | bytes 786440 | tf_op jit(solution)/shard_map/ppermute | solution.py:357

commit v23 on v21

--- a/solution.py
+++ b/solution.py
@@ -102,6 +102,15 @@
     return both[:half] + (both[half:] + dot(left[:half], low))
 
 
+def joined_dot(left, high, low):
+    half = left.shape[0] // 2
+    left_high, left_low = left[:half], left[half:]
+    return dot(
+        jnp.concatenate([left_high, left_low, left_high], axis=1),
+        jnp.concatenate([high, high, low], axis=0),
+    )
+
+
 def lookup(table, place, lane):
     found = jnp.int32(-1)
     for z, entries in enumerate(table):
@@ -151,7 +160,7 @@
         rows = pl.ds(pl.multiple_of(plane * depth, depth), depth)
         for n in range(part_ref.shape[1] // tile):
             cols = pl.ds(n * tile, tile)
-            part_ref[:, cols] += stacked_dot(left[:, rows], high[rows, cols], low[rows, cols])
+            part_ref[:, cols] += joined_dot(left[:, rows], high[rows, cols], low[rows, cols])
 
 
 def early_kernel(

time: 31.8 us -> 31.8 us (level)
  no operation moved by 1% of the time
where the time goes in v23:
time: 31.8 us; the launch traced here: 31.5 us
  starting transfers between devices  13.7 us (43%)
  waiting for transfers between devices  7.71 us (24%)
  Pallas kernels  7.6 us (24%)
  other arithmetic  2.24 us (7%)
    ppermute x10, starting transfers between devices, move(): return lax.ppermute(block, AXES, route)  11.5 us
    ppermute x10, waiting for transfers between devices, move(): return lax.ppermute(block, AXES, route)  4.5 us
    ppermute x1, waiting for transfers between devices, move_only(): return lax.ppermute(block, AXES, route)  3.21 us
    pallas_call x1, Pallas kernels, gather_local(): pl.pallas_call(functools.partial(late_kernel, tables), out_shape=[jax.Sha...  3.15 us
    pallas_call x1, Pallas kernels, gather_local(): pl.pallas_call(functools.partial(early_kernel, tables), out_shape=[jax.Sh...  3.1 us
    ppermute x1, starting transfers between devices, move_only(): return lax.ppermute(block, AXES, route)  2.28 us
    pallas_call x1, Pallas kernels, gather_local(): pl.pallas_call(functools.partial(middle_kernel, tables), out_shape=dense,...  1.35 us
    reduce_sum x1, other arithmetic, slot_table(): count = jnp.sum(here.astype(jnp.int32), axis=1, keepdims=True)  0.8 us
  transfers between devices with their start and end apart: 11, of which 6 were waited for; matrix products, arithmetic and copies ran while one was open for 7% of the time, Pallas kernels for 14%

profile of v23, /device:TPU:0, one launch (start us, length us, event | category | flops | bytes accessed | tf_op | source)
XLA Modules:
  0.0 31.5 jit_solution(172660685731609780)
XLA Ops:
  0.0 2.9 %collective-permute-start = (f32[2,4,128,128]{3,2,1,0:T(8,128)}, f32[2,4,128,128]{3,2,1,0:T(8,128)S(1)}, u32[]{:S(2)}, u32[]{:S(2)}) collective-permute-start(f32[2,4,128,128]{3,2,1,0:T(8,128)} %own_hbm.1), channel_id=1, source_target_pairs={{3,1},{1,4},{4,9},{9,12},{12,8},{8,5},{5,0},{0,2},{2,3},{14,13},{1... | collective-permute-start | bytes 1572872 | tf_op jit(solution)/shard_map/ppermute | solution.py:315
  2.9 0.2 collective-permute-start.1
  3.1 0.8 %fusion.1 = (s32[8]{0:T(128)S(1)}, s32[8,8]{1,0:T(8,128)S(1)}) fusion(s32[8,16]{1,0:T(8,128)} %param.3), kind=kLoop, calls=%fused_computation.7 | loop fusion | flops 184 | bytes 544 | tf_op jit(solution)/shard_map/reduce_sum | solution.py:280
  3.9 0.1 fusion
  4.1 0.2 convert_reduce_fusion
  4.3 0.8 %collective-permute-done.1.own_swap = f32[2,4,128,128]{3,2,1,0:T(8,128)S(1)} collective-permute-done((f32[2,4,128,128]{3,2,1,0:T(8,128)}, f32[2,4,128,128]{3,2,1,0:T(8,128)S(1)}, u32[]{:S(2)}, u32[]{:S(2)}) %collective-permute-start.1) | collective-permute-done | bytes 524320 | tf_op jit(solution)/shard_map/ppermute | solution.py:315
  5.1 2.3 %collective-permute-start.2 = (f32[2,4,128,128]{3,2,1,0:T(8,128)S(1)}, f32[2,4,128,128]{3,2,1,0:T(8,128)S(1)}, u32[]{:S(2)}, u32[]{:S(2)}) collective-permute-start(f32[2,4,128,128]{3,2,1,0:T(8,128)S(1)} %collective-permute-done.1.own_swap), channel_id=1, source_target_pairs={{1,4},{4,9},{9,13},{13,15},{12,8},{8,5},{5,0},{0,2},{17,20},{20,25... | collective-permute-start | bytes 1572872 | tf_op jit(solution)/shard_map/ppermute | solution.py:323
  7.3 0.1 add_select_fusion
  7.5 0.1 copy.10
  7.5 0.2 select_reduce_fusion
  7.8 0.7 %compare_select_fusion = s32[8,8]{1,0:T(8,128)S(1)} fusion(s32[8,8]{1,0:T(8,128)S(1)} %select_reduce_fusion, s32[8,16]{1,0:T(8,128)} %param.3), kind=kLoop, calls=%fused_computation.5 | loop fusion | flops 192 | bytes 768 | tf_op jit(solution)/shard_map/jit(_where)/select_n | solution.py:288
  8.5 0.1 pad_add_fusion.table_ref
  8.5 1.4 %collective-permute-done.r1 = f32[2,4,128,128]{3,2,1,0:T(8,128)S(1)} collective-permute-done((f32[2,4,128,128]{3,2,1,0:T(8,128)}, f32[2,4,128,128]{3,2,1,0:T(8,128)S(1)}, u32[]{:S(2)}, u32[]{:S(2)}) %collective-permute-start) | collective-permute-done | bytes 524320 | tf_op jit(solution)/shard_map/ppermute | solution.py:315
  10.0 2.4 %collective-permute-start.5 = (f32[2,4,128,128]{3,2,1,0:T(8,128)S(1)}, f32[2,4,128,128]{3,2,1,0:T(8,128)S(1)}, u32[]{:S(2)}, u32[]{:S(2)}) collective-permute-start(f32[2,4,128,128]{3,2,1,0:T(8,128)S(1)} %collective-permute-done.r1), channel_id=1, source_target_pairs={{15,1},{1,4},{4,9},{9,13},{13,15},{2,12},{12,8},{8,5},{5,0},{0,2},... | collective-permute-start | bytes 1572872 | tf_op jit(solution)/shard_map/ppermute | solution.py:315
  12.3 0.0 collective-permute-start.3
  12.3 3.2 %collective-permute-done.2.r2 = f32[2,4,128,128]{3,2,1,0:T(8,128)S(1)} collective-permute-done((f32[2,4,128,128]{3,2,1,0:T(8,128)S(1)}, f32[2,4,128,128]{3,2,1,0:T(8,128)S(1)}, u32[]{:S(2)}, u32[]{:S(2)}) %collective-permute-start.2) | collective-permute-done | bytes 524320 | tf_op jit(solution)/shard_map/ppermute | solution.py:323
  15.6 0.0 collective-permute-start.4
  15.6 2.5 %collective-permute-start.7 = (f32[1,4,128,128]{3,2,1,0:T(8,128)S(1)}, f32[1,4,128,128]{3,2,1,0:T(8,128)S(1)}, u32[]{:S(2)}, u32[]{:S(2)}) collective-permute-start(f32[1,4,128,128]{3,2,1,0:T(8,128)S(1)} %get-tuple-element.35), channel_id=1, source_target_pairs={{15,1},{1,4},{4,9},{9,13},{13,15},{2,12},{12,8},{8,5},{5,0},{0,2},... | collective-permute-start | bytes 786440 | tf_op jit(solution)/shard_map/ppermute | solution.py:315
  18.0 2.8 %collective-permute-start.6 = (f32[1,4,128,128]{3,2,1,0:T(8,128)S(1)}, f32[1,4,128,128]{3,2,1,0:T(8,128)S(1)}, u32[]{:S(2)}, u32[]{:S(2)}) collective-permute-start(f32[1,4,128,128]{3,2,1,0:T(8,128)S(1)} %get-tuple-element.36), channel_id=1, source_target_pairs={{15,1},{1,4},{4,9},{9,13},{13,15},{2,12},{12,8},{8,5},{5,0},{0,2},... | collective-permute-start | bytes 786440 | tf_op jit(solution)/shard_map/ppermute | solution.py:315
  20.9 0.3 collective-permute-done.5.r3
  21.2 0.0 collective-permute-start.10
  21.2 0.0 collective-permute-done.3.t1
  21.2 0.0 collective-permute-done.4.t2
  21.2 3.1 %early.1 = (bf16[1024,1024]{1,0:T(8,128)(2,1)S(1)}, bf16[1024,1024]{1,0:T(8,128)(2,1)S(1)}, bf16[512,1024]{1,0:T(8,128)(2,1)S(1)}, f32[256,1024]{1,0:T(8,128)S(1)}, s32[8,128]{1,0:T(8,128)S(1)}) custom-call(s32[8,9]{1,0:T(8,128)S(1)} %pad_add_fusion.table_ref, f32[2,4,128,128]{3,2,1,0:T(8,128)} %own_hbm.1, ...), custom_call_target="tpu_custom_call" | custom-call | tf_op jit(solution)/shard_map/early/pallas_call | solution.py:370
  24.3 0.0 collective-permute-done.7.r4a
  24.3 0.6 %collective-permute-start.8 = (f32[1,4,128,128]{3,2,1,0:T(8,128)S(1)}, f32[1,4,128,128]{3,2,1,0:T(8,128)S(1)}, u32[]{:S(2)}, u32[]{:S(2)}) collective-permute-start(f32[1,4,128,128]{3,2,1,0:T(8,128)S(1)} %collective-permute-done.7.r4a), channel_id=1, source_target_pairs={{1,0},{0,1},{17,16},{16,17},{3,2},{2,3},{19,18},{18,19},{5,4},{4,5... | collective-permute-start | bytes 786440 | tf_op jit(solution)/shard_map/ppermute | solution.py:315
  24.9 1.9 %collective-permute-done.6.r4b = f32[1,4,128,128]{3,2,1,0:T(8,128)S(1)} collective-permute-done((f32[1,4,128,128]{3,2,1,0:T(8,128)S(1)}, f32[1,4,128,128]{3,2,1,0:T(8,128)S(1)}, u32[]{:S(2)}, u32[]{:S(2)}) %collective-permute-start.6) | collective-permute-done | bytes 262176 | tf_op jit(solution)/shard_map/ppermute | solution.py:315
  26.8 0.0 collective-permute-done.8.t4a
  26.8 0.1 collective-permute-start.9
  26.9 1.3 %middle.1 = (bf16[1024,1024]{1,0:T(8,128)(2,1)S(1)}, bf16[1024,1024]{1,0:T(8,128)(2,1)S(1)}, f32[256,1024]{1,0:T(8,128)S(1)}) custom-call(s32[8,128]{1,0:T(8,128)S(1)} %get-tuple-element.22.notes_ref, f32[1,4,128,128]{3,2,1,0:T(8,128)S(1)} %collective-permute-done.7.r4a, ...), custom_call_target="tpu_custom_call", output_to_operand_aliasing={{0}: (5, {}), {1}: (6, {}), {2}: (8, {})} | custom-call | tf_op jit(solution)/shard_map/middle/pallas_call | solution.py:391
  28.2 0.1 collective-permute-done.9.t4b
  28.3 3.1 %late.1 = (f32[2,4,128,128]{3,2,1,0:T(8,128)}, bf16[1024,1024]{1,0:T(8,128)(2,1)S(1)}, bf16[1024,1024]{1,0:T(8,128)(2,1)S(1)}, f32[256,1024]{1,0:T(8,128)S(1)}) custom-call(s32[8,128]{1,0:T(8,128)S(1)} %get-tuple-element.22.notes_ref, f32[1,4,128,128]{3,2,1,0:T(8,128)S(1)} %collective-permute-done.9.t4b, ...), custom_call_target="tpu_custom_call", output_to_operand_aliasing={{1}: (2, {}), {2}: (3, {}), {3}: (5, {})} | custom-call | tf_op jit(solution)/shard_map/late/pallas_call | solution.py:400
  (5 shorter events, 0.1 us)
Async XLA Ops:
  0.0 10.0 %collective-permute-start = (f32[2,4,128,128]{3,2,1,0:T(8,128)}, f32[2,4,128,128]{3,2,1,0:T(8,128)S(1)}, u32[]{:S(2)}, u32[]{:S(2)}) collective-permute-start(f32[2,4,128,128]{3,2,1,0:T(8,128)} %own_hbm.1), channel_id=1, source_target_pairs={{3,1},{1,4},{4,9},{9,12},{12,8},{8,5},{5,0},{0,2},{2,3},{14,13},{1... | collective-permute-start | bytes 1572872 | tf_op jit(solution)/shard_map/ppermute | solution.py:315
  2.9 2.1 %collective-permute-start.1 = (f32[2,4,128,128]{3,2,1,0:T(8,128)}, f32[2,4,128,128]{3,2,1,0:T(8,128)S(1)}, u32[]{:S(2)}, u32[]{:S(2)}) collective-permute-start(f32[2,4,128,128]{3,2,1,0:T(8,128)} %own_hbm.1), channel_id=1, source_target_pairs={{1,0},{0,1},{17,16},{16,17},{3,2},{2,3},{19,18},{18,19},{5,4},{4,5... | collective-permute-start | bytes 1572872 | tf_op jit(solution)/shard_map/ppermute | solution.py:315
  5.1 10.5 %collective-permute-start.2 = (f32[2,4,128,128]{3,2,1,0:T(8,128)S(1)}, f32[2,4,128,128]{3,2,1,0:T(8,128)S(1)}, u32[]{:S(2)}, u32[]{:S(2)}) collective-permute-start(f32[2,4,128,128]{3,2,1,0:T(8,128)S(1)} %collective-permute-done.1.own_swap), channel_id=1, source_target_pairs={{1,4},{4,9},{9,13},{13,15},{12,8},{8,5},{5,0},{0,2},{17,20},{20,25... | collective-permute-start | bytes 1572872 | tf_op jit(solution)/shard_map/ppermute | solution.py:323
  10.0 11.2 %collective-permute-start.5 = (f32[2,4,128,128]{3,2,1,0:T(8,128)S(1)}, f32[2,4,128,128]{3,2,1,0:T(8,128)S(1)}, u32[]{:S(2)}, u32[]{:S(2)}) collective-permute-start(f32[2,4,128,128]{3,2,1,0:T(8,128)S(1)} %collective-permute-done.r1), channel_id=1, source_target_pairs={{15,1},{1,4},{4,9},{9,13},{13,15},{2,12},{12,8},{8,5},{5,0},{0,2},... | collective-permute-start | bytes 1572872 | tf_op jit(solution)/shard_map/ppermute | solution.py:315
  12.3 8.8 %collective-permute-start.3 = (f32[2,4,128,128]{3,2,1,0:T(8,128)S(1)}, f32[2,4,128,128]{3,2,1,0:T(8,128)S(1)}, u32[]{:S(2)}, u32[]{:S(2)}) collective-permute-start(f32[2,4,128,128]{3,2,1,0:T(8,128)S(1)} %collective-permute-done.r1), channel_id=1, source_target_pairs={{1,0},{0,1},{17,16},{16,17},{3,2},{2,3},{19,18},{18,19},{5,4},{4,5... | collective-permute-start | bytes 1572872 | tf_op jit(solution)/shard_map/ppermute | solution.py:315
  15.6 5.6 %collective-permute-start.4 = (f32[2,4,128,128]{3,2,1,0:T(8,128)S(1)}, f32[2,4,128,128]{3,2,1,0:T(8,128)S(1)}, u32[]{:S(2)}, u32[]{:S(2)}) collective-permute-start(f32[2,4,128,128]{3,2,1,0:T(8,128)S(1)} %collective-permute-done.2.r2), channel_id=1, source_target_pairs={{1,0},{0,1},{17,16},{16,17},{3,2},{2,3},{19,18},{18,19},{5,4},{4,5... | collective-permute-start | bytes 1572872 | tf_op jit(solution)/shard_map/ppermute | solution.py:315
  15.6 8.7 %collective-permute-start.7 = (f32[1,4,128,128]{3,2,1,0:T(8,128)S(1)}, f32[1,4,128,128]{3,2,1,0:T(8,128)S(1)}, u32[]{:S(2)}, u32[]{:S(2)}) collective-permute-start(f32[1,4,128,128]{3,2,1,0:T(8,128)S(1)} %get-tuple-element.35), channel_id=1, source_target_pairs={{15,1},{1,4},{4,9},{9,13},{13,15},{2,12},{12,8},{8,5},{5,0},{0,2},... | collective-permute-start | bytes 786440 | tf_op jit(solution)/shard_map/ppermute | solution.py:315
  18.0 8.7 %collective-permute-start.6 = (f32[1,4,128,128]{3,2,1,0:T(8,128)S(1)}, f32[1,4,128,128]{3,2,1,0:T(8,128)S(1)}, u32[]{:S(2)}, u32[]{:S(2)}) collective-permute-start(f32[1,4,128,128]{3,2,1,0:T(8,128)S(1)} %get-tuple-element.36), channel_id=1, source_target_pairs={{15,1},{1,4},{4,9},{9,13},{13,15},{2,12},{12,8},{8,5},{5,0},{0,2},... | collective-permute-start | bytes 786440 | tf_op jit(solution)/shard_map/ppermute | solution.py:315
  21.2 5.7 %collective-permute-start.10 = (f32[2,4,128,128]{3,2,1,0:T(8,128)S(1)}, f32[2,4,128,128]{3,2,1,0:T(8,128)S(1)}, u32[]{:S(2)}, u32[]{:S(2)}) collective-permute-start(f32[2,4,128,128]{3,2,1,0:T(8,128)S(1)} %collective-permute-done.5.r3), channel_id=1, source_target_pairs={{1,0},{0,1},{17,16},{16,17},{3,2},{2,3},{19,18},{18,19},{5,4},{4,5... | collective-permute-start | bytes 1572872 | tf_op jit(solution)/shard_map/ppermute | solution.py:315
  24.3 2.5 %collective-permute-start.8 = (f32[1,4,128,128]{3,2,1,0:T(8,128)S(1)}, f32[1,4,128,128]{3,2,1,0:T(8,128)S(1)}, u32[]{:S(2)}, u32[]{:S(2)}) collective-permute-start(f32[1,4,128,128]{3,2,1,0:T(8,128)S(1)} %collective-permute-done.7.r4a), channel_id=1, source_target_pairs={{1,0},{0,1},{17,16},{16,17},{3,2},{2,3},{19,18},{18,19},{5,4},{4,5... | collective-permute-start | bytes 786440 | tf_op jit(solution)/shard_map/ppermute | solution.py:315
  26.8 1.5 %collective-permute-start.9 = (f32[1,4,128,128]{3,2,1,0:T(8,128)S(1)}, f32[1,4,128,128]{3,2,1,0:T(8,128)S(1)}, u32[]{:S(2)}, u32[]{:S(2)}) collective-permute-start(f32[1,4,128,128]{3,2,1,0:T(8,128)S(1)} %collective-permute-done.6.r4b), channel_id=1, source_target_pairs={{1,0},{0,1},{17,16},{16,17},{3,2},{2,3},{19,18},{18,19},{5,4},{4,5... | collective-permute-start | bytes 786440 | tf_op jit(solution)/shard_map/ppermute | solution.py:315

commit v24 on v22

--- a/solution.py
+++ b/solution.py
@@ -173,22 +173,16 @@
     @pl.when(plane >= 0)
     def _():
         at = pl.ds(pl.multiple_of((plane * 2 + r) * edge, edge), edge)
-        for w in range(0, width, 2):
-            codes = [code_of(r, w + k) for k in range(2)]
-            cols = [pl.ds(pl.multiple_of(code % act * edge, edge), edge) for code in codes]
-            parts = [
-                split(jnp.where(code < act, piece[0, w + k], 0.0)) for k, code in enumerate(codes)
-            ]
-            for col, (block_high, block_low) in zip(cols, parts):
-                high[at, col] = block_high
-                low[at, col] = block_low
-            more = stacked_dot(
-                left[:, at],
-                jnp.concatenate([block_high for block_high, _ in parts], axis=1),
-                jnp.concatenate([block_low for _, block_low in parts], axis=1),
-            )
-            for k, col in enumerate(cols):
-                part_ref[:, col] += more[:, k * edge : (k + 1) * edge]
+        codes = [code_of(r, w) for w in range(width)]
+        cols = [pl.ds(pl.multiple_of(code % act * edge, edge), edge) for code in codes]
+        blocks = [jnp.where(code < act, piece[0, w], 0.0) for w, code in enumerate(codes)]
+        block_high, block_low = split(jnp.concatenate(blocks, axis=1))
+        more = stacked_dot(left[:, at], block_high, block_low)
+        sums = [part_ref[:, col] + more[:, w * edge : (w + 1) * edge] for w, col in enumerate(cols)]
+        for w, col in enumerate(cols):
+            part_ref[:, col] = sums[w]
+            high[at, col] = block_high[:, w * edge : (w + 1) * edge]
+            low[at, col] = block_low[:, w * edge : (w + 1) * edge]
 
 
 def early_kernel(

time: 31.8 us -> 31.7 us (level)
  no operation moved by 1% of the time
where the time goes in v24:
time: 31.7 us; the launch traced here: 31.4 us
  starting transfers between devices  13.7 us (43%)
  Pallas kernels  8.29 us (26%)
  waiting for transfers between devices  6.9 us (22%)
  other arithmetic  2.24 us (7%)
    ppermute x10, starting transfers between devices, move(): return lax.ppermute(block, AXES, route)  11.5 us
    ppermute x10, waiting for transfers between devices, move(): return lax.ppermute(block, AXES, route)  3.69 us
    ppermute x1, waiting for transfers between devices, move_only(): return lax.ppermute(block, AXES, route)  3.21 us
    pallas_call x1, Pallas kernels, gather_local(): pl.pallas_call(functools.partial(early_kernel, tables), out_shape=[jax.Sh...  3.03 us
    pallas_call x1, Pallas kernels, gather_local(): pl.pallas_call(functools.partial(late_kernel, tables), out_shape=[jax.Sha...  2.96 us
    pallas_call x2, Pallas kernels, add_to_square(): pl.pallas_call(functools.partial(kernel, tables), out_shape=dense, in_spe...  2.3 us
    ppermute x1, starting transfers between devices, move_only(): return lax.ppermute(block, AXES, route)  2.28 us
    reduce_sum x1, other arithmetic, slot_table(): count = jnp.sum(here.astype(jnp.int32), axis=1, keepdims=True)  0.8 us
  transfers between devices with their start and end apart: 11, of which 5 were waited for; matrix products, arithmetic and copies ran while one was open for 7% of the time, Pallas kernels for 17%

profile of v24, /device:TPU:0, one launch (start us, length us, event | category | flops | bytes accessed | tf_op | source)
XLA Modules:
  0.0 31.4 jit_solution(10939110318090456595)
XLA Ops:
  0.0 2.9 %collective-permute-start = (f32[2,4,128,128]{3,2,1,0:T(8,128)}, f32[2,4,128,128]{3,2,1,0:T(8,128)S(1)}, u32[]{:S(2)}, u32[]{:S(2)}) collective-permute-start(f32[2,4,128,128]{3,2,1,0:T(8,128)} %own_hbm.1), channel_id=1, source_target_pairs={{3,1},{1,4},{4,9},{9,12},{12,8},{8,5},{5,0},{0,2},{2,3},{14,13},{1... | collective-permute-start | bytes 1572872 | tf_op jit(solution)/shard_map/ppermute | solution.py:351
  2.9 0.2 collective-permute-start.1
  3.1 0.8 %fusion.1 = (s32[8]{0:T(128)S(1)}, s32[8,8]{1,0:T(8,128)S(1)}) fusion(s32[8,16]{1,0:T(8,128)} %param.3), kind=kLoop, calls=%fused_computation.7 | loop fusion | flops 184 | bytes 544 | tf_op jit(solution)/shard_map/reduce_sum | solution.py:316
  3.9 0.1 fusion
  4.1 0.2 convert_reduce_fusion
  4.3 0.8 %collective-permute-done.1.own_swap = f32[2,4,128,128]{3,2,1,0:T(8,128)S(1)} collective-permute-done((f32[2,4,128,128]{3,2,1,0:T(8,128)}, f32[2,4,128,128]{3,2,1,0:T(8,128)S(1)}, u32[]{:S(2)}, u32[]{:S(2)}) %collective-permute-start.1) | collective-permute-done | bytes 524320 | tf_op jit(solution)/shard_map/ppermute | solution.py:351
  5.1 2.3 %collective-permute-start.2 = (f32[2,4,128,128]{3,2,1,0:T(8,128)S(1)}, f32[2,4,128,128]{3,2,1,0:T(8,128)S(1)}, u32[]{:S(2)}, u32[]{:S(2)}) collective-permute-start(f32[2,4,128,128]{3,2,1,0:T(8,128)S(1)} %collective-permute-done.1.own_swap), channel_id=1, source_target_pairs={{1,4},{4,9},{9,13},{13,15},{12,8},{8,5},{5,0},{0,2},{17,20},{20,25... | collective-permute-start | bytes 1572872 | tf_op jit(solution)/shard_map/ppermute | solution.py:359
  7.3 0.1 add_select_fusion
  7.5 0.1 copy.13
  7.5 0.2 select_reduce_fusion
  7.8 0.7 %compare_select_fusion = s32[8,8]{1,0:T(8,128)S(1)} fusion(s32[8,8]{1,0:T(8,128)S(1)} %select_reduce_fusion, s32[8,16]{1,0:T(8,128)} %param.3), kind=kLoop, calls=%fused_computation.5 | loop fusion | flops 192 | bytes 768 | tf_op jit(solution)/shard_map/jit(_where)/select_n | solution.py:324
  8.5 0.1 pad_add_fusion.table_ref
  8.5 1.4 %collective-permute-done.r1 = f32[2,4,128,128]{3,2,1,0:T(8,128)S(1)} collective-permute-done((f32[2,4,128,128]{3,2,1,0:T(8,128)}, f32[2,4,128,128]{3,2,1,0:T(8,128)S(1)}, u32[]{:S(2)}, u32[]{:S(2)}) %collective-permute-start) | collective-permute-done | bytes 524320 | tf_op jit(solution)/shard_map/ppermute | solution.py:351
  10.0 2.4 %collective-permute-start.5 = (f32[2,4,128,128]{3,2,1,0:T(8,128)S(1)}, f32[2,4,128,128]{3,2,1,0:T(8,128)S(1)}, u32[]{:S(2)}, u32[]{:S(2)}) collective-permute-start(f32[2,4,128,128]{3,2,1,0:T(8,128)S(1)} %collective-permute-done.r1), channel_id=1, source_target_pairs={{15,1},{1,4},{4,9},{9,13},{13,15},{2,12},{12,8},{8,5},{5,0},{0,2},... | collective-permute-start | bytes 1572872 | tf_op jit(solution)/shard_map/ppermute | solution.py:351
  12.3 0.0 collective-permute-start.3
  12.3 3.2 %collective-permute-done.2.r2 = f32[2,4,128,128]{3,2,1,0:T(8,128)S(1)} collective-permute-done((f32[2,4,128,128]{3,2,1,0:T(8,128)S(1)}, f32[2,4,128,128]{3,2,1,0:T(8,128)S(1)}, u32[]{:S(2)}, u32[]{:S(2)}) %collective-permute-start.2) | collective-permute-done | bytes 524320 | tf_op jit(solution)/shard_map/ppermute | solution.py:359
  15.6 2.5 %collective-permute-start.7 = (f32[1,4,128,128]{3,2,1,0:T(8,128)S(1)}, f32[1,4,128,128]{3,2,1,0:T(8,128)S(1)}, u32[]{:S(2)}, u32[]{:S(2)}) collective-permute-start(f32[1,4,128,128]{3,2,1,0:T(8,128)S(1)} %get-tuple-element.43), channel_id=1, source_target_pairs={{15,1},{1,4},{4,9},{9,13},{13,15},{2,12},{12,8},{8,5},{5,0},{0,2},... | collective-permute-start | bytes 786440 | tf_op jit(solution)/shard_map/ppermute | solution.py:351
  18.0 2.8 %collective-permute-start.6 = (f32[1,4,128,128]{3,2,1,0:T(8,128)S(1)}, f32[1,4,128,128]{3,2,1,0:T(8,128)S(1)}, u32[]{:S(2)}, u32[]{:S(2)}) collective-permute-start(f32[1,4,128,128]{3,2,1,0:T(8,128)S(1)} %get-tuple-element.44), channel_id=1, source_target_pairs={{15,1},{1,4},{4,9},{9,13},{13,15},{2,12},{12,8},{8,5},{5,0},{0,2},... | collective-permute-start | bytes 786440 | tf_op jit(solution)/shard_map/ppermute | solution.py:351
  20.9 0.3 collective-permute-done.5.r3
  21.2 0.0 collective-permute-start.10
  21.2 0.0 collective-permute-done.3.t1
  21.2 0.0 collective-permute-done.4.t2
  21.2 3.0 %early.1 = (bf16[1024,1024]{1,0:T(8,128)(2,1)S(1)}, bf16[1024,1024]{1,0:T(8,128)(2,1)S(1)}, bf16[512,1024]{1,0:T(8,128)(2,1)S(1)}, f32[256,1024]{1,0:T(8,128)S(1)}, s32[8,128]{1,0:T(8,128)S(1)}) custom-call(s32[8,9]{1,0:T(8,128)S(1)} %pad_add_fusion.table_ref, f32[2,4,128,128]{3,2,1,0:T(8,128)} %own_hbm.1, ...), custom_call_target="tpu_custom_call" | custom-call | tf_op jit(solution)/shard_map/early/pallas_call | solution.py:406
  24.2 0.0 collective-permute-done.7.r4a
  24.2 0.6 %collective-permute-start.8 = (f32[1,4,128,128]{3,2,1,0:T(8,128)S(1)}, f32[1,4,128,128]{3,2,1,0:T(8,128)S(1)}, u32[]{:S(2)}, u32[]{:S(2)}) collective-permute-start(f32[1,4,128,128]{3,2,1,0:T(8,128)S(1)} %collective-permute-done.7.r4a), channel_id=1, source_target_pairs={{1,0},{0,1},{17,16},{16,17},{3,2},{2,3},{19,18},{18,19},{5,4},{4,5... | collective-permute-start | bytes 786440 | tf_op jit(solution)/shard_map/ppermute | solution.py:351
  24.8 0.8 %waiting.1 = (bf16[1024,1024]{1,0:T(8,128)(2,1)S(1)}, bf16[1024,1024]{1,0:T(8,128)(2,1)S(1)}, f32[256,1024]{1,0:T(8,128)S(1)}) custom-call(s32[8,128]{1,0:T(8,128)S(1)} %get-tuple-element.26.notes_ref, f32[1,4,128,128]{3,2,1,0:T(8,128)S(1)} %collective-permute-done.7.r4a, ...), custom_call_target="tpu_custom_call", output_to_operand_aliasing={{0}: (2, {}), {1}: (3, {}), {2}: (5, {})} | custom-call | tf_op jit(solution)/shard_map/waiting/pallas_call | solution.py:428
  25.6 1.2 %collective-permute-done.6.r4b = f32[1,4,128,128]{3,2,1,0:T(8,128)S(1)} collective-permute-done((f32[1,4,128,128]{3,2,1,0:T(8,128)S(1)}, f32[1,4,128,128]{3,2,1,0:T(8,128)S(1)}, u32[]{:S(2)}, u32[]{:S(2)}) %collective-permute-start.6) | collective-permute-done | bytes 262176 | tf_op jit(solution)/shard_map/ppermute | solution.py:351
  26.8 0.1 collective-permute-start.9
  26.9 0.0 collective-permute-done.10.t3
  26.9 1.5 %middle.1 = (bf16[1024,1024]{1,0:T(8,128)(2,1)S(1)}, bf16[1024,1024]{1,0:T(8,128)(2,1)S(1)}, f32[256,1024]{1,0:T(8,128)S(1)}) custom-call(s32[8,128]{1,0:T(8,128)S(1)} %get-tuple-element.26.notes_ref, f32[1,4,128,128]{3,2,1,0:T(8,128)S(1)} %collective-permute-done.6.r4b, ...), custom_call_target="tpu_custom_call", output_to_operand_aliasing={{0}: (4, {}), {1}: (5, {}), {2}: (7, {})} | custom-call | tf_op jit(solution)/shard_map/middle/pallas_call | solution.py:428
  28.4 0.0 collective-permute-done.9.t4b
  28.4 3.0 %late.1 = (f32[2,4,128,128]{3,2,1,0:T(8,128)}, bf16[1024,1024]{1,0:T(8,128)(2,1)S(1)}, bf16[1024,1024]{1,0:T(8,128)(2,1)S(1)}, f32[256,1024]{1,0:T(8,128)S(1)}) custom-call(s32[8,128]{1,0:T(8,128)S(1)} %get-tuple-element.26.notes_ref, f32[1,4,128,128]{3,2,1,0:T(8,128)S(1)} %collective-permute-done.9.t4b, ...), custom_call_target="tpu_custom_call", output_to_operand_aliasing={{1}: (2, {}), {2}: (3, {}), {3}: (5, {})} | custom-call | tf_op jit(solution)/shard_map/late/pallas_call | solution.py:442
  (6 shorter events, 0.1 us)
Async XLA Ops:
  0.0 10.0 %collective-permute-start = (f32[2,4,128,128]{3,2,1,0:T(8,128)}, f32[2,4,128,128]{3,2,1,0:T(8,128)S(1)}, u32[]{:S(2)}, u32[]{:S(2)}) collective-permute-start(f32[2,4,128,128]{3,2,1,0:T(8,128)} %own_hbm.1), channel_id=1, source_target_pairs={{3,1},{1,4},{4,9},{9,12},{12,8},{8,5},{5,0},{0,2},{2,3},{14,13},{1... | collective-permute-start | bytes 1572872 | tf_op jit(solution)/shard_map/ppermute | solution.py:351
  2.9 2.1 %collective-permute-start.1 = (f32[2,4,128,128]{3,2,1,0:T(8,128)}, f32[2,4,128,128]{3,2,1,0:T(8,128)S(1)}, u32[]{:S(2)}, u32[]{:S(2)}) collective-permute-start(f32[2,4,128,128]{3,2,1,0:T(8,128)} %own_hbm.1), channel_id=1, source_target_pairs={{1,0},{0,1},{17,16},{16,17},{3,2},{2,3},{19,18},{18,19},{5,4},{4,5... | collective-permute-start | bytes 1572872 | tf_op jit(solution)/shard_map/ppermute | solution.py:351
  5.1 10.5 %collective-permute-start.2 = (f32[2,4,128,128]{3,2,1,0:T(8,128)S(1)}, f32[2,4,128,128]{3,2,1,0:T(8,128)S(1)}, u32[]{:S(2)}, u32[]{:S(2)}) collective-permute-start(f32[2,4,128,128]{3,2,1,0:T(8,128)S(1)} %collective-permute-done.1.own_swap), channel_id=1, source_target_pairs={{1,4},{4,9},{9,13},{13,15},{12,8},{8,5},{5,0},{0,2},{17,20},{20,25... | collective-permute-start | bytes 1572872 | tf_op jit(solution)/shard_map/ppermute | solution.py:359
  10.0 11.2 %collective-permute-start.5 = (f32[2,4,128,128]{3,2,1,0:T(8,128)S(1)}, f32[2,4,128,128]{3,2,1,0:T(8,128)S(1)}, u32[]{:S(2)}, u32[]{:S(2)}) collective-permute-start(f32[2,4,128,128]{3,2,1,0:T(8,128)S(1)} %collective-permute-done.r1), channel_id=1, source_target_pairs={{15,1},{1,4},{4,9},{9,13},{13,15},{2,12},{12,8},{8,5},{5,0},{0,2},... | collective-permute-start | bytes 1572872 | tf_op jit(solution)/shard_map/ppermute | solution.py:351
  12.3 8.8 %collective-permute-start.3 = (f32[2,4,128,128]{3,2,1,0:T(8,128)S(1)}, f32[2,4,128,128]{3,2,1,0:T(8,128)S(1)}, u32[]{:S(2)}, u32[]{:S(2)}) collective-permute-start(f32[2,4,128,128]{3,2,1,0:T(8,128)S(1)} %collective-permute-done.r1), channel_id=1, source_target_pairs={{1,0},{0,1},{17,16},{16,17},{3,2},{2,3},{19,18},{18,19},{5,4},{4,5... | collective-permute-start | bytes 1572872 | tf_op jit(solution)/shard_map/ppermute | solution.py:351
  15.6 5.6 %collective-permute-start.4 = (f32[2,4,128,128]{3,2,1,0:T(8,128)S(1)}, f32[2,4,128,128]{3,2,1,0:T(8,128)S(1)}, u32[]{:S(2)}, u32[]{:S(2)}) collective-permute-start(f32[2,4,128,128]{3,2,1,0:T(8,128)S(1)} %collective-permute-done.2.r2), channel_id=1, source_target_pairs={{1,0},{0,1},{17,16},{16,17},{3,2},{2,3},{19,18},{18,19},{5,4},{4,5... | collective-permute-start | bytes 1572872 | tf_op jit(solution)/shard_map/ppermute | solution.py:351
  15.6 8.6 %collective-permute-start.7 = (f32[1,4,128,128]{3,2,1,0:T(8,128)S(1)}, f32[1,4,128,128]{3,2,1,0:T(8,128)S(1)}, u32[]{:S(2)}, u32[]{:S(2)}) collective-permute-start(f32[1,4,128,128]{3,2,1,0:T(8,128)S(1)} %get-tuple-element.43), channel_id=1, source_target_pairs={{15,1},{1,4},{4,9},{9,13},{13,15},{2,12},{12,8},{8,5},{5,0},{0,2},... | collective-permute-start | bytes 786440 | tf_op jit(solution)/shard_map/ppermute | solution.py:351
  18.0 8.7 %collective-permute-start.6 = (f32[1,4,128,128]{3,2,1,0:T(8,128)S(1)}, f32[1,4,128,128]{3,2,1,0:T(8,128)S(1)}, u32[]{:S(2)}, u32[]{:S(2)}) collective-permute-start(f32[1,4,128,128]{3,2,1,0:T(8,128)S(1)} %get-tuple-element.44), channel_id=1, source_target_pairs={{15,1},{1,4},{4,9},{9,13},{13,15},{2,12},{12,8},{8,5},{5,0},{0,2},... | collective-permute-start | bytes 786440 | tf_op jit(solution)/shard_map/ppermute | solution.py:351
  21.2 5.7 %collective-permute-start.10 = (f32[2,4,128,128]{3,2,1,0:T(8,128)S(1)}, f32[2,4,128,128]{3,2,1,0:T(8,128)S(1)}, u32[]{:S(2)}, u32[]{:S(2)}) collective-permute-start(f32[2,4,128,128]{3,2,1,0:T(8,128)S(1)} %collective-permute-done.5.r3), channel_id=1, source_target_pairs={{1,0},{0,1},{17,16},{16,17},{3,2},{2,3},{19,18},{18,19},{5,4},{4,5... | collective-permute-start | bytes 1572872 | tf_op jit(solution)/shard_map/ppermute | solution.py:351
  24.2 2.6 %collective-permute-start.8 = (f32[1,4,128,128]{3,2,1,0:T(8,128)S(1)}, f32[1,4,128,128]{3,2,1,0:T(8,128)S(1)}, u32[]{:S(2)}, u32[]{:S(2)}) collective-permute-start(f32[1,4,128,128]{3,2,1,0:T(8,128)S(1)} %collective-permute-done.7.r4a), channel_id=1, source_target_pairs={{1,0},{0,1},{17,16},{16,17},{3,2},{2,3},{19,18},{18,19},{5,4},{4,5... | collective-permute-start | bytes 786440 | tf_op jit(solution)/shard_map/ppermute | solution.py:351
  26.8 1.6 %collective-permute-start.9 = (f32[1,4,128,128]{3,2,1,0:T(8,128)S(1)}, f32[1,4,128,128]{3,2,1,0:T(8,128)S(1)}, u32[]{:S(2)}, u32[]{:S(2)}) collective-permute-start(f32[1,4,128,128]{3,2,1,0:T(8,128)S(1)} %collective-permute-done.6.r4b), channel_id=1, source_target_pairs={{1,0},{0,1},{17,16},{16,17},{3,2},{2,3},{19,18},{18,19},{5,4},{4,5... | collective-permute-start | bytes 786440 | tf_op jit(solution)/shard_map/ppermute | solution.py:351

commit v25 on v24

--- a/solution.py
+++ b/solution.py
@@ -120,7 +120,7 @@
             row = plane * slab + first + r
             for w in range(width):
                 code = code_of(first + r, w)
-                col = pl.ds(pl.multiple_of(code % act * edge, edge), edge)
+                col = pl.ds(pl.multiple_of((code & (act - 1)) * edge, edge), edge)
                 block = jnp.where(code < act, piece[r, w], 0.0)
                 block_high, block_low = split(block)
                 at = pl.ds(pl.multiple_of(row * edge, edge), edge)
@@ -139,8 +139,13 @@
 T3, R4, T4, OWN, KEPT = 0, 1, 2, 3, 4
 
 
-def noted_codes(notes, kind, slab, width):
-    return lambda r, w: notes[0, (kind * slab + r) * width + w]
+def packed(values, bits):
+    return functools.reduce(jnp.bitwise_or, [v << (bits * k) for k, v in enumerate(values)])
+
+
+def noted_codes(notes, kind, width):
+    codes = notes[0, kind]
+    return lambda r, w: (codes >> (4 * (r * width + w))) & 15
 
 
 def add_plane(plane, left, high, low, part_ref):
@@ -161,7 +166,7 @@
     def _():
         at = pl.ds(pl.multiple_of((plane * 2 + r) * edge, edge), edge)
         for w in range(width):
-            col = pl.ds(pl.multiple_of(code_of(r, w) % (2 * width) * edge, edge), edge)
+            col = pl.ds(pl.multiple_of((code_of(r, w) & (2 * width - 1)) * edge, edge), edge)
             high[at, col] = jnp.zeros((edge, edge), jnp.bfloat16)
             low[at, col] = jnp.zeros((edge, edge), jnp.bfloat16)
 
@@ -174,7 +179,7 @@
     def _():
         at = pl.ds(pl.multiple_of((plane * 2 + r) * edge, edge), edge)
         codes = [code_of(r, w) for w in range(width)]
-        cols = [pl.ds(pl.multiple_of(code % act * edge, edge), edge) for code in codes]
+        cols = [pl.ds(pl.multiple_of((code & (act - 1)) * edge, edge), edge) for code in codes]
         blocks = [jnp.where(code < act, piece[0, w], 0.0) for w, code in enumerate(codes)]
         block_high, block_low = split(jnp.concatenate(blocks, axis=1))
         more = stacked_dot(left[:, at], block_high, block_low)
@@ -212,17 +217,15 @@
         (far_there, 1 - far_other),
         (place, lane),
     )
+    values = [
+        packed([codes(plane, group)(r, w) for r in range(slab) for w in range(width)], 4)
+        for plane, group in kinds
+    ]
+    values.append(packed([table_ref[place * slab + r, act] for r in range(slab)], act))
     notes = jnp.zeros(notes_ref.shape, jnp.int32)
     index = lax.broadcasted_iota(jnp.int32, notes.shape, 1)
-    for kind, (plane, group) in enumerate(kinds):
-        for r in range(slab):
-            for w in range(width):
-                at = (kind * slab + r) * width + w
-                notes = jnp.where(index == at, codes(plane, group)(r, w), notes)
-    for r in range(slab):
-        notes = jnp.where(
-            index == KEPT * slab * width + r, table_ref[place * slab + r, act], notes
-        )
+    for at, value in enumerate(values):
+        notes = jnp.where(index == at, value, notes)
     notes_ref[...] = notes
 
     store_piece(own_swap, place, codes(place, 1 - lane), high, low, left)
@@ -241,7 +244,7 @@
     place, lane = lax.axis_index("blk"), lax.axis_index("depth")
     here = lookup(tables[-1][0], place, lane)
     width = r4a.shape[1]
-    codes = noted_codes(notes_ref[...], R4, 2, width)
+    codes = noted_codes(notes_ref[...], R4, width)
     store_piece(r4a, here, codes, high, low)
     clear_row(here, 1, codes, width, high, low)
     add_plane(here, left, high, low, part_ref)
@@ -254,13 +257,13 @@
     here, there = [lookup(tables[-1][0], place, c) for c in (lane, 1 - lane)]
     slab, width = t3.shape[:2]
     notes = notes_ref[...]
-    codes = noted_codes(notes, T4, slab, width)
-    store_piece(t3, there, noted_codes(notes, T3, slab, width), high, low)
+    codes = noted_codes(notes, T4, width)
+    store_piece(t3, there, noted_codes(notes, T3, width), high, low)
     store_piece(t4a, there, codes, high, low)
     clear_row(there, 1, codes, width, high, low)
     add_plane(there, left, high, low, part_ref)
     add_row_blocks(
-        r4b, here, 1, noted_codes(notes, R4, slab, width), left, high, low, part_ref
+        r4b, here, 1, noted_codes(notes, R4, width), left, high, low, part_ref
     )
 
 
@@ -274,14 +277,14 @@
     act = 2 * width
     holds = lax.axis_index("panel") == 0
     notes = notes_ref[...]
-    own_codes = noted_codes(notes, OWN, slab, width)
+    own_codes = noted_codes(notes, OWN, width)
     add_row_blocks(
-        t4b, there, 1, noted_codes(notes, T4, slab, width), left, high, low, square
-    )
+        t4b, there, 1, noted_codes(notes, T4, width), left, high, low, square
+    )
+    flags = notes[0, KEPT]
     for r in range(slab):
-        flags = notes[0, KEPT * slab * width + r]
         for c in range(square.shape[1] // edge):
-            kept = (flags >> c) % 2 > 0
+            kept = (flags >> (r * act + c)) & 1 > 0
             col = pl.ds(c * edge, edge)
             block = jnp.where(kept, square[pl.ds(r * edge, edge), col], 0.0)
             block_high, block_low = split(block)
@@ -291,7 +294,7 @@
     for r in range(slab):
         left_parts = square_parts[pl.ds(2 * r * edge, 2 * edge), :]
         codes = [own_codes(r, w) for w in range(width)]
-        cols = [pl.ds(pl.multiple_of(code % act * edge, edge), edge) for code in codes]
+        cols = [pl.ds(pl.multiple_of((code & (act - 1)) * edge, edge), edge) for code in codes]
         cube = stacked_dot(
             left_parts,
             jnp.concatenate([high[:, col] for col in cols], axis=1),
@@ -460,7 +463,7 @@
     slab, width, edge, _ = x_blocks.shape
     rows, slots = columns.shape
     _, chains, panels, lanes = (lax.axis_size(axis) for axis in AXES)
-    full = rows <= slots and rows == lanes * width and width % 2 == 0
+    full = rows <= slots and rows == lanes * width and width in (2, 4)
     if full and rows <= 8 and slab == 2 and edge == 128 and panels >= 2 and lanes == 2 and chains == 4:
         return gather_local(x_blocks, columns)
     return ring_local(x_blocks, columns)

time: 31.7 us -> 31.7 us (level)
  transfers between devices with their start and end apart: 11 -> 11, of which waited for: 5 -> 5; matrix products, arithmetic and copies ran while one was open for 7% -> 8% of each run, Pallas kernels for 17% -> 17%
where the time goes in v25:
time: 31.7 us; the launch traced here: 31.3 us
  starting transfers between devices  13.7 us (43%)
  Pallas kernels  8.33 us (26%)
  waiting for transfers between devices  6.84 us (22%)
  other arithmetic  2.24 us (7%)
    ppermute x10, starting transfers between devices, move(): return lax.ppermute(block, AXES, route)  11.4 us
    ppermute x10, waiting for transfers between devices, move(): return lax.ppermute(block, AXES, route)  3.62 us
    ppermute x1, waiting for transfers between devices, move_only(): return lax.ppermute(block, AXES, route)  3.21 us
    pallas_call x1, Pallas kernels, gather_local(): pl.pallas_call(functools.partial(early_kernel, tables), out_shape=[jax.Sh...  3.09 us
    pallas_call x1, Pallas kernels, gather_local(): pl.pallas_call(functools.partial(late_kernel, tables), out_shape=[jax.Sha...  2.94 us
    pallas_call x2, Pallas kernels, add_to_square(): pl.pallas_call(functools.partial(kernel, tables), out_shape=dense, in_spe...  2.31 us
    ppermute x1, starting transfers between devices, move_only(): return lax.ppermute(block, AXES, route)  2.28 us
    reduce_sum x1, other arithmetic, slot_table(): count = jnp.sum(here.astype(jnp.int32), axis=1, keepdims=True)  0.8 us
  transfers between devices with their start and end apart: 11, of which 5 were waited for; matrix products, arithmetic and copies ran while one was open for 8% of the time, Pallas kernels for 17%

profile of v25, /device:TPU:0, one launch (start us, length us, event | category | flops | bytes accessed | tf_op | source)
XLA Modules:
  0.0 31.3 jit_solution(16932678840997191537)
XLA Ops:
  0.0 2.9 %collective-permute-start = (f32[2,4,128,128]{3,2,1,0:T(8,128)}, f32[2,4,128,128]{3,2,1,0:T(8,128)S(1)}, u32[]{:S(2)}, u32[]{:S(2)}) collective-permute-start(f32[2,4,128,128]{3,2,1,0:T(8,128)} %own_hbm.1), channel_id=1, source_target_pairs={{3,1},{1,4},{4,9},{9,12},{12,8},{8,5},{5,0},{0,2},{2,3},{14,13},{1... | collective-permute-start | bytes 1572872 | tf_op jit(solution)/shard_map/ppermute | solution.py:354
  2.9 0.2 collective-permute-start.1
  3.1 0.8 %fusion.1 = (s32[8]{0:T(128)S(1)}, s32[8,8]{1,0:T(8,128)S(1)}) fusion(s32[8,16]{1,0:T(8,128)} %param.3), kind=kLoop, calls=%fused_computation.7 | loop fusion | flops 184 | bytes 544 | tf_op jit(solution)/shard_map/reduce_sum | solution.py:319
  3.9 0.1 fusion
  4.1 0.2 convert_reduce_fusion
  4.3 0.8 %collective-permute-done.1.own_swap = f32[2,4,128,128]{3,2,1,0:T(8,128)S(1)} collective-permute-done((f32[2,4,128,128]{3,2,1,0:T(8,128)}, f32[2,4,128,128]{3,2,1,0:T(8,128)S(1)}, u32[]{:S(2)}, u32[]{:S(2)}) %collective-permute-start.1) | collective-permute-done | bytes 524320 | tf_op jit(solution)/shard_map/ppermute | solution.py:354
  5.1 2.3 %collective-permute-start.2 = (f32[2,4,128,128]{3,2,1,0:T(8,128)S(1)}, f32[2,4,128,128]{3,2,1,0:T(8,128)S(1)}, u32[]{:S(2)}, u32[]{:S(2)}) collective-permute-start(f32[2,4,128,128]{3,2,1,0:T(8,128)S(1)} %collective-permute-done.1.own_swap), channel_id=1, source_target_pairs={{1,4},{4,9},{9,13},{13,15},{12,8},{8,5},{5,0},{0,2},{17,20},{20,25... | collective-permute-start | bytes 1572872 | tf_op jit(solution)/shard_map/ppermute | solution.py:362
  7.3 0.1 add_select_fusion
  7.5 0.1 copy.13
  7.5 0.2 select_reduce_fusion
  7.8 0.7 %compare_select_fusion = s32[8,8]{1,0:T(8,128)S(1)} fusion(s32[8,8]{1,0:T(8,128)S(1)} %select_reduce_fusion, s32[8,16]{1,0:T(8,128)} %param.3), kind=kLoop, calls=%fused_computation.5 | loop fusion | flops 192 | bytes 768 | tf_op jit(solution)/shard_map/jit(_where)/select_n | solution.py:327
  8.5 0.1 pad_add_fusion.table_ref
  8.5 1.4 %collective-permute-done.r1 = f32[2,4,128,128]{3,2,1,0:T(8,128)S(1)} collective-permute-done((f32[2,4,128,128]{3,2,1,0:T(8,128)}, f32[2,4,128,128]{3,2,1,0:T(8,128)S(1)}, u32[]{:S(2)}, u32[]{:S(2)}) %collective-permute-start) | collective-permute-done | bytes 524320 | tf_op jit(solution)/shard_map/ppermute | solution.py:354
  10.0 2.4 %collective-permute-start.5 = (f32[2,4,128,128]{3,2,1,0:T(8,128)S(1)}, f32[2,4,128,128]{3,2,1,0:T(8,128)S(1)}, u32[]{:S(2)}, u32[]{:S(2)}) collective-permute-start(f32[2,4,128,128]{3,2,1,0:T(8,128)S(1)} %collective-permute-done.r1), channel_id=1, source_target_pairs={{15,1},{1,4},{4,9},{9,13},{13,15},{2,12},{12,8},{8,5},{5,0},{0,2},... | collective-permute-start | bytes 1572872 | tf_op jit(solution)/shard_map/ppermute | solution.py:354
  12.3 0.0 collective-permute-start.3
  12.3 3.2 %collective-permute-done.2.r2 = f32[2,4,128,128]{3,2,1,0:T(8,128)S(1)} collective-permute-done((f32[2,4,128,128]{3,2,1,0:T(8,128)S(1)}, f32[2,4,128,128]{3,2,1,0:T(8,128)S(1)}, u32[]{:S(2)}, u32[]{:S(2)}) %collective-permute-start.2) | collective-permute-done | bytes 524320 | tf_op jit(solution)/shard_map/ppermute | solution.py:362
  15.6 0.0 collective-permute-start.4
  15.6 2.5 %collective-permute-start.7 = (f32[1,4,128,128]{3,2,1,0:T(8,128)S(1)}, f32[1,4,128,128]{3,2,1,0:T(8,128)S(1)}, u32[]{:S(2)}, u32[]{:S(2)}) collective-permute-start(f32[1,4,128,128]{3,2,1,0:T(8,128)S(1)} %get-tuple-element.43), channel_id=1, source_target_pairs={{15,1},{1,4},{4,9},{9,13},{13,15},{2,12},{12,8},{8,5},{5,0},{0,2},... | collective-permute-start | bytes 786440 | tf_op jit(solution)/shard_map/ppermute | solution.py:354
  18.0 2.8 %collective-permute-start.6 = (f32[1,4,128,128]{3,2,1,0:T(8,128)S(1)}, f32[1,4,128,128]{3,2,1,0:T(8,128)S(1)}, u32[]{:S(2)}, u32[]{:S(2)}) collective-permute-start(f32[1,4,128,128]{3,2,1,0:T(8,128)S(1)} %get-tuple-element.44), channel_id=1, source_target_pairs={{15,1},{1,4},{4,9},{9,13},{13,15},{2,12},{12,8},{8,5},{5,0},{0,2},... | collective-permute-start | bytes 786440 | tf_op jit(solution)/shard_map/ppermute | solution.py:354
  20.9 0.3 collective-permute-done.5.r3
  21.2 0.0 collective-permute-start.10
  21.2 0.0 collective-permute-done.3.t1
  21.2 0.0 collective-permute-done.4.t2
  21.2 3.1 %early.1 = (bf16[1024,1024]{1,0:T(8,128)(2,1)S(1)}, bf16[1024,1024]{1,0:T(8,128)(2,1)S(1)}, bf16[512,1024]{1,0:T(8,128)(2,1)S(1)}, f32[256,1024]{1,0:T(8,128)S(1)}, s32[8,128]{1,0:T(8,128)S(1)}) custom-call(s32[8,9]{1,0:T(8,128)S(1)} %pad_add_fusion.table_ref, f32[2,4,128,128]{3,2,1,0:T(8,128)} %own_hbm.1, ...), custom_call_target="tpu_custom_call" | custom-call | tf_op jit(solution)/shard_map/early/pallas_call | solution.py:409
  24.3 0.0 collective-permute-done.7.r4a
  24.3 0.6 %collective-permute-start.8 = (f32[1,4,128,128]{3,2,1,0:T(8,128)S(1)}, f32[1,4,128,128]{3,2,1,0:T(8,128)S(1)}, u32[]{:S(2)}, u32[]{:S(2)}) collective-permute-start(f32[1,4,128,128]{3,2,1,0:T(8,128)S(1)} %collective-permute-done.7.r4a), channel_id=1, source_target_pairs={{1,0},{0,1},{17,16},{16,17},{3,2},{2,3},{19,18},{18,19},{5,4},{4,5... | collective-permute-start | bytes 786440 | tf_op jit(solution)/shard_map/ppermute | solution.py:354
  24.8 0.8 %waiting.1 = (bf16[1024,1024]{1,0:T(8,128)(2,1)S(1)}, bf16[1024,1024]{1,0:T(8,128)(2,1)S(1)}, f32[256,1024]{1,0:T(8,128)S(1)}) custom-call(s32[8,128]{1,0:T(8,128)S(1)} %get-tuple-element.26.notes_ref, f32[1,4,128,128]{3,2,1,0:T(8,128)S(1)} %collective-permute-done.7.r4a, ...), custom_call_target="tpu_custom_call", output_to_operand_aliasing={{0}: (2, {}), {1}: (3, {}), {2}: (5, {})} | custom-call | tf_op jit(solution)/shard_map/waiting/pallas_call | solution.py:431
  25.7 1.1 %collective-permute-done.6.r4b = f32[1,4,128,128]{3,2,1,0:T(8,128)S(1)} collective-permute-done((f32[1,4,128,128]{3,2,1,0:T(8,128)S(1)}, f32[1,4,128,128]{3,2,1,0:T(8,128)S(1)}, u32[]{:S(2)}, u32[]{:S(2)}) %collective-permute-start.6) | collective-permute-done | bytes 262176 | tf_op jit(solution)/shard_map/ppermute | solution.py:354
  26.8 0.1 collective-permute-start.9
  26.9 0.0 collective-permute-done.10.t3
  26.9 1.5 %middle.1 = (bf16[1024,1024]{1,0:T(8,128)(2,1)S(1)}, bf16[1024,1024]{1,0:T(8,128)(2,1)S(1)}, f32[256,1024]{1,0:T(8,128)S(1)}) custom-call(s32[8,128]{1,0:T(8,128)S(1)} %get-tuple-element.26.notes_ref, f32[1,4,128,128]{3,2,1,0:T(8,128)S(1)} %collective-permute-done.6.r4b, ...), custom_call_target="tpu_custom_call", output_to_operand_aliasing={{0}: (4, {}), {1}: (5, {}), {2}: (7, {})} | custom-call | tf_op jit(solution)/shard_map/middle/pallas_call | solution.py:431
  28.4 2.9 %late.1 = (f32[2,4,128,128]{3,2,1,0:T(8,128)}, bf16[1024,1024]{1,0:T(8,128)(2,1)S(1)}, bf16[1024,1024]{1,0:T(8,128)(2,1)S(1)}, f32[256,1024]{1,0:T(8,128)S(1)}) custom-call(s32[8,128]{1,0:T(8,128)S(1)} %get-tuple-element.26.notes_ref, f32[1,4,128,128]{3,2,1,0:T(8,128)S(1)} %collective-permute-done.9.t4b, ...), custom_call_target="tpu_custom_call", output_to_operand_aliasing={{1}: (2, {}), {2}: (3, {}), {3}: (5, {})} | custom-call | tf_op jit(solution)/shard_map/late/pallas_call | solution.py:445
  (6 shorter events, 0.1 us)
Async XLA Ops:
  0.0 10.0 %collective-permute-start = (f32[2,4,128,128]{3,2,1,0:T(8,128)}, f32[2,4,128,128]{3,2,1,0:T(8,128)S(1)}, u32[]{:S(2)}, u32[]{:S(2)}) collective-permute-start(f32[2,4,128,128]{3,2,1,0:T(8,128)} %own_hbm.1), channel_id=1, source_target_pairs={{3,1},{1,4},{4,9},{9,12},{12,8},{8,5},{5,0},{0,2},{2,3},{14,13},{1... | collective-permute-start | bytes 1572872 | tf_op jit(solution)/shard_map/ppermute | solution.py:354
  2.9 2.1 %collective-permute-start.1 = (f32[2,4,128,128]{3,2,1,0:T(8,128)}, f32[2,4,128,128]{3,2,1,0:T(8,128)S(1)}, u32[]{:S(2)}, u32[]{:S(2)}) collective-permute-start(f32[2,4,128,128]{3,2,1,0:T(8,128)} %own_hbm.1), channel_id=1, source_target_pairs={{1,0},{0,1},{17,16},{16,17},{3,2},{2,3},{19,18},{18,19},{5,4},{4,5... | collective-permute-start | bytes 1572872 | tf_op jit(solution)/shard_map/ppermute | solution.py:354
  5.1 10.5 %collective-permute-start.2 = (f32[2,4,128,128]{3,2,1,0:T(8,128)S(1)}, f32[2,4,128,128]{3,2,1,0:T(8,128)S(1)}, u32[]{:S(2)}, u32[]{:S(2)}) collective-permute-start(f32[2,4,128,128]{3,2,1,0:T(8,128)S(1)} %collective-permute-done.1.own_swap), channel_id=1, source_target_pairs={{1,4},{4,9},{9,13},{13,15},{12,8},{8,5},{5,0},{0,2},{17,20},{20,25... | collective-permute-start | bytes 1572872 | tf_op jit(solution)/shard_map/ppermute | solution.py:362
  10.0 11.2 %collective-permute-start.5 = (f32[2,4,128,128]{3,2,1,0:T(8,128)S(1)}, f32[2,4,128,128]{3,2,1,0:T(8,128)S(1)}, u32[]{:S(2)}, u32[]{:S(2)}) collective-permute-start(f32[2,4,128,128]{3,2,1,0:T(8,128)S(1)} %collective-permute-done.r1), channel_id=1, source_target_pairs={{15,1},{1,4},{4,9},{9,13},{13,15},{2,12},{12,8},{8,5},{5,0},{0,2},... | collective-permute-start | bytes 1572872 | tf_op jit(solution)/shard_map/ppermute | solution.py:354
  12.3 8.8 %collective-permute-start.3 = (f32[2,4,128,128]{3,2,1,0:T(8,128)S(1)}, f32[2,4,128,128]{3,2,1,0:T(8,128)S(1)}, u32[]{:S(2)}, u32[]{:S(2)}) collective-permute-start(f32[2,4,128,128]{3,2,1,0:T(8,128)S(1)} %collective-permute-done.r1), channel_id=1, source_target_pairs={{1,0},{0,1},{17,16},{16,17},{3,2},{2,3},{19,18},{18,19},{5,4},{4,5... | collective-permute-start | bytes 1572872 | tf_op jit(solution)/shard_map/ppermute | solution.py:354
  15.6 5.6 %collective-permute-start.4 = (f32[2,4,128,128]{3,2,1,0:T(8,128)S(1)}, f32[2,4,128,128]{3,2,1,0:T(8,128)S(1)}, u32[]{:S(2)}, u32[]{:S(2)}) collective-permute-start(f32[2,4,128,128]{3,2,1,0:T(8,128)S(1)} %collective-permute-done.2.r2), channel_id=1, source_target_pairs={{1,0},{0,1},{17,16},{16,17},{3,2},{2,3},{19,18},{18,19},{5,4},{4,5... | collective-permute-start | bytes 1572872 | tf_op jit(solution)/shard_map/ppermute | solution.py:354
  15.6 8.7 %collective-permute-start.7 = (f32[1,4,128,128]{3,2,1,0:T(8,128)S(1)}, f32[1,4,128,128]{3,2,1,0:T(8,128)S(1)}, u32[]{:S(2)}, u32[]{:S(2)}) collective-permute-start(f32[1,4,128,128]{3,2,1,0:T(8,128)S(1)} %get-tuple-element.43), channel_id=1, source_target_pairs={{15,1},{1,4},{4,9},{9,13},{13,15},{2,12},{12,8},{8,5},{5,0},{0,2},... | collective-permute-start | bytes 786440 | tf_op jit(solution)/shard_map/ppermute | solution.py:354
  18.0 8.7 %collective-permute-start.6 = (f32[1,4,128,128]{3,2,1,0:T(8,128)S(1)}, f32[1,4,128,128]{3,2,1,0:T(8,128)S(1)}, u32[]{:S(2)}, u32[]{:S(2)}) collective-permute-start(f32[1,4,128,128]{3,2,1,0:T(8,128)S(1)} %get-tuple-element.44), channel_id=1, source_target_pairs={{15,1},{1,4},{4,9},{9,13},{13,15},{2,12},{12,8},{8,5},{5,0},{0,2},... | collective-permute-start | bytes 786440 | tf_op jit(solution)/shard_map/ppermute | solution.py:354
  21.2 5.7 %collective-permute-start.10 = (f32[2,4,128,128]{3,2,1,0:T(8,128)S(1)}, f32[2,4,128,128]{3,2,1,0:T(8,128)S(1)}, u32[]{:S(2)}, u32[]{:S(2)}) collective-permute-start(f32[2,4,128,128]{3,2,1,0:T(8,128)S(1)} %collective-permute-done.5.r3), channel_id=1, source_target_pairs={{1,0},{0,1},{17,16},{16,17},{3,2},{2,3},{19,18},{18,19},{5,4},{4,5... | collective-permute-start | bytes 1572872 | tf_op jit(solution)/shard_map/ppermute | solution.py:354
  24.3 2.5 %collective-permute-start.8 = (f32[1,4,128,128]{3,2,1,0:T(8,128)S(1)}, f32[1,4,128,128]{3,2,1,0:T(8,128)S(1)}, u32[]{:S(2)}, u32[]{:S(2)}) collective-permute-start(f32[1,4,128,128]{3,2,1,0:T(8,128)S(1)} %collective-permute-done.7.r4a), channel_id=1, source_target_pairs={{1,0},{0,1},{17,16},{16,17},{3,2},{2,3},{19,18},{18,19},{5,4},{4,5... | collective-permute-start | bytes 786440 | tf_op jit(solution)/shard_map/ppermute | solution.py:354
  26.8 1.6 %collective-permute-start.9 = (f32[1,4,128,128]{3,2,1,0:T(8,128)S(1)}, f32[1,4,128,128]{3,2,1,0:T(8,128)S(1)}, u32[]{:S(2)}, u32[]{:S(2)}) collective-permute-start(f32[1,4,128,128]{3,2,1,0:T(8,128)S(1)} %collective-permute-done.6.r4b), channel_id=1, source_target_pairs={{1,0},{0,1},{17,16},{16,17},{3,2},{2,3},{19,18},{18,19},{5,4},{4,5... | collective-permute-start | bytes 786440 | tf_op jit(solution)/shard_map/ppermute | solution.py:354

commit v26 on v25

--- a/solution.py
+++ b/solution.py
@@ -171,23 +171,23 @@
             low[at, col] = jnp.zeros((edge, edge), jnp.bfloat16)
 
 
-def add_row_blocks(piece, plane, r, code_of, left, high, low, part_ref):
+def last_row_blocks(piece, plane, r, code_of, left, high, low):
     _, width, edge, _ = piece.shape
     act = 2 * width
-
-    @pl.when(plane >= 0)
-    def _():
-        at = pl.ds(pl.multiple_of((plane * 2 + r) * edge, edge), edge)
-        codes = [code_of(r, w) for w in range(width)]
-        cols = [pl.ds(pl.multiple_of((code & (act - 1)) * edge, edge), edge) for code in codes]
-        blocks = [jnp.where(code < act, piece[0, w], 0.0) for w, code in enumerate(codes)]
-        block_high, block_low = split(jnp.concatenate(blocks, axis=1))
-        more = stacked_dot(left[:, at], block_high, block_low)
-        sums = [part_ref[:, col] + more[:, w * edge : (w + 1) * edge] for w, col in enumerate(cols)]
-        for w, col in enumerate(cols):
-            part_ref[:, col] = sums[w]
-            high[at, col] = block_high[:, w * edge : (w + 1) * edge]
-            low[at, col] = block_low[:, w * edge : (w + 1) * edge]
+    valid = plane >= 0
+    at = pl.ds(pl.multiple_of((jnp.maximum(plane, 0) * 2 + r) * edge, edge), edge)
+    codes = [code_of(r, w) for w in range(width)]
+    cols = [pl.ds(pl.multiple_of((code & (act - 1)) * edge, edge), edge) for code in codes]
+    blocks = [
+        jnp.where(valid & (code < act), piece[0, w], 0.0) for w, code in enumerate(codes)
+    ]
+    block_high, block_low = split(jnp.concatenate(blocks, axis=1))
+    more = stacked_dot(left[:, at], block_high, block_low)
+    for w, col in enumerate(cols):
+        part = slice(w * edge, (w + 1) * edge)
+        high[at, col] = jnp.where(valid, block_high[:, part], high[at, col])
+        low[at, col] = jnp.where(valid, block_low[:, part], low[at, col])
+    return codes, cols, more
 
 
 def early_kernel(
@@ -261,10 +261,17 @@
     store_piece(t3, there, noted_codes(notes, T3, width), high, low)
     store_piece(t4a, there, codes, high, low)
     clear_row(there, 1, codes, width, high, low)
-    add_plane(there, left, high, low, part_ref)
-    add_row_blocks(
-        r4b, here, 1, noted_codes(notes, R4, width), left, high, low, part_ref
-    )
+    edge, depth, tile = high.shape[0] // (2 * width), part_ref.shape[0], 512
+    _, cols, more = last_row_blocks(
+        r4b, here, 1, noted_codes(notes, R4, width), left, high, low
+    )
+    rows = pl.ds(pl.multiple_of(jnp.maximum(there, 0) * depth, depth), depth)
+    for n in range(part_ref.shape[1] // tile):
+        wide = pl.ds(n * tile, tile)
+        plane = stacked_dot(left[:, rows], high[rows, wide], low[rows, wide])
+        part_ref[:, wide] += jnp.where(there >= 0, plane, 0.0)
+    for w, col in enumerate(cols):
+        part_ref[:, col] += more[:, w * edge : (w + 1) * edge]
 
 
 def late_kernel(
@@ -278,18 +285,26 @@
     holds = lax.axis_index("panel") == 0
     notes = notes_ref[...]
     own_codes = noted_codes(notes, OWN, width)
-    add_row_blocks(
-        t4b, there, 1, noted_codes(notes, T4, width), left, high, low, square
+    codes, changed, more = last_row_blocks(
+        t4b, there, 1, noted_codes(notes, T4, width), left, high, low
     )
     flags = notes[0, KEPT]
+
+    def keep(r, c, col, block):
+        kept = (flags >> (r * act + c)) & 1 > 0
+        block_high, block_low = split(jnp.where(kept, block, 0.0))
+        square_parts[pl.ds(2 * r * edge, edge), col] = block_high
+        square_parts[pl.ds((2 * r + 1) * edge, edge), col] = block_low
+
     for r in range(slab):
         for c in range(square.shape[1] // edge):
-            kept = (flags >> (r * act + c)) & 1 > 0
             col = pl.ds(c * edge, edge)
-            block = jnp.where(kept, square[pl.ds(r * edge, edge), col], 0.0)
-            block_high, block_low = split(block)
-            square_parts[pl.ds(2 * r * edge, edge), col] = block_high
-            square_parts[pl.ds((2 * r + 1) * edge, edge), col] = block_low
+            keep(r, c, col, square[pl.ds(r * edge, edge), col])
+    sums = [square[:, col] + more[:, w * edge : (w + 1) * edge] for w, col in enumerate(changed)]
+    for code, col, total in zip(codes, changed, sums):
+        square[:, col] = total
+        for r in range(slab):
+            keep(r, code & (act - 1), col, total[r * edge : (r + 1) * edge])
     copies = []
     for r in range(slab):
         left_parts = square_parts[pl.ds(2 * r * edge, 2 * edge), :]

time: 31.7 us -> 31.8 us (level)
  transfers between devices with their start and end apart: 11 -> 11, of which waited for: 5 -> 5; matrix products, arithmetic and copies ran while one was open for 8% -> 7% of each run, Pallas kernels for 17% -> 17%
where the time goes in v26:
time: 31.8 us; the launch traced here: 31.4 us
  starting transfers between devices  13.7 us (43%)
  Pallas kernels  8.44 us (27%)
  waiting for transfers between devices  6.82 us (21%)
  other arithmetic  2.24 us (7%)
    ppermute x10, starting transfers between devices, move(): return lax.ppermute(block, AXES, route)  11.5 us
    ppermute x10, waiting for transfers between devices, move(): return lax.ppermute(block, AXES, route)  3.61 us
    ppermute x1, waiting for transfers between devices, move_only(): return lax.ppermute(block, AXES, route)  3.21 us
    pallas_call x1, Pallas kernels, gather_local(): pl.pallas_call(functools.partial(early_kernel, tables), out_shape=[jax.Sh...  3.09 us
    pallas_call x1, Pallas kernels, gather_local(): pl.pallas_call(functools.partial(late_kernel, tables), out_shape=[jax.Sha...  3.01 us
    pallas_call x2, Pallas kernels, add_to_square(): pl.pallas_call(functools.partial(kernel, tables), out_shape=dense, in_spe...  2.34 us
    ppermute x1, starting transfers between devices, move_only(): return lax.ppermute(block, AXES, route)  2.28 us
    reduce_sum x1, other arithmetic, slot_table(): count = jnp.sum(here.astype(jnp.int32), axis=1, keepdims=True)  0.8 us
  transfers between devices with their start and end apart: 11, of which 5 were waited for; matrix products, arithmetic and copies ran while one was open for 7% of the time, Pallas kernels for 17%

profile of v26, /device:TPU:0, one launch (start us, length us, event | category | flops | bytes accessed | tf_op | source)
XLA Modules:
  0.0 31.4 jit_solution(4237856913189819408)
XLA Ops:
  0.0 2.9 %collective-permute-start = (f32[2,4,128,128]{3,2,1,0:T(8,128)}, f32[2,4,128,128]{3,2,1,0:T(8,128)S(1)}, u32[]{:S(2)}, u32[]{:S(2)}) collective-permute-start(f32[2,4,128,128]{3,2,1,0:T(8,128)} %own_hbm.1), channel_id=1, source_target_pairs={{3,1},{1,4},{4,9},{9,12},{12,8},{8,5},{5,0},{0,2},{2,3},{14,13},{1... | collective-permute-start | bytes 1572872 | tf_op jit(solution)/shard_map/ppermute | solution.py:369
  2.9 0.2 collective-permute-start.1
  3.1 0.8 %fusion.1 = (s32[8]{0:T(128)S(1)}, s32[8,8]{1,0:T(8,128)S(1)}) fusion(s32[8,16]{1,0:T(8,128)} %param.3), kind=kLoop, calls=%fused_computation.7 | loop fusion | flops 184 | bytes 544 | tf_op jit(solution)/shard_map/reduce_sum | solution.py:334
  3.9 0.1 fusion
  4.1 0.2 convert_reduce_fusion
  4.3 0.8 %collective-permute-done.1.own_swap = f32[2,4,128,128]{3,2,1,0:T(8,128)S(1)} collective-permute-done((f32[2,4,128,128]{3,2,1,0:T(8,128)}, f32[2,4,128,128]{3,2,1,0:T(8,128)S(1)}, u32[]{:S(2)}, u32[]{:S(2)}) %collective-permute-start.1) | collective-permute-done | bytes 524320 | tf_op jit(solution)/shard_map/ppermute | solution.py:369
  5.1 2.3 %collective-permute-start.2 = (f32[2,4,128,128]{3,2,1,0:T(8,128)S(1)}, f32[2,4,128,128]{3,2,1,0:T(8,128)S(1)}, u32[]{:S(2)}, u32[]{:S(2)}) collective-permute-start(f32[2,4,128,128]{3,2,1,0:T(8,128)S(1)} %collective-permute-done.1.own_swap), channel_id=1, source_target_pairs={{1,4},{4,9},{9,13},{13,15},{12,8},{8,5},{5,0},{0,2},{17,20},{20,25... | collective-permute-start | bytes 1572872 | tf_op jit(solution)/shard_map/ppermute | solution.py:377
  7.3 0.1 add_select_fusion
  7.5 0.1 copy.13
  7.5 0.2 select_reduce_fusion
  7.8 0.7 %compare_select_fusion = s32[8,8]{1,0:T(8,128)S(1)} fusion(s32[8,8]{1,0:T(8,128)S(1)} %select_reduce_fusion, s32[8,16]{1,0:T(8,128)} %param.3), kind=kLoop, calls=%fused_computation.5 | loop fusion | flops 192 | bytes 768 | tf_op jit(solution)/shard_map/jit(_where)/select_n | solution.py:342
  8.5 0.1 pad_add_fusion.table_ref
  8.5 1.4 %collective-permute-done.r1 = f32[2,4,128,128]{3,2,1,0:T(8,128)S(1)} collective-permute-done((f32[2,4,128,128]{3,2,1,0:T(8,128)}, f32[2,4,128,128]{3,2,1,0:T(8,128)S(1)}, u32[]{:S(2)}, u32[]{:S(2)}) %collective-permute-start) | collective-permute-done | bytes 524320 | tf_op jit(solution)/shard_map/ppermute | solution.py:369
  10.0 2.4 %collective-permute-start.5 = (f32[2,4,128,128]{3,2,1,0:T(8,128)S(1)}, f32[2,4,128,128]{3,2,1,0:T(8,128)S(1)}, u32[]{:S(2)}, u32[]{:S(2)}) collective-permute-start(f32[2,4,128,128]{3,2,1,0:T(8,128)S(1)} %collective-permute-done.r1), channel_id=1, source_target_pairs={{15,1},{1,4},{4,9},{9,13},{13,15},{2,12},{12,8},{8,5},{5,0},{0,2},... | collective-permute-start | bytes 1572872 | tf_op jit(solution)/shard_map/ppermute | solution.py:369
  12.3 0.0 collective-permute-start.3
  12.3 3.2 %collective-permute-done.2.r2 = f32[2,4,128,128]{3,2,1,0:T(8,128)S(1)} collective-permute-done((f32[2,4,128,128]{3,2,1,0:T(8,128)S(1)}, f32[2,4,128,128]{3,2,1,0:T(8,128)S(1)}, u32[]{:S(2)}, u32[]{:S(2)}) %collective-permute-start.2) | collective-permute-done | bytes 524320 | tf_op jit(solution)/shard_map/ppermute | solution.py:377
  15.6 0.0 collective-permute-start.4
  15.6 2.5 %collective-permute-start.7 = (f32[1,4,128,128]{3,2,1,0:T(8,128)S(1)}, f32[1,4,128,128]{3,2,1,0:T(8,128)S(1)}, u32[]{:S(2)}, u32[]{:S(2)}) collective-permute-start(f32[1,4,128,128]{3,2,1,0:T(8,128)S(1)} %get-tuple-element.43), channel_id=1, source_target_pairs={{15,1},{1,4},{4,9},{9,13},{13,15},{2,12},{12,8},{8,5},{5,0},{0,2},... | collective-permute-start | bytes 786440 | tf_op jit(solution)/shard_map/ppermute | solution.py:369
  18.0 2.8 %collective-permute-start.6 = (f32[1,4,128,128]{3,2,1,0:T(8,128)S(1)}, f32[1,4,128,128]{3,2,1,0:T(8,128)S(1)}, u32[]{:S(2)}, u32[]{:S(2)}) collective-permute-start(f32[1,4,128,128]{3,2,1,0:T(8,128)S(1)} %get-tuple-element.44), channel_id=1, source_target_pairs={{15,1},{1,4},{4,9},{9,13},{13,15},{2,12},{12,8},{8,5},{5,0},{0,2},... | collective-permute-start | bytes 786440 | tf_op jit(solution)/shard_map/ppermute | solution.py:369
  20.9 0.3 collective-permute-done.5.r3
  21.2 0.0 collective-permute-start.10
  21.2 0.0 collective-permute-done.3.t1
  21.2 0.0 collective-permute-done.4.t2
  21.2 3.1 %early.1 = (bf16[1024,1024]{1,0:T(8,128)(2,1)S(1)}, bf16[1024,1024]{1,0:T(8,128)(2,1)S(1)}, bf16[512,1024]{1,0:T(8,128)(2,1)S(1)}, f32[256,1024]{1,0:T(8,128)S(1)}, s32[8,128]{1,0:T(8,128)S(1)}) custom-call(s32[8,9]{1,0:T(8,128)S(1)} %pad_add_fusion.table_ref, f32[2,4,128,128]{3,2,1,0:T(8,128)} %own_hbm.1, ...), custom_call_target="tpu_custom_call" | custom-call | tf_op jit(solution)/shard_map/early/pallas_call | solution.py:424
  24.3 0.6 %collective-permute-start.8 = (f32[1,4,128,128]{3,2,1,0:T(8,128)S(1)}, f32[1,4,128,128]{3,2,1,0:T(8,128)S(1)}, u32[]{:S(2)}, u32[]{:S(2)}) collective-permute-start(f32[1,4,128,128]{3,2,1,0:T(8,128)S(1)} %collective-permute-done.7.r4a), channel_id=1, source_target_pairs={{1,0},{0,1},{17,16},{16,17},{3,2},{2,3},{19,18},{18,19},{5,4},{4,5... | collective-permute-start | bytes 786440 | tf_op jit(solution)/shard_map/ppermute | solution.py:369
  24.9 0.8 %waiting.1 = (bf16[1024,1024]{1,0:T(8,128)(2,1)S(1)}, bf16[1024,1024]{1,0:T(8,128)(2,1)S(1)}, f32[256,1024]{1,0:T(8,128)S(1)}) custom-call(s32[8,128]{1,0:T(8,128)S(1)} %get-tuple-element.26.notes_ref, f32[1,4,128,128]{3,2,1,0:T(8,128)S(1)} %collective-permute-done.7.r4a, ...), custom_call_target="tpu_custom_call", output_to_operand_aliasing={{0}: (2, {}), {1}: (3, {}), {2}: (5, {})} | custom-call | tf_op jit(solution)/shard_map/waiting/pallas_call | solution.py:446
  25.7 1.1 %collective-permute-done.6.r4b = f32[1,4,128,128]{3,2,1,0:T(8,128)S(1)} collective-permute-done((f32[1,4,128,128]{3,2,1,0:T(8,128)S(1)}, f32[1,4,128,128]{3,2,1,0:T(8,128)S(1)}, u32[]{:S(2)}, u32[]{:S(2)}) %collective-permute-start.6) | collective-permute-done | bytes 262176 | tf_op jit(solution)/shard_map/ppermute | solution.py:369
  26.8 0.1 collective-permute-start.9
  26.9 0.0 collective-permute-done.10.t3
  26.9 1.5 %middle.1 = (bf16[1024,1024]{1,0:T(8,128)(2,1)S(1)}, bf16[1024,1024]{1,0:T(8,128)(2,1)S(1)}, f32[256,1024]{1,0:T(8,128)S(1)}) custom-call(s32[8,128]{1,0:T(8,128)S(1)} %get-tuple-element.26.notes_ref, f32[1,4,128,128]{3,2,1,0:T(8,128)S(1)} %collective-permute-done.6.r4b, ...), custom_call_target="tpu_custom_call", output_to_operand_aliasing={{0}: (4, {}), {1}: (5, {}), {2}: (7, {})} | custom-call | tf_op jit(solution)/shard_map/middle/pallas_call | solution.py:446
  28.4 0.0 collective-permute-done.9.t4b
  28.4 3.0 %late.1 = (f32[2,4,128,128]{3,2,1,0:T(8,128)}, bf16[1024,1024]{1,0:T(8,128)(2,1)S(1)}, bf16[1024,1024]{1,0:T(8,128)(2,1)S(1)}, f32[256,1024]{1,0:T(8,128)S(1)}) custom-call(s32[8,128]{1,0:T(8,128)S(1)} %get-tuple-element.26.notes_ref, f32[1,4,128,128]{3,2,1,0:T(8,128)S(1)} %collective-permute-done.9.t4b, ...), custom_call_target="tpu_custom_call", output_to_operand_aliasing={{1}: (2, {}), {2}: (3, {}), {3}: (5, {})} | custom-call | tf_op jit(solution)/shard_map/late/pallas_call | solution.py:460
  (6 shorter events, 0.1 us)
Async XLA Ops:
  0.0 10.0 %collective-permute-start = (f32[2,4,128,128]{3,2,1,0:T(8,128)}, f32[2,4,128,128]{3,2,1,0:T(8,128)S(1)}, u32[]{:S(2)}, u32[]{:S(2)}) collective-permute-start(f32[2,4,128,128]{3,2,1,0:T(8,128)} %own_hbm.1), channel_id=1, source_target_pairs={{3,1},{1,4},{4,9},{9,12},{12,8},{8,5},{5,0},{0,2},{2,3},{14,13},{1... | collective-permute-start | bytes 1572872 | tf_op jit(solution)/shard_map/ppermute | solution.py:369
  2.9 2.1 %collective-permute-start.1 = (f32[2,4,128,128]{3,2,1,0:T(8,128)}, f32[2,4,128,128]{3,2,1,0:T(8,128)S(1)}, u32[]{:S(2)}, u32[]{:S(2)}) collective-permute-start(f32[2,4,128,128]{3,2,1,0:T(8,128)} %own_hbm.1), channel_id=1, source_target_pairs={{1,0},{0,1},{17,16},{16,17},{3,2},{2,3},{19,18},{18,19},{5,4},{4,5... | collective-permute-start | bytes 1572872 | tf_op jit(solution)/shard_map/ppermute | solution.py:369
  5.1 10.5 %collective-permute-start.2 = (f32[2,4,128,128]{3,2,1,0:T(8,128)S(1)}, f32[2,4,128,128]{3,2,1,0:T(8,128)S(1)}, u32[]{:S(2)}, u32[]{:S(2)}) collective-permute-start(f32[2,4,128,128]{3,2,1,0:T(8,128)S(1)} %collective-permute-done.1.own_swap), channel_id=1, source_target_pairs={{1,4},{4,9},{9,13},{13,15},{12,8},{8,5},{5,0},{0,2},{17,20},{20,25... | collective-permute-start | bytes 1572872 | tf_op jit(solution)/shard_map/ppermute | solution.py:377
  10.0 11.2 %collective-permute-start.5 = (f32[2,4,128,128]{3,2,1,0:T(8,128)S(1)}, f32[2,4,128,128]{3,2,1,0:T(8,128)S(1)}, u32[]{:S(2)}, u32[]{:S(2)}) collective-permute-start(f32[2,4,128,128]{3,2,1,0:T(8,128)S(1)} %collective-permute-done.r1), channel_id=1, source_target_pairs={{15,1},{1,4},{4,9},{9,13},{13,15},{2,12},{12,8},{8,5},{5,0},{0,2},... | collective-permute-start | bytes 1572872 | tf_op jit(solution)/shard_map/ppermute | solution.py:369
  12.3 8.8 %collective-permute-start.3 = (f32[2,4,128,128]{3,2,1,0:T(8,128)S(1)}, f32[2,4,128,128]{3,2,1,0:T(8,128)S(1)}, u32[]{:S(2)}, u32[]{:S(2)}) collective-permute-start(f32[2,4,128,128]{3,2,1,0:T(8,128)S(1)} %collective-permute-done.r1), channel_id=1, source_target_pairs={{1,0},{0,1},{17,16},{16,17},{3,2},{2,3},{19,18},{18,19},{5,4},{4,5... | collective-permute-start | bytes 1572872 | tf_op jit(solution)/shard_map/ppermute | solution.py:369
  15.6 5.6 %collective-permute-start.4 = (f32[2,4,128,128]{3,2,1,0:T(8,128)S(1)}, f32[2,4,128,128]{3,2,1,0:T(8,128)S(1)}, u32[]{:S(2)}, u32[]{:S(2)}) collective-permute-start(f32[2,4,128,128]{3,2,1,0:T(8,128)S(1)} %collective-permute-done.2.r2), channel_id=1, source_target_pairs={{1,0},{0,1},{17,16},{16,17},{3,2},{2,3},{19,18},{18,19},{5,4},{4,5... | collective-permute-start | bytes 1572872 | tf_op jit(solution)/shard_map/ppermute | solution.py:369
  15.6 8.7 %collective-permute-start.7 = (f32[1,4,128,128]{3,2,1,0:T(8,128)S(1)}, f32[1,4,128,128]{3,2,1,0:T(8,128)S(1)}, u32[]{:S(2)}, u32[]{:S(2)}) collective-permute-start(f32[1,4,128,128]{3,2,1,0:T(8,128)S(1)} %get-tuple-element.43), channel_id=1, source_target_pairs={{15,1},{1,4},{4,9},{9,13},{13,15},{2,12},{12,8},{8,5},{5,0},{0,2},... | collective-permute-start | bytes 786440 | tf_op jit(solution)/shard_map/ppermute | solution.py:369
  18.0 8.7 %collective-permute-start.6 = (f32[1,4,128,128]{3,2,1,0:T(8,128)S(1)}, f32[1,4,128,128]{3,2,1,0:T(8,128)S(1)}, u32[]{:S(2)}, u32[]{:S(2)}) collective-permute-start(f32[1,4,128,128]{3,2,1,0:T(8,128)S(1)} %get-tuple-element.44), channel_id=1, source_target_pairs={{15,1},{1,4},{4,9},{9,13},{13,15},{2,12},{12,8},{8,5},{5,0},{0,2},... | collective-permute-start | bytes 786440 | tf_op jit(solution)/shard_map/ppermute | solution.py:369
  21.2 5.7 %collective-permute-start.10 = (f32[2,4,128,128]{3,2,1,0:T(8,128)S(1)}, f32[2,4,128,128]{3,2,1,0:T(8,128)S(1)}, u32[]{:S(2)}, u32[]{:S(2)}) collective-permute-start(f32[2,4,128,128]{3,2,1,0:T(8,128)S(1)} %collective-permute-done.5.r3), channel_id=1, source_target_pairs={{1,0},{0,1},{17,16},{16,17},{3,2},{2,3},{19,18},{18,19},{5,4},{4,5... | collective-permute-start | bytes 1572872 | tf_op jit(solution)/shard_map/ppermute | solution.py:369
  24.3 2.5 %collective-permute-start.8 = (f32[1,4,128,128]{3,2,1,0:T(8,128)S(1)}, f32[1,4,128,128]{3,2,1,0:T(8,128)S(1)}, u32[]{:S(2)}, u32[]{:S(2)}) collective-permute-start(f32[1,4,128,128]{3,2,1,0:T(8,128)S(1)} %collective-permute-done.7.r4a), channel_id=1, source_target_pairs={{1,0},{0,1},{17,16},{16,17},{3,2},{2,3},{19,18},{18,19},{5,4},{4,5... | collective-permute-start | bytes 786440 | tf_op jit(solution)/shard_map/ppermute | solution.py:369
  26.8 1.6 %collective-permute-start.9 = (f32[1,4,128,128]{3,2,1,0:T(8,128)S(1)}, f32[1,4,128,128]{3,2,1,0:T(8,128)S(1)}, u32[]{:S(2)}, u32[]{:S(2)}) collective-permute-start(f32[1,4,128,128]{3,2,1,0:T(8,128)S(1)} %collective-permute-done.6.r4b), channel_id=1, source_target_pairs={{1,0},{0,1},{17,16},{16,17},{3,2},{2,3},{19,18},{18,19},{5,4},{4,5... | collective-permute-start | bytes 786440 | tf_op jit(solution)/shard_map/ppermute | solution.py:369

commit v27 on v25

--- a/solution.py
+++ b/solution.py
@@ -293,19 +293,25 @@
     copies = []
     for r in range(slab):
         left_parts = square_parts[pl.ds(2 * r * edge, 2 * edge), :]
-        codes = [own_codes(r, w) for w in range(width)]
-        cols = [pl.ds(pl.multiple_of((code & (act - 1)) * edge, edge), edge) for code in codes]
-        cube = stacked_dot(
-            left_parts,
-            jnp.concatenate([high[:, col] for col in cols], axis=1),
-            jnp.concatenate([low[:, col] for col in cols], axis=1),
-        )
-        for w in range(width):
-            value = 3.0 * square[pl.ds(r * edge, edge), cols[w]]
-            value = value - 2.0 * cube[:, w * edge : (w + 1) * edge]
-            out_ref[r, w] = jnp.where(holds & (codes[w] < act), value, 0.0)
-        copies.append(pltpu.make_async_copy(out_ref.at[r], out_hbm.at[r], out_sem.at[r]))
-        copies[-1].start()
+        for first in range(0, width, 2):
+            codes = [own_codes(r, first + k) for k in range(2)]
+            cols = [pl.ds(pl.multiple_of((code & (act - 1)) * edge, edge), edge) for code in codes]
+            cube = stacked_dot(
+                left_parts,
+                jnp.concatenate([high[:, col] for col in cols], axis=1),
+                jnp.concatenate([low[:, col] for col in cols], axis=1),
+            )
+            for k in range(2):
+                w = first + k
+                value = 3.0 * square[pl.ds(r * edge, edge), cols[k]]
+                value = value - 2.0 * cube[:, k * edge : (k + 1) * edge]
+                out_ref[r, w] = jnp.where(holds & (codes[k] < act), value, 0.0)
+                copies.append(
+                    pltpu.make_async_copy(
+                        out_ref.at[r, w], out_hbm.at[r, w], out_sem.at[len(copies)]
+                    )
+                )
+                copies[-1].start()
     for copy in copies:
         copy.wait()
 
@@ -451,7 +457,7 @@
         scratch_shapes=[
             pltpu.VMEM((2 * own, order), jnp.bfloat16),
             pltpu.VMEM(x_blocks.shape, jnp.float32),
-            pltpu.SemaphoreType.DMA((slab,)),
+            pltpu.SemaphoreType.DMA((slab * width,)),
         ],
         compiler_params=params,
         name="late",

time: 31.7 us -> 31.8 us (level)
  transfers between devices with their start and end apart: 11 -> 11, of which waited for: 5 -> 5; matrix products, arithmetic and copies ran while one was open for 8% -> 7% of each run, Pallas kernels for 17% -> 17%
where the time goes in v27:
time: 31.8 us; the launch traced here: 31.4 us
  starting transfers between devices  13.7 us (43%)
  Pallas kernels  8.43 us (27%)
  waiting for transfers between devices  6.83 us (21%)
  other arithmetic  2.24 us (7%)
    ppermute x10, starting transfers between devices, move(): return lax.ppermute(block, AXES, route)  11.5 us
    ppermute x10, waiting for transfers between devices, move(): return lax.ppermute(block, AXES, route)  3.62 us
    ppermute x1, waiting for transfers between devices, move_only(): return lax.ppermute(block, AXES, route)  3.21 us
    pallas_call x1, Pallas kernels, gather_local(): pl.pallas_call(functools.partial(early_kernel, tables), out_shape=[jax.Sh...  3.09 us
    pallas_call x1, Pallas kernels, gather_local(): pl.pallas_call(functools.partial(late_kernel, tables), out_shape=[jax.Sha...  3.04 us
    pallas_call x2, Pallas kernels, add_to_square(): pl.pallas_call(functools.partial(kernel, tables), out_shape=dense, in_spe...  2.31 us
    ppermute x1, starting transfers between devices, move_only(): return lax.ppermute(block, AXES, route)  2.28 us
    reduce_sum x1, other arithmetic, slot_table(): count = jnp.sum(here.astype(jnp.int32), axis=1, keepdims=True)  0.8 us
  transfers between devices with their start and end apart: 11, of which 5 were waited for; matrix products, arithmetic and copies ran while one was open for 7% of the time, Pallas kernels for 17%

profile of v27, /device:TPU:0, one launch (start us, length us, event | category | flops | bytes accessed | tf_op | source)
XLA Modules:
  0.0 31.4 jit_solution(9306867768540350215)
XLA Ops:
  0.0 2.9 %collective-permute-start = (f32[2,4,128,128]{3,2,1,0:T(8,128)}, f32[2,4,128,128]{3,2,1,0:T(8,128)S(1)}, u32[]{:S(2)}, u32[]{:S(2)}) collective-permute-start(f32[2,4,128,128]{3,2,1,0:T(8,128)} %own_hbm.1), channel_id=1, source_target_pairs={{3,1},{1,4},{4,9},{9,12},{12,8},{8,5},{5,0},{0,2},{2,3},{14,13},{1... | collective-permute-start | bytes 1572872 | tf_op jit(solution)/shard_map/ppermute | solution.py:360
  2.9 0.2 collective-permute-start.1
  3.1 0.8 %fusion.1 = (s32[8]{0:T(128)S(1)}, s32[8,8]{1,0:T(8,128)S(1)}) fusion(s32[8,16]{1,0:T(8,128)} %param.3), kind=kLoop, calls=%fused_computation.7 | loop fusion | flops 184 | bytes 544 | tf_op jit(solution)/shard_map/reduce_sum | solution.py:325
  3.9 0.1 fusion
  4.1 0.2 convert_reduce_fusion
  4.3 0.8 %collective-permute-done.1.own_swap = f32[2,4,128,128]{3,2,1,0:T(8,128)S(1)} collective-permute-done((f32[2,4,128,128]{3,2,1,0:T(8,128)}, f32[2,4,128,128]{3,2,1,0:T(8,128)S(1)}, u32[]{:S(2)}, u32[]{:S(2)}) %collective-permute-start.1) | collective-permute-done | bytes 524320 | tf_op jit(solution)/shard_map/ppermute | solution.py:360
  5.1 2.3 %collective-permute-start.2 = (f32[2,4,128,128]{3,2,1,0:T(8,128)S(1)}, f32[2,4,128,128]{3,2,1,0:T(8,128)S(1)}, u32[]{:S(2)}, u32[]{:S(2)}) collective-permute-start(f32[2,4,128,128]{3,2,1,0:T(8,128)S(1)} %collective-permute-done.1.own_swap), channel_id=1, source_target_pairs={{1,4},{4,9},{9,13},{13,15},{12,8},{8,5},{5,0},{0,2},{17,20},{20,25... | collective-permute-start | bytes 1572872 | tf_op jit(solution)/shard_map/ppermute | solution.py:368
  7.3 0.1 add_select_fusion
  7.5 0.1 copy.13
  7.5 0.2 select_reduce_fusion
  7.8 0.7 %compare_select_fusion = s32[8,8]{1,0:T(8,128)S(1)} fusion(s32[8,8]{1,0:T(8,128)S(1)} %select_reduce_fusion, s32[8,16]{1,0:T(8,128)} %param.3), kind=kLoop, calls=%fused_computation.5 | loop fusion | flops 192 | bytes 768 | tf_op jit(solution)/shard_map/jit(_where)/select_n | solution.py:333
  8.5 0.1 pad_add_fusion.table_ref
  8.5 1.4 %collective-permute-done.r1 = f32[2,4,128,128]{3,2,1,0:T(8,128)S(1)} collective-permute-done((f32[2,4,128,128]{3,2,1,0:T(8,128)}, f32[2,4,128,128]{3,2,1,0:T(8,128)S(1)}, u32[]{:S(2)}, u32[]{:S(2)}) %collective-permute-start) | collective-permute-done | bytes 524320 | tf_op jit(solution)/shard_map/ppermute | solution.py:360
  10.0 2.4 %collective-permute-start.5 = (f32[2,4,128,128]{3,2,1,0:T(8,128)S(1)}, f32[2,4,128,128]{3,2,1,0:T(8,128)S(1)}, u32[]{:S(2)}, u32[]{:S(2)}) collective-permute-start(f32[2,4,128,128]{3,2,1,0:T(8,128)S(1)} %collective-permute-done.r1), channel_id=1, source_target_pairs={{15,1},{1,4},{4,9},{9,13},{13,15},{2,12},{12,8},{8,5},{5,0},{0,2},... | collective-permute-start | bytes 1572872 | tf_op jit(solution)/shard_map/ppermute | solution.py:360
  12.3 0.0 collective-permute-start.3
  12.3 3.2 %collective-permute-done.2.r2 = f32[2,4,128,128]{3,2,1,0:T(8,128)S(1)} collective-permute-done((f32[2,4,128,128]{3,2,1,0:T(8,128)S(1)}, f32[2,4,128,128]{3,2,1,0:T(8,128)S(1)}, u32[]{:S(2)}, u32[]{:S(2)}) %collective-permute-start.2) | collective-permute-done | bytes 524320 | tf_op jit(solution)/shard_map/ppermute | solution.py:368
  15.6 0.0 collective-permute-start.4
  15.6 2.5 %collective-permute-start.7 = (f32[1,4,128,128]{3,2,1,0:T(8,128)S(1)}, f32[1,4,128,128]{3,2,1,0:T(8,128)S(1)}, u32[]{:S(2)}, u32[]{:S(2)}) collective-permute-start(f32[1,4,128,128]{3,2,1,0:T(8,128)S(1)} %get-tuple-element.43), channel_id=1, source_target_pairs={{15,1},{1,4},{4,9},{9,13},{13,15},{2,12},{12,8},{8,5},{5,0},{0,2},... | collective-permute-start | bytes 786440 | tf_op jit(solution)/shard_map/ppermute | solution.py:360
  18.0 2.8 %collective-permute-start.6 = (f32[1,4,128,128]{3,2,1,0:T(8,128)S(1)}, f32[1,4,128,128]{3,2,1,0:T(8,128)S(1)}, u32[]{:S(2)}, u32[]{:S(2)}) collective-permute-start(f32[1,4,128,128]{3,2,1,0:T(8,128)S(1)} %get-tuple-element.44), channel_id=1, source_target_pairs={{15,1},{1,4},{4,9},{9,13},{13,15},{2,12},{12,8},{8,5},{5,0},{0,2},... | collective-permute-start | bytes 786440 | tf_op jit(solution)/shard_map/ppermute | solution.py:360
  20.9 0.3 collective-permute-done.5.r3
  21.2 0.0 collective-permute-start.10
  21.2 0.0 collective-permute-done.3.t1
  21.2 3.1 %early.1 = (bf16[1024,1024]{1,0:T(8,128)(2,1)S(1)}, bf16[1024,1024]{1,0:T(8,128)(2,1)S(1)}, bf16[512,1024]{1,0:T(8,128)(2,1)S(1)}, f32[256,1024]{1,0:T(8,128)S(1)}, s32[8,128]{1,0:T(8,128)S(1)}) custom-call(s32[8,9]{1,0:T(8,128)S(1)} %pad_add_fusion.table_ref, f32[2,4,128,128]{3,2,1,0:T(8,128)} %own_hbm.1, ...), custom_call_target="tpu_custom_call" | custom-call | tf_op jit(solution)/shard_map/early/pallas_call | solution.py:415
  24.3 0.0 collective-permute-done.7.r4a
  24.3 0.6 %collective-permute-start.8 = (f32[1,4,128,128]{3,2,1,0:T(8,128)S(1)}, f32[1,4,128,128]{3,2,1,0:T(8,128)S(1)}, u32[]{:S(2)}, u32[]{:S(2)}) collective-permute-start(f32[1,4,128,128]{3,2,1,0:T(8,128)S(1)} %collective-permute-done.7.r4a), channel_id=1, source_target_pairs={{1,0},{0,1},{17,16},{16,17},{3,2},{2,3},{19,18},{18,19},{5,4},{4,5... | collective-permute-start | bytes 786440 | tf_op jit(solution)/shard_map/ppermute | solution.py:360
  24.9 0.8 %waiting.1 = (bf16[1024,1024]{1,0:T(8,128)(2,1)S(1)}, bf16[1024,1024]{1,0:T(8,128)(2,1)S(1)}, f32[256,1024]{1,0:T(8,128)S(1)}) custom-call(s32[8,128]{1,0:T(8,128)S(1)} %get-tuple-element.26.notes_ref, f32[1,4,128,128]{3,2,1,0:T(8,128)S(1)} %collective-permute-done.7.r4a, ...), custom_call_target="tpu_custom_call", output_to_operand_aliasing={{0}: (2, {}), {1}: (3, {}), {2}: (5, {})} | custom-call | tf_op jit(solution)/shard_map/waiting/pallas_call | solution.py:437
  25.7 1.1 %collective-permute-done.6.r4b = f32[1,4,128,128]{3,2,1,0:T(8,128)S(1)} collective-permute-done((f32[1,4,128,128]{3,2,1,0:T(8,128)S(1)}, f32[1,4,128,128]{3,2,1,0:T(8,128)S(1)}, u32[]{:S(2)}, u32[]{:S(2)}) %collective-permute-start.6) | collective-permute-done | bytes 262176 | tf_op jit(solution)/shard_map/ppermute | solution.py:360
  26.8 0.0 collective-permute-done.8.t4a
  26.8 0.1 collective-permute-start.9
  26.9 1.5 %middle.1 = (bf16[1024,1024]{1,0:T(8,128)(2,1)S(1)}, bf16[1024,1024]{1,0:T(8,128)(2,1)S(1)}, f32[256,1024]{1,0:T(8,128)S(1)}) custom-call(s32[8,128]{1,0:T(8,128)S(1)} %get-tuple-element.26.notes_ref, f32[1,4,128,128]{3,2,1,0:T(8,128)S(1)} %collective-permute-done.6.r4b, ...), custom_call_target="tpu_custom_call", output_to_operand_aliasing={{0}: (4, {}), {1}: (5, {}), {2}: (7, {})} | custom-call | tf_op jit(solution)/shard_map/middle/pallas_call | solution.py:437
  28.4 0.0 collective-permute-done.9.t4b
  28.4 3.0 %late.1 = (f32[2,4,128,128]{3,2,1,0:T(8,128)}, bf16[1024,1024]{1,0:T(8,128)(2,1)S(1)}, bf16[1024,1024]{1,0:T(8,128)(2,1)S(1)}, f32[256,1024]{1,0:T(8,128)S(1)}) custom-call(s32[8,128]{1,0:T(8,128)S(1)} %get-tuple-element.26.notes_ref, f32[1,4,128,128]{3,2,1,0:T(8,128)S(1)} %collective-permute-done.9.t4b, ...), custom_call_target="tpu_custom_call", output_to_operand_aliasing={{1}: (2, {}), {2}: (3, {}), {3}: (5, {})} | custom-call | tf_op jit(solution)/shard_map/late/pallas_call | solution.py:451
  (6 shorter events, 0.1 us)
Async XLA Ops:
  0.0 10.0 %collective-permute-start = (f32[2,4,128,128]{3,2,1,0:T(8,128)}, f32[2,4,128,128]{3,2,1,0:T(8,128)S(1)}, u32[]{:S(2)}, u32[]{:S(2)}) collective-permute-start(f32[2,4,128,128]{3,2,1,0:T(8,128)} %own_hbm.1), channel_id=1, source_target_pairs={{3,1},{1,4},{4,9},{9,12},{12,8},{8,5},{5,0},{0,2},{2,3},{14,13},{1... | collective-permute-start | bytes 1572872 | tf_op jit(solution)/shard_map/ppermute | solution.py:360
  2.9 2.1 %collective-permute-start.1 = (f32[2,4,128,128]{3,2,1,0:T(8,128)}, f32[2,4,128,128]{3,2,1,0:T(8,128)S(1)}, u32[]{:S(2)}, u32[]{:S(2)}) collective-permute-start(f32[2,4,128,128]{3,2,1,0:T(8,128)} %own_hbm.1), channel_id=1, source_target_pairs={{1,0},{0,1},{17,16},{16,17},{3,2},{2,3},{19,18},{18,19},{5,4},{4,5... | collective-permute-start | bytes 1572872 | tf_op jit(solution)/shard_map/ppermute | solution.py:360
  5.1 10.5 %collective-permute-start.2 = (f32[2,4,128,128]{3,2,1,0:T(8,128)S(1)}, f32[2,4,128,128]{3,2,1,0:T(8,128)S(1)}, u32[]{:S(2)}, u32[]{:S(2)}) collective-permute-start(f32[2,4,128,128]{3,2,1,0:T(8,128)S(1)} %collective-permute-done.1.own_swap), channel_id=1, source_target_pairs={{1,4},{4,9},{9,13},{13,15},{12,8},{8,5},{5,0},{0,2},{17,20},{20,25... | collective-permute-start | bytes 1572872 | tf_op jit(solution)/shard_map/ppermute | solution.py:368
  10.0 11.2 %collective-permute-start.5 = (f32[2,4,128,128]{3,2,1,0:T(8,128)S(1)}, f32[2,4,128,128]{3,2,1,0:T(8,128)S(1)}, u32[]{:S(2)}, u32[]{:S(2)}) collective-permute-start(f32[2,4,128,128]{3,2,1,0:T(8,128)S(1)} %collective-permute-done.r1), channel_id=1, source_target_pairs={{15,1},{1,4},{4,9},{9,13},{13,15},{2,12},{12,8},{8,5},{5,0},{0,2},... | collective-permute-start | bytes 1572872 | tf_op jit(solution)/shard_map/ppermute | solution.py:360
  12.3 8.8 %collective-permute-start.3 = (f32[2,4,128,128]{3,2,1,0:T(8,128)S(1)}, f32[2,4,128,128]{3,2,1,0:T(8,128)S(1)}, u32[]{:S(2)}, u32[]{:S(2)}) collective-permute-start(f32[2,4,128,128]{3,2,1,0:T(8,128)S(1)} %collective-permute-done.r1), channel_id=1, source_target_pairs={{1,0},{0,1},{17,16},{16,17},{3,2},{2,3},{19,18},{18,19},{5,4},{4,5... | collective-permute-start | bytes 1572872 | tf_op jit(solution)/shard_map/ppermute | solution.py:360
  15.6 5.6 %collective-permute-start.4 = (f32[2,4,128,128]{3,2,1,0:T(8,128)S(1)}, f32[2,4,128,128]{3,2,1,0:T(8,128)S(1)}, u32[]{:S(2)}, u32[]{:S(2)}) collective-permute-start(f32[2,4,128,128]{3,2,1,0:T(8,128)S(1)} %collective-permute-done.2.r2), channel_id=1, source_target_pairs={{1,0},{0,1},{17,16},{16,17},{3,2},{2,3},{19,18},{18,19},{5,4},{4,5... | collective-permute-start | bytes 1572872 | tf_op jit(solution)/shard_map/ppermute | solution.py:360
  15.6 8.7 %collective-permute-start.7 = (f32[1,4,128,128]{3,2,1,0:T(8,128)S(1)}, f32[1,4,128,128]{3,2,1,0:T(8,128)S(1)}, u32[]{:S(2)}, u32[]{:S(2)}) collective-permute-start(f32[1,4,128,128]{3,2,1,0:T(8,128)S(1)} %get-tuple-element.43), channel_id=1, source_target_pairs={{15,1},{1,4},{4,9},{9,13},{13,15},{2,12},{12,8},{8,5},{5,0},{0,2},... | collective-permute-start | bytes 786440 | tf_op jit(solution)/shard_map/ppermute | solution.py:360
  18.0 8.7 %collective-permute-start.6 = (f32[1,4,128,128]{3,2,1,0:T(8,128)S(1)}, f32[1,4,128,128]{3,2,1,0:T(8,128)S(1)}, u32[]{:S(2)}, u32[]{:S(2)}) collective-permute-start(f32[1,4,128,128]{3,2,1,0:T(8,128)S(1)} %get-tuple-element.44), channel_id=1, source_target_pairs={{15,1},{1,4},{4,9},{9,13},{13,15},{2,12},{12,8},{8,5},{5,0},{0,2},... | collective-permute-start | bytes 786440 | tf_op jit(solution)/shard_map/ppermute | solution.py:360
  21.2 5.7 %collective-permute-start.10 = (f32[2,4,128,128]{3,2,1,0:T(8,128)S(1)}, f32[2,4,128,128]{3,2,1,0:T(8,128)S(1)}, u32[]{:S(2)}, u32[]{:S(2)}) collective-permute-start(f32[2,4,128,128]{3,2,1,0:T(8,128)S(1)} %collective-permute-done.5.r3), channel_id=1, source_target_pairs={{1,0},{0,1},{17,16},{16,17},{3,2},{2,3},{19,18},{18,19},{5,4},{4,5... | collective-permute-start | bytes 1572872 | tf_op jit(solution)/shard_map/ppermute | solution.py:360
  24.3 2.5 %collective-permute-start.8 = (f32[1,4,128,128]{3,2,1,0:T(8,128)S(1)}, f32[1,4,128,128]{3,2,1,0:T(8,128)S(1)}, u32[]{:S(2)}, u32[]{:S(2)}) collective-permute-start(f32[1,4,128,128]{3,2,1,0:T(8,128)S(1)} %collective-permute-done.7.r4a), channel_id=1, source_target_pairs={{1,0},{0,1},{17,16},{16,17},{3,2},{2,3},{19,18},{18,19},{5,4},{4,5... | collective-permute-start | bytes 786440 | tf_op jit(solution)/shard_map/ppermute | solution.py:360
  26.8 1.6 %collective-permute-start.9 = (f32[1,4,128,128]{3,2,1,0:T(8,128)S(1)}, f32[1,4,128,128]{3,2,1,0:T(8,128)S(1)}, u32[]{:S(2)}, u32[]{:S(2)}) collective-permute-start(f32[1,4,128,128]{3,2,1,0:T(8,128)S(1)} %collective-permute-done.6.r4b), channel_id=1, source_target_pairs={{1,0},{0,1},{17,16},{16,17},{3,2},{2,3},{19,18},{18,19},{5,4},{4,5... | collective-permute-start | bytes 786440 | tf_op jit(solution)/shard_map/ppermute | solution.py:360

commit v28 on v26

--- a/solution.py
+++ b/solution.py
@@ -276,7 +276,7 @@
 
 def late_kernel(
     tables, notes_ref, t4b, high_in, low_in, left, part_in,
-    out_hbm, high, low, square, square_parts, out_ref, out_sem,
+    out_hbm, high, low, square, parts_0, parts_1, out_ref, out_sem,
 ):
     place, lane = lax.axis_index("blk"), lax.axis_index("depth")
     there = lookup(tables[-1][0], place, 1 - lane)
@@ -290,35 +290,34 @@
     )
     flags = notes[0, KEPT]
 
-    def keep(r, c, col, block):
+    def keep(parts, r, c, col, block):
         kept = (flags >> (r * act + c)) & 1 > 0
         block_high, block_low = split(jnp.where(kept, block, 0.0))
-        square_parts[pl.ds(2 * r * edge, edge), col] = block_high
-        square_parts[pl.ds((2 * r + 1) * edge, edge), col] = block_low
-
-    for r in range(slab):
-        for c in range(square.shape[1] // edge):
-            col = pl.ds(c * edge, edge)
-            keep(r, c, col, square[pl.ds(r * edge, edge), col])
+        parts[pl.ds(0, edge), col] = block_high
+        parts[pl.ds(edge, edge), col] = block_low
+
+    before = [square[:, c * edge : (c + 1) * edge] for c in range(square.shape[1] // edge)]
     sums = [square[:, col] + more[:, w * edge : (w + 1) * edge] for w, col in enumerate(changed)]
-    for code, col, total in zip(codes, changed, sums):
+    for col, total in zip(changed, sums):
         square[:, col] = total
-        for r in range(slab):
-            keep(r, code & (act - 1), col, total[r * edge : (r + 1) * edge])
     copies = []
-    for r in range(slab):
-        left_parts = square_parts[pl.ds(2 * r * edge, 2 * edge), :]
-        codes = [own_codes(r, w) for w in range(width)]
-        cols = [pl.ds(pl.multiple_of((code & (act - 1)) * edge, edge), edge) for code in codes]
+    for r, parts in enumerate((parts_0, parts_1)):
+        mine = slice(r * edge, (r + 1) * edge)
+        for c, block in enumerate(before):
+            keep(parts, r, c, pl.ds(c * edge, edge), block[mine])
+        for code, col, total in zip(codes, changed, sums):
+            keep(parts, r, code & (act - 1), col, total[mine])
+        own = [own_codes(r, w) for w in range(width)]
+        cols = [pl.ds(pl.multiple_of((code & (act - 1)) * edge, edge), edge) for code in own]
         cube = stacked_dot(
-            left_parts,
+            parts[...],
             jnp.concatenate([high[:, col] for col in cols], axis=1),
             jnp.concatenate([low[:, col] for col in cols], axis=1),
         )
         for w in range(width):
-            value = 3.0 * square[pl.ds(r * edge, edge), cols[w]]
+            value = 3.0 * square[mine, cols[w]]
             value = value - 2.0 * cube[:, w * edge : (w + 1) * edge]
-            out_ref[r, w] = jnp.where(holds & (codes[w] < act), value, 0.0)
+            out_ref[r, w] = jnp.where(holds & (own[w] < act), value, 0.0)
         copies.append(pltpu.make_async_copy(out_ref.at[r], out_hbm.at[r], out_sem.at[r]))
         copies[-1].start()
     for copy in copies:
@@ -464,7 +463,8 @@
         out_specs=[pl.BlockSpec(memory_space=pltpu.HBM)] + [vmem] * 3,
         input_output_aliases={2: 1, 3: 2, 5: 3},
         scratch_shapes=[
-            pltpu.VMEM((2 * own, order), jnp.bfloat16),
+            pltpu.VMEM((2 * edge, order), jnp.bfloat16),
+            pltpu.VMEM((2 * edge, order), jnp.bfloat16),
             pltpu.VMEM(x_blocks.shape, jnp.float32),
             pltpu.SemaphoreType.DMA((slab,)),
         ],

time: 31.8 us -> 31.8 us (level)
  no operation moved by 1% of the time
where the time goes in v28:
time: 31.8 us; the launch traced here: 31.5 us
  starting transfers between devices  13.7 us (43%)
  Pallas kernels  8.47 us (27%)
  waiting for transfers between devices  6.82 us (21%)
  other arithmetic  2.24 us (7%)
    ppermute x10, starting transfers between devices, move(): return lax.ppermute(block, AXES, route)  11.5 us
    ppermute x10, waiting for transfers between devices, move(): return lax.ppermute(block, AXES, route)  3.6 us
    ppermute x1, waiting for transfers between devices, move_only(): return lax.ppermute(block, AXES, route)  3.21 us
    pallas_call x1, Pallas kernels, gather_local(): pl.pallas_call(functools.partial(early_kernel, tables), out_shape=[jax.Sh...  3.09 us
    pallas_call x1, Pallas kernels, gather_local(): pl.pallas_call(functools.partial(late_kernel, tables), out_shape=[jax.Sha...  3.03 us
    pallas_call x2, Pallas kernels, add_to_square(): pl.pallas_call(functools.partial(kernel, tables), out_shape=dense, in_spe...  2.35 us
    ppermute x1, starting transfers between devices, move_only(): return lax.ppermute(block, AXES, route)  2.28 us
    reduce_sum x1, other arithmetic, slot_table(): count = jnp.sum(here.astype(jnp.int32), axis=1, keepdims=True)  0.8 us
  transfers between devices with their start and end apart: 11, of which 5 were waited for; matrix products, arithmetic and copies ran while one was open for 7% of the time, Pallas kernels for 17%

profile of v28, /device:TPU:0, one launch (start us, length us, event | category | flops | bytes accessed | tf_op | source)
XLA Modules:
  0.0 31.5 jit_solution(6318748463381483146)
XLA Ops:
  0.0 2.9 %collective-permute-start = (f32[2,4,128,128]{3,2,1,0:T(8,128)}, f32[2,4,128,128]{3,2,1,0:T(8,128)S(1)}, u32[]{:S(2)}, u32[]{:S(2)}) collective-permute-start(f32[2,4,128,128]{3,2,1,0:T(8,128)} %own_hbm.1), channel_id=1, source_target_pairs={{3,1},{1,4},{4,9},{9,12},{12,8},{8,5},{5,0},{0,2},{2,3},{14,13},{1... | collective-permute-start | bytes 1572872 | tf_op jit(solution)/shard_map/ppermute | solution.py:368
  2.9 0.2 collective-permute-start.1
  3.1 0.8 %fusion.1 = (s32[8]{0:T(128)S(1)}, s32[8,8]{1,0:T(8,128)S(1)}) fusion(s32[8,16]{1,0:T(8,128)} %param.3), kind=kLoop, calls=%fused_computation.7 | loop fusion | flops 184 | bytes 544 | tf_op jit(solution)/shard_map/reduce_sum | solution.py:333
  3.9 0.1 fusion
  4.1 0.2 convert_reduce_fusion
  4.3 0.8 %collective-permute-done.1.own_swap = f32[2,4,128,128]{3,2,1,0:T(8,128)S(1)} collective-permute-done((f32[2,4,128,128]{3,2,1,0:T(8,128)}, f32[2,4,128,128]{3,2,1,0:T(8,128)S(1)}, u32[]{:S(2)}, u32[]{:S(2)}) %collective-permute-start.1) | collective-permute-done | bytes 524320 | tf_op jit(solution)/shard_map/ppermute | solution.py:368
  5.1 2.3 %collective-permute-start.2 = (f32[2,4,128,128]{3,2,1,0:T(8,128)S(1)}, f32[2,4,128,128]{3,2,1,0:T(8,128)S(1)}, u32[]{:S(2)}, u32[]{:S(2)}) collective-permute-start(f32[2,4,128,128]{3,2,1,0:T(8,128)S(1)} %collective-permute-done.1.own_swap), channel_id=1, source_target_pairs={{1,4},{4,9},{9,13},{13,15},{12,8},{8,5},{5,0},{0,2},{17,20},{20,25... | collective-permute-start | bytes 1572872 | tf_op jit(solution)/shard_map/ppermute | solution.py:376
  7.3 0.1 add_select_fusion
  7.5 0.1 copy.13
  7.5 0.2 select_reduce_fusion
  7.8 0.7 %compare_select_fusion = s32[8,8]{1,0:T(8,128)S(1)} fusion(s32[8,8]{1,0:T(8,128)S(1)} %select_reduce_fusion, s32[8,16]{1,0:T(8,128)} %param.3), kind=kLoop, calls=%fused_computation.5 | loop fusion | flops 192 | bytes 768 | tf_op jit(solution)/shard_map/jit(_where)/select_n | solution.py:341
  8.5 0.1 pad_add_fusion.table_ref
  8.5 1.4 %collective-permute-done.r1 = f32[2,4,128,128]{3,2,1,0:T(8,128)S(1)} collective-permute-done((f32[2,4,128,128]{3,2,1,0:T(8,128)}, f32[2,4,128,128]{3,2,1,0:T(8,128)S(1)}, u32[]{:S(2)}, u32[]{:S(2)}) %collective-permute-start) | collective-permute-done | bytes 524320 | tf_op jit(solution)/shard_map/ppermute | solution.py:368
  10.0 2.4 %collective-permute-start.5 = (f32[2,4,128,128]{3,2,1,0:T(8,128)S(1)}, f32[2,4,128,128]{3,2,1,0:T(8,128)S(1)}, u32[]{:S(2)}, u32[]{:S(2)}) collective-permute-start(f32[2,4,128,128]{3,2,1,0:T(8,128)S(1)} %collective-permute-done.r1), channel_id=1, source_target_pairs={{15,1},{1,4},{4,9},{9,13},{13,15},{2,12},{12,8},{8,5},{5,0},{0,2},... | collective-permute-start | bytes 1572872 | tf_op jit(solution)/shard_map/ppermute | solution.py:368
  12.3 0.0 collective-permute-start.3
  12.3 3.2 %collective-permute-done.2.r2 = f32[2,4,128,128]{3,2,1,0:T(8,128)S(1)} collective-permute-done((f32[2,4,128,128]{3,2,1,0:T(8,128)S(1)}, f32[2,4,128,128]{3,2,1,0:T(8,128)S(1)}, u32[]{:S(2)}, u32[]{:S(2)}) %collective-permute-start.2) | collective-permute-done | bytes 524320 | tf_op jit(solution)/shard_map/ppermute | solution.py:376
  15.6 0.0 collective-permute-start.4
  15.6 2.5 %collective-permute-start.7 = (f32[1,4,128,128]{3,2,1,0:T(8,128)S(1)}, f32[1,4,128,128]{3,2,1,0:T(8,128)S(1)}, u32[]{:S(2)}, u32[]{:S(2)}) collective-permute-start(f32[1,4,128,128]{3,2,1,0:T(8,128)S(1)} %get-tuple-element.43), channel_id=1, source_target_pairs={{15,1},{1,4},{4,9},{9,13},{13,15},{2,12},{12,8},{8,5},{5,0},{0,2},... | collective-permute-start | bytes 786440 | tf_op jit(solution)/shard_map/ppermute | solution.py:368
  18.0 2.8 %collective-permute-start.6 = (f32[1,4,128,128]{3,2,1,0:T(8,128)S(1)}, f32[1,4,128,128]{3,2,1,0:T(8,128)S(1)}, u32[]{:S(2)}, u32[]{:S(2)}) collective-permute-start(f32[1,4,128,128]{3,2,1,0:T(8,128)S(1)} %get-tuple-element.44), channel_id=1, source_target_pairs={{15,1},{1,4},{4,9},{9,13},{13,15},{2,12},{12,8},{8,5},{5,0},{0,2},... | collective-permute-start | bytes 786440 | tf_op jit(solution)/shard_map/ppermute | solution.py:368
  20.9 0.3 collective-permute-done.5.r3
  21.2 0.0 collective-permute-start.10
  21.2 0.0 collective-permute-done.3.t1
  21.2 3.1 %early.1 = (bf16[1024,1024]{1,0:T(8,128)(2,1)S(1)}, bf16[1024,1024]{1,0:T(8,128)(2,1)S(1)}, bf16[512,1024]{1,0:T(8,128)(2,1)S(1)}, f32[256,1024]{1,0:T(8,128)S(1)}, s32[8,128]{1,0:T(8,128)S(1)}) custom-call(s32[8,9]{1,0:T(8,128)S(1)} %pad_add_fusion.table_ref, f32[2,4,128,128]{3,2,1,0:T(8,128)} %own_hbm.1, ...), custom_call_target="tpu_custom_call" | custom-call | tf_op jit(solution)/shard_map/early/pallas_call | solution.py:423
  24.3 0.6 %collective-permute-start.8 = (f32[1,4,128,128]{3,2,1,0:T(8,128)S(1)}, f32[1,4,128,128]{3,2,1,0:T(8,128)S(1)}, u32[]{:S(2)}, u32[]{:S(2)}) collective-permute-start(f32[1,4,128,128]{3,2,1,0:T(8,128)S(1)} %collective-permute-done.7.r4a), channel_id=1, source_target_pairs={{1,0},{0,1},{17,16},{16,17},{3,2},{2,3},{19,18},{18,19},{5,4},{4,5... | collective-permute-start | bytes 786440 | tf_op jit(solution)/shard_map/ppermute | solution.py:368
  24.9 0.8 %waiting.1 = (bf16[1024,1024]{1,0:T(8,128)(2,1)S(1)}, bf16[1024,1024]{1,0:T(8,128)(2,1)S(1)}, f32[256,1024]{1,0:T(8,128)S(1)}) custom-call(s32[8,128]{1,0:T(8,128)S(1)} %get-tuple-element.26.notes_ref, f32[1,4,128,128]{3,2,1,0:T(8,128)S(1)} %collective-permute-done.7.r4a, ...), custom_call_target="tpu_custom_call", output_to_operand_aliasing={{0}: (2, {}), {1}: (3, {}), {2}: (5, {})} | custom-call | tf_op jit(solution)/shard_map/waiting/pallas_call | solution.py:445
  25.7 1.1 %collective-permute-done.6.r4b = f32[1,4,128,128]{3,2,1,0:T(8,128)S(1)} collective-permute-done((f32[1,4,128,128]{3,2,1,0:T(8,128)S(1)}, f32[1,4,128,128]{3,2,1,0:T(8,128)S(1)}, u32[]{:S(2)}, u32[]{:S(2)}) %collective-permute-start.6) | collective-permute-done | bytes 262176 | tf_op jit(solution)/shard_map/ppermute | solution.py:368
  26.8 0.0 collective-permute-done.8.t4a
  26.8 0.1 collective-permute-start.9
  26.9 0.0 collective-permute-done.10.t3
  26.9 1.5 %middle.1 = (bf16[1024,1024]{1,0:T(8,128)(2,1)S(1)}, bf16[1024,1024]{1,0:T(8,128)(2,1)S(1)}, f32[256,1024]{1,0:T(8,128)S(1)}) custom-call(s32[8,128]{1,0:T(8,128)S(1)} %get-tuple-element.26.notes_ref, f32[1,4,128,128]{3,2,1,0:T(8,128)S(1)} %collective-permute-done.6.r4b, ...), custom_call_target="tpu_custom_call", output_to_operand_aliasing={{0}: (4, {}), {1}: (5, {}), {2}: (7, {})} | custom-call | tf_op jit(solution)/shard_map/middle/pallas_call | solution.py:445
  28.4 0.0 collective-permute-done.9.t4b
  28.4 3.0 %late.1 = (f32[2,4,128,128]{3,2,1,0:T(8,128)}, bf16[1024,1024]{1,0:T(8,128)(2,1)S(1)}, bf16[1024,1024]{1,0:T(8,128)(2,1)S(1)}, f32[256,1024]{1,0:T(8,128)S(1)}) custom-call(s32[8,128]{1,0:T(8,128)S(1)} %get-tuple-element.26.notes_ref, f32[1,4,128,128]{3,2,1,0:T(8,128)S(1)} %collective-permute-done.9.t4b, ...), custom_call_target="tpu_custom_call", output_to_operand_aliasing={{1}: (2, {}), {2}: (3, {}), {3}: (5, {})} | custom-call | tf_op jit(solution)/shard_map/late/pallas_call | solution.py:459
  (6 shorter events, 0.1 us)
Async XLA Ops:
  0.0 10.0 %collective-permute-start = (f32[2,4,128,128]{3,2,1,0:T(8,128)}, f32[2,4,128,128]{3,2,1,0:T(8,128)S(1)}, u32[]{:S(2)}, u32[]{:S(2)}) collective-permute-start(f32[2,4,128,128]{3,2,1,0:T(8,128)} %own_hbm.1), channel_id=1, source_target_pairs={{3,1},{1,4},{4,9},{9,12},{12,8},{8,5},{5,0},{0,2},{2,3},{14,13},{1... | collective-permute-start | bytes 1572872 | tf_op jit(solution)/shard_map/ppermute | solution.py:368
  2.9 2.1 %collective-permute-start.1 = (f32[2,4,128,128]{3,2,1,0:T(8,128)}, f32[2,4,128,128]{3,2,1,0:T(8,128)S(1)}, u32[]{:S(2)}, u32[]{:S(2)}) collective-permute-start(f32[2,4,128,128]{3,2,1,0:T(8,128)} %own_hbm.1), channel_id=1, source_target_pairs={{1,0},{0,1},{17,16},{16,17},{3,2},{2,3},{19,18},{18,19},{5,4},{4,5... | collective-permute-start | bytes 1572872 | tf_op jit(solution)/shard_map/ppermute | solution.py:368
  5.1 10.5 %collective-permute-start.2 = (f32[2,4,128,128]{3,2,1,0:T(8,128)S(1)}, f32[2,4,128,128]{3,2,1,0:T(8,128)S(1)}, u32[]{:S(2)}, u32[]{:S(2)}) collective-permute-start(f32[2,4,128,128]{3,2,1,0:T(8,128)S(1)} %collective-permute-done.1.own_swap), channel_id=1, source_target_pairs={{1,4},{4,9},{9,13},{13,15},{12,8},{8,5},{5,0},{0,2},{17,20},{20,25... | collective-permute-start | bytes 1572872 | tf_op jit(solution)/shard_map/ppermute | solution.py:376
  10.0 11.2 %collective-permute-start.5 = (f32[2,4,128,128]{3,2,1,0:T(8,128)S(1)}, f32[2,4,128,128]{3,2,1,0:T(8,128)S(1)}, u32[]{:S(2)}, u32[]{:S(2)}) collective-permute-start(f32[2,4,128,128]{3,2,1,0:T(8,128)S(1)} %collective-permute-done.r1), channel_id=1, source_target_pairs={{15,1},{1,4},{4,9},{9,13},{13,15},{2,12},{12,8},{8,5},{5,0},{0,2},... | collective-permute-start | bytes 1572872 | tf_op jit(solution)/shard_map/ppermute | solution.py:368
  12.3 8.8 %collective-permute-start.3 = (f32[2,4,128,128]{3,2,1,0:T(8,128)S(1)}, f32[2,4,128,128]{3,2,1,0:T(8,128)S(1)}, u32[]{:S(2)}, u32[]{:S(2)}) collective-permute-start(f32[2,4,128,128]{3,2,1,0:T(8,128)S(1)} %collective-permute-done.r1), channel_id=1, source_target_pairs={{1,0},{0,1},{17,16},{16,17},{3,2},{2,3},{19,18},{18,19},{5,4},{4,5... | collective-permute-start | bytes 1572872 | tf_op jit(solution)/shard_map/ppermute | solution.py:368
  15.6 5.6 %collective-permute-start.4 = (f32[2,4,128,128]{3,2,1,0:T(8,128)S(1)}, f32[2,4,128,128]{3,2,1,0:T(8,128)S(1)}, u32[]{:S(2)}, u32[]{:S(2)}) collective-permute-start(f32[2,4,128,128]{3,2,1,0:T(8,128)S(1)} %collective-permute-done.2.r2), channel_id=1, source_target_pairs={{1,0},{0,1},{17,16},{16,17},{3,2},{2,3},{19,18},{18,19},{5,4},{4,5... | collective-permute-start | bytes 1572872 | tf_op jit(solution)/shard_map/ppermute | solution.py:368
  15.6 8.7 %collective-permute-start.7 = (f32[1,4,128,128]{3,2,1,0:T(8,128)S(1)}, f32[1,4,128,128]{3,2,1,0:T(8,128)S(1)}, u32[]{:S(2)}, u32[]{:S(2)}) collective-permute-start(f32[1,4,128,128]{3,2,1,0:T(8,128)S(1)} %get-tuple-element.43), channel_id=1, source_target_pairs={{15,1},{1,4},{4,9},{9,13},{13,15},{2,12},{12,8},{8,5},{5,0},{0,2},... | collective-permute-start | bytes 786440 | tf_op jit(solution)/shard_map/ppermute | solution.py:368
  18.0 8.7 %collective-permute-start.6 = (f32[1,4,128,128]{3,2,1,0:T(8,128)S(1)}, f32[1,4,128,128]{3,2,1,0:T(8,128)S(1)}, u32[]{:S(2)}, u32[]{:S(2)}) collective-permute-start(f32[1,4,128,128]{3,2,1,0:T(8,128)S(1)} %get-tuple-element.44), channel_id=1, source_target_pairs={{15,1},{1,4},{4,9},{9,13},{13,15},{2,12},{12,8},{8,5},{5,0},{0,2},... | collective-permute-start | bytes 786440 | tf_op jit(solution)/shard_map/ppermute | solution.py:368
  21.2 5.7 %collective-permute-start.10 = (f32[2,4,128,128]{3,2,1,0:T(8,128)S(1)}, f32[2,4,128,128]{3,2,1,0:T(8,128)S(1)}, u32[]{:S(2)}, u32[]{:S(2)}) collective-permute-start(f32[2,4,128,128]{3,2,1,0:T(8,128)S(1)} %collective-permute-done.5.r3), channel_id=1, source_target_pairs={{1,0},{0,1},{17,16},{16,17},{3,2},{2,3},{19,18},{18,19},{5,4},{4,5... | collective-permute-start | bytes 1572872 | tf_op jit(solution)/shard_map/ppermute | solution.py:368
  24.3 2.5 %collective-permute-start.8 = (f32[1,4,128,128]{3,2,1,0:T(8,128)S(1)}, f32[1,4,128,128]{3,2,1,0:T(8,128)S(1)}, u32[]{:S(2)}, u32[]{:S(2)}) collective-permute-start(f32[1,4,128,128]{3,2,1,0:T(8,128)S(1)} %collective-permute-done.7.r4a), channel_id=1, source_target_pairs={{1,0},{0,1},{17,16},{16,17},{3,2},{2,3},{19,18},{18,19},{5,4},{4,5... | collective-permute-start | bytes 786440 | tf_op jit(solution)/shard_map/ppermute | solution.py:368
  26.8 1.6 %collective-permute-start.9 = (f32[1,4,128,128]{3,2,1,0:T(8,128)S(1)}, f32[1,4,128,128]{3,2,1,0:T(8,128)S(1)}, u32[]{:S(2)}, u32[]{:S(2)}) collective-permute-start(f32[1,4,128,128]{3,2,1,0:T(8,128)S(1)} %collective-permute-done.6.r4b), channel_id=1, source_target_pairs={{1,0},{0,1},{17,16},{16,17},{3,2},{2,3},{19,18},{18,19},{5,4},{4,5... | collective-permute-start | bytes 786440 | tf_op jit(solution)/shard_map/ppermute | solution.py:368

commit v29 on v26

--- a/solution.py
+++ b/solution.py
@@ -384,7 +384,10 @@
         up[:last] + down + [(0, 1, up_lane[0])],
         [up[last], up[-1], (last, 1, down_lane[last])],
     ]
-    second = [up, down]
+    second = [
+        up[:-1] + [(last, 1, down_lane[last]), up[-1]],
+        down[:-1] + [(0, 1, up_lane[0]), down[-1]],
+    ]
 
     def received(hops):
         planes, senders = [], []

time: 31.8 us -> 31.8 us (level)
  waiting for transfers between devices: 6.82 us -> 9.84 us
  starting transfers between devices: 13.7 us -> 10.7 us
    ppermute x10, starting transfers between devices: 11.5 us -> 8.45 us  [move(): return lax.ppermute(block, AXES, route)]
    ppermute x10, waiting for transfers between devices: 3.61 us -> 6.25 us  [move(): return lax.ppermute(block, AXES, route)]
    ppermute x1, waiting for transfers between devices: 3.21 us -> 3.59 us  [move_only(): return lax.ppermute(block, AXES, route)]
where the time goes in v29:
time: 31.8 us; the launch traced here: 31.5 us
  starting transfers between devices  10.7 us (34%)
  waiting for transfers between devices  9.84 us (31%)
  Pallas kernels  8.44 us (27%)
  other arithmetic  2.24 us (7%)
    ppermute x10, starting transfers between devices, move(): return lax.ppermute(block, AXES, route)  8.45 us
    ppermute x10, waiting for transfers between devices, move(): return lax.ppermute(block, AXES, route)  6.25 us
    ppermute x1, waiting for transfers between devices, move_only(): return lax.ppermute(block, AXES, route)  3.59 us
    pallas_call x1, Pallas kernels, gather_local(): pl.pallas_call(functools.partial(early_kernel, tables), out_shape=[jax.Sh...  3.09 us
    pallas_call x1, Pallas kernels, gather_local(): pl.pallas_call(functools.partial(late_kernel, tables), out_shape=[jax.Sha...  3.02 us
    pallas_call x2, Pallas kernels, add_to_square(): pl.pallas_call(functools.partial(kernel, tables), out_shape=dense, in_spe...  2.34 us
    ppermute x1, starting transfers between devices, move_only(): return lax.ppermute(block, AXES, route)  2.28 us
    reduce_sum x1, other arithmetic, slot_table(): count = jnp.sum(here.astype(jnp.int32), axis=1, keepdims=True)  0.8 us
  transfers between devices with their start and end apart: 11, of which 5 were waited for; matrix products, arithmetic and copies ran while one was open for 7% of the time, Pallas kernels for 17%

profile of v29, /device:TPU:0, one launch (start us, length us, event | category | flops | bytes accessed | tf_op | source)
XLA Modules:
  0.0 31.5 jit_solution(5803911189831036344)
XLA Ops:
  0.0 2.9 %collective-permute-start = (f32[2,4,128,128]{3,2,1,0:T(8,128)}, f32[2,4,128,128]{3,2,1,0:T(8,128)S(1)}, u32[]{:S(2)}, u32[]{:S(2)}) collective-permute-start(f32[2,4,128,128]{3,2,1,0:T(8,128)} %own_hbm.1), channel_id=1, source_target_pairs={{3,1},{1,4},{4,9},{9,12},{12,8},{8,5},{5,0},{0,2},{2,3},{14,13},{1... | collective-permute-start | bytes 1572872 | tf_op jit(solution)/shard_map/ppermute | solution.py:369
  2.9 0.2 collective-permute-start.1
  3.1 0.8 %fusion.1 = (s32[8]{0:T(128)S(1)}, s32[8,8]{1,0:T(8,128)S(1)}) fusion(s32[8,16]{1,0:T(8,128)} %param.3), kind=kLoop, calls=%fused_computation.7 | loop fusion | flops 184 | bytes 544 | tf_op jit(solution)/shard_map/reduce_sum | solution.py:334
  3.9 0.1 fusion
  4.1 0.2 convert_reduce_fusion
  4.3 0.8 %collective-permute-done.1.own_swap = f32[2,4,128,128]{3,2,1,0:T(8,128)S(1)} collective-permute-done((f32[2,4,128,128]{3,2,1,0:T(8,128)}, f32[2,4,128,128]{3,2,1,0:T(8,128)S(1)}, u32[]{:S(2)}, u32[]{:S(2)}) %collective-permute-start.1) | collective-permute-done | bytes 524320 | tf_op jit(solution)/shard_map/ppermute | solution.py:369
  5.1 2.3 %collective-permute-start.2 = (f32[2,4,128,128]{3,2,1,0:T(8,128)S(1)}, f32[2,4,128,128]{3,2,1,0:T(8,128)S(1)}, u32[]{:S(2)}, u32[]{:S(2)}) collective-permute-start(f32[2,4,128,128]{3,2,1,0:T(8,128)S(1)} %collective-permute-done.1.own_swap), channel_id=1, source_target_pairs={{1,4},{4,9},{9,13},{13,15},{12,8},{8,5},{5,0},{0,2},{17,20},{20,25... | collective-permute-start | bytes 1572872 | tf_op jit(solution)/shard_map/ppermute | solution.py:377
  7.3 0.1 add_select_fusion
  7.5 0.1 copy.13
  7.5 0.2 select_reduce_fusion
  7.8 0.7 %compare_select_fusion = s32[8,8]{1,0:T(8,128)S(1)} fusion(s32[8,8]{1,0:T(8,128)S(1)} %select_reduce_fusion, s32[8,16]{1,0:T(8,128)} %param.3), kind=kLoop, calls=%fused_computation.5 | loop fusion | flops 192 | bytes 768 | tf_op jit(solution)/shard_map/jit(_where)/select_n | solution.py:342
  8.5 0.1 pad_add_fusion.table_ref
  8.5 1.4 %collective-permute-done.r1 = f32[2,4,128,128]{3,2,1,0:T(8,128)S(1)} collective-permute-done((f32[2,4,128,128]{3,2,1,0:T(8,128)}, f32[2,4,128,128]{3,2,1,0:T(8,128)S(1)}, u32[]{:S(2)}, u32[]{:S(2)}) %collective-permute-start) | collective-permute-done | bytes 524320 | tf_op jit(solution)/shard_map/ppermute | solution.py:369
  10.0 0.0 collective-permute-start.5
  10.0 2.0 %collective-permute-start.3 = (f32[2,4,128,128]{3,2,1,0:T(8,128)S(1)}, f32[2,4,128,128]{3,2,1,0:T(8,128)S(1)}, u32[]{:S(2)}, u32[]{:S(2)}) collective-permute-start(f32[2,4,128,128]{3,2,1,0:T(8,128)S(1)} %collective-permute-done.r1), channel_id=1, source_target_pairs={{1,0},{0,1},{17,16},{16,17},{3,2},{2,3},{19,18},{18,19},{5,4},{4,5... | collective-permute-start | bytes 1572872 | tf_op jit(solution)/shard_map/ppermute | solution.py:369
  12.0 3.6 %collective-permute-done.2.r2 = f32[2,4,128,128]{3,2,1,0:T(8,128)S(1)} collective-permute-done((f32[2,4,128,128]{3,2,1,0:T(8,128)S(1)}, f32[2,4,128,128]{3,2,1,0:T(8,128)S(1)}, u32[]{:S(2)}, u32[]{:S(2)}) %collective-permute-start.2) | collective-permute-done | bytes 524320 | tf_op jit(solution)/shard_map/ppermute | solution.py:377
  15.6 0.0 collective-permute-start.4
  15.6 2.6 %collective-permute-start.7 = (f32[1,4,128,128]{3,2,1,0:T(8,128)S(1)}, f32[1,4,128,128]{3,2,1,0:T(8,128)S(1)}, u32[]{:S(2)}, u32[]{:S(2)}) collective-permute-start(f32[1,4,128,128]{3,2,1,0:T(8,128)S(1)} %get-tuple-element.43), channel_id=1, source_target_pairs={{15,1},{1,4},{4,9},{9,13},{13,14},{14,15},{2,12},{12,8},{8,5},{5,0... | collective-permute-start | bytes 786440 | tf_op jit(solution)/shard_map/ppermute | solution.py:369
  18.2 0.1 collective-permute-start.6
  18.2 2.9 %collective-permute-done.5.r3 = f32[2,4,128,128]{3,2,1,0:T(8,128)S(1)} collective-permute-done((f32[2,4,128,128]{3,2,1,0:T(8,128)S(1)}, f32[2,4,128,128]{3,2,1,0:T(8,128)S(1)}, u32[]{:S(2)}, u32[]{:S(2)}) %collective-permute-start.5) | collective-permute-done | bytes 524320 | tf_op jit(solution)/shard_map/ppermute | solution.py:369
  21.2 0.0 collective-permute-start.10
  21.2 0.0 collective-permute-done.3.t1
  21.2 0.0 collective-permute-done.4.t2
  21.2 3.1 %early.1 = (bf16[1024,1024]{1,0:T(8,128)(2,1)S(1)}, bf16[1024,1024]{1,0:T(8,128)(2,1)S(1)}, bf16[512,1024]{1,0:T(8,128)(2,1)S(1)}, f32[256,1024]{1,0:T(8,128)S(1)}, s32[8,128]{1,0:T(8,128)S(1)}) custom-call(s32[8,9]{1,0:T(8,128)S(1)} %pad_add_fusion.table_ref, f32[2,4,128,128]{3,2,1,0:T(8,128)} %own_hbm.1, ...), custom_call_target="tpu_custom_call" | custom-call | tf_op jit(solution)/shard_map/early/pallas_call | solution.py:427
  24.3 0.0 collective-permute-done.7.r4a
  24.3 0.6 %collective-permute-start.8 = (f32[1,4,128,128]{3,2,1,0:T(8,128)S(1)}, f32[1,4,128,128]{3,2,1,0:T(8,128)S(1)}, u32[]{:S(2)}, u32[]{:S(2)}) collective-permute-start(f32[1,4,128,128]{3,2,1,0:T(8,128)S(1)} %collective-permute-done.7.r4a), channel_id=1, source_target_pairs={{1,0},{0,1},{17,16},{16,17},{3,2},{2,3},{19,18},{18,19},{5,4},{4,5... | collective-permute-start | bytes 786440 | tf_op jit(solution)/shard_map/ppermute | solution.py:369
  24.8 0.8 %waiting.1 = (bf16[1024,1024]{1,0:T(8,128)(2,1)S(1)}, bf16[1024,1024]{1,0:T(8,128)(2,1)S(1)}, f32[256,1024]{1,0:T(8,128)S(1)}) custom-call(s32[8,128]{1,0:T(8,128)S(1)} %get-tuple-element.26.notes_ref, f32[1,4,128,128]{3,2,1,0:T(8,128)S(1)} %collective-permute-done.7.r4a, ...), custom_call_target="tpu_custom_call", output_to_operand_aliasing={{0}: (2, {}), {1}: (3, {}), {2}: (5, {})} | custom-call | tf_op jit(solution)/shard_map/waiting/pallas_call | solution.py:449
  25.7 1.1 %collective-permute-done.6.r4b = f32[1,4,128,128]{3,2,1,0:T(8,128)S(1)} collective-permute-done((f32[1,4,128,128]{3,2,1,0:T(8,128)S(1)}, f32[1,4,128,128]{3,2,1,0:T(8,128)S(1)}, u32[]{:S(2)}, u32[]{:S(2)}) %collective-permute-start.6) | collective-permute-done | bytes 262176 | tf_op jit(solution)/shard_map/ppermute | solution.py:369
  26.8 0.1 collective-permute-start.9
  26.9 1.5 %middle.1 = (bf16[1024,1024]{1,0:T(8,128)(2,1)S(1)}, bf16[1024,1024]{1,0:T(8,128)(2,1)S(1)}, f32[256,1024]{1,0:T(8,128)S(1)}) custom-call(s32[8,128]{1,0:T(8,128)S(1)} %get-tuple-element.26.notes_ref, f32[1,4,128,128]{3,2,1,0:T(8,128)S(1)} %collective-permute-done.6.r4b, ...), custom_call_target="tpu_custom_call", output_to_operand_aliasing={{0}: (4, {}), {1}: (5, {}), {2}: (7, {})} | custom-call | tf_op jit(solution)/shard_map/middle/pallas_call | solution.py:449
  28.4 0.0 collective-permute-done.9.t4b
  28.4 3.0 %late.1 = (f32[2,4,128,128]{3,2,1,0:T(8,128)}, bf16[1024,1024]{1,0:T(8,128)(2,1)S(1)}, bf16[1024,1024]{1,0:T(8,128)(2,1)S(1)}, f32[256,1024]{1,0:T(8,128)S(1)}) custom-call(s32[8,128]{1,0:T(8,128)S(1)} %get-tuple-element.26.notes_ref, f32[1,4,128,128]{3,2,1,0:T(8,128)S(1)} %collective-permute-done.9.t4b, ...), custom_call_target="tpu_custom_call", output_to_operand_aliasing={{1}: (2, {}), {2}: (3, {}), {3}: (5, {})} | custom-call | tf_op jit(solution)/shard_map/late/pallas_call | solution.py:463
  (6 shorter events, 0.1 us)
Async XLA Ops:
  0.0 10.0 %collective-permute-start = (f32[2,4,128,128]{3,2,1,0:T(8,128)}, f32[2,4,128,128]{3,2,1,0:T(8,128)S(1)}, u32[]{:S(2)}, u32[]{:S(2)}) collective-permute-start(f32[2,4,128,128]{3,2,1,0:T(8,128)} %own_hbm.1), channel_id=1, source_target_pairs={{3,1},{1,4},{4,9},{9,12},{12,8},{8,5},{5,0},{0,2},{2,3},{14,13},{1... | collective-permute-start | bytes 1572872 | tf_op jit(solution)/shard_map/ppermute | solution.py:369
  2.9 2.1 %collective-permute-start.1 = (f32[2,4,128,128]{3,2,1,0:T(8,128)}, f32[2,4,128,128]{3,2,1,0:T(8,128)S(1)}, u32[]{:S(2)}, u32[]{:S(2)}) collective-permute-start(f32[2,4,128,128]{3,2,1,0:T(8,128)} %own_hbm.1), channel_id=1, source_target_pairs={{1,0},{0,1},{17,16},{16,17},{3,2},{2,3},{19,18},{18,19},{5,4},{4,5... | collective-permute-start | bytes 1572872 | tf_op jit(solution)/shard_map/ppermute | solution.py:369
  5.1 10.5 %collective-permute-start.2 = (f32[2,4,128,128]{3,2,1,0:T(8,128)S(1)}, f32[2,4,128,128]{3,2,1,0:T(8,128)S(1)}, u32[]{:S(2)}, u32[]{:S(2)}) collective-permute-start(f32[2,4,128,128]{3,2,1,0:T(8,128)S(1)} %collective-permute-done.1.own_swap), channel_id=1, source_target_pairs={{1,4},{4,9},{9,13},{13,15},{12,8},{8,5},{5,0},{0,2},{17,20},{20,25... | collective-permute-start | bytes 1572872 | tf_op jit(solution)/shard_map/ppermute | solution.py:377
  10.0 11.2 %collective-permute-start.5 = (f32[2,4,128,128]{3,2,1,0:T(8,128)S(1)}, f32[2,4,128,128]{3,2,1,0:T(8,128)S(1)}, u32[]{:S(2)}, u32[]{:S(2)}) collective-permute-start(f32[2,4,128,128]{3,2,1,0:T(8,128)S(1)} %collective-permute-done.r1), channel_id=1, source_target_pairs={{15,1},{1,4},{4,9},{9,13},{13,14},{14,15},{2,12},{12,8},{8,5},{5,0... | collective-permute-start | bytes 1572872 | tf_op jit(solution)/shard_map/ppermute | solution.py:369
  10.0 11.2 %collective-permute-start.3 = (f32[2,4,128,128]{3,2,1,0:T(8,128)S(1)}, f32[2,4,128,128]{3,2,1,0:T(8,128)S(1)}, u32[]{:S(2)}, u32[]{:S(2)}) collective-permute-start(f32[2,4,128,128]{3,2,1,0:T(8,128)S(1)} %collective-permute-done.r1), channel_id=1, source_target_pairs={{1,0},{0,1},{17,16},{16,17},{3,2},{2,3},{19,18},{18,19},{5,4},{4,5... | collective-permute-start | bytes 1572872 | tf_op jit(solution)/shard_map/ppermute | solution.py:369
  15.6 5.6 %collective-permute-start.4 = (f32[2,4,128,128]{3,2,1,0:T(8,128)S(1)}, f32[2,4,128,128]{3,2,1,0:T(8,128)S(1)}, u32[]{:S(2)}, u32[]{:S(2)}) collective-permute-start(f32[2,4,128,128]{3,2,1,0:T(8,128)S(1)} %collective-permute-done.2.r2), channel_id=1, source_target_pairs={{1,0},{0,1},{17,16},{16,17},{3,2},{2,3},{19,18},{18,19},{5,4},{4,5... | collective-permute-start | bytes 1572872 | tf_op jit(solution)/shard_map/ppermute | solution.py:369
  15.6 8.7 %collective-permute-start.7 = (f32[1,4,128,128]{3,2,1,0:T(8,128)S(1)}, f32[1,4,128,128]{3,2,1,0:T(8,128)S(1)}, u32[]{:S(2)}, u32[]{:S(2)}) collective-permute-start(f32[1,4,128,128]{3,2,1,0:T(8,128)S(1)} %get-tuple-element.43), channel_id=1, source_target_pairs={{15,1},{1,4},{4,9},{9,13},{13,14},{14,15},{2,12},{12,8},{8,5},{5,0... | collective-permute-start | bytes 786440 | tf_op jit(solution)/shard_map/ppermute | solution.py:369
  18.2 8.6 %collective-permute-start.6 = (f32[1,4,128,128]{3,2,1,0:T(8,128)S(1)}, f32[1,4,128,128]{3,2,1,0:T(8,128)S(1)}, u32[]{:S(2)}, u32[]{:S(2)}) collective-permute-start(f32[1,4,128,128]{3,2,1,0:T(8,128)S(1)} %get-tuple-element.44), channel_id=1, source_target_pairs={{15,1},{1,4},{4,9},{9,13},{13,14},{14,15},{2,12},{12,8},{8,5},{5,0... | collective-permute-start | bytes 786440 | tf_op jit(solution)/shard_map/ppermute | solution.py:369
  21.2 5.7 %collective-permute-start.10 = (f32[2,4,128,128]{3,2,1,0:T(8,128)S(1)}, f32[2,4,128,128]{3,2,1,0:T(8,128)S(1)}, u32[]{:S(2)}, u32[]{:S(2)}) collective-permute-start(f32[2,4,128,128]{3,2,1,0:T(8,128)S(1)} %collective-permute-done.5.r3), channel_id=1, source_target_pairs={{1,0},{0,1},{17,16},{16,17},{3,2},{2,3},{19,18},{18,19},{5,4},{4,5... | collective-permute-start | bytes 1572872 | tf_op jit(solution)/shard_map/ppermute | solution.py:369
  24.3 2.5 %collective-permute-start.8 = (f32[1,4,128,128]{3,2,1,0:T(8,128)S(1)}, f32[1,4,128,128]{3,2,1,0:T(8,128)S(1)}, u32[]{:S(2)}, u32[]{:S(2)}) collective-permute-start(f32[1,4,128,128]{3,2,1,0:T(8,128)S(1)} %collective-permute-done.7.r4a), channel_id=1, source_target_pairs={{1,0},{0,1},{17,16},{16,17},{3,2},{2,3},{19,18},{18,19},{5,4},{4,5... | collective-permute-start | bytes 786440 | tf_op jit(solution)/shard_map/ppermute | solution.py:369
  26.8 1.6 %collective-permute-start.9 = (f32[1,4,128,128]{3,2,1,0:T(8,128)S(1)}, f32[1,4,128,128]{3,2,1,0:T(8,128)S(1)}, u32[]{:S(2)}, u32[]{:S(2)}) collective-permute-start(f32[1,4,128,128]{3,2,1,0:T(8,128)S(1)} %collective-permute-done.6.r4b), channel_id=1, source_target_pairs={{1,0},{0,1},{17,16},{16,17},{3,2},{2,3},{19,18},{18,19},{5,4},{4,5... | collective-permute-start | bytes 786440 | tf_op jit(solution)/shard_map/ppermute | solution.py:369

commit v30 on v26

--- a/solution.py
+++ b/solution.py
@@ -376,7 +376,7 @@
         route = [(index(g, a), index(g, b)) for g in range(groups) for a, b in pairs]
         return lax.ppermute(block, AXES, route)
 
-    down_lane = [1 if z == 1 else 0 for z in range(chains)]
+    down_lane = [1 if z in (1, 2) else 0 for z in range(chains)]
     up_lane = [1 - c for c in down_lane]
     up = [(z, 0, up_lane[z]) for z in range(chains)] + [(last, 1, up_lane[last])]
     down = [(z, 0, down_lane[z]) for z in reversed(range(chains))] + [(0, 1, down_lane[0])]

time: 31.8 us -> 32.4 us (1.019)
  the two profiles are of different devices: /device:TPU:0 before, /device:TPU:25 now
where the time goes in v30:
time: 32.4 us; the launch traced here: 32.1 us
  waiting for transfers between devices  13.2 us (41%)
  Pallas kernels  8.42 us (26%)
  starting transfers between devices  8.08 us (25%)
  other arithmetic  2.24 us (7%)
    ppermute x10, waiting for transfers between devices, move(): return lax.ppermute(block, AXES, route)  8.24 us
    ppermute x10, starting transfers between devices, move(): return lax.ppermute(block, AXES, route)  5.14 us
    ppermute x1, waiting for transfers between devices, move_only(): return lax.ppermute(block, AXES, route)  4.92 us
    pallas_call x1, Pallas kernels, gather_local(): pl.pallas_call(functools.partial(early_kernel, tables), out_shape=[jax.Sh...  3.09 us
    pallas_call x1, Pallas kernels, gather_local(): pl.pallas_call(functools.partial(late_kernel, tables), out_shape=[jax.Sha...  3 us
    ppermute x1, starting transfers between devices, move_only(): return lax.ppermute(block, AXES, route)  2.95 us
    pallas_call x2, Pallas kernels, add_to_square(): pl.pallas_call(functools.partial(kernel, tables), out_shape=dense, in_spe...  2.32 us
    reduce_sum x1, other arithmetic, slot_table(): count = jnp.sum(here.astype(jnp.int32), axis=1, keepdims=True)  0.8 us
  transfers between devices with their start and end apart: 11, of which 6 were waited for; matrix products, arithmetic and copies ran while one was open for 7% of the time, Pallas kernels for 17%

profile of v30, /device:TPU:25, one launch (start us, length us, event | category | flops | bytes accessed | tf_op | source)
XLA Modules:
  0.0 32.1 jit_solution(7103419875581862174)
XLA Ops:
  0.0 1.2 %collective-permute-start = (f32[2,4,128,128]{3,2,1,0:T(8,128)}, f32[2,4,128,128]{3,2,1,0:T(8,128)S(1)}, u32[]{:S(2)}, u32[]{:S(2)}) collective-permute-start(f32[2,4,128,128]{3,2,1,0:T(8,128)} %own_hbm.1), channel_id=1, source_target_pairs={{3,1},{1,4},{4,8},{8,12},{12,9},{9,5},{5,0},{0,2},{2,3},{14,13},{1... | collective-permute-start | bytes 1572872 | tf_op jit(solution)/shard_map/ppermute | solution.py:369
  1.2 0.0 collective-permute-start.1
  1.2 0.8 %fusion.1 = (s32[8]{0:T(128)S(1)}, s32[8,8]{1,0:T(8,128)S(1)}) fusion(s32[8,16]{1,0:T(8,128)} %param.3), kind=kLoop, calls=%fused_computation.7 | loop fusion | flops 184 | bytes 544 | tf_op jit(solution)/shard_map/reduce_sum | solution.py:334
  2.0 0.1 fusion
  2.1 0.2 convert_reduce_fusion
  2.4 1.0 %collective-permute-done.1.own_swap = f32[2,4,128,128]{3,2,1,0:T(8,128)S(1)} collective-permute-done((f32[2,4,128,128]{3,2,1,0:T(8,128)}, f32[2,4,128,128]{3,2,1,0:T(8,128)S(1)}, u32[]{:S(2)}, u32[]{:S(2)}) %collective-permute-start.1) | collective-permute-done | bytes 524320 | tf_op jit(solution)/shard_map/ppermute | solution.py:369
  3.3 2.9 %collective-permute-start.2 = (f32[2,4,128,128]{3,2,1,0:T(8,128)S(1)}, f32[2,4,128,128]{3,2,1,0:T(8,128)S(1)}, u32[]{:S(2)}, u32[]{:S(2)}) collective-permute-start(f32[2,4,128,128]{3,2,1,0:T(8,128)S(1)} %collective-permute-done.1.own_swap), channel_id=1, source_target_pairs={{1,4},{4,8},{8,13},{13,15},{12,9},{9,5},{5,0},{0,2},{17,20},{20,24... | collective-permute-start | bytes 1572872 | tf_op jit(solution)/shard_map/ppermute | solution.py:377
  6.3 0.1 add_select_fusion
  6.4 0.1 copy.13
  6.5 0.2 select_reduce_fusion
  6.7 0.7 %compare_select_fusion = s32[8,8]{1,0:T(8,128)S(1)} fusion(s32[8,8]{1,0:T(8,128)S(1)} %select_reduce_fusion, s32[8,16]{1,0:T(8,128)} %param.3), kind=kLoop, calls=%fused_computation.5 | loop fusion | flops 192 | bytes 768 | tf_op jit(solution)/shard_map/jit(_where)/select_n | solution.py:342
  7.4 0.1 pad_add_fusion.table_ref
  7.5 1.7 %collective-permute-done.r1 = f32[2,4,128,128]{3,2,1,0:T(8,128)S(1)} collective-permute-done((f32[2,4,128,128]{3,2,1,0:T(8,128)}, f32[2,4,128,128]{3,2,1,0:T(8,128)S(1)}, u32[]{:S(2)}, u32[]{:S(2)}) %collective-permute-start) | collective-permute-done | bytes 524320 | tf_op jit(solution)/shard_map/ppermute | solution.py:369
  9.1 0.3 collective-permute-start.5
  9.5 0.6 %collective-permute-start.3 = (f32[2,4,128,128]{3,2,1,0:T(8,128)S(1)}, f32[2,4,128,128]{3,2,1,0:T(8,128)S(1)}, u32[]{:S(2)}, u32[]{:S(2)}) collective-permute-start(f32[2,4,128,128]{3,2,1,0:T(8,128)S(1)} %collective-permute-done.r1), channel_id=1, source_target_pairs={{1,0},{0,1},{17,16},{16,17},{3,2},{2,3},{19,18},{18,19},{5,4},{4,5... | collective-permute-start | bytes 1572872 | tf_op jit(solution)/shard_map/ppermute | solution.py:369
  10.1 4.9 %collective-permute-done.2.r2 = f32[2,4,128,128]{3,2,1,0:T(8,128)S(1)} collective-permute-done((f32[2,4,128,128]{3,2,1,0:T(8,128)S(1)}, f32[2,4,128,128]{3,2,1,0:T(8,128)S(1)}, u32[]{:S(2)}, u32[]{:S(2)}) %collective-permute-start.2) | collective-permute-done | bytes 524320 | tf_op jit(solution)/shard_map/ppermute | solution.py:377
  15.0 0.0 collective-permute-start.4
  15.0 0.4 %collective-permute-start.7 = (f32[1,4,128,128]{3,2,1,0:T(8,128)S(1)}, f32[1,4,128,128]{3,2,1,0:T(8,128)S(1)}, u32[]{:S(2)}, u32[]{:S(2)}) collective-permute-start(f32[1,4,128,128]{3,2,1,0:T(8,128)S(1)} %get-tuple-element.43), channel_id=1, source_target_pairs={{15,1},{1,4},{4,8},{8,13},{13,15},{2,12},{12,9},{9,5},{5,0},{0,2},... | collective-permute-start | bytes 786440 | tf_op jit(solution)/shard_map/ppermute | solution.py:369
  15.5 0.5 %collective-permute-start.6 = (f32[1,4,128,128]{3,2,1,0:T(8,128)S(1)}, f32[1,4,128,128]{3,2,1,0:T(8,128)S(1)}, u32[]{:S(2)}, u32[]{:S(2)}) collective-permute-start(f32[1,4,128,128]{3,2,1,0:T(8,128)S(1)} %get-tuple-element.44), channel_id=1, source_target_pairs={{15,1},{1,4},{4,8},{8,13},{13,15},{2,12},{12,9},{9,5},{5,0},{0,2},... | collective-permute-start | bytes 786440 | tf_op jit(solution)/shard_map/ppermute | solution.py:369
  16.0 4.9 %collective-permute-done.5.r3 = f32[2,4,128,128]{3,2,1,0:T(8,128)S(1)} collective-permute-done((f32[2,4,128,128]{3,2,1,0:T(8,128)S(1)}, f32[2,4,128,128]{3,2,1,0:T(8,128)S(1)}, u32[]{:S(2)}, u32[]{:S(2)}) %collective-permute-start.5) | collective-permute-done | bytes 524320 | tf_op jit(solution)/shard_map/ppermute | solution.py:369
  20.9 1.0 %collective-permute-start.10 = (f32[2,4,128,128]{3,2,1,0:T(8,128)S(1)}, f32[2,4,128,128]{3,2,1,0:T(8,128)S(1)}, u32[]{:S(2)}, u32[]{:S(2)}) collective-permute-start(f32[2,4,128,128]{3,2,1,0:T(8,128)S(1)} %collective-permute-done.5.r3), channel_id=1, source_target_pairs={{1,0},{0,1},{17,16},{16,17},{3,2},{2,3},{19,18},{18,19},{5,4},{4,5... | collective-permute-start | bytes 1572872 | tf_op jit(solution)/shard_map/ppermute | solution.py:369
  21.9 0.0 collective-permute-done.3.t1
  22.0 3.1 %early.1 = (bf16[1024,1024]{1,0:T(8,128)(2,1)S(1)}, bf16[1024,1024]{1,0:T(8,128)(2,1)S(1)}, bf16[512,1024]{1,0:T(8,128)(2,1)S(1)}, f32[256,1024]{1,0:T(8,128)S(1)}, s32[8,128]{1,0:T(8,128)S(1)}) custom-call(s32[8,9]{1,0:T(8,128)S(1)} %pad_add_fusion.table_ref, f32[2,4,128,128]{3,2,1,0:T(8,128)} %own_hbm.1, ...), custom_call_target="tpu_custom_call" | custom-call | tf_op jit(solution)/shard_map/early/pallas_call | solution.py:424
  25.1 0.0 collective-permute-done.7.r4a
  25.1 0.1 collective-permute-start.8
  25.2 0.8 %waiting.1 = (bf16[1024,1024]{1,0:T(8,128)(2,1)S(1)}, bf16[1024,1024]{1,0:T(8,128)(2,1)S(1)}, f32[256,1024]{1,0:T(8,128)S(1)}) custom-call(s32[8,128]{1,0:T(8,128)S(1)} %get-tuple-element.26.notes_ref, f32[1,4,128,128]{3,2,1,0:T(8,128)S(1)} %collective-permute-done.7.r4a, ...), custom_call_target="tpu_custom_call", output_to_operand_aliasing={{0}: (2, {}), {1}: (3, {}), {2}: (5, {})} | custom-call | tf_op jit(solution)/shard_map/waiting/pallas_call | solution.py:446
  26.0 0.6 %collective-permute-done.6.r4b = f32[1,4,128,128]{3,2,1,0:T(8,128)S(1)} collective-permute-done((f32[1,4,128,128]{3,2,1,0:T(8,128)S(1)}, f32[1,4,128,128]{3,2,1,0:T(8,128)S(1)}, u32[]{:S(2)}, u32[]{:S(2)}) %collective-permute-start.6) | collective-permute-done | bytes 262176 | tf_op jit(solution)/shard_map/ppermute | solution.py:369
  26.5 0.1 collective-permute-done.8.t4a
  26.7 0.9 %collective-permute-start.9 = (f32[1,4,128,128]{3,2,1,0:T(8,128)S(1)}, f32[1,4,128,128]{3,2,1,0:T(8,128)S(1)}, u32[]{:S(2)}, u32[]{:S(2)}) collective-permute-start(f32[1,4,128,128]{3,2,1,0:T(8,128)S(1)} %collective-permute-done.6.r4b), channel_id=1, source_target_pairs={{1,0},{0,1},{17,16},{16,17},{3,2},{2,3},{19,18},{18,19},{5,4},{4,5... | collective-permute-start | bytes 786440 | tf_op jit(solution)/shard_map/ppermute | solution.py:369
  27.6 1.5 %middle.1 = (bf16[1024,1024]{1,0:T(8,128)(2,1)S(1)}, bf16[1024,1024]{1,0:T(8,128)(2,1)S(1)}, f32[256,1024]{1,0:T(8,128)S(1)}) custom-call(s32[8,128]{1,0:T(8,128)S(1)} %get-tuple-element.26.notes_ref, f32[1,4,128,128]{3,2,1,0:T(8,128)S(1)} %collective-permute-done.6.r4b, ...), custom_call_target="tpu_custom_call", output_to_operand_aliasing={{0}: (4, {}), {1}: (5, {}), {2}: (7, {})} | custom-call | tf_op jit(solution)/shard_map/middle/pallas_call | solution.py:446
  29.1 0.0 collective-permute-done.9.t4b
  29.1 3.0 %late.1 = (f32[2,4,128,128]{3,2,1,0:T(8,128)}, bf16[1024,1024]{1,0:T(8,128)(2,1)S(1)}, bf16[1024,1024]{1,0:T(8,128)(2,1)S(1)}, f32[256,1024]{1,0:T(8,128)S(1)}) custom-call(s32[8,128]{1,0:T(8,128)S(1)} %get-tuple-element.26.notes_ref, f32[1,4,128,128]{3,2,1,0:T(8,128)S(1)} %collective-permute-done.9.t4b, ...), custom_call_target="tpu_custom_call", output_to_operand_aliasing={{1}: (2, {}), {2}: (3, {}), {3}: (5, {})} | custom-call | tf_op jit(solution)/shard_map/late/pallas_call | solution.py:460
  (6 shorter events, 0.1 us)
Async XLA Ops:
  0.0 9.1 %collective-permute-start = (f32[2,4,128,128]{3,2,1,0:T(8,128)}, f32[2,4,128,128]{3,2,1,0:T(8,128)S(1)}, u32[]{:S(2)}, u32[]{:S(2)}) collective-permute-start(f32[2,4,128,128]{3,2,1,0:T(8,128)} %own_hbm.1), channel_id=1, source_target_pairs={{3,1},{1,4},{4,8},{8,12},{12,9},{9,5},{5,0},{0,2},{2,3},{14,13},{1... | collective-permute-start | bytes 1572872 | tf_op jit(solution)/shard_map/ppermute | solution.py:369
  1.2 2.1 %collective-permute-start.1 = (f32[2,4,128,128]{3,2,1,0:T(8,128)}, f32[2,4,128,128]{3,2,1,0:T(8,128)S(1)}, u32[]{:S(2)}, u32[]{:S(2)}) collective-permute-start(f32[2,4,128,128]{3,2,1,0:T(8,128)} %own_hbm.1), channel_id=1, source_target_pairs={{1,0},{0,1},{17,16},{16,17},{3,2},{2,3},{19,18},{18,19},{5,4},{4,5... | collective-permute-start | bytes 1572872 | tf_op jit(solution)/shard_map/ppermute | solution.py:369
  3.3 11.7 %collective-permute-start.2 = (f32[2,4,128,128]{3,2,1,0:T(8,128)S(1)}, f32[2,4,128,128]{3,2,1,0:T(8,128)S(1)}, u32[]{:S(2)}, u32[]{:S(2)}) collective-permute-start(f32[2,4,128,128]{3,2,1,0:T(8,128)S(1)} %collective-permute-done.1.own_swap), channel_id=1, source_target_pairs={{1,4},{4,8},{8,13},{13,15},{12,9},{9,5},{5,0},{0,2},{17,20},{20,24... | collective-permute-start | bytes 1572872 | tf_op jit(solution)/shard_map/ppermute | solution.py:377
  9.1 11.8 %collective-permute-start.5 = (f32[2,4,128,128]{3,2,1,0:T(8,128)S(1)}, f32[2,4,128,128]{3,2,1,0:T(8,128)S(1)}, u32[]{:S(2)}, u32[]{:S(2)}) collective-permute-start(f32[2,4,128,128]{3,2,1,0:T(8,128)S(1)} %collective-permute-done.r1), channel_id=1, source_target_pairs={{15,1},{1,4},{4,8},{8,13},{13,15},{2,12},{12,9},{9,5},{5,0},{0,2},... | collective-permute-start | bytes 1572872 | tf_op jit(solution)/shard_map/ppermute | solution.py:369
  9.5 12.5 %collective-permute-start.3 = (f32[2,4,128,128]{3,2,1,0:T(8,128)S(1)}, f32[2,4,128,128]{3,2,1,0:T(8,128)S(1)}, u32[]{:S(2)}, u32[]{:S(2)}) collective-permute-start(f32[2,4,128,128]{3,2,1,0:T(8,128)S(1)} %collective-permute-done.r1), channel_id=1, source_target_pairs={{1,0},{0,1},{17,16},{16,17},{3,2},{2,3},{19,18},{18,19},{5,4},{4,5... | collective-permute-start | bytes 1572872 | tf_op jit(solution)/shard_map/ppermute | solution.py:369
  15.0 7.0 %collective-permute-start.4 = (f32[2,4,128,128]{3,2,1,0:T(8,128)S(1)}, f32[2,4,128,128]{3,2,1,0:T(8,128)S(1)}, u32[]{:S(2)}, u32[]{:S(2)}) collective-permute-start(f32[2,4,128,128]{3,2,1,0:T(8,128)S(1)} %collective-permute-done.2.r2), channel_id=1, source_target_pairs={{1,0},{0,1},{17,16},{16,17},{3,2},{2,3},{19,18},{18,19},{5,4},{4,5... | collective-permute-start | bytes 1572872 | tf_op jit(solution)/shard_map/ppermute | solution.py:369
  15.0 10.0 %collective-permute-start.7 = (f32[1,4,128,128]{3,2,1,0:T(8,128)S(1)}, f32[1,4,128,128]{3,2,1,0:T(8,128)S(1)}, u32[]{:S(2)}, u32[]{:S(2)}) collective-permute-start(f32[1,4,128,128]{3,2,1,0:T(8,128)S(1)} %get-tuple-element.43), channel_id=1, source_target_pairs={{15,1},{1,4},{4,8},{8,13},{13,15},{2,12},{12,9},{9,5},{5,0},{0,2},... | collective-permute-start | bytes 786440 | tf_op jit(solution)/shard_map/ppermute | solution.py:369
  15.5 11.1 %collective-permute-start.6 = (f32[1,4,128,128]{3,2,1,0:T(8,128)S(1)}, f32[1,4,128,128]{3,2,1,0:T(8,128)S(1)}, u32[]{:S(2)}, u32[]{:S(2)}) collective-permute-start(f32[1,4,128,128]{3,2,1,0:T(8,128)S(1)} %get-tuple-element.44), channel_id=1, source_target_pairs={{15,1},{1,4},{4,8},{8,13},{13,15},{2,12},{12,9},{9,5},{5,0},{0,2},... | collective-permute-start | bytes 786440 | tf_op jit(solution)/shard_map/ppermute | solution.py:369
  20.9 6.7 %collective-permute-start.10 = (f32[2,4,128,128]{3,2,1,0:T(8,128)S(1)}, f32[2,4,128,128]{3,2,1,0:T(8,128)S(1)}, u32[]{:S(2)}, u32[]{:S(2)}) collective-permute-start(f32[2,4,128,128]{3,2,1,0:T(8,128)S(1)} %collective-permute-done.5.r3), channel_id=1, source_target_pairs={{1,0},{0,1},{17,16},{16,17},{3,2},{2,3},{19,18},{18,19},{5,4},{4,5... | collective-permute-start | bytes 1572872 | tf_op jit(solution)/shard_map/ppermute | solution.py:369
  25.1 1.6 %collective-permute-start.8 = (f32[1,4,128,128]{3,2,1,0:T(8,128)S(1)}, f32[1,4,128,128]{3,2,1,0:T(8,128)S(1)}, u32[]{:S(2)}, u32[]{:S(2)}) collective-permute-start(f32[1,4,128,128]{3,2,1,0:T(8,128)S(1)} %collective-permute-done.7.r4a), channel_id=1, source_target_pairs={{1,0},{0,1},{17,16},{16,17},{3,2},{2,3},{19,18},{18,19},{5,4},{4,5... | collective-permute-start | bytes 786440 | tf_op jit(solution)/shard_map/ppermute | solution.py:369
  26.7 2.4 %collective-permute-start.9 = (f32[1,4,128,128]{3,2,1,0:T(8,128)S(1)}, f32[1,4,128,128]{3,2,1,0:T(8,128)S(1)}, u32[]{:S(2)}, u32[]{:S(2)}) collective-permute-start(f32[1,4,128,128]{3,2,1,0:T(8,128)S(1)} %collective-permute-done.6.r4b), channel_id=1, source_target_pairs={{1,0},{0,1},{17,16},{16,17},{3,2},{2,3},{19,18},{18,19},{5,4},{4,5... | collective-permute-start | bytes 786440 | tf_op jit(solution)/shard_map/ppermute | solution.py:369

commit v31 on v26

--- a/solution.py
+++ b/solution.py
@@ -169,6 +169,25 @@
             col = pl.ds(pl.multiple_of((code_of(r, w) & (2 * width - 1)) * edge, edge), edge)
             high[at, col] = jnp.zeros((edge, edge), jnp.bfloat16)
             low[at, col] = jnp.zeros((edge, edge), jnp.bfloat16)
+
+
+def add_row_blocks(piece, plane, r, code_of, left, high, low, part_ref):
+    _, width, edge, _ = piece.shape
+    act = 2 * width
+
+    @pl.when(plane >= 0)
+    def _():
+        at = pl.ds(pl.multiple_of((plane * 2 + r) * edge, edge), edge)
+        codes = [code_of(r, w) for w in range(width)]
+        cols = [pl.ds(pl.multiple_of((code & (act - 1)) * edge, edge), edge) for code in codes]
+        blocks = [jnp.where(code < act, piece[0, w], 0.0) for w, code in enumerate(codes)]
+        block_high, block_low = split(jnp.concatenate(blocks, axis=1))
+        more = stacked_dot(left[:, at], block_high, block_low)
+        sums = [part_ref[:, col] + more[:, w * edge : (w + 1) * edge] for w, col in enumerate(cols)]
+        for w, col in enumerate(cols):
+            part_ref[:, col] = sums[w]
+            high[at, col] = block_high[:, w * edge : (w + 1) * edge]
+            low[at, col] = block_low[:, w * edge : (w + 1) * edge]
 
 
 def last_row_blocks(piece, plane, r, code_of, left, high, low):
@@ -261,17 +280,10 @@
     store_piece(t3, there, noted_codes(notes, T3, width), high, low)
     store_piece(t4a, there, codes, high, low)
     clear_row(there, 1, codes, width, high, low)
-    edge, depth, tile = high.shape[0] // (2 * width), part_ref.shape[0], 512
-    _, cols, more = last_row_blocks(
-        r4b, here, 1, noted_codes(notes, R4, width), left, high, low
+    add_plane(there, left, high, low, part_ref)
+    add_row_blocks(
+        r4b, here, 1, noted_codes(notes, R4, width), left, high, low, part_ref
     )
-    rows = pl.ds(pl.multiple_of(jnp.maximum(there, 0) * depth, depth), depth)
-    for n in range(part_ref.shape[1] // tile):
-        wide = pl.ds(n * tile, tile)
-        plane = stacked_dot(left[:, rows], high[rows, wide], low[rows, wide])
-        part_ref[:, wide] += jnp.where(there >= 0, plane, 0.0)
-    for w, col in enumerate(cols):
-        part_ref[:, col] += more[:, w * edge : (w + 1) * edge]
 
 
 def late_kernel(

time: 31.8 us -> 31.8 us (level)
  no operation moved by 1% of the time
where the time goes in v31:
time: 31.8 us; the launch traced here: 31.4 us
  starting transfers between devices  13.7 us (43%)
  Pallas kernels  8.4 us (26%)
  waiting for transfers between devices  6.84 us (22%)
  other arithmetic  2.24 us (7%)
    ppermute x10, starting transfers between devices, move(): return lax.ppermute(block, AXES, route)  11.5 us
    ppermute x10, waiting for transfers between devices, move(): return lax.ppermute(block, AXES, route)  3.62 us
    ppermute x1, waiting for transfers between devices, move_only(): return lax.ppermute(block, AXES, route)  3.21 us
    pallas_call x1, Pallas kernels, gather_local(): pl.pallas_call(functools.partial(early_kernel, tables), out_shape=[jax.Sh...  3.09 us
    pallas_call x1, Pallas kernels, gather_local(): pl.pallas_call(functools.partial(late_kernel, tables), out_shape=[jax.Sha...  3 us
    pallas_call x2, Pallas kernels, add_to_square(): pl.pallas_call(functools.partial(kernel, tables), out_shape=dense, in_spe...  2.31 us
    ppermute x1, starting transfers between devices, move_only(): return lax.ppermute(block, AXES, route)  2.28 us
    reduce_sum x1, other arithmetic, slot_table(): count = jnp.sum(here.astype(jnp.int32), axis=1, keepdims=True)  0.8 us
  transfers between devices with their start and end apart: 11, of which 5 were waited for; matrix products, arithmetic and copies ran while one was open for 7% of the time, Pallas kernels for 17%

profile of v31, /device:TPU:0, one launch (start us, length us, event | category | flops | bytes accessed | tf_op | source)
XLA Modules:
  0.0 31.4 jit_solution(16001796753907922109)
XLA Ops:
  0.0 2.9 %collective-permute-start = (f32[2,4,128,128]{3,2,1,0:T(8,128)}, f32[2,4,128,128]{3,2,1,0:T(8,128)S(1)}, u32[]{:S(2)}, u32[]{:S(2)}) collective-permute-start(f32[2,4,128,128]{3,2,1,0:T(8,128)} %own_hbm.1), channel_id=1, source_target_pairs={{3,1},{1,4},{4,9},{9,12},{12,8},{8,5},{5,0},{0,2},{2,3},{14,13},{1... | collective-permute-start | bytes 1572872 | tf_op jit(solution)/shard_map/ppermute | solution.py:381
  2.9 0.2 collective-permute-start.1
  3.1 0.8 %fusion.1 = (s32[8]{0:T(128)S(1)}, s32[8,8]{1,0:T(8,128)S(1)}) fusion(s32[8,16]{1,0:T(8,128)} %param.3), kind=kLoop, calls=%fused_computation.7 | loop fusion | flops 184 | bytes 544 | tf_op jit(solution)/shard_map/reduce_sum | solution.py:346
  3.9 0.1 fusion
  4.1 0.2 convert_reduce_fusion
  4.3 0.8 %collective-permute-done.1.own_swap = f32[2,4,128,128]{3,2,1,0:T(8,128)S(1)} collective-permute-done((f32[2,4,128,128]{3,2,1,0:T(8,128)}, f32[2,4,128,128]{3,2,1,0:T(8,128)S(1)}, u32[]{:S(2)}, u32[]{:S(2)}) %collective-permute-start.1) | collective-permute-done | bytes 524320 | tf_op jit(solution)/shard_map/ppermute | solution.py:381
  5.1 2.3 %collective-permute-start.2 = (f32[2,4,128,128]{3,2,1,0:T(8,128)S(1)}, f32[2,4,128,128]{3,2,1,0:T(8,128)S(1)}, u32[]{:S(2)}, u32[]{:S(2)}) collective-permute-start(f32[2,4,128,128]{3,2,1,0:T(8,128)S(1)} %collective-permute-done.1.own_swap), channel_id=1, source_target_pairs={{1,4},{4,9},{9,13},{13,15},{12,8},{8,5},{5,0},{0,2},{17,20},{20,25... | collective-permute-start | bytes 1572872 | tf_op jit(solution)/shard_map/ppermute | solution.py:389
  7.3 0.1 add_select_fusion
  7.5 0.1 copy.13
  7.5 0.2 select_reduce_fusion
  7.8 0.7 %compare_select_fusion = s32[8,8]{1,0:T(8,128)S(1)} fusion(s32[8,8]{1,0:T(8,128)S(1)} %select_reduce_fusion, s32[8,16]{1,0:T(8,128)} %param.3), kind=kLoop, calls=%fused_computation.5 | loop fusion | flops 192 | bytes 768 | tf_op jit(solution)/shard_map/jit(_where)/select_n | solution.py:354
  8.5 0.1 pad_add_fusion.table_ref
  8.5 1.4 %collective-permute-done.r1 = f32[2,4,128,128]{3,2,1,0:T(8,128)S(1)} collective-permute-done((f32[2,4,128,128]{3,2,1,0:T(8,128)}, f32[2,4,128,128]{3,2,1,0:T(8,128)S(1)}, u32[]{:S(2)}, u32[]{:S(2)}) %collective-permute-start) | collective-permute-done | bytes 524320 | tf_op jit(solution)/shard_map/ppermute | solution.py:381
  10.0 2.4 %collective-permute-start.5 = (f32[2,4,128,128]{3,2,1,0:T(8,128)S(1)}, f32[2,4,128,128]{3,2,1,0:T(8,128)S(1)}, u32[]{:S(2)}, u32[]{:S(2)}) collective-permute-start(f32[2,4,128,128]{3,2,1,0:T(8,128)S(1)} %collective-permute-done.r1), channel_id=1, source_target_pairs={{15,1},{1,4},{4,9},{9,13},{13,15},{2,12},{12,8},{8,5},{5,0},{0,2},... | collective-permute-start | bytes 1572872 | tf_op jit(solution)/shard_map/ppermute | solution.py:381
  12.3 0.0 collective-permute-start.3
  12.3 3.2 %collective-permute-done.2.r2 = f32[2,4,128,128]{3,2,1,0:T(8,128)S(1)} collective-permute-done((f32[2,4,128,128]{3,2,1,0:T(8,128)S(1)}, f32[2,4,128,128]{3,2,1,0:T(8,128)S(1)}, u32[]{:S(2)}, u32[]{:S(2)}) %collective-permute-start.2) | collective-permute-done | bytes 524320 | tf_op jit(solution)/shard_map/ppermute | solution.py:389
  15.6 2.5 %collective-permute-start.7 = (f32[1,4,128,128]{3,2,1,0:T(8,128)S(1)}, f32[1,4,128,128]{3,2,1,0:T(8,128)S(1)}, u32[]{:S(2)}, u32[]{:S(2)}) collective-permute-start(f32[1,4,128,128]{3,2,1,0:T(8,128)S(1)} %get-tuple-element.43), channel_id=1, source_target_pairs={{15,1},{1,4},{4,9},{9,13},{13,15},{2,12},{12,8},{8,5},{5,0},{0,2},... | collective-permute-start | bytes 786440 | tf_op jit(solution)/shard_map/ppermute | solution.py:381
  18.0 2.8 %collective-permute-start.6 = (f32[1,4,128,128]{3,2,1,0:T(8,128)S(1)}, f32[1,4,128,128]{3,2,1,0:T(8,128)S(1)}, u32[]{:S(2)}, u32[]{:S(2)}) collective-permute-start(f32[1,4,128,128]{3,2,1,0:T(8,128)S(1)} %get-tuple-element.44), channel_id=1, source_target_pairs={{15,1},{1,4},{4,9},{9,13},{13,15},{2,12},{12,8},{8,5},{5,0},{0,2},... | collective-permute-start | bytes 786440 | tf_op jit(solution)/shard_map/ppermute | solution.py:381
  20.9 0.3 collective-permute-done.5.r3
  21.2 0.0 collective-permute-done.3.t1
  21.2 0.0 collective-permute-done.4.t2
  21.2 3.1 %early.1 = (bf16[1024,1024]{1,0:T(8,128)(2,1)S(1)}, bf16[1024,1024]{1,0:T(8,128)(2,1)S(1)}, bf16[512,1024]{1,0:T(8,128)(2,1)S(1)}, f32[256,1024]{1,0:T(8,128)S(1)}, s32[8,128]{1,0:T(8,128)S(1)}) custom-call(s32[8,9]{1,0:T(8,128)S(1)} %pad_add_fusion.table_ref, f32[2,4,128,128]{3,2,1,0:T(8,128)} %own_hbm.1, ...), custom_call_target="tpu_custom_call" | custom-call | tf_op jit(solution)/shard_map/early/pallas_call | solution.py:436
  24.3 0.0 collective-permute-done.7.r4a
  24.3 0.6 %collective-permute-start.8 = (f32[1,4,128,128]{3,2,1,0:T(8,128)S(1)}, f32[1,4,128,128]{3,2,1,0:T(8,128)S(1)}, u32[]{:S(2)}, u32[]{:S(2)}) collective-permute-start(f32[1,4,128,128]{3,2,1,0:T(8,128)S(1)} %collective-permute-done.7.r4a), channel_id=1, source_target_pairs={{1,0},{0,1},{17,16},{16,17},{3,2},{2,3},{19,18},{18,19},{5,4},{4,5... | collective-permute-start | bytes 786440 | tf_op jit(solution)/shard_map/ppermute | solution.py:381
  24.8 0.8 %waiting.1 = (bf16[1024,1024]{1,0:T(8,128)(2,1)S(1)}, bf16[1024,1024]{1,0:T(8,128)(2,1)S(1)}, f32[256,1024]{1,0:T(8,128)S(1)}) custom-call(s32[8,128]{1,0:T(8,128)S(1)} %get-tuple-element.26.notes_ref, f32[1,4,128,128]{3,2,1,0:T(8,128)S(1)} %collective-permute-done.7.r4a, ...), custom_call_target="tpu_custom_call", output_to_operand_aliasing={{0}: (2, {}), {1}: (3, {}), {2}: (5, {})} | custom-call | tf_op jit(solution)/shard_map/waiting/pallas_call | solution.py:458
  25.7 1.1 %collective-permute-done.6.r4b = f32[1,4,128,128]{3,2,1,0:T(8,128)S(1)} collective-permute-done((f32[1,4,128,128]{3,2,1,0:T(8,128)S(1)}, f32[1,4,128,128]{3,2,1,0:T(8,128)S(1)}, u32[]{:S(2)}, u32[]{:S(2)}) %collective-permute-start.6) | collective-permute-done | bytes 262176 | tf_op jit(solution)/shard_map/ppermute | solution.py:381
  26.8 0.0 collective-permute-done.8.t4a
  26.8 0.1 collective-permute-start.9
  26.9 0.0 collective-permute-done.10.t3
  26.9 1.5 %middle.1 = (bf16[1024,1024]{1,0:T(8,128)(2,1)S(1)}, bf16[1024,1024]{1,0:T(8,128)(2,1)S(1)}, f32[256,1024]{1,0:T(8,128)S(1)}) custom-call(s32[8,128]{1,0:T(8,128)S(1)} %get-tuple-element.26.notes_ref, f32[1,4,128,128]{3,2,1,0:T(8,128)S(1)} %collective-permute-done.6.r4b, ...), custom_call_target="tpu_custom_call", output_to_operand_aliasing={{0}: (4, {}), {1}: (5, {}), {2}: (7, {})} | custom-call | tf_op jit(solution)/shard_map/middle/pallas_call | solution.py:458
  28.4 0.0 collective-permute-done.9.t4b
  28.4 3.0 %late.1 = (f32[2,4,128,128]{3,2,1,0:T(8,128)}, bf16[1024,1024]{1,0:T(8,128)(2,1)S(1)}, bf16[1024,1024]{1,0:T(8,128)(2,1)S(1)}, f32[256,1024]{1,0:T(8,128)S(1)}) custom-call(s32[8,128]{1,0:T(8,128)S(1)} %get-tuple-element.26.notes_ref, f32[1,4,128,128]{3,2,1,0:T(8,128)S(1)} %collective-permute-done.9.t4b, ...), custom_call_target="tpu_custom_call", output_to_operand_aliasing={{1}: (2, {}), {2}: (3, {}), {3}: (5, {})} | custom-call | tf_op jit(solution)/shard_map/late/pallas_call | solution.py:472
  (6 shorter events, 0.1 us)
Async XLA Ops:
  0.0 10.0 %collective-permute-start = (f32[2,4,128,128]{3,2,1,0:T(8,128)}, f32[2,4,128,128]{3,2,1,0:T(8,128)S(1)}, u32[]{:S(2)}, u32[]{:S(2)}) collective-permute-start(f32[2,4,128,128]{3,2,1,0:T(8,128)} %own_hbm.1), channel_id=1, source_target_pairs={{3,1},{1,4},{4,9},{9,12},{12,8},{8,5},{5,0},{0,2},{2,3},{14,13},{1... | collective-permute-start | bytes 1572872 | tf_op jit(solution)/shard_map/ppermute | solution.py:381
  2.9 2.1 %collective-permute-start.1 = (f32[2,4,128,128]{3,2,1,0:T(8,128)}, f32[2,4,128,128]{3,2,1,0:T(8,128)S(1)}, u32[]{:S(2)}, u32[]{:S(2)}) collective-permute-start(f32[2,4,128,128]{3,2,1,0:T(8,128)} %own_hbm.1), channel_id=1, source_target_pairs={{1,0},{0,1},{17,16},{16,17},{3,2},{2,3},{19,18},{18,19},{5,4},{4,5... | collective-permute-start | bytes 1572872 | tf_op jit(solution)/shard_map/ppermute | solution.py:381
  5.1 10.5 %collective-permute-start.2 = (f32[2,4,128,128]{3,2,1,0:T(8,128)S(1)}, f32[2,4,128,128]{3,2,1,0:T(8,128)S(1)}, u32[]{:S(2)}, u32[]{:S(2)}) collective-permute-start(f32[2,4,128,128]{3,2,1,0:T(8,128)S(1)} %collective-permute-done.1.own_swap), channel_id=1, source_target_pairs={{1,4},{4,9},{9,13},{13,15},{12,8},{8,5},{5,0},{0,2},{17,20},{20,25... | collective-permute-start | bytes 1572872 | tf_op jit(solution)/shard_map/ppermute | solution.py:389
  10.0 11.2 %collective-permute-start.5 = (f32[2,4,128,128]{3,2,1,0:T(8,128)S(1)}, f32[2,4,128,128]{3,2,1,0:T(8,128)S(1)}, u32[]{:S(2)}, u32[]{:S(2)}) collective-permute-start(f32[2,4,128,128]{3,2,1,0:T(8,128)S(1)} %collective-permute-done.r1), channel_id=1, source_target_pairs={{15,1},{1,4},{4,9},{9,13},{13,15},{2,12},{12,8},{8,5},{5,0},{0,2},... | collective-permute-start | bytes 1572872 | tf_op jit(solution)/shard_map/ppermute | solution.py:381
  12.3 8.8 %collective-permute-start.3 = (f32[2,4,128,128]{3,2,1,0:T(8,128)S(1)}, f32[2,4,128,128]{3,2,1,0:T(8,128)S(1)}, u32[]{:S(2)}, u32[]{:S(2)}) collective-permute-start(f32[2,4,128,128]{3,2,1,0:T(8,128)S(1)} %collective-permute-done.r1), channel_id=1, source_target_pairs={{1,0},{0,1},{17,16},{16,17},{3,2},{2,3},{19,18},{18,19},{5,4},{4,5... | collective-permute-start | bytes 1572872 | tf_op jit(solution)/shard_map/ppermute | solution.py:381
  15.6 5.6 %collective-permute-start.4 = (f32[2,4,128,128]{3,2,1,0:T(8,128)S(1)}, f32[2,4,128,128]{3,2,1,0:T(8,128)S(1)}, u32[]{:S(2)}, u32[]{:S(2)}) collective-permute-start(f32[2,4,128,128]{3,2,1,0:T(8,128)S(1)} %collective-permute-done.2.r2), channel_id=1, source_target_pairs={{1,0},{0,1},{17,16},{16,17},{3,2},{2,3},{19,18},{18,19},{5,4},{4,5... | collective-permute-start | bytes 1572872 | tf_op jit(solution)/shard_map/ppermute | solution.py:381
  15.6 8.7 %collective-permute-start.7 = (f32[1,4,128,128]{3,2,1,0:T(8,128)S(1)}, f32[1,4,128,128]{3,2,1,0:T(8,128)S(1)}, u32[]{:S(2)}, u32[]{:S(2)}) collective-permute-start(f32[1,4,128,128]{3,2,1,0:T(8,128)S(1)} %get-tuple-element.43), channel_id=1, source_target_pairs={{15,1},{1,4},{4,9},{9,13},{13,15},{2,12},{12,8},{8,5},{5,0},{0,2},... | collective-permute-start | bytes 786440 | tf_op jit(solution)/shard_map/ppermute | solution.py:381
  18.0 8.7 %collective-permute-start.6 = (f32[1,4,128,128]{3,2,1,0:T(8,128)S(1)}, f32[1,4,128,128]{3,2,1,0:T(8,128)S(1)}, u32[]{:S(2)}, u32[]{:S(2)}) collective-permute-start(f32[1,4,128,128]{3,2,1,0:T(8,128)S(1)} %get-tuple-element.44), channel_id=1, source_target_pairs={{15,1},{1,4},{4,9},{9,13},{13,15},{2,12},{12,8},{8,5},{5,0},{0,2},... | collective-permute-start | bytes 786440 | tf_op jit(solution)/shard_map/ppermute | solution.py:381
  21.2 5.7 %collective-permute-start.10 = (f32[2,4,128,128]{3,2,1,0:T(8,128)S(1)}, f32[2,4,128,128]{3,2,1,0:T(8,128)S(1)}, u32[]{:S(2)}, u32[]{:S(2)}) collective-permute-start(f32[2,4,128,128]{3,2,1,0:T(8,128)S(1)} %collective-permute-done.5.r3), channel_id=1, source_target_pairs={{1,0},{0,1},{17,16},{16,17},{3,2},{2,3},{19,18},{18,19},{5,4},{4,5... | collective-permute-start | bytes 1572872 | tf_op jit(solution)/shard_map/ppermute | solution.py:381
  24.3 2.5 %collective-permute-start.8 = (f32[1,4,128,128]{3,2,1,0:T(8,128)S(1)}, f32[1,4,128,128]{3,2,1,0:T(8,128)S(1)}, u32[]{:S(2)}, u32[]{:S(2)}) collective-permute-start(f32[1,4,128,128]{3,2,1,0:T(8,128)S(1)} %collective-permute-done.7.r4a), channel_id=1, source_target_pairs={{1,0},{0,1},{17,16},{16,17},{3,2},{2,3},{19,18},{18,19},{5,4},{4,5... | collective-permute-start | bytes 786440 | tf_op jit(solution)/shard_map/ppermute | solution.py:381
  26.8 1.6 %collective-permute-start.9 = (f32[1,4,128,128]{3,2,1,0:T(8,128)S(1)}, f32[1,4,128,128]{3,2,1,0:T(8,128)S(1)}, u32[]{:S(2)}, u32[]{:S(2)}) collective-permute-start(f32[1,4,128,128]{3,2,1,0:T(8,128)S(1)} %collective-permute-done.6.r4b), channel_id=1, source_target_pairs={{1,0},{0,1},{17,16},{16,17},{3,2},{2,3},{19,18},{18,19},{5,4},{4,5... | collective-permute-start | bytes 786440 | tf_op jit(solution)/shard_map/ppermute | solution.py:381
